TPU v7x, 32 devices: a whole 2x2x4 slice. The times are simulated.
32 devices in a mesh: parts: 2 (over y), pts: 16 (over z, x, core).
Axes of the slice: x: 2, y: 2, z: 4, core: 2. Of those that a mesh axis runs over, the one named last changes fastest.
Arguments:
- rhs: bfloat16 [32768, 1024], P(('parts', 'pts')), parts along dimension 0, may hold values from -6 to 6
- near_blocks: bfloat16 [128, 12, 256, 256], P(('parts', 'pts')), parts along dimension 0, may hold values from -0.109375 to 0.109375
- near_ids: int32 [128, 12], P(('parts', 'pts')), parts along dimension 0, may hold values from 0 to 63, as said below
- near_count: int32 [128], P(('parts', 'pts')), parts along dimension 0, may hold values from 5 to 12, as said below
- source_basis: bfloat16 [128, 64, 256], P(('parts', 'pts')), parts along dimension 0, may hold values from -0.375 to 0.375
- target_basis: bfloat16 [128, 64, 256], P(('parts', 'pts')), parts along dimension 0, may hold values from -1.5 to 1.5
- leaf_transfer: bfloat16 [128, 64, 64], P(('parts', 'pts')), parts along dimension 0, may hold values from -0.5 to 0.5
- mid_transfer: bfloat16 [64, 64, 64], P(('parts', 'pts')), parts along dimension 0, may hold values from -0.5 to 0.5
- far_coupling: bfloat16 [32, 6, 64, 64], P(('parts', 'pts')), parts along dimension 0, may hold values from -0.3125 to 0.3125
- far_ids: int32 [32, 6], P(('parts', 'pts')), parts along dimension 0, may hold values from 0 to 15, as said below
Outputs:
- product: bfloat16 [32768, 1024], P(('parts', 'pts')), parts along dimension 0
There are 2 independent parts, one for each index of `parts`. A program takes and returns all parts, laid end to end along the dimension named above; each array names one. Nothing has to cross between parts.
Inputs may be any that keep to these rules, and one draw needn't show every extreme that they name: `near_ids`: entry 0 of box b's list is b, entries 0 to 3 are the boxes of b's own group, and the other entries are boxes of the groups at distance 1 to 2 around the loop of 16 groups, distinct within a list. The live entries of the boxes of one group name at most 2 distinct boxes of any other group, and exactly 2 for some pairs of groups. Entries at or after near_count are padding. `near_count`: box b with b % 4 == 0 has all 12 entries live. `far_ids`: each list names distinct groups at distance 3 to 7 around the loop of groups.
All inputs are finite; a program needn't handle non-finite values.
Results may differ from a plain program's by a relative error of at most 0.0041.
Values may be sent and summed in bfloat16 or wider, within the bound.
No kernel may reach another device: no remote copies, remote signals or barrier semaphores. Data moves between devices by JAX's collectives and lax.ppermute only.
A program may use at most 128 MiB of HBM per device.

v0:
```python
import jax
import jax.numpy as jnp
from jax import lax
from jax.sharding import PartitionSpec as P

LEAF = 256
RANK = 64
B_DEV = 4
REACH = 2
NEAR = 12
FARW = 5


def from_behind(value, axis, steps):
    count = lax.axis_size(axis)
    pairs = [(source, (source + steps) % count) for source in range(count)]
    return lax.ppermute(value, axis, pairs)


def on_device(
    rhs,
    near_blocks,
    near_ids,
    near_count,
    source_basis,
    target_basis,
    leaf_transfer,
    mid_transfer,
    far_coupling,
    far_ids,
):
    highest = lax.Precision.HIGHEST
    members = lax.axis_size("pts")
    position = lax.axis_index("pts")
    columns = rhs.shape[1]
    leaf_rows = rhs.reshape(B_DEV, LEAF, columns)
    slot_index = jnp.arange(NEAR, dtype=jnp.int32)
    live = slot_index[None, :] < near_count[:, None]
    offsets = [radius * sign for radius in range(1, REACH + 1) for sign in (1, -1)]
    pieces = {0: leaf_rows}
    for offset in offsets:
        pieces[-offset] = from_behind(leaf_rows, "pts", offset)
    neighbours = jnp.concatenate(
        [pieces[spot] for spot in range(-REACH, REACH + 1)]
        + [jnp.zeros((1, LEAF, columns), jnp.bfloat16)],
        axis=0,
    )
    owner = near_ids // B_DEV
    distance = jnp.mod(owner - position + REACH, members) - REACH
    local_index = (distance + REACH) * B_DEV + near_ids % B_DEV
    local_index = jnp.where(live, local_index, (2 * REACH + 1) * B_DEV)
    gathered = neighbours[local_index]
    near_part = jnp.einsum(
        "bnij,bnjr->bir", near_blocks, gathered, preferred_element_type=jnp.float32
    )
    leaf_coef = jnp.einsum(
        "bkl,blr->bkr", source_basis, leaf_rows, preferred_element_type=jnp.float32
    )
    mid_coef = jnp.einsum(
        "bpk,bkr->bpr", leaf_transfer.astype(jnp.float32), leaf_coef, precision=highest
    )
    mid_coef = mid_coef.reshape(B_DEV // 2, 2, RANK, columns).sum(axis=1)
    panel = jnp.einsum(
        "kab,kbr->ar", mid_transfer.astype(jnp.float32), mid_coef, precision=highest
    ).astype(jnp.bfloat16)[None]
    far_list = far_ids[0]
    chosen = jnp.zeros((far_list.shape[0], RANK, columns), jnp.float32)
    for radius in range(REACH + 1, REACH + FARW + 1):
        for sign in (1, -1):
            offset = radius * sign
            arrived = from_behind(panel, "pts", offset)
            source = jnp.mod(position - offset, members)
            matches = (far_list == source).astype(jnp.float32)
            chosen = chosen + matches[:, None, None] * arrived[0].astype(jnp.float32)[None]
    coupled = jnp.einsum(
        "fpq,fqr->pr",
        far_coupling[0],
        chosen.astype(jnp.bfloat16),
        preferred_element_type=jnp.float32,
    )
    mid_down = jnp.einsum(
        "kab,ar->kbr", mid_transfer.astype(jnp.float32), coupled, precision=highest
    )
    leaf_down = jnp.einsum(
        "jab,jar->jbr",
        leaf_transfer.astype(jnp.float32),
        jnp.repeat(mid_down, 2, axis=0),
        precision=highest,
    )
    far_part = jnp.einsum(
        "jkl,jkr->jlr", target_basis.astype(jnp.float32), leaf_down, precision=highest
    )
    return (near_part + far_part).reshape(B_DEV * LEAF, columns).astype(jnp.bfloat16)


def solution(mesh):
    return jax.shard_map(
        on_device,
        mesh=mesh,
        in_specs=(
            P(("parts", "pts"), None),
            P(("parts", "pts"), None, None, None),
            P(("parts", "pts"), None),
            P(("parts", "pts")),
            P(("parts", "pts"), None, None),
            P(("parts", "pts"), None, None),
            P(("parts", "pts"), None, None),
            P(("parts", "pts"), None, None),
            P(("parts", "pts"), None, None, None),
            P(("parts", "pts"), None),
        ),
        out_specs=P(("parts", "pts"), None),
        check_vma=False,
    )
```

profile of v0, /device:TPU:14, one launch (start us, length us, event | category | flops | bytes accessed | tf_op | source)
XLA Modules:
  0.0 213.8 jit_solution(10601174380631338488)
XLA Ops:
  0.0 0.0 copy-start
  0.0 0.0 copy-start.3
  0.0 0.0 copy-start.4
  0.0 2.2 %fusion.40 = f32[4,64,1024]{2,1,0:T(8,128)S(1)} fusion(bf16[4,64,256]{2,1,0:T(8,128)(2,1)} %param.14, bf16[4,256,1024]{2,1,0:T(8,128)(2,1)} %bitcast.101), kind=kOutput, calls=%fused_computation.84 | convolution fusion | flops 134217728 | bytes 3276800 | tf_op jit(solution)/shard_map/bkl,blr->bkr/dot_general | solution.py:56
  2.2 0.0 copy-done.3
  2.2 0.0 copy-start.7
  2.2 0.0 copy-start.5
  2.2 0.0 copy-start.6
  2.2 0.0 copy-start.2
  2.3 0.7 bitcast_reduce_fusion
  3.0 0.0 copy-done.4
  3.0 0.3 fusion.2
  3.3 2.1 collective-permute-start.13
  5.4 1.5 collective-permute-start.12
  6.9 0.0 collective-permute-start.11
  6.9 3.8 %collective-permute-start.10 = (bf16[1,64,1024]{2,1,0:T(8,128)(2,1)S(1)}, bf16[1,64,1024]{2,1,0:T(8,128)(2,1)S(1)}, u32[]{:S(2)}, u32[]{:S(2)}) collective-permute-start(bf16[1,64,1024]{2,1,0:T(8,128)(2,1)S(1)} %fusion.2), channel_id=1, source_target_pairs={{0,6},{1,7},{2,8},{3,9},{4,10},{5,11},{6,12},{7,13},{8,14},{9,15},... | collective-permute-start | bytes 393224 | tf_op jit(solution)/shard_map/ppermute | solution.py:17
  10.7 0.0 collective-permute-start.9
  10.7 0.0 copy-start.8
  10.7 0.0 copy-done.7
  10.8 0.0 copy-done.5
  10.8 0.0 copy-done.6
  10.8 0.1 compare_select_fusion
  10.9 0.1 copy.11
  11.0 0.1 reshape.137
  11.0 13.6 %collective-permute-done.13 = bf16[1,64,1024]{2,1,0:T(8,128)(2,1)S(1)} collective-permute-done((bf16[1,64,1024]{2,1,0:T(8,128)(2,1)S(1)}, bf16[1,64,1024]{2,1,0:T(8,128)(2,1)S(1)}, u32[]{:S(2)}, u32[]{:S(2)}) %collective-permute-start.13) | collective-permute-done | bytes 131104 | tf_op jit(solution)/shard_map/ppermute | solution.py:17
  24.6 0.0 collective-permute-start.8
  24.6 2.8 %collective-permute-done.12 = bf16[1,64,1024]{2,1,0:T(8,128)(2,1)S(1)} collective-permute-done((bf16[1,64,1024]{2,1,0:T(8,128)(2,1)S(1)}, bf16[1,64,1024]{2,1,0:T(8,128)(2,1)S(1)}, u32[]{:S(2)}, u32[]{:S(2)}) %collective-permute-start.12) | collective-permute-done | bytes 131104 | tf_op jit(solution)/shard_map/ppermute | solution.py:17
  27.4 0.0 collective-permute-start.7
  27.4 0.0 collective-permute-done.11
  27.4 2.1 collective-permute-start.6
  29.5 3.5 %collective-permute-done.10 = bf16[1,64,1024]{2,1,0:T(8,128)(2,1)S(1)} collective-permute-done((bf16[1,64,1024]{2,1,0:T(8,128)(2,1)S(1)}, bf16[1,64,1024]{2,1,0:T(8,128)(2,1)S(1)}, u32[]{:S(2)}, u32[]{:S(2)}) %collective-permute-start.10) | collective-permute-done | bytes 131104 | tf_op jit(solution)/shard_map/ppermute | solution.py:17
  33.1 0.0 collective-permute-start.5
  33.1 0.0 collective-permute-done.9
  33.1 2.7 %collective-permute-start.4 = (bf16[1,64,1024]{2,1,0:T(8,128)(2,1)S(1)}, bf16[1,64,1024]{2,1,0:T(8,128)(2,1)S(1)}, u32[]{:S(2)}, u32[]{:S(2)}) collective-permute-start(bf16[1,64,1024]{2,1,0:T(8,128)(2,1)S(1)} %fusion.2), channel_id=1, source_target_pairs={{0,3},{1,4},{2,5},{3,6},{4,7},{5,8},{6,9},{7,10},{8,11},{9,12},{10... | collective-permute-start | bytes 393224 | tf_op jit(solution)/shard_map/ppermute | solution.py:17
  35.8 0.1 collective-permute-done.8
  35.9 0.0 copy-done.2
  35.9 0.3 collective-permute-start.3
  36.2 0.0 collective-permute-done.7
  36.2 2.7 %collective-permute-start = (bf16[4,256,1024]{2,1,0:T(8,128)(2,1)S(1)}, bf16[4,256,1024]{2,1,0:T(8,128)(2,1)S(1)}, u32[]{:S(2)}, u32[]{:S(2)}) collective-permute-start(bf16[4,256,1024]{2,1,0:T(8,128)(2,1)S(1)} %bitcast.103), channel_id=1, source_target_pairs={{0,2},{1,3},{2,4},{3,5},{4,6},{5,7},{6,8},{7,9},{8,10},{9,11},{10,... | collective-permute-start | bytes 6291464 | tf_op jit(solution)/shard_map/ppermute | solution.py:17
  38.9 1.2 collective-permute-done.6
  40.1 0.0 collective-permute-start.1
  40.1 1.3 collective-permute-done.5
  41.4 0.7 collective-permute-start.2
  42.1 0.7 collective-permute-done.4
  42.8 0.0 copy-done.8
  42.8 1.5 convolution_bitcast_fusion
  44.4 0.4 fusion.41
  44.8 0.1 broadcast_in_dim.16
  44.9 0.6 fusion.42
  45.5 0.0 copy-done
  45.5 3.9 %fusion.43 = f32[4,1024,256]{1,2,0:T(8,128)} fusion(f32[4,1024,64]{1,2,0:T(8,128)S(1)} %fusion.42, bf16[4,64,256]{2,1,0:T(8,128)(2,1)S(1)} %copy-done), kind=kOutput, calls=%fused_computation.87 | convolution fusion | flops 805306368 | bytes 5373952 | tf_op jit(solution)/shard_map/jkl,jkr->jlr/dot_general | solution.py:90
  49.4 103.0 %collective-permute-done = bf16[4,256,1024]{2,1,0:T(8,128)(2,1)S(1)} collective-permute-done((bf16[4,256,1024]{2,1,0:T(8,128)(2,1)S(1)}, bf16[4,256,1024]{2,1,0:T(8,128)(2,1)S(1)}, u32[]{:S(2)}, u32[]{:S(2)}) %collective-permute-start) | collective-permute-done | bytes 2097184 | tf_op jit(solution)/shard_map/ppermute | solution.py:17
  152.4 1.6 constant_dynamic-update-slice_fusion.4
  154.0 21.2 %collective-permute-done.1 = bf16[4,256,1024]{2,1,0:T(8,128)(2,1)S(1)} collective-permute-done((bf16[4,256,1024]{2,1,0:T(8,128)(2,1)S(1)}, bf16[4,256,1024]{2,1,0:T(8,128)(2,1)S(1)}, u32[]{:S(2)}, u32[]{:S(2)}) %collective-permute-start.1) | collective-permute-done | bytes 2097184 | tf_op jit(solution)/shard_map/ppermute | solution.py:17
  175.2 1.5 constant_dynamic-update-slice_fusion.3
  176.7 1.6 constant_dynamic-update-slice_fusion.2
  178.3 0.0 collective-permute-done.2
  178.3 1.5 constant_dynamic-update-slice_fusion.1
  179.8 0.0 collective-permute-done.3
  179.8 1.5 constant_dynamic-update-slice_fusion
  181.2 0.9 broadcast_dynamic-update-slice_fusion
  182.1 14.0 %gather_fusion = bf16[48,256,1024]{2,1,0:T(8,128)(2,1)} fusion(bf16[21,256,1024]{2,1,0:T(8,128)(2,1)} %broadcast_dynamic-update-slice_fusion, s32[1024]{0:T(1024)S(1)} %pad_clamp_fusion), kind=kCustom, calls=%fused_computation | custom fusion | bytes 50331840 | tf_op jit(solution)/shard_map/gather | solution.py:52
  196.1 17.6 %fusion = bf16[4,1024,256]{1,2,0:T(8,128)(2,1)} fusion(f32[4,1024,256]{1,2,0:T(8,128)} %fusion.43, bf16[4,12,256,256]{3,2,1,0:T(8,128)(2,1)} %param.11, bf16[4,12,256,1024]{3,2,1,0:T(8,128)(2,1)} %bitcast.100), kind=kOutput, calls=%fused_computation.2 | convolution fusion | flops 6444548096 | bytes 37748736 | tf_op jit(solution)/shard_map/bnij,bnjr->bir/dot_general | solution.py:53
  213.8 0.0 copy-done.1
  (13 shorter events, 0.2 us)
Async XLA Ops:
  0.0 45.5 %copy-start = (bf16[4,64,256]{2,1,0:T(8,128)(2,1)S(1)}, bf16[4,64,256]{2,1,0:T(8,128)(2,1)}, u32[]{:S(2)}) copy-start(bf16[4,64,256]{2,1,0:T(8,128)(2,1)} %param.15) | copy-start | bytes 393220
  0.0 2.2 %copy-start.3 = (bf16[4,64,64]{2,1,0:T(8,128)(2,1)S(1)}, bf16[4,64,64]{2,1,0:T(8,128)(2,1)}, u32[]{:S(2)}) copy-start(bf16[4,64,64]{2,1,0:T(8,128)(2,1)} %param.16) | copy-start | bytes 98308
  0.0 3.0 %copy-start.4 = (bf16[2,64,64]{2,1,0:T(8,128)(2,1)S(1)}, bf16[2,64,64]{2,1,0:T(8,128)(2,1)}, u32[]{:S(2)}) copy-start(bf16[2,64,64]{2,1,0:T(8,128)(2,1)} %param.17) | copy-start | bytes 49156
  2.2 8.5 %copy-start.7 = (s32[1,6]{1,0:T(1,128)S(1)}, s32[1,6]{1,0:T(1,128)}, u32[]{:S(2)}) copy-start(s32[1,6]{1,0:T(1,128)} %param.19) | copy-start | bytes 76
  2.2 8.5 %copy-start.5 = (s32[4,12]{1,0:T(4,128)S(1)}, s32[4,12]{1,0:T(4,128)}, u32[]{:S(2)}) copy-start(s32[4,12]{1,0:T(4,128)} %param.12) | copy-start | bytes 580
  2.2 8.5 %copy-start.6 = (s32[4]{0:T(128)S(1)}, s32[4]{0:T(128)}, u32[]{:S(2)}) copy-start(s32[4]{0:T(128)} %param.13) | copy-start | bytes 52
  2.2 33.6 %copy-start.2 = (bf16[1024,1024]{1,0:T(8,128)(2,1)S(1)}, bf16[1024,1024]{1,0:T(8,128)(2,1)}, u32[]{:S(2)}) copy-start(bf16[1024,1024]{1,0:T(8,128)(2,1)} %param.10) | copy-start | bytes 6291460
  3.3 21.3 %collective-permute-start.13 = (bf16[1,64,1024]{2,1,0:T(8,128)(2,1)S(1)}, bf16[1,64,1024]{2,1,0:T(8,128)(2,1)S(1)}, u32[]{:S(2)}, u32[]{:S(2)}) collective-permute-start(bf16[1,64,1024]{2,1,0:T(8,128)(2,1)S(1)} %fusion.2), channel_id=1, source_target_pairs={{0,9},{1,10},{2,11},{3,12},{4,13},{5,14},{6,15},{7,0},{8,1},{9,2},... | collective-permute-start | bytes 393224 | tf_op jit(solution)/shard_map/ppermute | solution.py:17
  5.4 22.0 %collective-permute-start.12 = (bf16[1,64,1024]{2,1,0:T(8,128)(2,1)S(1)}, bf16[1,64,1024]{2,1,0:T(8,128)(2,1)S(1)}, u32[]{:S(2)}, u32[]{:S(2)}) collective-permute-start(bf16[1,64,1024]{2,1,0:T(8,128)(2,1)S(1)} %fusion.2), channel_id=1, source_target_pairs={{0,7},{1,8},{2,9},{3,10},{4,11},{5,12},{6,13},{7,14},{8,15},{9,0},... | collective-permute-start | bytes 393224 | tf_op jit(solution)/shard_map/ppermute | solution.py:17
  6.9 20.5 %collective-permute-start.11 = (bf16[1,64,1024]{2,1,0:T(8,128)(2,1)S(1)}, bf16[1,64,1024]{2,1,0:T(8,128)(2,1)S(1)}, u32[]{:S(2)}, u32[]{:S(2)}) collective-permute-start(bf16[1,64,1024]{2,1,0:T(8,128)(2,1)S(1)} %fusion.2), channel_id=1, source_target_pairs={{0,10},{1,11},{2,12},{3,13},{4,14},{5,15},{6,0},{7,1},{8,2},{9,3},... | collective-permute-start | bytes 393224 | tf_op jit(solution)/shard_map/ppermute | solution.py:17
  6.9 26.2 %collective-permute-start.10 = (bf16[1,64,1024]{2,1,0:T(8,128)(2,1)S(1)}, bf16[1,64,1024]{2,1,0:T(8,128)(2,1)S(1)}, u32[]{:S(2)}, u32[]{:S(2)}) collective-permute-start(bf16[1,64,1024]{2,1,0:T(8,128)(2,1)S(1)} %fusion.2), channel_id=1, source_target_pairs={{0,6},{1,7},{2,8},{3,9},{4,10},{5,11},{6,12},{7,13},{8,14},{9,15},... | collective-permute-start | bytes 393224 | tf_op jit(solution)/shard_map/ppermute | solution.py:17
  10.7 22.4 %collective-permute-start.9 = (bf16[1,64,1024]{2,1,0:T(8,128)(2,1)S(1)}, bf16[1,64,1024]{2,1,0:T(8,128)(2,1)S(1)}, u32[]{:S(2)}, u32[]{:S(2)}) collective-permute-start(bf16[1,64,1024]{2,1,0:T(8,128)(2,1)S(1)} %fusion.2), channel_id=1, source_target_pairs={{0,11},{1,12},{2,13},{3,14},{4,15},{5,0},{6,1},{7,2},{8,3},{9,4},{... | collective-permute-start | bytes 393224 | tf_op jit(solution)/shard_map/ppermute | solution.py:17
  10.7 32.1 %copy-start.8 = (bf16[1,6,64,64]{3,2,1,0:T(8,128)(2,1)S(1)}, bf16[1,6,64,64]{3,2,1,0:T(8,128)(2,1)}, u32[]{:S(2)}) copy-start(bf16[1,6,64,64]{3,2,1,0:T(8,128)(2,1)} %param.18) | copy-start | bytes 147460
  24.6 11.3 %collective-permute-start.8 = (bf16[1,64,1024]{2,1,0:T(8,128)(2,1)S(1)}, bf16[1,64,1024]{2,1,0:T(8,128)(2,1)S(1)}, u32[]{:S(2)}, u32[]{:S(2)}) collective-permute-start(bf16[1,64,1024]{2,1,0:T(8,128)(2,1)S(1)} %fusion.2), channel_id=1, source_target_pairs={{0,5},{1,6},{2,7},{3,8},{4,9},{5,10},{6,11},{7,12},{8,13},{9,14},{... | collective-permute-start | bytes 393224 | tf_op jit(solution)/shard_map/ppermute | solution.py:17
  27.4 8.8 %collective-permute-start.7 = (bf16[1,64,1024]{2,1,0:T(8,128)(2,1)S(1)}, bf16[1,64,1024]{2,1,0:T(8,128)(2,1)S(1)}, u32[]{:S(2)}, u32[]{:S(2)}) collective-permute-start(bf16[1,64,1024]{2,1,0:T(8,128)(2,1)S(1)} %fusion.2), channel_id=1, source_target_pairs={{0,12},{1,13},{2,14},{3,15},{4,0},{5,1},{6,2},{7,3},{8,4},{9,5},{1... | collective-permute-start | bytes 393224 | tf_op jit(solution)/shard_map/ppermute | solution.py:17
  27.4 12.6 %collective-permute-start.6 = (bf16[1,64,1024]{2,1,0:T(8,128)(2,1)S(1)}, bf16[1,64,1024]{2,1,0:T(8,128)(2,1)S(1)}, u32[]{:S(2)}, u32[]{:S(2)}) collective-permute-start(bf16[1,64,1024]{2,1,0:T(8,128)(2,1)S(1)} %fusion.2), channel_id=1, source_target_pairs={{0,4},{1,5},{2,6},{3,7},{4,8},{5,9},{6,10},{7,11},{8,12},{9,13},{1... | collective-permute-start | bytes 393224 | tf_op jit(solution)/shard_map/ppermute | solution.py:17
  33.1 8.3 %collective-permute-start.5 = (bf16[1,64,1024]{2,1,0:T(8,128)(2,1)S(1)}, bf16[1,64,1024]{2,1,0:T(8,128)(2,1)S(1)}, u32[]{:S(2)}, u32[]{:S(2)}) collective-permute-start(bf16[1,64,1024]{2,1,0:T(8,128)(2,1)S(1)} %fusion.2), channel_id=1, source_target_pairs={{0,13},{1,14},{2,15},{3,0},{4,1},{5,2},{6,3},{7,4},{8,5},{9,6},{10... | collective-permute-start | bytes 393224 | tf_op jit(solution)/shard_map/ppermute | solution.py:17
  33.1 9.7 %collective-permute-start.4 = (bf16[1,64,1024]{2,1,0:T(8,128)(2,1)S(1)}, bf16[1,64,1024]{2,1,0:T(8,128)(2,1)S(1)}, u32[]{:S(2)}, u32[]{:S(2)}) collective-permute-start(bf16[1,64,1024]{2,1,0:T(8,128)(2,1)S(1)} %fusion.2), channel_id=1, source_target_pairs={{0,3},{1,4},{2,5},{3,6},{4,7},{5,8},{6,9},{7,10},{8,11},{9,12},{10... | collective-permute-start | bytes 393224 | tf_op jit(solution)/shard_map/ppermute | solution.py:17
  35.9 143.9 %collective-permute-start.3 = (bf16[4,256,1024]{2,1,0:T(8,128)(2,1)S(1)}, bf16[4,256,1024]{2,1,0:T(8,128)(2,1)S(1)}, u32[]{:S(2)}, u32[]{:S(2)}) collective-permute-start(bf16[4,256,1024]{2,1,0:T(8,128)(2,1)S(1)} %bitcast.102), channel_id=1, source_target_pairs={{0,14},{1,15},{2,0},{3,1},{4,2},{5,3},{6,4},{7,5},{8,6},{9,7},{10,... | collective-permute-start | bytes 6291464 | tf_op jit(solution)/shard_map/ppermute | solution.py:17
  36.2 116.2 %collective-permute-start = (bf16[4,256,1024]{2,1,0:T(8,128)(2,1)S(1)}, bf16[4,256,1024]{2,1,0:T(8,128)(2,1)S(1)}, u32[]{:S(2)}, u32[]{:S(2)}) collective-permute-start(bf16[4,256,1024]{2,1,0:T(8,128)(2,1)S(1)} %bitcast.103), channel_id=1, source_target_pairs={{0,2},{1,3},{2,4},{3,5},{4,6},{5,7},{6,8},{7,9},{8,10},{9,11},{10,... | collective-permute-start | bytes 6291464 | tf_op jit(solution)/shard_map/ppermute | solution.py:17
  40.1 135.1 %collective-permute-start.1 = (bf16[4,256,1024]{2,1,0:T(8,128)(2,1)S(1)}, bf16[4,256,1024]{2,1,0:T(8,128)(2,1)S(1)}, u32[]{:S(2)}, u32[]{:S(2)}) collective-permute-start(bf16[4,256,1024]{2,1,0:T(8,128)(2,1)S(1)} %bitcast.104), channel_id=1, source_target_pairs={{0,1},{1,2},{2,3},{3,4},{4,5},{5,6},{6,7},{7,8},{8,9},{9,10},{10,1... | collective-permute-start | bytes 6291464 | tf_op jit(solution)/shard_map/ppermute | solution.py:17
  41.4 136.9 %collective-permute-start.2 = (bf16[4,256,1024]{2,1,0:T(8,128)(2,1)S(1)}, bf16[4,256,1024]{2,1,0:T(8,128)(2,1)S(1)}, u32[]{:S(2)}, u32[]{:S(2)}) collective-permute-start(bf16[4,256,1024]{2,1,0:T(8,128)(2,1)S(1)} %bitcast.105), channel_id=1, source_target_pairs={{0,15},{1,0},{2,1},{3,2},{4,3},{5,4},{6,5},{7,6},{8,7},{9,8},{10,9... | collective-permute-start | bytes 6291464 | tf_op jit(solution)/shard_map/ppermute | solution.py:17
  196.1 17.6 %copy-start.1 = (bf16[4,64,256]{2,1,0:T(8,128)(2,1)S(1)}, bf16[4,64,256]{2,1,0:T(8,128)(2,1)}, u32[]{:S(2)}) copy-start(bf16[4,64,256]{2,1,0:T(8,128)(2,1)} %param.15) | copy-start | bytes 393220
where the time goes:
time: 214 us
  waiting for transfers between devices  147 us (69%)
  matrix products  27.2 us (13%)
  local copies, waits for them, and re-layouts  22.8 us (11%)
  starting transfers between devices  15.9 us (7%)
    ppermute x14, waiting for transfers between devices, from_behind(): return lax.ppermute(value, axis, pairs)  147 us
    dot_general x1, matrix products, on_device(): jnp.einsum('bnij,bnjr->bir', near_blocks, gathered, preferred_element_typ...  17.6 us
    ppermute x14, starting transfers between devices, from_behind(): return lax.ppermute(value, axis, pairs)  15.9 us
    gather x1, local copies, waits for them, and re-layouts, on_device(): gathered = neighbours[local_index]  14 us
    unnamed x24, local copies, waits for them, and re-layouts  7.71 us
  transfers between devices with their start and end apart: 14, of which 9 were waited for; matrix products, arithmetic and copies ran while one was open for 6% of the time, Pallas kernels for 0%

commit v1 on v0

v1 whole, which is shorter than its diff:
```python
import functools

import jax
import jax.numpy as jnp
from jax import lax
from jax.experimental import pallas as pl
from jax.experimental.pallas import tpu as pltpu
from jax.sharding import PartitionSpec as P

LEAF = 256
RANK = 64
B_DEV = 4
NEAR = 12
ROWS = B_DEV * LEAF
PIECES = 5
SLABS = ((0, 256), (256, 256), (512, 256), (768, 128), (896, 128))
SLOTS = ((3, 4, 0, 1, 2), (3, 1, 0, 4, 2), (2, 4, 0, 1, 3), (2, 1, 0, 4, 3))
MIB = 1024 * 1024


def split(value):
    high = value.astype(jnp.bfloat16)
    low = (value - high.astype(jnp.float32)).astype(jnp.bfloat16)
    return high, low


def dot(a, b):
    return jnp.dot(a, b, preferred_element_type=jnp.float32)


def dot32(a, b):
    return jnp.dot(
        a.astype(jnp.float32),
        b.astype(jnp.float32),
        precision=lax.Precision.HIGHEST,
        preferred_element_type=jnp.float32,
    )


def up_kernel(rhs_ref, source_ref, target_ref, leaf_ref, mid_ref, panel_ref, down_ref):
    ups = []
    for box in range(B_DEV):
        chain = dot32(mid_ref[box // 2], leaf_ref[box])
        ups.append(dot32(chain, source_ref[box]))
        high, low = split(dot32(chain, target_ref[box]).T)
        down_ref[box] = jnp.concatenate([high, low, high], axis=1)
    high, low = split(jnp.concatenate(ups, axis=1))
    both = dot(jnp.concatenate([high, low], axis=0), rhs_ref[...])
    panel_ref[...] = (both[:RANK] + both[RANK:]).astype(jnp.bfloat16)


def up(rhs, source_basis, target_basis, leaf_transfer, mid_transfer):
    columns = rhs.shape[1]
    return pl.pallas_call(
        up_kernel,
        out_shape=(
            jax.ShapeDtypeStruct((RANK, columns), jnp.bfloat16),
            jax.ShapeDtypeStruct((B_DEV, LEAF, 3 * RANK), jnp.bfloat16),
        ),
        compiler_params=pltpu.CompilerParams(vmem_limit_bytes=24 * MIB),
        cost_estimate=pl.CostEstimate(
            flops=2 * 2 * RANK * ROWS * columns, bytes_accessed=4 * MIB, transcendentals=0
        ),
    )(rhs, source_basis, target_basis, leaf_transfer, mid_transfer)


def slab_kernel(
    start,
    width,
    entry_ref,
    far_ref,
    near_ref,
    own_ref,
    core_ref,
    across_ref,
    along_ref,
    other_ref,
    panels_ref,
    coupling_ref,
    down_ref,
    *rest,
):
    out_ref, held, chosen, coupled, sems = rest[-5:]
    far = far_ref.shape[0]
    box = pl.program_id(0)

    @pl.when(box == 0)
    def _():
        columns = pl.ds(start, width)
        copies = [
            pltpu.make_async_copy(
                panels_ref.at[far_ref[f], :, columns], chosen.at[pl.ds(f * RANK, RANK)], sems.at[PIECES + f]
            )
            for f in range(far)
        ]
        for piece, ref in enumerate((own_ref, core_ref, across_ref, along_ref, other_ref)):
            source = ref.at[:, columns] if piece < 2 else ref
            copies.append(
                pltpu.make_async_copy(source, held.at[pl.ds(piece * ROWS, ROWS)], sems.at[piece])
            )
        for copy in copies:
            copy.start()
        held[pl.ds(PIECES * ROWS, LEAF)] = jnp.zeros((LEAF, width), jnp.bfloat16)
        for copy in copies:
            copy.wait()
        high, low = split(
            dot(jnp.concatenate([coupling_ref[f] for f in range(far)], axis=1), chosen[...])
        )
        coupled[...] = jnp.concatenate([high, high, low], axis=0)

    total = dot(down_ref[0], coupled[...])
    left = jnp.concatenate([near_ref[0, n] for n in range(NEAR)], axis=1)
    right = jnp.concatenate(
        [held[pl.ds(pl.multiple_of(entry_ref[box, n] * LEAF, LEAF), LEAF)] for n in range(NEAR)], axis=0
    )
    out_ref[...] = (total + dot(left, right)).astype(jnp.bfloat16)


def slab(start, width, entry, far_list, near_blocks, pieces, panels, coupling, down, product):
    rows, columns = pieces[0].shape
    far = far_list.shape[0]
    anywhere = pl.BlockSpec(memory_space=pl.ANY)
    in_specs = [
        pl.BlockSpec((1, NEAR, LEAF, LEAF), lambda b, *_: (b, 0, 0, 0)),
        *[anywhere] * (PIECES + 1),
        pl.BlockSpec((far, RANK, RANK), lambda b, *_: (0, 0, 0)),
        pl.BlockSpec((1, LEAF, 3 * RANK), lambda b, *_: (b, 0, 0)),
    ]
    operands = [near_blocks, *pieces, panels, coupling, down]
    aliases = {}
    if product is not None:
        aliases = {2 + len(operands): 0}
        in_specs.append(anywhere)
        operands.append(product)
    return pl.pallas_call(
        functools.partial(slab_kernel, start, width),
        grid_spec=pltpu.PrefetchScalarGridSpec(
            num_scalar_prefetch=2,
            grid=(B_DEV,),
            in_specs=in_specs,
            out_specs=pl.BlockSpec((LEAF, width), lambda b, *_: (b, start // width)),
            scratch_shapes=[
                pltpu.VMEM((PIECES * ROWS + LEAF, width), jnp.bfloat16),
                pltpu.VMEM((far * RANK, width), jnp.bfloat16),
                pltpu.VMEM((3 * RANK, width), jnp.bfloat16),
                pltpu.SemaphoreType.DMA((PIECES + far,)),
            ],
        ),
        out_shape=jax.ShapeDtypeStruct((rows, columns), jnp.bfloat16),
        input_output_aliases=aliases,
        compiler_params=pltpu.CompilerParams(vmem_limit_bytes=24 * MIB),
        cost_estimate=pl.CostEstimate(
            flops=2 * B_DEV * NEAR * LEAF * LEAF * width, bytes_accessed=10 * MIB, transcendentals=0
        ),
    )(entry, far_list, *operands)


def on_device(
    rhs,
    near_blocks,
    near_ids,
    near_count,
    source_basis,
    target_basis,
    leaf_transfer,
    mid_transfer,
    far_coupling,
    far_ids,
):
    members = lax.axis_size("pts")
    position = lax.axis_index("pts")
    across_pairs = [(i, i ^ 2) for i in range(members)]
    core_pairs = [(i, i ^ 1) for i in range(members)]
    along_pairs = [(i, (i + (-4 if i & 2 else 4)) % members) for i in range(members)]

    across = [lax.ppermute(rhs[:, start : start + width], "pts", across_pairs) for start, width in SLABS]
    core = lax.ppermute(rhs, "pts", core_pairs)
    panel, down = up(rhs, source_basis, target_basis, leaf_transfer, mid_transfer)
    panels = lax.all_gather(panel, "pts")

    distance = jnp.mod(near_ids // B_DEV - position + 2, members)
    slots = jnp.asarray(SLOTS, jnp.int32)[position % 4]
    held_in = sum(jnp.where(distance == d, slots[d], 0) for d in range(5))
    live = jnp.arange(NEAR, dtype=jnp.int32)[None, :] < near_count[:, None]
    entry = jnp.where(live, held_in * B_DEV + near_ids % B_DEV, PIECES * B_DEV)

    sends_across = (position % 4 == 0) | (position % 4 == 3)
    product = None
    for (start, width), arrived in zip(SLABS, across):
        along = lax.ppermute(arrived, "pts", along_pairs)
        other = lax.ppermute(jnp.where(sends_across, arrived, along), "pts", core_pairs)
        product = slab(
            start,
            width,
            entry,
            far_ids[0],
            near_blocks,
            (rhs, core, arrived, along, other),
            panels,
            far_coupling[0],
            down,
            product,
        )
    return product


def solution(mesh):
    return jax.shard_map(
        on_device,
        mesh=mesh,
        in_specs=(
            P(("parts", "pts"), None),
            P(("parts", "pts"), None, None, None),
            P(("parts", "pts"), None),
            P(("parts", "pts")),
            P(("parts", "pts"), None, None),
            P(("parts", "pts"), None, None),
            P(("parts", "pts"), None, None),
            P(("parts", "pts"), None, None),
            P(("parts", "pts"), None, None, None),
            P(("parts", "pts"), None),
        ),
        out_specs=P(("parts", "pts"), None),
        check_vma=False,
    )
```

time: 214 us -> 155 us (0.72)
  the two profiles are of different devices: /device:TPU:14 before, /device:TPU:0 now
where the time goes in v1:
time: 155 us; the launch traced here: 154 us
  waiting for transfers between devices  71.8 us (46%)
  Pallas kernels  29.5 us (19%)
  local copies, waits for them, and re-layouts  16.1 us (10%)
  between operations  13.6 us (9%)
  starting transfers between devices  13.3 us (9%)
  other arithmetic  9.6 us (6%)
    ppermute x5, waiting for transfers between devices, on_device(): lax.ppermute(rhs[:, start:start + width], 'pts', across_pairs)  36.4 us
    ppermute x5, waiting for transfers between devices, on_device(): along = lax.ppermute(arrived, 'pts', along_pairs)  35.4 us
    pallas_call x5, Pallas kernels, slab(): pl.pallas_call(functools.partial(slab_kernel, start, width), grid_spec=pl...  27.2 us
    unnamed x36, local copies, waits for them, and re-layouts  12.7 us
    ppermute x5, starting transfers between devices, on_device(): lax.ppermute(rhs[:, start:start + width], 'pts', across_pairs)  7.48 us
    select_n x5, other arithmetic, on_device(): jnp.where(sends_across, arrived, along)  6.42 us
    ppermute x5, starting transfers between devices, on_device(): along = lax.ppermute(arrived, 'pts', along_pairs)  5.32 us
    select_n x1, other arithmetic, on_device(): entry = jnp.where(live, held_in * B_DEV + near_ids % B_DEV, PIECES * B_DEV)  3.18 us
  transfers between devices with their start and end apart: 17, of which 6 were waited for; matrix products, arithmetic and copies ran while one was open for 8% of the time, Pallas kernels for 14%

profile of v1, /device:TPU:0, one launch (start us, length us, event | category | flops | bytes accessed | tf_op | source)
XLA Modules:
  0.0 153.8 jit_solution(5202001248987306843)
XLA Ops:
  6.5 1.6 %copy-done.1 = bf16[1024,1024]{1,0:T(8,128)(2,1)S(1)} copy-done((bf16[1024,1024]{1,0:T(8,128)(2,1)S(1)}, bf16[1024,1024]{1,0:T(8,128)(2,1)}, u32[]{:S(2)}) %copy-start.1) | copy-done | bytes 2097176
  8.1 0.9 copy-done.11
  9.0 0.9 copy-done.12
  9.9 0.8 copy-done.13
  10.8 0.8 copy-done.14
  11.5 2.2 %shard_map.109 = (bf16[64,1024]{1,0:T(8,128)(2,1)}, bf16[4,256,192]{2,1,0:T(8,128)(2,1)S(1)}) custom-call(bf16[1024,1024]{1,0:T(8,128)(2,1)S(1)} %copy-done.1, bf16[4,64,256]{2,1,0:T(8,128)(2,1)S(1)} %copy-done.11, bf16[4,64,256]{2,1,0:T(8,128)(2,1)S(1)} %copy-done.12, bf16[4,64,64]{2,1,0:T(8,128)(2,1)S(1)} %copy-done.13, bf16[2,64,64]{2,1,0:T(8,128)(2,1)S(1)} %copy-done.14), custom_call_target="tpu_custom_call" | custom-call | flops 268435456 | bytes 4194304 | tf_op jit(solution)/shard_map/pallas_call | solution.py:54
  13.8 0.0 all-gather.3.cloned.1.call-update
  13.8 0.0 copy-start.16
  13.8 0.0 copy-start.17
  13.8 1.2 fusion.6
  15.1 2.9 %collective-permute-start.13 = (bf16[1024,256]{1,0:T(8,128)(2,1)}, bf16[1024,256]{1,0:T(8,128)(2,1)}, u32[]{:S(2)}, u32[]{:S(2)}) collective-permute-start(bf16[1024,256]{1,0:T(8,128)(2,1)} %get-tuple-element.9), channel_id=1, source_target_pairs={{0,2},{1,3},{2,0},{3,1},{4,6},{5,7},{6,4},{7,5},{8,10},{9,11},{10,... | collective-permute-start | bytes 1572872 | tf_op jit(solution)/shard_map/ppermute | solution.py:176
  18.0 0.0 collective-permute-start
  18.0 0.0 collective-permute-start.10
  18.0 0.9 fusion.7
  18.9 2.0 %collective-permute-start.4 = (bf16[1024,128]{1,0:T(8,128)(2,1)}, bf16[1024,128]{1,0:T(8,128)(2,1)}, u32[]{:S(2)}, u32[]{:S(2)}) collective-permute-start(bf16[1024,128]{1,0:T(8,128)(2,1)} %get-tuple-element.12), channel_id=1, source_target_pairs={{0,2},{1,3},{2,0},{3,1},{4,6},{5,7},{6,4},{7,5},{8,10},{9,11},{10,... | collective-permute-start | bytes 786440 | tf_op jit(solution)/shard_map/ppermute | solution.py:176
  20.9 0.0 collective-permute-start.1
  20.9 0.7 constant_dynamic-slice_fusion
  21.6 32.9 %collective-permute-done.4.across_ref = bf16[1024,128]{1,0:T(8,128)(2,1)} collective-permute-done((bf16[1024,128]{1,0:T(8,128)(2,1)}, bf16[1024,128]{1,0:T(8,128)(2,1)}, u32[]{:S(2)}, u32[]{:S(2)}) %collective-permute-start.4) | collective-permute-done | bytes 262176 | tf_op jit(solution)/shard_map/ppermute | solution.py:176
  54.5 2.5 %collective-permute-start.7 = (bf16[1024,256]{1,0:T(8,128)(2,1)}, bf16[1024,256]{1,0:T(8,128)(2,1)}, u32[]{:S(2)}, u32[]{:S(2)}) collective-permute-start(bf16[1024,256]{1,0:T(8,128)(2,1)} %get-tuple-element.11), channel_id=1, source_target_pairs={{0,2},{1,3},{2,0},{3,1},{4,6},{5,7},{6,4},{7,5},{8,10},{9,11},{10,... | collective-permute-start | bytes 1572872 | tf_op jit(solution)/shard_map/ppermute | solution.py:176
  57.0 3.5 %collective-permute-done.1.across_ref = bf16[1024,128]{1,0:T(8,128)(2,1)S(1)} collective-permute-done((bf16[1024,128]{1,0:T(8,128)(2,1)}, bf16[1024,128]{1,0:T(8,128)(2,1)S(1)}, u32[]{:S(2)}, u32[]{:S(2)}) %collective-permute-start.1) | collective-permute-done | bytes 262176 | tf_op jit(solution)/shard_map/ppermute | solution.py:176
  60.4 2.2 %collective-permute-start.5 = (bf16[1024,128]{1,0:T(8,128)(2,1)}, bf16[1024,128]{1,0:T(8,128)(2,1)}, u32[]{:S(2)}, u32[]{:S(2)}) collective-permute-start(bf16[1024,128]{1,0:T(8,128)(2,1)} %collective-permute-done.4.across_ref), channel_id=1, source_target_pairs={{0,4},{1,5},{2,14},{3,15},{4,8},{5,9},{6,2},{7,3},{8,12},{9,13},{1... | collective-permute-start | bytes 786440 | tf_op jit(solution)/shard_map/ppermute | solution.py:190
  62.6 0.0 collective-permute-done.13.across_ref
  62.6 1.6 %collective-permute-start.14 = (bf16[1024,256]{1,0:T(8,128)(2,1)}, bf16[1024,256]{1,0:T(8,128)(2,1)}, u32[]{:S(2)}, u32[]{:S(2)}) collective-permute-start(bf16[1024,256]{1,0:T(8,128)(2,1)} %collective-permute-done.13.across_ref), channel_id=1, source_target_pairs={{0,4},{1,5},{2,14},{3,15},{4,8},{5,9},{6,2},{7,3},{8,12},{9,13},{1... | collective-permute-start | bytes 1572872 | tf_op jit(solution)/shard_map/ppermute | solution.py:190
  64.2 0.6 fusion.8
  64.8 0.0 collective-permute-done.10.across_ref
  64.8 1.6 %collective-permute-start.11 = (bf16[1024,256]{1,0:T(8,128)(2,1)S(1)}, bf16[1024,256]{1,0:T(8,128)(2,1)}, u32[]{:S(2)}, u32[]{:S(2)}) collective-permute-start(bf16[1024,256]{1,0:T(8,128)(2,1)S(1)} %collective-permute-done.10.across_ref), channel_id=1, source_target_pairs={{0,4},{1,5},{2,14},{3,15},{4,8},{5,9},{6,2},{7,3},{8,12},{9,13},{1... | collective-permute-start | bytes 1572872 | tf_op jit(solution)/shard_map/ppermute | solution.py:190
  66.4 3.2 %fusion.4.entry_ref = s32[4,12]{1,0:T(4,128)S(1)} fusion(s32[4,12]{1,0:T(4,128)S(1)} %copy-done.16, s32[]{:T(128)} %bitcast.4, s32[]{:T(128)} %bitcast.3, s32[]{:T(128)} %bitcast.2, s32[]{:T(128)} %bitcast.1, s32[]{:T(128)} %bitcast, s32[]{:T(128)S(6)} %axis_index.12, s32[4]{0:T(128)S(1)} %copy-done.17), kind=kLoop, calls=%fused_computation.17 | loop fusion | flops 2400 | bytes 424 | tf_op jit(solution)/shard_map/jit(_where)/select_n | solution.py:185
  69.6 2.6 %collective-permute-done.5.along_ref = bf16[1024,128]{1,0:T(8,128)(2,1)} collective-permute-done((bf16[1024,128]{1,0:T(8,128)(2,1)}, bf16[1024,128]{1,0:T(8,128)(2,1)}, u32[]{:S(2)}, u32[]{:S(2)}) %collective-permute-start.5) | collective-permute-done | bytes 262176 | tf_op jit(solution)/shard_map/ppermute | solution.py:190
  72.2 0.0 collective-permute-start.2
  72.2 1.7 %broadcast_select_fusion.3 = bf16[1024,128]{1,0:T(8,128)(2,1)} fusion(bf16[1024,128]{1,0:T(8,128)(2,1)} %collective-permute-done.4.across_ref, bf16[1024,128]{1,0:T(8,128)(2,1)} %collective-permute-done.5.along_ref, pred[]{:T(512)S(6)} %or.3), kind=kLoop, calls=%fused_computation.3 | loop fusion | flops 131072 | bytes 786433 | tf_op jit(solution)/shard_map/jit(_where)/select_n | solution.py:191
  73.9 0.0 collective-permute-done.7.across_ref
  73.9 0.0 collective-permute-start.6
  73.9 9.5 %collective-permute-done.14.along_ref = bf16[1024,256]{1,0:T(8,128)(2,1)} collective-permute-done((bf16[1024,256]{1,0:T(8,128)(2,1)}, bf16[1024,256]{1,0:T(8,128)(2,1)}, u32[]{:S(2)}, u32[]{:S(2)}) %collective-permute-start.14) | collective-permute-done | bytes 524320 | tf_op jit(solution)/shard_map/ppermute | solution.py:190
  83.4 0.0 collective-permute-start.8
  83.4 1.1 broadcast_select_fusion
  84.5 0.0 copy-start.4
  84.5 0.0 copy-start.15
  84.5 10.1 %collective-permute-done.11.along_ref = bf16[1024,256]{1,0:T(8,128)(2,1)} collective-permute-done((bf16[1024,256]{1,0:T(8,128)(2,1)S(1)}, bf16[1024,256]{1,0:T(8,128)(2,1)}, u32[]{:S(2)}, u32[]{:S(2)}) %collective-permute-start.11) | collective-permute-done | bytes 524320 | tf_op jit(solution)/shard_map/ppermute | solution.py:190
  94.6 0.0 collective-permute-start.15
  94.6 0.9 broadcast_select_fusion.1
  95.5 13.1 %collective-permute-done.8.along_ref = bf16[1024,256]{1,0:T(8,128)(2,1)S(1)} collective-permute-done((bf16[1024,256]{1,0:T(8,128)(2,1)}, bf16[1024,256]{1,0:T(8,128)(2,1)S(1)}, u32[]{:S(2)}, u32[]{:S(2)}) %collective-permute-start.8) | collective-permute-done | bytes 524320 | tf_op jit(solution)/shard_map/ppermute | solution.py:190
  108.7 0.0 collective-permute-start.12
  108.7 2.0 %broadcast_select_fusion.2 = bf16[1024,256]{1,0:T(8,128)(2,1)} fusion(bf16[1024,256]{1,0:T(8,128)(2,1)} %collective-permute-done.7.across_ref, bf16[1024,256]{1,0:T(8,128)(2,1)S(1)} %collective-permute-done.8.along_ref, pred[]{:T(512)S(6)} %or.3), kind=kLoop, calls=%fused_computation.2 | loop fusion | flops 262144 | bytes 1572865 | tf_op jit(solution)/shard_map/jit(_where)/select_n | solution.py:191
  110.7 0.8 copy-done.5
  111.4 0.0 collective-permute-done.2.along_ref
  111.4 0.0 collective-permute-start.9
  111.5 0.7 broadcast_select_fusion.4
  112.2 0.7 copy-done.7
  112.9 0.0 collective-permute-done.15.other_ref
  112.9 0.8 copy-done.9
  113.7 0.5 collective-permute-start.3
  114.2 0.0 collective-permute-done.core_ref
  114.2 0.0 copy-start
  114.2 2.8 %copy-done = bf16[4,12,256,256]{3,2,1,0:T(8,128)(2,1)S(1)} copy-done((bf16[4,12,256,256]{3,2,1,0:T(8,128)(2,1)S(1)}, bf16[4,12,256,256]{3,2,1,0:T(8,128)(2,1)}, u32[]{:S(2)}) %copy-start) | copy-done | bytes 6291480
  117.0 1.6 %copy-done.3 = bf16[1024,1024]{1,0:T(8,128)(2,1)S(1)} copy-done((bf16[1024,1024]{1,0:T(8,128)(2,1)S(1)}, bf16[1024,1024]{1,0:T(8,128)(2,1)}, u32[]{:S(2)}) %copy-start.3) | copy-done | bytes 2097176
  118.6 1.0 copy-done.10
  119.6 5.6 %shard_map.110.rest_0_ = bf16[1024,1024]{1,0:T(8,128)(2,1)} custom-call(s32[4,12]{1,0:T(4,128)S(1)} %fusion.4.entry_ref, s32[6]{0:T(128)S(1)} %bitcast.18, bf16[4,12,256,256]{3,2,1,0:T(8,128)(2,1)S(1)} %copy-done, bf16[1024,1024]{1,0:T(8,128)(2,1)S(1)} %copy-done.2, bf16[1024,1024]{1,0:T(8,128)(2,1)} %collective-permute-done.core_ref, ...), custom_call_target="tpu_custom_call" | custom-call | flops 1610612736 | bytes 10485760 | tf_op jit(solution)/shard_map/pallas_call | solution.py:135
  125.2 0.0 collective-permute-done.12.other_ref
  125.2 5.6 %shard_map.111.rest_0_ = bf16[1024,1024]{1,0:T(8,128)(2,1)} custom-call(s32[4,12]{1,0:T(4,128)S(1)} %fusion.4.entry_ref, s32[6]{0:T(128)S(1)} %bitcast.19, bf16[4,12,256,256]{3,2,1,0:T(8,128)(2,1)S(1)} %copy-done, bf16[1024,1024]{1,0:T(8,128)(2,1)S(1)} %copy-done.2, ...), custom_call_target="tpu_custom_call", output_to_operand_aliasing={{}: (11, {})} | custom-call | flops 1610612736 | bytes 10485760 | tf_op jit(solution)/shard_map/pallas_call | solution.py:135
  130.8 0.0 collective-permute-done.9.other_ref
  130.9 5.6 %shard_map.112.rest_0_ = bf16[1024,1024]{1,0:T(8,128)(2,1)} custom-call(s32[4,12]{1,0:T(4,128)S(1)} %fusion.4.entry_ref, s32[6]{0:T(128)S(1)} %bitcast.20, bf16[4,12,256,256]{3,2,1,0:T(8,128)(2,1)S(1)} %copy-done, bf16[1024,1024]{1,0:T(8,128)(2,1)S(1)} %copy-done.2, ...), custom_call_target="tpu_custom_call", output_to_operand_aliasing={{}: (11, {})} | custom-call | flops 1610612736 | bytes 10485760 | tf_op jit(solution)/shard_map/pallas_call | solution.py:135
  136.5 0.0 collective-permute-done.6.other_ref
  136.5 5.3 %shard_map.113.rest_0_ = bf16[1024,1024]{1,0:T(8,128)(2,1)} custom-call(s32[4,12]{1,0:T(4,128)S(1)} %fusion.4.entry_ref, s32[6]{0:T(128)S(1)} %bitcast.21, bf16[4,12,256,256]{3,2,1,0:T(8,128)(2,1)S(1)} %copy-done, bf16[1024,1024]{1,0:T(8,128)(2,1)S(1)} %copy-done.2, ...), custom_call_target="tpu_custom_call", output_to_operand_aliasing={{}: (11, {})} | custom-call | flops 805306368 | bytes 10485760 | tf_op jit(solution)/shard_map/pallas_call | solution.py:135
  141.8 5.1 %shard_map.114 = bf16[1024,1024]{1,0:T(8,128)(2,1)} custom-call(s32[4,12]{1,0:T(4,128)S(1)} %fusion.4.entry_ref, s32[6]{0:T(128)S(1)} %bitcast.22, bf16[4,12,256,256]{3,2,1,0:T(8,128)(2,1)S(1)} %copy-done, bf16[1024,1024]{1,0:T(8,128)(2,1)S(1)} %copy-done.2, bf16[1024,1024]{1,0:T(8,128)(2,1)} %collective-permute-done.core_ref, ...), custom_call_target="tpu_custom_call", output_to_operand_aliasing={{}: (11, {})} | custom-call | flops 805306368 | bytes 10485760 | tf_op jit(solution)/shard_map/pallas_call | solution.py:135
  (23 shorter events, 0.0 us)
Async XLA Ops:
  6.5 107.7 %all-gather.3.cloned.1.call-start = ((), (), s32[]{:S(2)}) async-start(), calls=%async_computation | async-start | bytes 2228224 | tf_op jit(solution)/shard_map/all_gather | solution.py:179
  6.5 1.6 %copy-start.1 = (bf16[1024,1024]{1,0:T(8,128)(2,1)S(1)}, bf16[1024,1024]{1,0:T(8,128)(2,1)}, u32[]{:S(2)}) copy-start(bf16[1024,1024]{1,0:T(8,128)(2,1)} %own_ref.9) | copy-start | bytes 6291460
  8.1 0.9 copy-start.11
  9.0 0.9 copy-start.12
  9.9 0.8 copy-start.13
  10.8 0.8 copy-start.14
  11.5 2.3 %copy-start.2 = (bf16[1024,1024]{1,0:T(8,128)(2,1)S(1)}, bf16[1024,1024]{1,0:T(8,128)(2,1)}, u32[]{:S(2)}) copy-start(bf16[1024,1024]{1,0:T(8,128)(2,1)} %own_ref.9) | copy-start | bytes 6291460
  13.8 52.6 %copy-start.16 = (s32[4,12]{1,0:T(4,128)S(1)}, s32[4,12]{1,0:T(4,128)}, u32[]{:S(2)}) copy-start(s32[4,12]{1,0:T(4,128)} %param.13) | copy-start | bytes 580
  13.8 52.6 %copy-start.17 = (s32[4]{0:T(128)S(1)}, s32[4]{0:T(128)}, u32[]{:S(2)}) copy-start(s32[4]{0:T(128)} %param.14) | copy-start | bytes 52
  15.1 47.5 %collective-permute-start.13 = (bf16[1024,256]{1,0:T(8,128)(2,1)}, bf16[1024,256]{1,0:T(8,128)(2,1)}, u32[]{:S(2)}, u32[]{:S(2)}) collective-permute-start(bf16[1024,256]{1,0:T(8,128)(2,1)} %get-tuple-element.9), channel_id=1, source_target_pairs={{0,2},{1,3},{2,0},{3,1},{4,6},{5,7},{6,4},{7,5},{8,10},{9,11},{10,... | collective-permute-start | bytes 1572872 | tf_op jit(solution)/shard_map/ppermute | solution.py:176
  18.0 96.2 %collective-permute-start = (bf16[1024,1024]{1,0:T(8,128)(2,1)S(1)}, bf16[1024,1024]{1,0:T(8,128)(2,1)}, u32[]{:S(2)}, u32[]{:S(2)}) collective-permute-start(bf16[1024,1024]{1,0:T(8,128)(2,1)S(1)} %copy-done.2), channel_id=1, source_target_pairs={{0,1},{1,0},{2,3},{3,2},{4,5},{5,4},{6,7},{7,6},{8,9},{9,8},{10,11... | collective-permute-start | bytes 6291464 | tf_op jit(solution)/shard_map/ppermute | solution.py:177
  18.0 46.8 %collective-permute-start.10 = (bf16[1024,256]{1,0:T(8,128)(2,1)}, bf16[1024,256]{1,0:T(8,128)(2,1)S(1)}, u32[]{:S(2)}, u32[]{:S(2)}) collective-permute-start(bf16[1024,256]{1,0:T(8,128)(2,1)} %get-tuple-element.10), channel_id=1, source_target_pairs={{0,2},{1,3},{2,0},{3,1},{4,6},{5,7},{6,4},{7,5},{8,10},{9,11},{10,... | collective-permute-start | bytes 1572872 | tf_op jit(solution)/shard_map/ppermute | solution.py:176
  18.9 35.6 %collective-permute-start.4 = (bf16[1024,128]{1,0:T(8,128)(2,1)}, bf16[1024,128]{1,0:T(8,128)(2,1)}, u32[]{:S(2)}, u32[]{:S(2)}) collective-permute-start(bf16[1024,128]{1,0:T(8,128)(2,1)} %get-tuple-element.12), channel_id=1, source_target_pairs={{0,2},{1,3},{2,0},{3,1},{4,6},{5,7},{6,4},{7,5},{8,10},{9,11},{10,... | collective-permute-start | bytes 786440 | tf_op jit(solution)/shard_map/ppermute | solution.py:176
  20.9 39.6 %collective-permute-start.1 = (bf16[1024,128]{1,0:T(8,128)(2,1)}, bf16[1024,128]{1,0:T(8,128)(2,1)S(1)}, u32[]{:S(2)}, u32[]{:S(2)}) collective-permute-start(bf16[1024,128]{1,0:T(8,128)(2,1)} %get-tuple-element.13), channel_id=1, source_target_pairs={{0,2},{1,3},{2,0},{3,1},{4,6},{5,7},{6,4},{7,5},{8,10},{9,11},{10,... | collective-permute-start | bytes 786440 | tf_op jit(solution)/shard_map/ppermute | solution.py:176
  54.5 19.4 %collective-permute-start.7 = (bf16[1024,256]{1,0:T(8,128)(2,1)}, bf16[1024,256]{1,0:T(8,128)(2,1)}, u32[]{:S(2)}, u32[]{:S(2)}) collective-permute-start(bf16[1024,256]{1,0:T(8,128)(2,1)} %get-tuple-element.11), channel_id=1, source_target_pairs={{0,2},{1,3},{2,0},{3,1},{4,6},{5,7},{6,4},{7,5},{8,10},{9,11},{10,... | collective-permute-start | bytes 1572872 | tf_op jit(solution)/shard_map/ppermute | solution.py:176
  60.4 11.7 %collective-permute-start.5 = (bf16[1024,128]{1,0:T(8,128)(2,1)}, bf16[1024,128]{1,0:T(8,128)(2,1)}, u32[]{:S(2)}, u32[]{:S(2)}) collective-permute-start(bf16[1024,128]{1,0:T(8,128)(2,1)} %collective-permute-done.4.across_ref), channel_id=1, source_target_pairs={{0,4},{1,5},{2,14},{3,15},{4,8},{5,9},{6,2},{7,3},{8,12},{9,13},{1... | collective-permute-start | bytes 786440 | tf_op jit(solution)/shard_map/ppermute | solution.py:190
  62.6 20.8 %collective-permute-start.14 = (bf16[1024,256]{1,0:T(8,128)(2,1)}, bf16[1024,256]{1,0:T(8,128)(2,1)}, u32[]{:S(2)}, u32[]{:S(2)}) collective-permute-start(bf16[1024,256]{1,0:T(8,128)(2,1)} %collective-permute-done.13.across_ref), channel_id=1, source_target_pairs={{0,4},{1,5},{2,14},{3,15},{4,8},{5,9},{6,2},{7,3},{8,12},{9,13},{1... | collective-permute-start | bytes 1572872 | tf_op jit(solution)/shard_map/ppermute | solution.py:190
  64.8 29.8 %collective-permute-start.11 = (bf16[1024,256]{1,0:T(8,128)(2,1)S(1)}, bf16[1024,256]{1,0:T(8,128)(2,1)}, u32[]{:S(2)}, u32[]{:S(2)}) collective-permute-start(bf16[1024,256]{1,0:T(8,128)(2,1)S(1)} %collective-permute-done.10.across_ref), channel_id=1, source_target_pairs={{0,4},{1,5},{2,14},{3,15},{4,8},{5,9},{6,2},{7,3},{8,12},{9,13},{1... | collective-permute-start | bytes 1572872 | tf_op jit(solution)/shard_map/ppermute | solution.py:190
  72.2 39.3 %collective-permute-start.2 = (bf16[1024,128]{1,0:T(8,128)(2,1)S(1)}, bf16[1024,128]{1,0:T(8,128)(2,1)S(1)}, u32[]{:S(2)}, u32[]{:S(2)}) collective-permute-start(bf16[1024,128]{1,0:T(8,128)(2,1)S(1)} %collective-permute-done.1.across_ref), channel_id=1, source_target_pairs={{0,4},{1,5},{2,14},{3,15},{4,8},{5,9},{6,2},{7,3},{8,12},{9,13},{1... | collective-permute-start | bytes 786440 | tf_op jit(solution)/shard_map/ppermute | solution.py:190
  73.9 62.6 %collective-permute-start.6 = (bf16[1024,128]{1,0:T(8,128)(2,1)}, bf16[1024,128]{1,0:T(8,128)(2,1)}, u32[]{:S(2)}, u32[]{:S(2)}) collective-permute-start(bf16[1024,128]{1,0:T(8,128)(2,1)} %broadcast_select_fusion.3), channel_id=1, source_target_pairs={{0,1},{1,0},{2,3},{3,2},{4,5},{5,4},{6,7},{7,6},{8,9},{9,8},{10,11... | collective-permute-start | bytes 786440 | tf_op jit(solution)/shard_map/ppermute | solution.py:191
  83.4 25.3 %collective-permute-start.8 = (bf16[1024,256]{1,0:T(8,128)(2,1)}, bf16[1024,256]{1,0:T(8,128)(2,1)S(1)}, u32[]{:S(2)}, u32[]{:S(2)}) collective-permute-start(bf16[1024,256]{1,0:T(8,128)(2,1)} %collective-permute-done.7.across_ref), channel_id=1, source_target_pairs={{0,4},{1,5},{2,14},{3,15},{4,8},{5,9},{6,2},{7,3},{8,12},{9,13},{1... | collective-permute-start | bytes 1572872 | tf_op jit(solution)/shard_map/ppermute | solution.py:190
  84.5 29.7 %copy-start.4 = (bf16[1,6,64,64]{3,2,1,0:T(8,128)(2,1)S(1)}, bf16[1,6,64,64]{3,2,1,0:T(8,128)(2,1)}, u32[]{:S(2)}) copy-start(bf16[1,6,64,64]{3,2,1,0:T(8,128)(2,1)} %param.19) | copy-start | bytes 147460
  84.5 29.7 %copy-start.15 = (s32[1,6]{1,0:T(1,128)S(1)}, s32[1,6]{1,0:T(1,128)}, u32[]{:S(2)}) copy-start(s32[1,6]{1,0:T(1,128)} %param.20) | copy-start | bytes 76
  94.6 18.3 %collective-permute-start.15 = (bf16[1024,256]{1,0:T(8,128)(2,1)S(1)}, bf16[1024,256]{1,0:T(8,128)(2,1)S(1)}, u32[]{:S(2)}, u32[]{:S(2)}) collective-permute-start(bf16[1024,256]{1,0:T(8,128)(2,1)S(1)} %broadcast_select_fusion), channel_id=1, source_target_pairs={{0,1},{1,0},{2,3},{3,2},{4,5},{5,4},{6,7},{7,6},{8,9},{9,8},{10,11... | collective-permute-start | bytes 1572872 | tf_op jit(solution)/shard_map/ppermute | solution.py:191
  108.7 16.6 %collective-permute-start.12 = (bf16[1024,256]{1,0:T(8,128)(2,1)}, bf16[1024,256]{1,0:T(8,128)(2,1)}, u32[]{:S(2)}, u32[]{:S(2)}) collective-permute-start(bf16[1024,256]{1,0:T(8,128)(2,1)} %broadcast_select_fusion.1), channel_id=1, source_target_pairs={{0,1},{1,0},{2,3},{3,2},{4,5},{5,4},{6,7},{7,6},{8,9},{9,8},{10,11... | collective-permute-start | bytes 1572872 | tf_op jit(solution)/shard_map/ppermute | solution.py:191
  110.7 0.8 copy-start.5
  111.4 19.4 %collective-permute-start.9 = (bf16[1024,256]{1,0:T(8,128)(2,1)}, bf16[1024,256]{1,0:T(8,128)(2,1)}, u32[]{:S(2)}, u32[]{:S(2)}) collective-permute-start(bf16[1024,256]{1,0:T(8,128)(2,1)} %broadcast_select_fusion.2), channel_id=1, source_target_pairs={{0,1},{1,0},{2,3},{3,2},{4,5},{5,4},{6,7},{7,6},{8,9},{9,8},{10,11... | collective-permute-start | bytes 1572872 | tf_op jit(solution)/shard_map/ppermute | solution.py:191
  112.2 0.7 copy-start.7
  112.9 0.8 copy-start.9
  113.7 28.1 %collective-permute-start.3 = (bf16[1024,128]{1,0:T(8,128)(2,1)}, bf16[1024,128]{1,0:T(8,128)(2,1)}, u32[]{:S(2)}, u32[]{:S(2)}) collective-permute-start(bf16[1024,128]{1,0:T(8,128)(2,1)} %broadcast_select_fusion.4), channel_id=1, source_target_pairs={{0,1},{1,0},{2,3},{3,2},{4,5},{5,4},{6,7},{7,6},{8,9},{9,8},{10,11... | collective-permute-start | bytes 786440 | tf_op jit(solution)/shard_map/ppermute | solution.py:191
  114.2 2.8 %copy-start = (bf16[4,12,256,256]{3,2,1,0:T(8,128)(2,1)S(1)}, bf16[4,12,256,256]{3,2,1,0:T(8,128)(2,1)}, u32[]{:S(2)}) copy-start(bf16[4,12,256,256]{3,2,1,0:T(8,128)(2,1)} %near_ref.9) | copy-start | bytes 18874372
  117.0 1.6 %copy-start.3 = (bf16[1024,1024]{1,0:T(8,128)(2,1)S(1)}, bf16[1024,1024]{1,0:T(8,128)(2,1)}, u32[]{:S(2)}) copy-start(bf16[1024,1024]{1,0:T(8,128)(2,1)} %all-gather.3.cloned.1.call-done) | copy-start | bytes 6291460
  118.6 1.0 copy-start.10
  125.2 5.6 %copy-start.6 = (bf16[1024,256]{1,0:T(8,128)(2,1)S(1)}, bf16[1024,256]{1,0:T(8,128)(2,1)}, u32[]{:S(2)}) copy-start(bf16[1024,256]{1,0:T(8,128)(2,1)} %copy-done.5) | copy-start | bytes 1572868
  136.5 5.4 %copy-start.8 = (bf16[1024,128]{1,0:T(8,128)(2,1)S(1)}, bf16[1024,128]{1,0:T(8,128)(2,1)}, u32[]{:S(2)}) copy-start(bf16[1024,128]{1,0:T(8,128)(2,1)} %copy-done.7) | copy-start | bytes 786436
Sparse Core Ops, SparseCore 0:
  13.9 49.6 all-gather.2

commit v2 on v0

v2 whole, which is shorter than its diff:
```python
import functools

import jax
import jax.numpy as jnp
from jax import lax
from jax.experimental import pallas as pl
from jax.experimental.pallas import tpu as pltpu
from jax.sharding import PartitionSpec as P

LEAF = 256
RANK = 64
B_DEV = 4
NEAR = 12
ROWS = B_DEV * LEAF
SLABS = ((0, 256), (256, 256), (512, 256), (768, 128), (896, 128))
OWN, CORE, ACROSS, ACROSS_CORE, ALONG, ALONG_CORE, ZERO = 0, 4, 8, 12, 16, 18, 20
HELD = 21
HELD_AT = (
    (ALONG, ALONG_CORE, OWN, CORE, ACROSS),
    (ALONG, CORE, OWN, ACROSS_CORE, ACROSS),
    (ACROSS, ACROSS_CORE, OWN, CORE, ALONG),
    (ACROSS, CORE, OWN, ALONG_CORE, ALONG),
)
MIB = 1024 * 1024
ANYWHERE = pl.BlockSpec(memory_space=pl.ANY)
VECTOR = pl.BlockSpec(memory_space=pltpu.VMEM)
SCALAR = pl.BlockSpec(memory_space=pltpu.SMEM)


def cost(mib):
    return pl.CostEstimate(flops=1024, bytes_accessed=mib * MIB, transcendentals=0)


def split(value):
    high = value.astype(jnp.bfloat16)
    low = (value - high.astype(jnp.float32)).astype(jnp.bfloat16)
    return high, low


def dot(a, b):
    return jnp.dot(a, b, preferred_element_type=jnp.float32)


def dot32(a, b):
    return jnp.dot(
        a.astype(jnp.float32),
        b.astype(jnp.float32),
        precision=lax.Precision.HIGHEST,
        preferred_element_type=jnp.float32,
    )


def cut_kernel(rhs_any, *rest):
    parts, sems = rest[:-1], rest[-1]
    copies = [
        pltpu.make_async_copy(rhs_any.at[:, pl.ds(start, width)], part, sems.at[k])
        for k, ((start, width), part) in enumerate(zip(SLABS, parts))
    ]
    for copy in copies:
        copy.start()
    for copy in copies:
        copy.wait()


def cut(rhs):
    return pl.pallas_call(
        cut_kernel,
        in_specs=[ANYWHERE],
        out_shape=tuple(jax.ShapeDtypeStruct((ROWS, width), rhs.dtype) for _, width in SLABS),
        scratch_shapes=[pltpu.SemaphoreType.DMA((len(SLABS),))],
        compiler_params=pltpu.CompilerParams(vmem_limit_bytes=16 * MIB),
        cost_estimate=cost(4),
    )(rhs)


def first_two(mask):
    first = jnp.where(mask & 1 != 0, 0, jnp.where(mask & 2 != 0, 1, jnp.where(mask & 4 != 0, 2, 3)))
    mask = mask & (mask - 1)
    second = jnp.where(mask & 2 != 0, 1, jnp.where(mask & 4 != 0, 2, 3))
    return first, second


def plan(members, ids_ref, count_ref, entry_ref, wish_refs):
    position = lax.axis_index("pts")
    kind = position & 3
    held_at = []
    for d in range(5):
        at = jnp.int32(HELD_AT[0][d])
        for other in range(1, 4):
            at = jnp.where(kind == other, HELD_AT[other][d], at)
        held_at.append(at)
    masks = [jnp.int32(0), jnp.int32(0)]
    bases = {}
    for box in range(B_DEV):
        live = count_ref[box]
        for n in range(NEAR):
            number = ids_ref[box, n]
            distance = (number >> 2) - position + 2
            distance = jnp.where(distance < 0, distance + members, distance)
            distance = jnp.where(distance >= members, distance - members, distance)
            base = held_at[0]
            for d in range(1, 5):
                base = jnp.where(distance == d, held_at[d], base)
            base = jnp.where(n < live, base, ZERO)
            bit = jnp.int32(1) << (number & 3)
            masks[0] = masks[0] | jnp.where(base == ALONG, bit, 0)
            masks[1] = masks[1] | jnp.where(base == ALONG_CORE, bit, 0)
            bases[box, n] = (base, number & 3)
    picks = [first_two(mask) for mask in masks]
    for (box, n), (base, inner) in bases.items():
        first = jnp.where(base == ALONG, picks[0][0], picks[1][0])
        inner = jnp.where(base == ZERO, 0, jnp.where(base >= ALONG, jnp.where(inner == first, 0, 1), inner))
        entry_ref[box, n] = base + inner
    for (first, second), wish_ref in zip(picks, wish_refs):
        lane = lax.broadcasted_iota(jnp.int32, wish_ref.shape, 1)
        wish_ref[...] = jnp.where(lane == 0, first, second)


def up_kernel(
    reach,
    members,
    source_any,
    target_any,
    leaf_any,
    mid_any,
    coupling_any,
    far_any,
    count_any,
    ids_any,
    *rest,
):
    parts = rest[: len(SLABS)]
    panel_ref, down_ref, placed_ref, partner_placed_ref, entry_ref, wish_ref, core_wish_ref = rest[len(SLABS) : -9]
    source_ref, target_ref, leaf_ref, mid_ref, coupling_ref, far_ref, count_ref, ids_ref, sems = rest[-9:]
    pairs = (
        (leaf_any, leaf_ref),
        (mid_any, mid_ref),
        (source_any, source_ref),
        (far_any, far_ref),
        (count_any, count_ref),
        (ids_any, ids_ref),
        (target_any, target_ref),
        (coupling_any, coupling_ref),
    )
    copies = [pltpu.make_async_copy(a, b, sems.at[i]) for i, (a, b) in enumerate(pairs)]
    for copy in copies:
        copy.start()
    for copy in copies:
        copy.wait()
    chains = [dot32(mid_ref[box // 2], leaf_ref[box]) for box in range(B_DEV)]
    ups = [dot32(chains[box], source_ref[box]) for box in range(B_DEV)]
    high, low = split(jnp.concatenate(ups, axis=1))
    both = jnp.concatenate([high, low], axis=0)
    for (start, width), part in zip(SLABS, parts):
        sums = dot(both, part[...])
        panel_ref[:, pl.ds(start, width)] = (sums[:RANK] + sums[RANK:]).astype(jnp.bfloat16)
    for box in range(B_DEV):
        high, low = split(dot32(chains[box], target_ref[box]).T)
        down_ref[box] = jnp.concatenate([high, low, high], axis=1)
    plan(members, ids_ref, count_ref, entry_ref, (wish_ref, core_wish_ref))
    position = lax.axis_index("pts")
    quad, side, core = position >> 2, (position >> 1) & 1, position & 1
    for half, ref in enumerate((placed_ref, partner_placed_ref)):
        blocks = []
        for other in range(2):
            for step in reach:
                held_quad = quad + step
                held_quad = jnp.where(held_quad >= members // 4, held_quad - members // 4, held_quad)
                group = held_quad * 4 + 2 * (side ^ half) + (core ^ other)
                block = jnp.zeros((RANK, RANK), jnp.float32)
                for f in range(coupling_ref.shape[0]):
                    block = jnp.where(far_ref[0, f] == group, coupling_ref[f].astype(jnp.float32), block)
                blocks.append(block)
        ref[...] = jnp.concatenate(blocks, axis=1).astype(jnp.bfloat16)


def up(reach, members, parts, arrays, far_ids, near_count, near_ids):
    columns = sum(width for _, width in SLABS)
    placed = jax.ShapeDtypeStruct((RANK, 2 * len(reach) * RANK), jnp.bfloat16)
    wish = jax.ShapeDtypeStruct((1, 128), jnp.int32)
    return pl.pallas_call(
        functools.partial(up_kernel, reach, members),
        in_specs=[ANYWHERE] * 8 + [VECTOR] * len(parts),
        out_specs=(VECTOR,) * 4 + (SCALAR,) + (VECTOR,) * 2,
        out_shape=(
            jax.ShapeDtypeStruct((RANK, columns), jnp.bfloat16),
            jax.ShapeDtypeStruct((B_DEV, LEAF, 3 * RANK), jnp.bfloat16),
            placed,
            placed,
            jax.ShapeDtypeStruct(near_ids.shape, jnp.int32),
            wish,
            wish,
        ),
        scratch_shapes=[pltpu.VMEM(a.shape, a.dtype) for a in arrays]
        + [pltpu.SMEM(a.shape, jnp.int32) for a in (far_ids, near_count, near_ids)]
        + [pltpu.SemaphoreType.DMA((8,))],
        compiler_params=pltpu.CompilerParams(vmem_limit_bytes=32 * MIB),
        cost_estimate=cost(512),
    )(*arrays, far_ids, near_count, near_ids, *parts)


def couple_kernel(mine_ref, core_ref, own_ref, partner_ref, own_sum_ref, partner_sum_ref):
    table = jnp.concatenate([mine_ref[...], core_ref[...]], axis=0)
    partner_sum_ref[...] = dot(partner_ref[...], table)
    own_sum_ref[...] = dot(own_ref[...], table)


def couple(mine, core, own, partner):
    shape = jax.ShapeDtypeStruct((RANK, mine.shape[1]), jnp.float32)
    return pl.pallas_call(
        couple_kernel,
        out_shape=(shape, shape),
        compiler_params=pltpu.CompilerParams(vmem_limit_bytes=16 * MIB),
        cost_estimate=cost(1),
    )(mine, core, own, partner)


def pack_kernel(wish_ref, core_wish_ref, arrived_ref, along_ref, along_core_ref):
    for wishes, picked_ref in ((wish_ref, along_ref), (core_wish_ref, along_core_ref)):
        for k in range(2):
            rows = pl.ds(pl.multiple_of(wishes[0, k] * LEAF, LEAF), LEAF)
            picked_ref[pl.ds(k * LEAF, LEAF)] = arrived_ref[rows]


def pack(wish, core_wish, arrived):
    shape = jax.ShapeDtypeStruct((2 * LEAF, arrived.shape[1]), arrived.dtype)
    return pl.pallas_call(
        pack_kernel,
        in_specs=[SCALAR, SCALAR, VECTOR],
        out_shape=(shape, shape),
        compiler_params=pltpu.CompilerParams(vmem_limit_bytes=8 * MIB),
        cost_estimate=cost(1),
    )(wish, core_wish, arrived)


def near_kernel(start, entry_ref, near_ref, own_ref, core_ref, across_ref, across_core_ref, along_ref, along_core_ref, sum_ref, held):
    width = sum_ref.shape[1]
    pieces = (
        (OWN, own_ref),
        (CORE, core_ref.at[:, pl.ds(start, width)]),
        (ACROSS, across_ref),
        (ACROSS_CORE, across_core_ref),
        (ALONG, along_ref),
        (ALONG_CORE, along_core_ref),
    )
    for at, ref in pieces:
        held[pl.ds(at * LEAF, ref.shape[0])] = ref[...]
    held[pl.ds(ZERO * LEAF, LEAF)] = jnp.zeros((LEAF, width), jnp.bfloat16)
    for box in range(B_DEV):
        left = [near_ref[box, n] for n in range(NEAR)]
        right = [held[pl.ds(pl.multiple_of(entry_ref[box, n] * LEAF, LEAF), LEAF)] for n in range(NEAR)]
        sum_ref[pl.ds(box * LEAF, LEAF)] = dot(
            jnp.concatenate(left, axis=1), jnp.concatenate(right, axis=0)
        )


def near(start, width, entry, near_blocks, pieces):
    return pl.pallas_call(
        functools.partial(near_kernel, start),
        in_specs=[SCALAR] + [VECTOR] * (1 + len(pieces)),
        out_specs=VECTOR,
        scratch_shapes=[pltpu.VMEM((HELD * LEAF, width), jnp.bfloat16)],
        out_shape=jax.ShapeDtypeStruct((ROWS, width), jnp.float32),
        compiler_params=pltpu.CompilerParams(vmem_limit_bytes=24 * MIB),
        cost_estimate=cost(8),
    )(entry, near_blocks, *pieces)


def finish_kernel(slabs, own_sum_ref, partner_sum_ref, down_ref, *rest):
    sum_refs = rest[: len(slabs)]
    out_ref, made, sems = rest[-3:]
    start, stop = slabs[0][0], slabs[-1][0] + slabs[-1][1]
    taken = pl.ds(start, stop - start)
    high, low = split(own_sum_ref[:, taken] + partner_sum_ref[:, taken])
    coupled = jnp.concatenate([high, high, low], axis=0)
    copies = []
    for box in range(B_DEV):
        rows = pl.ds(box * LEAF, LEAF)
        far = dot(down_ref[box], coupled)
        for (at, width), sum_ref in zip(slabs, sum_refs):
            columns = slice(at - start, at - start + width)
            made[rows, columns] = (far[:, columns] + sum_ref[rows]).astype(jnp.bfloat16)
        copy = pltpu.make_async_copy(made.at[rows], out_ref.at[rows, taken], sems.at[box])
        copy.start()
        copies.append(copy)
    for copy in copies:
        copy.wait()


def finish(slabs, sums, down, nears, product):
    columns = sums[0].shape[1]
    operands = [*sums, down, *nears]
    in_specs = [VECTOR] * len(operands)
    aliases = {}
    if product is not None:
        aliases = {len(operands): 0}
        in_specs.append(ANYWHERE)
        operands.append(product)
    return pl.pallas_call(
        functools.partial(finish_kernel, slabs),
        in_specs=in_specs,
        out_specs=ANYWHERE,
        scratch_shapes=[
            pltpu.VMEM((ROWS, sum(width for _, width in slabs)), jnp.bfloat16),
            pltpu.SemaphoreType.DMA((B_DEV,)),
        ],
        out_shape=jax.ShapeDtypeStruct((ROWS, columns), jnp.bfloat16),
        input_output_aliases=aliases,
        compiler_params=pltpu.CompilerParams(vmem_limit_bytes=24 * MIB),
        cost_estimate=cost(4),
    )(*operands)


def on_device(
    rhs,
    near_blocks,
    near_ids,
    near_count,
    source_basis,
    target_basis,
    leaf_transfer,
    mid_transfer,
    far_coupling,
    far_ids,
):
    members = lax.axis_size("pts")
    every = range(members)
    across_pairs = [(i, i ^ 2) for i in every]
    core_pairs = [(i, i ^ 1) for i in every]
    along_pairs = [(i, (i + (-4 if i & 2 else 4)) % members) for i in every]
    along_core_pairs = [(i, (i + (-3 if i & 2 else 3)) % members) for i in every if i % 4 in (1, 2)]
    back = lambda pairs: [(b, a) for a, b in pairs]
    permute = lambda value, pairs: lax.ppermute(value, "pts", pairs)
    meet = lambda *values: lax.optimization_barrier(values)
    reach = sorted({step % (members // 4) for step in range(-2, 3)})
    count = len(SLABS)

    parts = list(cut(rhs))
    across = [permute(part, across_pairs) for part in parts[:2]]
    panel, down, placed, partner_placed, entry, wish, core_wish = up(
        reach,
        members,
        parts,
        (source_basis, target_basis, leaf_transfer, mid_transfer, far_coupling[0]),
        far_ids,
        near_count,
        near_ids,
    )
    wish = permute(wish, back(along_pairs))
    core_wish = permute(core_wish, back(along_core_pairs))
    others = [permute(panel, [(i, (i - 4 * step) % members) for i in every]) for step in reach[1:]]
    rhs_core = permute(rhs, core_pairs)
    partner_placed = permute(partner_placed, across_pairs)

    across_core, along, nears = [], [], []

    def relay(k):
        picked, core_picked = pack(wish, core_wish, across[k])
        along.append((permute(picked, along_pairs), permute(core_picked, along_core_pairs)))
        across_core.append(permute(across[k], core_pairs))

    def multiply(k):
        pieces = (parts[k], rhs_core, across[k], across_core[k], *along[k])
        nears.append(near(*SLABS[k], entry, near_blocks, pieces))

    across[0], panel, parts[2], wish, core_wish, *others = meet(
        across[0], panel, parts[2], wish, core_wish, *others
    )
    across.append(permute(parts[2], across_pairs))
    relay(0)
    mine = jnp.concatenate([panel, *others], axis=0)
    mine_core = permute(mine, core_pairs)

    along[0] = list(along[0])
    across[1], parts[3], along[0][0], along[0][1], mine_core, partner_placed = meet(
        across[1], parts[3], *along[0], mine_core, partner_placed
    )
    across.append(permute(parts[3], across_pairs))
    relay(1)
    own_sum, partner_sum = couple(mine, mine_core, placed, partner_placed)

    across[2], parts[4], across_core[0], partner_sum, *along[1] = meet(
        across[2], parts[4], across_core[0], partner_sum, *along[1]
    )
    across.append(permute(parts[4], across_pairs))
    relay(2)
    multiply(0)

    across[3], across_core[1], partner_sum, nears[0] = meet(across[3], across_core[1], partner_sum, nears[0])
    relay(3)
    partner_sum = permute(partner_sum, across_pairs)
    multiply(1)

    across[4], across_core[2], nears[1], *along[2] = meet(across[4], across_core[2], nears[1], *along[2])
    relay(4)
    multiply(2)
    multiply(3)
    sums = (own_sum, partner_sum)
    product = finish(SLABS[:-1], sums, down, nears, None)
    multiply(4)
    return finish(SLABS[-1:], sums, down, nears[-1:], product)


def solution(mesh):
    return jax.shard_map(
        on_device,
        mesh=mesh,
        in_specs=(
            P(("parts", "pts"), None),
            P(("parts", "pts"), None, None, None),
            P(("parts", "pts"), None),
            P(("parts", "pts")),
            P(("parts", "pts"), None, None),
            P(("parts", "pts"), None, None),
            P(("parts", "pts"), None, None),
            P(("parts", "pts"), None, None),
            P(("parts", "pts"), None, None, None),
            P(("parts", "pts"), None),
        ),
        out_specs=P(("parts", "pts"), None),
        check_vma=False,
    )
```

time: 214 us -> 92.3 us (0.43)
  the two profiles are of different devices: /device:TPU:14 before, /device:TPU:0 now
where the time goes in v2:
time: 92.3 us; the launch traced here: 92 us
  waiting for transfers between devices  34 us (37%)
  starting transfers between devices  33.1 us (36%)
  Pallas kernels  22.7 us (25%)
  local copies, waits for them, and re-layouts  1.67 us (2%)
    ppermute x29, waiting for transfers between devices, on_device(): permute = lambda value, pairs: lax.ppermute(value, 'pts', pairs)  34 us
    ppermute x29, starting transfers between devices, on_device(): permute = lambda value, pairs: lax.ppermute(value, 'pts', pairs)  33.1 us
    pallas_call x5, Pallas kernels, near(): pl.pallas_call(functools.partial(near_kernel, start), in_specs=[SCALAR] +...  12.8 us
    pallas_call x1, Pallas kernels, up(): pl.pallas_call(functools.partial(up_kernel, reach, members), in_specs=[AN...  3.59 us
    pallas_call x5, Pallas kernels, pack(): pl.pallas_call(pack_kernel, in_specs=[SCALAR, SCALAR, VECTOR], out_shape=...  2.88 us
    pallas_call x2, Pallas kernels, finish(): pl.pallas_call(functools.partial(finish_kernel, slabs), in_specs=in_specs...  2.56 us
  transfers between devices with their start and end apart: 29, of which 12 were waited for; matrix products, arithmetic and copies ran while one was open for 0% of the time, Pallas kernels for 22%

profile of v2, /device:TPU:0, one launch (start us, length us, event | category | flops | bytes accessed | tf_op | source)
XLA Modules:
  0.0 92.0 jit_solution(18309873355918924926)
XLA Ops:
  0.0 0.5 collective-permute-start.17
  0.5 1.6 %copy-done.1 = bf16[1024,1024]{1,0:T(8,128)(2,1)S(1)} copy-done((bf16[1024,1024]{1,0:T(8,128)(2,1)S(1)}, bf16[1024,1024]{1,0:T(8,128)(2,1)}, u32[]{:S(2)}) %copy-start.1) | copy-done | bytes 2097176
  2.1 0.4 shard_map.100
  2.5 2.6 %collective-permute-start = (bf16[1024,256]{1,0:T(8,128)(2,1)S(1)}, bf16[1024,256]{1,0:T(8,128)(2,1)S(1)}, u32[]{:S(2)}, u32[]{:S(2)}) collective-permute-start(bf16[1024,256]{1,0:T(8,128)(2,1)S(1)} %get-tuple-element.58.rest_0_.own_ref), channel_id=1, source_target_pairs={{0,2},{1,3},{2,0},{3,1},{4,6},{5,7},{6,4},{7,5},{8,10},{9,11},{10,... | collective-permute-start | bytes 1572872 | tf_op jit(solution)/shard_map/ppermute | solution.py:333
  5.1 0.0 copy-start
  5.1 3.6 %shard_map.101 = (bf16[64,1024]{1,0:T(8,128)(2,1)S(1)}, bf16[4,256,192]{2,1,0:T(8,128)(2,1)S(1)}, bf16[64,512]{1,0:T(8,128)(2,1)S(1)}, bf16[64,512]{1,0:T(8,128)...) custom-call(bf16[4,64,256]{2,1,0:T(8,128)(2,1)S(1)} %copy-done.2, ...), custom_call_target="tpu_custom_call" | custom-call | flops 1024 | bytes 536870912 | tf_op jit(solution)/shard_map/pallas_call | solution.py:181
  8.7 3.7 %collective-permute-start.1 = (s32[1,128]{1,0:T(1,128)S(1)}, s32[1,128]{1,0:T(1,128)S(1)}, u32[]{:S(2)}, u32[]{:S(2)}) collective-permute-start(s32[1,128]{1,0:T(1,128)S(1)} %get-tuple-element.64), channel_id=1, source_target_pairs={{4,0},{5,1},{14,2},{15,3},{8,4},{9,5},{2,6},{3,7},{12,8},{13,9},{6... | collective-permute-start | bytes 1544 | tf_op jit(solution)/shard_map/ppermute | solution.py:333
  12.4 1.9 %collective-permute-start.2 = (s32[1,128]{1,0:T(1,128)S(1)}, s32[1,128]{1,0:T(1,128)S(1)}, u32[]{:S(2)}, u32[]{:S(2)}) collective-permute-start(s32[1,128]{1,0:T(1,128)S(1)} %get-tuple-element.65), channel_id=1, source_target_pairs={{4,1},{15,2},{8,5},{3,6},{12,9},{7,10},{0,13},{11,14},{20,17},{31,... | collective-permute-start | bytes 1544 | tf_op jit(solution)/shard_map/ppermute | solution.py:333
  14.3 0.5 collective-permute-start.3
  14.8 0.0 collective-permute-done.1.wish_ref
  14.8 2.6 %collective-permute-start.4 = (bf16[64,1024]{1,0:T(8,128)(2,1)S(1)}, bf16[64,1024]{1,0:T(8,128)(2,1)S(1)}, u32[]{:S(2)}, u32[]{:S(2)}) collective-permute-start(bf16[64,1024]{1,0:T(8,128)(2,1)S(1)} %get-tuple-element.66), channel_id=1, source_target_pairs={{0,8},{1,9},{2,10},{3,11},{4,12},{5,13},{6,14},{7,15},{8,0},{9,1},... | collective-permute-start | bytes 393224 | tf_op jit(solution)/shard_map/ppermute | solution.py:333
  17.4 0.9 collective-permute-start.5
  18.3 2.1 %collective-permute-done.3 = bf16[64,1024]{1,0:T(8,128)(2,1)S(1)} collective-permute-done((bf16[64,1024]{1,0:T(8,128)(2,1)S(1)}, bf16[64,1024]{1,0:T(8,128)(2,1)S(1)}, u32[]{:S(2)}, u32[]{:S(2)}) %collective-permute-start.3) | collective-permute-done | bytes 131104 | tf_op jit(solution)/shard_map/ppermute | solution.py:333
  20.4 0.0 collective-permute-start.6
  20.4 6.8 %collective-permute-done.4 = bf16[64,1024]{1,0:T(8,128)(2,1)S(1)} collective-permute-done((bf16[64,1024]{1,0:T(8,128)(2,1)S(1)}, bf16[64,1024]{1,0:T(8,128)(2,1)S(1)}, u32[]{:S(2)}, u32[]{:S(2)}) %collective-permute-start.4) | collective-permute-done | bytes 131104 | tf_op jit(solution)/shard_map/ppermute | solution.py:333
  27.3 0.1 collective-permute-start.9
  27.4 0.6 shard_map.102
  28.0 0.1 collective-permute-start.7
  28.0 1.2 %collective-permute-start.10 = (bf16[64,512]{1,0:T(8,128)(2,1)S(1)}, bf16[64,512]{1,0:T(8,128)(2,1)S(1)}, u32[]{:S(2)}, u32[]{:S(2)}) collective-permute-start(bf16[64,512]{1,0:T(8,128)(2,1)S(1)} %get-tuple-element.75), channel_id=1, source_target_pairs={{0,2},{1,3},{2,0},{3,1},{4,6},{5,7},{6,4},{7,5},{8,10},{9,11},{10,... | collective-permute-start | bytes 196616 | tf_op jit(solution)/shard_map/ppermute | solution.py:333
  29.2 5.0 %collective-permute-done.10.partner_ref = bf16[64,512]{1,0:T(8,128)(2,1)S(1)} collective-permute-done((bf16[64,512]{1,0:T(8,128)(2,1)S(1)}, bf16[64,512]{1,0:T(8,128)(2,1)S(1)}, u32[]{:S(2)}, u32[]{:S(2)}) %collective-permute-start.10) | collective-permute-done | bytes 65568 | tf_op jit(solution)/shard_map/ppermute | solution.py:333
  34.2 0.9 collective-permute-start.13
  35.2 0.0 collective-permute-done.6.arrived_ref.across_ref
  35.2 1.3 %collective-permute-start.8 = (bf16[512,256]{1,0:T(8,128)(2,1)S(1)}, bf16[512,256]{1,0:T(8,128)(2,1)S(1)}, u32[]{:S(2)}, u32[]{:S(2)}) collective-permute-start(bf16[512,256]{1,0:T(8,128)(2,1)S(1)} %get-tuple-element.74), channel_id=1, source_target_pairs={{1,4},{2,15},{5,8},{6,3},{9,12},{10,7},{13,0},{14,11},{17,20},{18,... | collective-permute-start | bytes 786440 | tf_op jit(solution)/shard_map/ppermute | solution.py:333
  36.4 2.1 %collective-permute-done.7.along_ref = bf16[512,256]{1,0:T(8,128)(2,1)S(1)} collective-permute-done((bf16[512,256]{1,0:T(8,128)(2,1)S(1)}, bf16[512,256]{1,0:T(8,128)(2,1)S(1)}, u32[]{:S(2)}, u32[]{:S(2)}) %collective-permute-start.7) | collective-permute-done | bytes 262176 | tf_op jit(solution)/shard_map/ppermute | solution.py:333
  38.5 0.6 collective-permute-start.14
  39.1 5.6 %collective-permute-done.8.along_core_ref = bf16[512,256]{1,0:T(8,128)(2,1)S(1)} collective-permute-done((bf16[512,256]{1,0:T(8,128)(2,1)S(1)}, bf16[512,256]{1,0:T(8,128)(2,1)S(1)}, u32[]{:S(2)}, u32[]{:S(2)}) %collective-permute-start.8) | collective-permute-done | bytes 262176 | tf_op jit(solution)/shard_map/ppermute | solution.py:333
  44.6 0.0 collective-permute-done.9.core_ref
  44.6 0.6 shard_map.104
  45.2 0.1 collective-permute-start.15
  45.3 1.3 %collective-permute-start.16 = (bf16[512,256]{1,0:T(8,128)(2,1)S(1)}, bf16[512,256]{1,0:T(8,128)(2,1)S(1)}, u32[]{:S(2)}, u32[]{:S(2)}) collective-permute-start(bf16[512,256]{1,0:T(8,128)(2,1)S(1)} %get-tuple-element.85), channel_id=1, source_target_pairs={{1,4},{2,15},{5,8},{6,3},{9,12},{10,7},{13,0},{14,11},{17,20},{18,... | collective-permute-start | bytes 786440 | tf_op jit(solution)/shard_map/ppermute | solution.py:333
  46.6 0.8 collective-permute-start.12
  47.4 0.5 shard_map.103
  47.9 0.0 collective-permute-done.14.across_core_ref
  47.9 3.6 %collective-permute-start.11 = (bf16[1024,128]{1,0:T(8,128)(2,1)S(1)}, bf16[1024,128]{1,0:T(8,128)(2,1)S(1)}, u32[]{:S(2)}, u32[]{:S(2)}) collective-permute-start(bf16[1024,128]{1,0:T(8,128)(2,1)S(1)} %get-tuple-element.80.rest_3_.own_ref), channel_id=1, source_target_pairs={{0,2},{1,3},{2,0},{3,1},{4,6},{5,7},{6,4},{7,5},{8,10},{9,11},{10,... | collective-permute-start | bytes 786440 | tf_op jit(solution)/shard_map/ppermute | solution.py:333
  51.5 3.3 %collective-permute-done.15.along_ref = bf16[512,256]{1,0:T(8,128)(2,1)S(1)} collective-permute-done((bf16[512,256]{1,0:T(8,128)(2,1)S(1)}, bf16[512,256]{1,0:T(8,128)(2,1)S(1)}, u32[]{:S(2)}, u32[]{:S(2)}) %collective-permute-start.15) | collective-permute-done | bytes 262176 | tf_op jit(solution)/shard_map/ppermute | solution.py:333
  54.9 1.4 %collective-permute-done.16.along_core_ref = bf16[512,256]{1,0:T(8,128)(2,1)S(1)} collective-permute-done((bf16[512,256]{1,0:T(8,128)(2,1)S(1)}, bf16[512,256]{1,0:T(8,128)(2,1)S(1)}, u32[]{:S(2)}, u32[]{:S(2)}) %collective-permute-start.16) | collective-permute-done | bytes 262176 | tf_op jit(solution)/shard_map/ppermute | solution.py:333
  56.3 0.0 collective-permute-start.20
  56.3 0.6 shard_map.107
  56.9 0.1 collective-permute-start.21
  56.9 1.6 %collective-permute-done.11.arrived_ref.across_ref = bf16[1024,128]{1,0:T(8,128)(2,1)S(1)} collective-permute-done((bf16[1024,128]{1,0:T(8,128)(2,1)S(1)}, bf16[1024,128]{1,0:T(8,128)(2,1)S(1)}, u32[]{:S(2)}, u32[]{:S(2)}) %collective-permute-start.11) | collective-permute-done | bytes 262176 | tf_op jit(solution)/shard_map/ppermute | solution.py:333
  58.5 1.3 %collective-permute-start.22 = (bf16[512,256]{1,0:T(8,128)(2,1)S(1)}, bf16[512,256]{1,0:T(8,128)(2,1)S(1)}, u32[]{:S(2)}, u32[]{:S(2)}) collective-permute-start(bf16[512,256]{1,0:T(8,128)(2,1)S(1)} %get-tuple-element.99), channel_id=1, source_target_pairs={{1,4},{2,15},{5,8},{6,3},{9,12},{10,7},{13,0},{14,11},{17,20},{18,... | collective-permute-start | bytes 786440 | tf_op jit(solution)/shard_map/ppermute | solution.py:333
  59.8 0.0 collective-permute-done.17.core_ref
  59.8 3.8 %collective-permute-start.19 = (bf16[1024,128]{1,0:T(8,128)(2,1)S(1)}, bf16[1024,128]{1,0:T(8,128)(2,1)S(1)}, u32[]{:S(2)}, u32[]{:S(2)}) collective-permute-start(bf16[1024,128]{1,0:T(8,128)(2,1)S(1)} %get-tuple-element.93.rest_4_.own_ref), channel_id=1, source_target_pairs={{0,2},{1,3},{2,0},{3,1},{4,6},{5,7},{6,4},{7,5},{8,10},{9,11},{10,... | collective-permute-start | bytes 786440 | tf_op jit(solution)/shard_map/ppermute | solution.py:333
  63.6 2.6 %shard_map.105.rest_0_ = f32[1024,256]{1,0:T(8,128)S(1)} custom-call(s32[4,12]{1,0:T(4,128)S(1)} %get-tuple-element.87.entry_ref, bf16[4,12,256,256]{3,2,1,0:T(8,128)(2,1)S(1)} %copy-done, bf16[1024,256]{1,0:T(8,128)(2,1)S(1)} %get-tuple-element.58.rest_0_.own_ref, bf16[1024,1024]{1,0:T(8,128)(2,1)S(1)} %collective-permute-done.17.core_ref, ...), custom_call_target="tpu_custom_call" | custom-call | flops 1024 | bytes 8388608 | tf_op jit(solution)/shard_map/pallas_call | solution.py:258
  66.2 0.0 collective-permute-done.12.across_core_ref
  66.2 0.6 shard_map.111
  66.8 0.1 collective-permute-start.26
  66.9 2.6 %shard_map.106.rest_1_ = f32[1024,256]{1,0:T(8,128)S(1)} custom-call(s32[4,12]{1,0:T(4,128)S(1)} %get-tuple-element.87.entry_ref, bf16[4,12,256,256]{3,2,1,0:T(8,128)(2,1)S(1)} %copy-done, bf16[1024,256]{1,0:T(8,128)(2,1)S(1)} %get-tuple-element.59.rest_1_.own_ref, bf16[1024,1024]{1,0:T(8,128)(2,1)S(1)} %collective-permute-done.17.core_ref, ...), custom_call_target="tpu_custom_call" | custom-call | flops 1024 | bytes 8388608 | tf_op jit(solution)/shard_map/pallas_call | solution.py:258
  69.5 0.0 collective-permute-done.21.along_ref
  69.5 0.1 collective-permute-start.27
  69.6 0.7 collective-permute-done.22.along_core_ref
  70.2 1.3 %collective-permute-start.28 = (bf16[512,128]{1,0:T(8,128)(2,1)S(1)}, bf16[512,128]{1,0:T(8,128)(2,1)S(1)}, u32[]{:S(2)}, u32[]{:S(2)}) collective-permute-start(bf16[512,128]{1,0:T(8,128)(2,1)S(1)} %get-tuple-element.110), channel_id=1, source_target_pairs={{1,4},{2,15},{5,8},{6,3},{9,12},{10,7},{13,0},{14,11},{17,20},{18,... | collective-permute-start | bytes 393224 | tf_op jit(solution)/shard_map/ppermute | solution.py:333
  71.5 1.8 %collective-permute-start.23 = (bf16[1024,128]{1,0:T(8,128)(2,1)S(1)}, bf16[1024,128]{1,0:T(8,128)(2,1)S(1)}, u32[]{:S(2)}, u32[]{:S(2)}) collective-permute-start(bf16[1024,128]{1,0:T(8,128)(2,1)S(1)} %collective-permute-done.19.arrived_ref.across_ref), channel_id=1, source_target_pairs={{0,1},{1,0},{2,3},{3,2},{4,5},{5,4},{6,7},{7,6},{8,9},{9,8},{10,11... | collective-permute-start | bytes 786440 | tf_op jit(solution)/shard_map/ppermute | solution.py:333
  73.3 0.8 collective-permute-start.18
  74.1 0.6 shard_map.108
  74.7 2.8 %collective-permute-done.27.along_ref = bf16[512,128]{1,0:T(8,128)(2,1)S(1)} collective-permute-done((bf16[512,128]{1,0:T(8,128)(2,1)S(1)}, bf16[512,128]{1,0:T(8,128)(2,1)S(1)}, u32[]{:S(2)}, u32[]{:S(2)}) %collective-permute-start.27) | collective-permute-done | bytes 131104 | tf_op jit(solution)/shard_map/ppermute | solution.py:333
  77.5 1.1 %collective-permute-done.28.along_core_ref = bf16[512,128]{1,0:T(8,128)(2,1)S(1)} collective-permute-done((bf16[512,128]{1,0:T(8,128)(2,1)S(1)}, bf16[512,128]{1,0:T(8,128)(2,1)S(1)}, u32[]{:S(2)}, u32[]{:S(2)}) %collective-permute-start.28) | collective-permute-done | bytes 131104 | tf_op jit(solution)/shard_map/ppermute | solution.py:333
  78.7 1.5 %collective-permute-start.25 = (bf16[512,128]{1,0:T(8,128)(2,1)S(1)}, bf16[512,128]{1,0:T(8,128)(2,1)S(1)}, u32[]{:S(2)}, u32[]{:S(2)}) collective-permute-start(bf16[512,128]{1,0:T(8,128)(2,1)S(1)} %get-tuple-element.102), channel_id=1, source_target_pairs={{1,4},{2,15},{5,8},{6,3},{9,12},{10,7},{13,0},{14,11},{17,20},{18,... | collective-permute-start | bytes 393224 | tf_op jit(solution)/shard_map/ppermute | solution.py:333
  80.1 2.6 %shard_map.110.rest_2_ = f32[1024,256]{1,0:T(8,128)S(1)} custom-call(s32[4,12]{1,0:T(4,128)S(1)} %get-tuple-element.87.entry_ref, bf16[4,12,256,256]{3,2,1,0:T(8,128)(2,1)S(1)} %copy-done, bf16[1024,256]{1,0:T(8,128)(2,1)S(1)} %get-tuple-element.82.rest_2_.own_ref, bf16[1024,1024]{1,0:T(8,128)(2,1)S(1)} %collective-permute-done.17.core_ref, ...), custom_call_target="tpu_custom_call" | custom-call | flops 1024 | bytes 8388608 | tf_op jit(solution)/shard_map/pallas_call | solution.py:258
  82.7 2.5 %shard_map.112.rest_3_ = f32[1024,128]{1,0:T(8,128)S(1)} custom-call(s32[4,12]{1,0:T(4,128)S(1)} %get-tuple-element.87.entry_ref, bf16[4,12,256,256]{3,2,1,0:T(8,128)(2,1)S(1)} %copy-done, bf16[1024,128]{1,0:T(8,128)(2,1)S(1)} %get-tuple-element.80.rest_3_.own_ref, bf16[1024,1024]{1,0:T(8,128)(2,1)S(1)} %collective-permute-done.17.core_ref, ...), custom_call_target="tpu_custom_call" | custom-call | flops 1024 | bytes 8388608 | tf_op jit(solution)/shard_map/pallas_call | solution.py:258
  85.3 1.4 %collective-permute-done.25.along_core_ref = bf16[512,128]{1,0:T(8,128)(2,1)S(1)} collective-permute-done((bf16[512,128]{1,0:T(8,128)(2,1)S(1)}, bf16[512,128]{1,0:T(8,128)(2,1)S(1)}, u32[]{:S(2)}, u32[]{:S(2)}) %collective-permute-start.25) | collective-permute-done | bytes 131104 | tf_op jit(solution)/shard_map/ppermute | solution.py:333
  86.7 2.5 %shard_map.109.rest_0_ = f32[1024,128]{1,0:T(8,128)S(1)} custom-call(s32[4,12]{1,0:T(4,128)S(1)} %get-tuple-element.87.entry_ref, bf16[4,12,256,256]{3,2,1,0:T(8,128)(2,1)S(1)} %copy-done, bf16[1024,128]{1,0:T(8,128)(2,1)S(1)} %get-tuple-element.93.rest_4_.own_ref, bf16[1024,1024]{1,0:T(8,128)(2,1)S(1)} %collective-permute-done.17.core_ref, ...), custom_call_target="tpu_custom_call" | custom-call | flops 1024 | bytes 8388608 | tf_op jit(solution)/shard_map/pallas_call | solution.py:258
  89.3 1.6 %shard_map.113.rest_1_ = bf16[1024,1024]{1,0:T(8,128)(2,1)} custom-call(f32[64,1024]{1,0:T(8,128)S(1)} %get-tuple-element.79.own_sum_ref, f32[64,1024]{1,0:T(8,128)S(1)} %collective-permute-done.18.partner_sum_ref, bf16[4,256,192]{2,1,0:T(8,128)(2,1)S(1)} %get-tuple-element.92.down_ref, f32[1024,256]{1,0:T(8,128)S(1)} %shard_map.105.rest_0_, ...), custom_call_target="tpu_custom_call" | custom-call | flops 1024 | bytes 4194304 | tf_op jit(solution)/shard_map/pallas_call | solution.py:299
  90.9 1.0 %shard_map.114 = bf16[1024,1024]{1,0:T(8,128)(2,1)} custom-call(f32[64,1024]{1,0:T(8,128)S(1)} %get-tuple-element.79.own_sum_ref, f32[64,1024]{1,0:T(8,128)S(1)} %collective-permute-done.18.partner_sum_ref, bf16[4,256,192]{2,1,0:T(8,128)(2,1)S(1)} %get-tuple-element.92.down_ref, f32[1024,128]{1,0:T(8,128)S(1)} %shard_map.109.rest_0_, ...), custom_call_target="tpu_custom_call", output_to_operand_aliasing={{}: (4, {})} | custom-call | flops 1024 | bytes 4194304 | tf_op jit(solution)/shard_map/pallas_call | solution.py:299
  (33 shorter events, 0.1 us)
Async XLA Ops:
  0.0 59.8 %collective-permute-start.17 = (bf16[1024,1024]{1,0:T(8,128)(2,1)}, bf16[1024,1024]{1,0:T(8,128)(2,1)S(1)}, u32[]{:S(2)}, u32[]{:S(2)}) collective-permute-start(bf16[1024,1024]{1,0:T(8,128)(2,1)} %rhs_any.1), channel_id=1, source_target_pairs={{0,1},{1,0},{2,3},{3,2},{4,5},{5,4},{6,7},{7,6},{8,9},{9,8},{10,11... | collective-permute-start | bytes 6291464 | tf_op jit(solution)/shard_map/ppermute | solution.py:333
  0.5 1.6 %copy-start.1 = (bf16[1024,1024]{1,0:T(8,128)(2,1)S(1)}, bf16[1024,1024]{1,0:T(8,128)(2,1)}, u32[]{:S(2)}) copy-start(bf16[1024,1024]{1,0:T(8,128)(2,1)} %rhs_any.1) | copy-start | bytes 6291460
  2.0 3.0 %copy-start.2 = (bf16[4,64,256]{2,1,0:T(8,128)(2,1)S(1)}, bf16[4,64,256]{2,1,0:T(8,128)(2,1)}, u32[]{:S(2)}) copy-start(bf16[4,64,256]{2,1,0:T(8,128)(2,1)} %source_any.1) | copy-start | bytes 393220
  2.0 3.0 %copy-start.3 = (bf16[4,64,256]{2,1,0:T(8,128)(2,1)S(1)}, bf16[4,64,256]{2,1,0:T(8,128)(2,1)}, u32[]{:S(2)}) copy-start(bf16[4,64,256]{2,1,0:T(8,128)(2,1)} %target_any.1) | copy-start | bytes 393220
  2.0 3.0 %copy-start.4 = (bf16[1,6,64,64]{3,2,1,0:T(8,128)(2,1)S(1)}, bf16[1,6,64,64]{3,2,1,0:T(8,128)(2,1)}, u32[]{:S(2)}) copy-start(bf16[1,6,64,64]{3,2,1,0:T(8,128)(2,1)} %param.18) | copy-start | bytes 147460
  2.1 3.0 %copy-start.5 = (bf16[4,64,64]{2,1,0:T(8,128)(2,1)S(1)}, bf16[4,64,64]{2,1,0:T(8,128)(2,1)}, u32[]{:S(2)}) copy-start(bf16[4,64,64]{2,1,0:T(8,128)(2,1)} %leaf_any.1) | copy-start | bytes 98308
  2.1 3.0 %copy-start.6 = (bf16[2,64,64]{2,1,0:T(8,128)(2,1)S(1)}, bf16[2,64,64]{2,1,0:T(8,128)(2,1)}, u32[]{:S(2)}) copy-start(bf16[2,64,64]{2,1,0:T(8,128)(2,1)} %mid_any.1) | copy-start | bytes 49156
  2.1 3.0 %copy-start.7 = (s32[4,12]{1,0:T(4,128)S(1)}, s32[4,12]{1,0:T(4,128)}, u32[]{:S(2)}) copy-start(s32[4,12]{1,0:T(4,128)} %ids_any.1) | copy-start | bytes 580
  2.1 3.0 %copy-start.8 = (s32[1,6]{1,0:T(1,128)S(1)}, s32[1,6]{1,0:T(1,128)}, u32[]{:S(2)}) copy-start(s32[1,6]{1,0:T(1,128)} %far_any.1) | copy-start | bytes 76
  2.1 3.0 %copy-start.9 = (s32[4]{0:T(128)S(1)}, s32[4]{0:T(128)}, u32[]{:S(2)}) copy-start(s32[4]{0:T(128)} %count_any.1) | copy-start | bytes 52
  2.5 24.7 %collective-permute-start = (bf16[1024,256]{1,0:T(8,128)(2,1)S(1)}, bf16[1024,256]{1,0:T(8,128)(2,1)S(1)}, u32[]{:S(2)}, u32[]{:S(2)}) collective-permute-start(bf16[1024,256]{1,0:T(8,128)(2,1)S(1)} %get-tuple-element.58.rest_0_.own_ref), channel_id=1, source_target_pairs={{0,2},{1,3},{2,0},{3,1},{4,6},{5,7},{6,4},{7,5},{8,10},{9,11},{10,... | collective-permute-start | bytes 1572872 | tf_op jit(solution)/shard_map/ppermute | solution.py:333
  5.1 58.5 %copy-start = (bf16[4,12,256,256]{3,2,1,0:T(8,128)(2,1)S(1)}, bf16[4,12,256,256]{3,2,1,0:T(8,128)(2,1)}, u32[]{:S(2)}) copy-start(bf16[4,12,256,256]{3,2,1,0:T(8,128)(2,1)} %near_ref.9) | copy-start | bytes 18874372
  8.7 6.1 %collective-permute-start.1 = (s32[1,128]{1,0:T(1,128)S(1)}, s32[1,128]{1,0:T(1,128)S(1)}, u32[]{:S(2)}, u32[]{:S(2)}) collective-permute-start(s32[1,128]{1,0:T(1,128)S(1)} %get-tuple-element.64), channel_id=1, source_target_pairs={{4,0},{5,1},{14,2},{15,3},{8,4},{9,5},{2,6},{3,7},{12,8},{13,9},{6... | collective-permute-start | bytes 1544 | tf_op jit(solution)/shard_map/ppermute | solution.py:333
  12.4 5.0 %collective-permute-start.2 = (s32[1,128]{1,0:T(1,128)S(1)}, s32[1,128]{1,0:T(1,128)S(1)}, u32[]{:S(2)}, u32[]{:S(2)}) collective-permute-start(s32[1,128]{1,0:T(1,128)S(1)} %get-tuple-element.65), channel_id=1, source_target_pairs={{4,1},{15,2},{8,5},{3,6},{12,9},{7,10},{0,13},{11,14},{20,17},{31,... | collective-permute-start | bytes 1544 | tf_op jit(solution)/shard_map/ppermute | solution.py:333
  14.3 6.1 %collective-permute-start.3 = (bf16[64,1024]{1,0:T(8,128)(2,1)S(1)}, bf16[64,1024]{1,0:T(8,128)(2,1)S(1)}, u32[]{:S(2)}, u32[]{:S(2)}) collective-permute-start(bf16[64,1024]{1,0:T(8,128)(2,1)S(1)} %get-tuple-element.66), channel_id=1, source_target_pairs={{0,12},{1,13},{2,14},{3,15},{4,0},{5,1},{6,2},{7,3},{8,4},{9,5},{1... | collective-permute-start | bytes 393224 | tf_op jit(solution)/shard_map/ppermute | solution.py:333
  14.8 12.4 %collective-permute-start.4 = (bf16[64,1024]{1,0:T(8,128)(2,1)S(1)}, bf16[64,1024]{1,0:T(8,128)(2,1)S(1)}, u32[]{:S(2)}, u32[]{:S(2)}) collective-permute-start(bf16[64,1024]{1,0:T(8,128)(2,1)S(1)} %get-tuple-element.66), channel_id=1, source_target_pairs={{0,8},{1,9},{2,10},{3,11},{4,12},{5,13},{6,14},{7,15},{8,0},{9,1},... | collective-permute-start | bytes 393224 | tf_op jit(solution)/shard_map/ppermute | solution.py:333
  17.4 9.8 %collective-permute-start.5 = (bf16[64,1024]{1,0:T(8,128)(2,1)S(1)}, bf16[64,1024]{1,0:T(8,128)(2,1)S(1)}, u32[]{:S(2)}, u32[]{:S(2)}) collective-permute-start(bf16[64,1024]{1,0:T(8,128)(2,1)S(1)} %get-tuple-element.66), channel_id=1, source_target_pairs={{0,4},{1,5},{2,6},{3,7},{4,8},{5,9},{6,10},{7,11},{8,12},{9,13},{1... | collective-permute-start | bytes 393224 | tf_op jit(solution)/shard_map/ppermute | solution.py:333
  20.4 14.8 %collective-permute-start.6 = (bf16[1024,256]{1,0:T(8,128)(2,1)S(1)}, bf16[1024,256]{1,0:T(8,128)(2,1)S(1)}, u32[]{:S(2)}, u32[]{:S(2)}) collective-permute-start(bf16[1024,256]{1,0:T(8,128)(2,1)S(1)} %get-tuple-element.59.rest_1_.own_ref), channel_id=1, source_target_pairs={{0,2},{1,3},{2,0},{3,1},{4,6},{5,7},{6,4},{7,5},{8,10},{9,11},{10,... | collective-permute-start | bytes 1572872 | tf_op jit(solution)/shard_map/ppermute | solution.py:333
  27.3 17.3 %collective-permute-start.9 = (bf16[256,1024]{1,0:T(8,128)(2,1)S(1)}, bf16[256,1024]{1,0:T(8,128)(2,1)S(1)}, u32[]{:S(2)}, u32[]{:S(2)}) collective-permute-start(bf16[256,1024]{1,0:T(8,128)(2,1)S(1)} %constant_dynamic-update-slice_fusion.mine_ref), channel_id=1, source_target_pairs={{0,1},{1,0},{2,3},{3,2},{4,5},{5,4},{6,7},{7,6},{8,9},{9,8},{10,11... | collective-permute-start | bytes 1572872 | tf_op jit(solution)/shard_map/ppermute | solution.py:333
  28.0 10.6 %collective-permute-start.7 = (bf16[512,256]{1,0:T(8,128)(2,1)S(1)}, bf16[512,256]{1,0:T(8,128)(2,1)S(1)}, u32[]{:S(2)}, u32[]{:S(2)}) collective-permute-start(bf16[512,256]{1,0:T(8,128)(2,1)S(1)} %get-tuple-element.73), channel_id=1, source_target_pairs={{0,4},{1,5},{2,14},{3,15},{4,8},{5,9},{6,2},{7,3},{8,12},{9,13},{1... | collective-permute-start | bytes 786440 | tf_op jit(solution)/shard_map/ppermute | solution.py:333
  28.0 6.2 %collective-permute-start.10 = (bf16[64,512]{1,0:T(8,128)(2,1)S(1)}, bf16[64,512]{1,0:T(8,128)(2,1)S(1)}, u32[]{:S(2)}, u32[]{:S(2)}) collective-permute-start(bf16[64,512]{1,0:T(8,128)(2,1)S(1)} %get-tuple-element.75), channel_id=1, source_target_pairs={{0,2},{1,3},{2,0},{3,1},{4,6},{5,7},{6,4},{7,5},{8,10},{9,11},{10,... | collective-permute-start | bytes 196616 | tf_op jit(solution)/shard_map/ppermute | solution.py:333
  34.2 12.3 %collective-permute-start.13 = (bf16[1024,256]{1,0:T(8,128)(2,1)S(1)}, bf16[1024,256]{1,0:T(8,128)(2,1)S(1)}, u32[]{:S(2)}, u32[]{:S(2)}) collective-permute-start(bf16[1024,256]{1,0:T(8,128)(2,1)S(1)} %get-tuple-element.82.rest_2_.own_ref), channel_id=1, source_target_pairs={{0,2},{1,3},{2,0},{3,1},{4,6},{5,7},{6,4},{7,5},{8,10},{9,11},{10,... | collective-permute-start | bytes 1572872 | tf_op jit(solution)/shard_map/ppermute | solution.py:333
  35.2 9.5 %collective-permute-start.8 = (bf16[512,256]{1,0:T(8,128)(2,1)S(1)}, bf16[512,256]{1,0:T(8,128)(2,1)S(1)}, u32[]{:S(2)}, u32[]{:S(2)}) collective-permute-start(bf16[512,256]{1,0:T(8,128)(2,1)S(1)} %get-tuple-element.74), channel_id=1, source_target_pairs={{1,4},{2,15},{5,8},{6,3},{9,12},{10,7},{13,0},{14,11},{17,20},{18,... | collective-permute-start | bytes 786440 | tf_op jit(solution)/shard_map/ppermute | solution.py:333
  38.5 9.4 %collective-permute-start.14 = (bf16[1024,256]{1,0:T(8,128)(2,1)S(1)}, bf16[1024,256]{1,0:T(8,128)(2,1)S(1)}, u32[]{:S(2)}, u32[]{:S(2)}) collective-permute-start(bf16[1024,256]{1,0:T(8,128)(2,1)S(1)} %collective-permute-done.arrived_ref.across_ref), channel_id=1, source_target_pairs={{0,1},{1,0},{2,3},{3,2},{4,5},{5,4},{6,7},{7,6},{8,9},{9,8},{10,11... | collective-permute-start | bytes 1572872 | tf_op jit(solution)/shard_map/ppermute | solution.py:333
  45.2 9.7 %collective-permute-start.15 = (bf16[512,256]{1,0:T(8,128)(2,1)S(1)}, bf16[512,256]{1,0:T(8,128)(2,1)S(1)}, u32[]{:S(2)}, u32[]{:S(2)}) collective-permute-start(bf16[512,256]{1,0:T(8,128)(2,1)S(1)} %get-tuple-element.84), channel_id=1, source_target_pairs={{0,4},{1,5},{2,14},{3,15},{4,8},{5,9},{6,2},{7,3},{8,12},{9,13},{1... | collective-permute-start | bytes 786440 | tf_op jit(solution)/shard_map/ppermute | solution.py:333
  45.3 11.0 %collective-permute-start.16 = (bf16[512,256]{1,0:T(8,128)(2,1)S(1)}, bf16[512,256]{1,0:T(8,128)(2,1)S(1)}, u32[]{:S(2)}, u32[]{:S(2)}) collective-permute-start(bf16[512,256]{1,0:T(8,128)(2,1)S(1)} %get-tuple-element.85), channel_id=1, source_target_pairs={{1,4},{2,15},{5,8},{6,3},{9,12},{10,7},{13,0},{14,11},{17,20},{18,... | collective-permute-start | bytes 786440 | tf_op jit(solution)/shard_map/ppermute | solution.py:333
  46.6 19.6 %collective-permute-start.12 = (bf16[1024,256]{1,0:T(8,128)(2,1)S(1)}, bf16[1024,256]{1,0:T(8,128)(2,1)S(1)}, u32[]{:S(2)}, u32[]{:S(2)}) collective-permute-start(bf16[1024,256]{1,0:T(8,128)(2,1)S(1)} %collective-permute-done.6.arrived_ref.across_ref), channel_id=1, source_target_pairs={{0,1},{1,0},{2,3},{3,2},{4,5},{5,4},{6,7},{7,6},{8,9},{9,8},{10,11... | collective-permute-start | bytes 1572872 | tf_op jit(solution)/shard_map/ppermute | solution.py:333
  47.9 10.6 %collective-permute-start.11 = (bf16[1024,128]{1,0:T(8,128)(2,1)S(1)}, bf16[1024,128]{1,0:T(8,128)(2,1)S(1)}, u32[]{:S(2)}, u32[]{:S(2)}) collective-permute-start(bf16[1024,128]{1,0:T(8,128)(2,1)S(1)} %get-tuple-element.80.rest_3_.own_ref), channel_id=1, source_target_pairs={{0,2},{1,3},{2,0},{3,1},{4,6},{5,7},{6,4},{7,5},{8,10},{9,11},{10,... | collective-permute-start | bytes 786440 | tf_op jit(solution)/shard_map/ppermute | solution.py:333
  56.3 15.3 %collective-permute-start.20 = (bf16[1024,256]{1,0:T(8,128)(2,1)S(1)}, bf16[1024,256]{1,0:T(8,128)(2,1)S(1)}, u32[]{:S(2)}, u32[]{:S(2)}) collective-permute-start(bf16[1024,256]{1,0:T(8,128)(2,1)S(1)} %collective-permute-done.13.arrived_ref.across_ref), channel_id=1, source_target_pairs={{0,1},{1,0},{2,3},{3,2},{4,5},{5,4},{6,7},{7,6},{8,9},{9,8},{10,11... | collective-permute-start | bytes 1572872 | tf_op jit(solution)/shard_map/ppermute | solution.py:333
  56.9 12.6 %collective-permute-start.21 = (bf16[512,256]{1,0:T(8,128)(2,1)S(1)}, bf16[512,256]{1,0:T(8,128)(2,1)S(1)}, u32[]{:S(2)}, u32[]{:S(2)}) collective-permute-start(bf16[512,256]{1,0:T(8,128)(2,1)S(1)} %get-tuple-element.98), channel_id=1, source_target_pairs={{0,4},{1,5},{2,14},{3,15},{4,8},{5,9},{6,2},{7,3},{8,12},{9,13},{1... | collective-permute-start | bytes 786440 | tf_op jit(solution)/shard_map/ppermute | solution.py:333
  58.5 11.7 %collective-permute-start.22 = (bf16[512,256]{1,0:T(8,128)(2,1)S(1)}, bf16[512,256]{1,0:T(8,128)(2,1)S(1)}, u32[]{:S(2)}, u32[]{:S(2)}) collective-permute-start(bf16[512,256]{1,0:T(8,128)(2,1)S(1)} %get-tuple-element.99), channel_id=1, source_target_pairs={{1,4},{2,15},{5,8},{6,3},{9,12},{10,7},{13,0},{14,11},{17,20},{18,... | collective-permute-start | bytes 786440 | tf_op jit(solution)/shard_map/ppermute | solution.py:333
  59.8 11.7 %collective-permute-start.19 = (bf16[1024,128]{1,0:T(8,128)(2,1)S(1)}, bf16[1024,128]{1,0:T(8,128)(2,1)S(1)}, u32[]{:S(2)}, u32[]{:S(2)}) collective-permute-start(bf16[1024,128]{1,0:T(8,128)(2,1)S(1)} %get-tuple-element.93.rest_4_.own_ref), channel_id=1, source_target_pairs={{0,2},{1,3},{2,0},{3,1},{4,6},{5,7},{6,4},{7,5},{8,10},{9,11},{10,... | collective-permute-start | bytes 786440 | tf_op jit(solution)/shard_map/ppermute | solution.py:333
  66.8 15.9 %collective-permute-start.26 = (bf16[1024,128]{1,0:T(8,128)(2,1)S(1)}, bf16[1024,128]{1,0:T(8,128)(2,1)S(1)}, u32[]{:S(2)}, u32[]{:S(2)}) collective-permute-start(bf16[1024,128]{1,0:T(8,128)(2,1)S(1)} %collective-permute-done.11.arrived_ref.across_ref), channel_id=1, source_target_pairs={{0,1},{1,0},{2,3},{3,2},{4,5},{5,4},{6,7},{7,6},{8,9},{9,8},{10,11... | collective-permute-start | bytes 786440 | tf_op jit(solution)/shard_map/ppermute | solution.py:333
  69.5 8.0 %collective-permute-start.27 = (bf16[512,128]{1,0:T(8,128)(2,1)S(1)}, bf16[512,128]{1,0:T(8,128)(2,1)S(1)}, u32[]{:S(2)}, u32[]{:S(2)}) collective-permute-start(bf16[512,128]{1,0:T(8,128)(2,1)S(1)} %get-tuple-element.109), channel_id=1, source_target_pairs={{0,4},{1,5},{2,14},{3,15},{4,8},{5,9},{6,2},{7,3},{8,12},{9,13},{1... | collective-permute-start | bytes 393224 | tf_op jit(solution)/shard_map/ppermute | solution.py:333
  70.2 8.4 %collective-permute-start.28 = (bf16[512,128]{1,0:T(8,128)(2,1)S(1)}, bf16[512,128]{1,0:T(8,128)(2,1)S(1)}, u32[]{:S(2)}, u32[]{:S(2)}) collective-permute-start(bf16[512,128]{1,0:T(8,128)(2,1)S(1)} %get-tuple-element.110), channel_id=1, source_target_pairs={{1,4},{2,15},{5,8},{6,3},{9,12},{10,7},{13,0},{14,11},{17,20},{18,... | collective-permute-start | bytes 393224 | tf_op jit(solution)/shard_map/ppermute | solution.py:333
  71.5 15.2 %collective-permute-start.23 = (bf16[1024,128]{1,0:T(8,128)(2,1)S(1)}, bf16[1024,128]{1,0:T(8,128)(2,1)S(1)}, u32[]{:S(2)}, u32[]{:S(2)}) collective-permute-start(bf16[1024,128]{1,0:T(8,128)(2,1)S(1)} %collective-permute-done.19.arrived_ref.across_ref), channel_id=1, source_target_pairs={{0,1},{1,0},{2,3},{3,2},{4,5},{5,4},{6,7},{7,6},{8,9},{9,8},{10,11... | collective-permute-start | bytes 786440 | tf_op jit(solution)/shard_map/ppermute | solution.py:333
  73.3 16.0 %collective-permute-start.18 = (f32[64,1024]{1,0:T(8,128)S(1)}, f32[64,1024]{1,0:T(8,128)S(1)}, u32[]{:S(2)}, u32[]{:S(2)}) collective-permute-start(f32[64,1024]{1,0:T(8,128)S(1)} %get-tuple-element.91), channel_id=1, source_target_pairs={{0,2},{1,3},{2,0},{3,1},{4,6},{5,7},{6,4},{7,5},{8,10},{9,11},{10,... | collective-permute-start | bytes 786440 | tf_op jit(solution)/shard_map/ppermute | solution.py:333
  77.5 7.7 %collective-permute-start.24 = (bf16[512,128]{1,0:T(8,128)(2,1)S(1)}, bf16[512,128]{1,0:T(8,128)(2,1)S(1)}, u32[]{:S(2)}, u32[]{:S(2)}) collective-permute-start(bf16[512,128]{1,0:T(8,128)(2,1)S(1)} %get-tuple-element.101), channel_id=1, source_target_pairs={{0,4},{1,5},{2,14},{3,15},{4,8},{5,9},{6,2},{7,3},{8,12},{9,13},{1... | collective-permute-start | bytes 393224 | tf_op jit(solution)/shard_map/ppermute | solution.py:333
  78.7 8.1 %collective-permute-start.25 = (bf16[512,128]{1,0:T(8,128)(2,1)S(1)}, bf16[512,128]{1,0:T(8,128)(2,1)S(1)}, u32[]{:S(2)}, u32[]{:S(2)}) collective-permute-start(bf16[512,128]{1,0:T(8,128)(2,1)S(1)} %get-tuple-element.102), channel_id=1, source_target_pairs={{1,4},{2,15},{5,8},{6,3},{9,12},{10,7},{13,0},{14,11},{17,20},{18,... | collective-permute-start | bytes 393224 | tf_op jit(solution)/shard_map/ppermute | solution.py:333

commit v3 on v2

v3 whole, which is shorter than its diff:
```python
import functools

import jax
import jax.numpy as jnp
from jax import lax
from jax.experimental import pallas as pl
from jax.experimental.pallas import tpu as pltpu
from jax.sharding import PartitionSpec as P

LEAF = 256
RANK = 64
B_DEV = 4
NEAR = 12
ROWS = B_DEV * LEAF
SLABS = ((0, 256), (256, 256), (512, 256), (768, 256))
CARRIER = 2
WISH = 16
OWN, CORE, ACROSS, ACROSS_CORE, ALONG, ALONG_CORE, ZERO = 0, 4, 8, 12, 16, 18, 20
HELD = 21
HELD_AT = (
    (ALONG, ALONG_CORE, OWN, CORE, ACROSS),
    (ALONG, CORE, OWN, ACROSS_CORE, ACROSS),
    (ACROSS, ACROSS_CORE, OWN, CORE, ALONG),
    (ACROSS, CORE, OWN, ALONG_CORE, ALONG),
)
MIB = 1024 * 1024
ANYWHERE = pl.BlockSpec(memory_space=pl.ANY)
VECTOR = pl.BlockSpec(memory_space=pltpu.VMEM)
SCALAR = pl.BlockSpec(memory_space=pltpu.SMEM)


def cost(mib):
    return pl.CostEstimate(flops=1024, bytes_accessed=mib * MIB, transcendentals=0)


def split(value):
    high = value.astype(jnp.bfloat16)
    low = (value - high.astype(jnp.float32)).astype(jnp.bfloat16)
    return high, low


def dot(a, b):
    return jnp.dot(a, b, preferred_element_type=jnp.float32)


def dot32(a, b):
    return jnp.dot(
        a.astype(jnp.float32),
        b.astype(jnp.float32),
        precision=lax.Precision.HIGHEST,
        preferred_element_type=jnp.float32,
    )


def cut_kernel(rhs_any, *rest):
    parts, sems = rest[:-1], rest[-1]
    copies = [
        pltpu.make_async_copy(rhs_any.at[:, pl.ds(start, width)], part.at[pl.ds(0, ROWS)], sems.at[k])
        for k, ((start, width), part) in enumerate(zip(SLABS, parts))
    ]
    for copy in copies:
        copy.start()
    for copy in copies:
        copy.wait()


def cut(rhs, carried):
    shapes = [(ROWS, width) for _, width in SLABS]
    shapes[CARRIER] = (ROWS + RANK * -(-carried // SLABS[CARRIER][1]), SLABS[CARRIER][1])
    return pl.pallas_call(
        cut_kernel,
        in_specs=[ANYWHERE],
        out_shape=tuple(jax.ShapeDtypeStruct(shape, rhs.dtype) for shape in shapes),
        scratch_shapes=[pltpu.SemaphoreType.DMA((len(SLABS),))],
        compiler_params=pltpu.CompilerParams(vmem_limit_bytes=16 * MIB),
        cost_estimate=cost(4),
    )(rhs)


def first_two(named):
    first = jnp.where(named[0], 0, jnp.where(named[1], 1, jnp.where(named[2], 2, 3)))
    second = jnp.where(named[1] & (first < 1), 1, jnp.where(named[2] & (first < 2), 2, 3))
    return first, second


def places(members, position, lists):
    numbers = lists[:, :NEAR]
    distance = (numbers >> 2) - position + 2
    distance = jnp.where(distance < 0, distance + members, distance)
    distance = jnp.where(distance >= members, distance - members, distance)
    base = jnp.full(numbers.shape, ZERO, jnp.int32)
    for d in range(5):
        at = jnp.int32(HELD_AT[0][d])
        for kind in range(1, 4):
            at = jnp.where(position & 3 == kind, HELD_AT[kind][d], at)
        base = jnp.where(distance == d, at, base)
    live = lax.broadcasted_iota(jnp.int32, numbers.shape, 1) < lists[:, NEAR:]
    base = jnp.where(live, base, ZERO)
    inner = numbers & 3
    picks = []
    for group in (ALONG, ALONG_CORE):
        named = []
        for box in range(B_DEV):
            here = jnp.where((base == group) & (inner == box), 1, 0)
            named.append(jnp.max(jnp.max(here, axis=1, keepdims=True), axis=0, keepdims=True) > 0)
        picks.append(first_two(named))
    return base, inner, picks


def up_kernel(members, source_any, leaf_any, mid_any, lists_ref, core_lists_ref, *rest):
    parts = rest[: len(SLABS)]
    panel_ref, entry_ref, source_ref, leaf_ref, mid_ref, sems = rest[len(SLABS) :]
    pairs = ((leaf_any, leaf_ref), (mid_any, mid_ref), (source_any, source_ref))
    copies = [pltpu.make_async_copy(a, b, sems.at[i]) for i, (a, b) in enumerate(pairs)]
    for copy in copies:
        copy.start()
    position = lax.axis_index("pts")
    base, inner, (picks, core_side_picks) = places(members, position, lists_ref[...])
    first = jnp.where(base == ALONG, picks[0], core_side_picks[0])
    picked = jnp.where(inner == first, 0, 1)
    entry_ref[...] = base + jnp.where(base == ZERO, 0, jnp.where(base >= ALONG, picked, inner))
    _, _, (_, partner_picks) = places(members, position ^ 1, core_lists_ref[...])
    quarter = panel_ref.shape[1] // 4
    for k, name in enumerate((*picks, *partner_picks)):
        panel_ref[pl.ds(RANK, WISH), pl.ds(k * quarter, quarter)] = jnp.broadcast_to(
            name.astype(jnp.float32), (WISH, quarter)
        ).astype(jnp.bfloat16)
    for copy in copies:
        copy.wait()
    ups = [dot32(dot32(mid_ref[box // 2], leaf_ref[box]), source_ref[box]) for box in range(B_DEV)]
    high, low = split(jnp.concatenate(ups, axis=1))
    both = jnp.concatenate([high, low], axis=0)
    for (start, width), part in zip(SLABS, parts):
        sums = dot(both, part[pl.ds(0, ROWS)])
        panel_ref[pl.ds(0, RANK), pl.ds(start, width)] = (sums[:RANK] + sums[RANK:]).astype(jnp.bfloat16)


def up(members, parts, source_basis, leaf_transfer, mid_transfer, lists, core_lists):
    columns = sum(width for _, width in SLABS)
    arrays = (source_basis, leaf_transfer, mid_transfer)
    return pl.pallas_call(
        functools.partial(up_kernel, members),
        in_specs=[ANYWHERE] * 3 + [VECTOR] * (2 + len(parts)),
        out_shape=(
            jax.ShapeDtypeStruct((RANK + WISH, columns), jnp.bfloat16),
            jax.ShapeDtypeStruct((B_DEV, NEAR), jnp.int32),
        ),
        scratch_shapes=[pltpu.VMEM(a.shape, a.dtype) for a in arrays] + [pltpu.SemaphoreType.DMA((3,))],
        compiler_params=pltpu.CompilerParams(vmem_limit_bytes=16 * MIB),
        cost_estimate=cost(512),
    )(*arrays, lists, core_lists, *parts)


def down_kernel(reach, members, far_ref, target_ref, leaf_ref, mid_ref, coupling_ref, part_in, part_ref, down_ref, placed_ref):
    for box in range(B_DEV):
        chain = dot32(mid_ref[box // 2], leaf_ref[box])
        high, low = split(dot32(chain, target_ref[box]).T)
        down_ref[box] = jnp.concatenate([high, low, high], axis=1)
    position = lax.axis_index("pts")
    quad, side, core = position >> 2, (position >> 1) & 1, position & 1
    for half in range(2):
        blocks = []
        for other in range(2):
            for step in reach:
                held_quad = quad + step
                held_quad = jnp.where(held_quad >= members // 4, held_quad - members // 4, held_quad)
                group = held_quad * 4 + 2 * (side ^ half) + (core ^ other)
                block = jnp.zeros((RANK, RANK), jnp.float32)
                for f in range(coupling_ref.shape[0]):
                    block = jnp.where(far_ref[0, f] == group, coupling_ref[f].astype(jnp.float32), block)
                blocks.append(block)
        placed = jnp.concatenate(blocks, axis=1).astype(jnp.bfloat16)
        if half == 0:
            placed_ref[...] = placed
            continue
        width = part_ref.shape[1]
        for line, at in enumerate(range(0, placed.shape[1], width)):
            taken = placed[:, at : at + width]
            part_ref[pl.ds(ROWS + line * RANK, RANK), pl.ds(0, taken.shape[1])] = taken


def down(reach, members, far_ids, target_basis, leaf_transfer, mid_transfer, coupling, part):
    return pl.pallas_call(
        functools.partial(down_kernel, reach, members),
        in_specs=[SCALAR] + [VECTOR] * 5,
        out_specs=(VECTOR,) * 3,
        out_shape=(
            jax.ShapeDtypeStruct(part.shape, part.dtype),
            jax.ShapeDtypeStruct((B_DEV, LEAF, 3 * RANK), jnp.bfloat16),
            jax.ShapeDtypeStruct((RANK, 2 * len(reach) * RANK), jnp.bfloat16),
        ),
        input_output_aliases={5: 0},
        compiler_params=pltpu.CompilerParams(vmem_limit_bytes=16 * MIB),
        cost_estimate=cost(1),
    )(far_ids, target_basis, leaf_transfer, mid_transfer, coupling, part)


def wishes_kernel(behind_ref, ahead_ref, wish_ref):
    forth = (lax.axis_index("pts") & 2) == 0
    quarter = behind_ref.shape[1] // 4
    for k in range(4):
        at = (pl.ds(RANK, WISH), pl.ds(k * quarter, 128))
        value = jnp.where(forth, ahead_ref[at].astype(jnp.float32), behind_ref[at].astype(jnp.float32))
        wish_ref[0, k] = jnp.max(value).astype(jnp.int32)


def wishes(behind, ahead):
    return pl.pallas_call(
        wishes_kernel,
        in_specs=[VECTOR, VECTOR],
        out_specs=SCALAR,
        out_shape=jax.ShapeDtypeStruct((1, 4), jnp.int32),
        compiler_params=pltpu.CompilerParams(vmem_limit_bytes=8 * MIB),
        cost_estimate=cost(1),
    )(behind, ahead)


def couple_kernel(own_ref, carrier_ref, *rest):
    tables, (own_sum_ref, partner_sum_ref) = rest[:-2], rest[-2:]
    depth = own_ref.shape[1]
    table = jnp.concatenate([ref[pl.ds(0, RANK)] for ref in tables], axis=0)
    lines = [carrier_ref[pl.ds(row, RANK)] for row in range(ROWS, carrier_ref.shape[0], RANK)]
    partner_sum_ref[...] = dot(jnp.concatenate(lines, axis=1)[:, :depth], table)
    own_sum_ref[...] = dot(own_ref[...], table)


def couple(own, carrier, tables):
    shape = jax.ShapeDtypeStruct((RANK, tables[0].shape[1]), jnp.float32)
    return pl.pallas_call(
        couple_kernel,
        out_shape=(shape, shape),
        compiler_params=pltpu.CompilerParams(vmem_limit_bytes=16 * MIB),
        cost_estimate=cost(1),
    )(own, carrier, *tables)


def pack_kernel(wish_ref, arrived_ref, along_ref, along_core_ref):
    for side, picked_ref in enumerate((along_ref, along_core_ref)):
        for k in range(2):
            rows = pl.ds(pl.multiple_of(wish_ref[0, 2 * side + k] * LEAF, LEAF), LEAF)
            picked_ref[pl.ds(k * LEAF, LEAF)] = arrived_ref[rows]


def pack(wish, arrived):
    shape = jax.ShapeDtypeStruct((2 * LEAF, arrived.shape[1]), arrived.dtype)
    return pl.pallas_call(
        pack_kernel,
        in_specs=[SCALAR, VECTOR],
        out_shape=(shape, shape),
        compiler_params=pltpu.CompilerParams(vmem_limit_bytes=8 * MIB),
        cost_estimate=cost(1),
    )(wish, arrived)


def gather(start, width, held, pieces):
    own_ref, core_ref, across_ref, across_core_ref, along_ref, along_core_ref = pieces
    for at, ref, boxes in (
        (OWN, own_ref, B_DEV),
        (CORE, core_ref.at[:, pl.ds(start, width)], B_DEV),
        (ACROSS, across_ref, B_DEV),
        (ACROSS_CORE, across_core_ref, B_DEV),
        (ALONG, along_ref, 2),
        (ALONG_CORE, along_core_ref, 2),
    ):
        held[pl.ds(at * LEAF, boxes * LEAF)] = ref[pl.ds(0, boxes * LEAF)]
    held[pl.ds(ZERO * LEAF, LEAF)] = jnp.zeros((LEAF, width), jnp.bfloat16)


def operands(box, entry_ref, near_ref, held):
    left = [near_ref[box, n] for n in range(NEAR)]
    right = [held[pl.ds(pl.multiple_of(entry_ref[box, n] * LEAF, LEAF), LEAF)] for n in range(NEAR)]
    return left, right


def near_kernel(start, entry_ref, near_ref, *rest):
    pieces, (sum_ref, held) = rest[:-2], rest[-2:]
    gather(start, sum_ref.shape[1], held, pieces)
    for box in range(B_DEV):
        left, right = operands(box, entry_ref, near_ref, held)
        sum_ref[pl.ds(box * LEAF, LEAF)] = dot(
            jnp.concatenate(left, axis=1), jnp.concatenate(right, axis=0)
        )


def near(start, width, entry, near_blocks, pieces):
    return pl.pallas_call(
        functools.partial(near_kernel, start),
        in_specs=[SCALAR] + [VECTOR] * (1 + len(pieces)),
        out_specs=VECTOR,
        scratch_shapes=[pltpu.VMEM((HELD * LEAF, width), jnp.bfloat16)],
        out_shape=jax.ShapeDtypeStruct((ROWS, width), jnp.float32),
        compiler_params=pltpu.CompilerParams(vmem_limit_bytes=16 * MIB),
        cost_estimate=cost(8),
    )(entry, near_blocks, *pieces)


def last_kernel(start, width, entry_ref, near_ref, own_sum_ref, partner_sum_ref, down_ref, *rest):
    pieces, (_, out_ref, held, made, sems) = rest[:-5], rest[-5:]
    gather(start, width, held, pieces)
    taken = pl.ds(start, width)
    high, low = split(own_sum_ref[:, taken] + partner_sum_ref[:, taken])
    coupled = jnp.concatenate([high, high, low], axis=0)
    copies = []
    for box in range(B_DEV):
        left, right = operands(box, entry_ref, near_ref, held)
        rows = pl.ds(box * LEAF, LEAF)
        near_sum = dot(jnp.concatenate(left, axis=1), jnp.concatenate(right, axis=0))
        made[rows] = (near_sum + dot(down_ref[box], coupled)).astype(jnp.bfloat16)
        copy = pltpu.make_async_copy(made.at[rows], out_ref.at[rows, taken], sems.at[box])
        copy.start()
        copies.append(copy)
    for copy in copies:
        copy.wait()


def last(start, width, entry, near_blocks, sums, down_basis, pieces, product):
    given = [entry, near_blocks, *sums, down_basis, *pieces, product]
    return pl.pallas_call(
        functools.partial(last_kernel, start, width),
        in_specs=[SCALAR] + [VECTOR] * (len(given) - 2) + [ANYWHERE],
        out_specs=ANYWHERE,
        scratch_shapes=[
            pltpu.VMEM((HELD * LEAF, width), jnp.bfloat16),
            pltpu.VMEM((ROWS, width), jnp.bfloat16),
            pltpu.SemaphoreType.DMA((B_DEV,)),
        ],
        out_shape=jax.ShapeDtypeStruct(product.shape, product.dtype),
        input_output_aliases={len(given) - 1: 0},
        compiler_params=pltpu.CompilerParams(vmem_limit_bytes=16 * MIB),
        cost_estimate=cost(8),
    )(*given)


def finish_kernel(slabs, own_sum_ref, partner_sum_ref, down_ref, *rest):
    sum_refs = rest[: len(slabs)]
    out_ref, made, sems = rest[-3:]
    start, stop = slabs[0][0], slabs[-1][0] + slabs[-1][1]
    taken = pl.ds(start, stop - start)
    high, low = split(own_sum_ref[:, taken] + partner_sum_ref[:, taken])
    coupled = jnp.concatenate([high, high, low], axis=0)
    copies = []
    for box in range(B_DEV):
        rows = pl.ds(box * LEAF, LEAF)
        far = dot(down_ref[box], coupled)
        for (at, width), sum_ref in zip(slabs, sum_refs):
            columns = slice(at - start, at - start + width)
            made[rows, columns] = (far[:, columns] + sum_ref[rows]).astype(jnp.bfloat16)
        copy = pltpu.make_async_copy(made.at[rows], out_ref.at[rows, taken], sems.at[box])
        copy.start()
        copies.append(copy)
    for copy in copies:
        copy.wait()


def finish(slabs, sums, down_basis, nears):
    columns = sums[0].shape[1]
    given = [*sums, down_basis, *nears]
    return pl.pallas_call(
        functools.partial(finish_kernel, slabs),
        in_specs=[VECTOR] * len(given),
        out_specs=ANYWHERE,
        scratch_shapes=[
            pltpu.VMEM((ROWS, sum(width for _, width in slabs)), jnp.bfloat16),
            pltpu.SemaphoreType.DMA((B_DEV,)),
        ],
        out_shape=jax.ShapeDtypeStruct((ROWS, columns), jnp.bfloat16),
        compiler_params=pltpu.CompilerParams(vmem_limit_bytes=16 * MIB),
        cost_estimate=cost(4),
    )(*given)


def on_device(
    rhs,
    near_blocks,
    near_ids,
    near_count,
    source_basis,
    target_basis,
    leaf_transfer,
    mid_transfer,
    far_coupling,
    far_ids,
):
    members = lax.axis_size("pts")
    every = range(members)
    across_pairs = [(i, i ^ 2) for i in every]
    core_pairs = [(i, i ^ 1) for i in every]
    along_pairs = [(i, (i + (-4 if i & 2 else 4)) % members) for i in every]
    along_core_pairs = [(i, (i + (-3 if i & 2 else 3)) % members) for i in every if i % 4 in (1, 2)]
    permute = lambda value, pairs: lax.ppermute(value, "pts", pairs)
    meet = lambda *values: lax.optimization_barrier(values)
    quads = members // 4
    reach = sorted({step % quads for step in range(-2, 3)})

    lists = jnp.concatenate([near_ids, near_count[:, None]], axis=1)
    core_lists = permute(lists, core_pairs)
    rhs_core = permute(rhs, core_pairs)
    parts = list(cut(rhs, 2 * len(reach) * RANK))
    panel, entry = up(members, parts, source_basis, leaf_transfer, mid_transfer, lists, core_lists)
    parts[CARRIER], down_basis, placed = down(
        reach, members, far_ids, target_basis, leaf_transfer, mid_transfer, far_coupling[0], parts[CARRIER]
    )
    across = [permute(part, across_pairs) for part in parts]
    others = [permute(panel, [(i, (i - 4 * step) % members) for i in every]) for step in reach[1:]]

    across_core, along, nears = [], [], []

    def relay(k):
        picked, core_picked = pack(wish, across[k])
        along.append([permute(picked, along_pairs), permute(core_picked, along_core_pairs)])
        across_core.append(permute(across[k], core_pairs))

    def pieces(k):
        return (parts[k], rhs_core, across[k], across_core[k], *along[k])

    def multiply(k):
        nears.append(near(*SLABS[k], entry, near_blocks, pieces(k)))

    behind, ahead = reach.index(quads - 1) - 1, reach.index(1) - 1
    across[0], panel, others[behind], others[ahead] = meet(across[0], panel, others[behind], others[ahead])
    wish = wishes(others[behind], others[ahead])
    relay(0)

    across[1], along[0][0], panel, *others = meet(across[1], along[0][0], panel, *others)
    relay(1)

    across[2], across_core[0], panel, along[0][1], along[1][0] = meet(
        across[2], across_core[0], panel, along[0][1], along[1][0]
    )
    relay(2)
    multiply(0)
    mine = [panel, *others]
    own_sum, partner_sum = couple(placed, across[2], mine + [permute(each, core_pairs) for each in mine])

    across[3], across_core[1], partner_sum, nears[0], along[1][1], along[2][0] = meet(
        across[3], across_core[1], partner_sum, nears[0], along[1][1], along[2][0]
    )
    relay(3)
    partner_sum = permute(partner_sum, across_pairs)
    multiply(1)
    multiply(2)
    sums = (own_sum, partner_sum)
    product = finish(SLABS[:-1], sums, down_basis, nears)
    product, *along[3] = meet(product, *along[3])
    return last(*SLABS[3], entry, near_blocks, sums, down_basis, pieces(3), product)


def solution(mesh):
    return jax.shard_map(
        on_device,
        mesh=mesh,
        in_specs=(
            P(("parts", "pts"), None),
            P(("parts", "pts"), None, None, None),
            P(("parts", "pts"), None),
            P(("parts", "pts")),
            P(("parts", "pts"), None, None),
            P(("parts", "pts"), None, None),
            P(("parts", "pts"), None, None),
            P(("parts", "pts"), None, None),
            P(("parts", "pts"), None, None, None),
            P(("parts", "pts"), None),
        ),
        out_specs=P(("parts", "pts"), None),
        check_vma=False,
    )
```

time: 92.3 us -> 83 us (0.90)
  starting transfers between devices: 33.1 us -> 24.7 us
  waiting for transfers between devices: 34 us -> 30.4 us
  local copies, waits for them, and re-layouts: 1.67 us -> 4.48 us
    ppermute x29 -> x26, starting transfers between devices: 33.1 us -> 24.7 us  [on_device(): permute = lambda value, pairs: lax.ppermute(value, 'pts', pairs)]
    pallas_call x5 -> x3, Pallas kernels: 12.8 us -> 8.7 us  [near(): pl.pallas_call(functools.partial(near_kernel, start), in_specs=[SCALAR] +...]
    ppermute x29 -> x26, waiting for transfers between devices: 34 us -> 30.4 us  [on_device(): permute = lambda value, pairs: lax.ppermute(value, 'pts', pairs)]
    pallas_call x8 -> x9, Pallas kernels: 9.03 us -> 12.3 us  [the longest x1 3.41 us: last(): pl.pallas_call(functools.partial(last_kernel, start, width), in_specs=[SC...]
    unnamed x23 -> x26, local copies, waits for them, and re-layouts: 1.66 us -> 4.39 us
  transfers between devices with their start and end apart: 29 -> 26, of which waited for: 12 -> 13; matrix products, arithmetic and copies ran while one was open for 0% -> 0% of each run, Pallas kernels for 22% -> 23%
where the time goes in v3:
time: 83 us; the launch traced here: 82.7 us
  waiting for transfers between devices  30.4 us (37%)
  starting transfers between devices  24.7 us (30%)
  Pallas kernels  22.8 us (27%)
  local copies, waits for them, and re-layouts  4.48 us (5%)
    ppermute x26, waiting for transfers between devices, on_device(): permute = lambda value, pairs: lax.ppermute(value, 'pts', pairs)  30.4 us
    ppermute x26, starting transfers between devices, on_device(): permute = lambda value, pairs: lax.ppermute(value, 'pts', pairs)  24.7 us
    pallas_call x3, Pallas kernels, near(): pl.pallas_call(functools.partial(near_kernel, start), in_specs=[SCALAR] +...  8.7 us
    unnamed x26, local copies, waits for them, and re-layouts  4.39 us
    pallas_call x1, Pallas kernels, last(): pl.pallas_call(functools.partial(last_kernel, start, width), in_specs=[SC...  3.41 us
    pallas_call x1, Pallas kernels, up(): pl.pallas_call(functools.partial(up_kernel, members), in_specs=[ANYWHERE]...  2.93 us
    pallas_call x4, Pallas kernels, pack(): pl.pallas_call(pack_kernel, in_specs=[SCALAR, VECTOR], out_shape=(shape,...  2.31 us
  transfers between devices with their start and end apart: 26, of which 13 were waited for; matrix products, arithmetic and copies ran while one was open for 0% of the time, Pallas kernels for 23%

profile of v3, /device:TPU:0, one launch (start us, length us, event | category | flops | bytes accessed | tf_op | source)
XLA Modules:
  0.0 82.7 jit_solution(17609832808188766081)
XLA Ops:
  0.0 0.5 collective-permute-start.17
  0.5 1.6 %copy-done.1 = bf16[1024,1024]{1,0:T(8,128)(2,1)S(1)} copy-done((bf16[1024,1024]{1,0:T(8,128)(2,1)S(1)}, bf16[1024,1024]{1,0:T(8,128)(2,1)}, u32[]{:S(2)}) %copy-start.1) | copy-done | bytes 2097176
  2.1 1.3 %shard_map.100 = (bf16[1024,256]{1,0:T(8,128)(2,1)}, bf16[1024,256]{1,0:T(8,128)(2,1)}, bf16[1152,256]{1,0:T(8,128)(2,1)S(1)}, bf16[1024,256]{1,0:T(8,128)(2,1)S(1)}) custom-call(bf16[1024,1024]{1,0:T(8,128)(2,1)S(1)} %copy-done.1), custom_call_target="tpu_custom_call" | custom-call | flops 1024 | bytes 4194304 | tf_op jit(solution)/shard_map/pallas_call | solution.py:70
  3.4 0.8 copy-done.2
  4.2 2.5 %collective-permute-start.2 = (bf16[1024,256]{1,0:T(8,128)(2,1)}, bf16[1024,256]{1,0:T(8,128)(2,1)S(1)}, u32[]{:S(2)}, u32[]{:S(2)}) collective-permute-start(bf16[1024,256]{1,0:T(8,128)(2,1)} %get-tuple-element.48.rest_0_), channel_id=1, source_target_pairs={{0,2},{1,3},{2,0},{3,1},{4,6},{5,7},{6,4},{7,5},{8,10},{9,11},{10,... | collective-permute-start | bytes 1572872 | tf_op jit(solution)/shard_map/ppermute | solution.py:390
  6.7 0.1 copy.13
  6.8 0.1 pad_add_fusion.lists_ref
  6.9 0.2 collective-permute-start
  7.1 0.9 %collective-permute-done.core_lists_ref = s32[4,13]{1,0:T(4,128)S(1)} collective-permute-done((s32[4,13]{1,0:T(4,128)S(1)}, s32[4,13]{1,0:T(4,128)S(1)}, u32[]{:S(2)}, u32[]{:S(2)}) %collective-permute-start) | collective-permute-done | bytes 240 | tf_op jit(solution)/shard_map/ppermute | solution.py:390
  8.1 1.0 %copy-done.3 = bf16[1024,256]{1,0:T(8,128)(2,1)S(1)} copy-done((bf16[1024,256]{1,0:T(8,128)(2,1)S(1)}, bf16[1024,256]{1,0:T(8,128)(2,1)}, u32[]{:S(2)}) %copy-start.3) | copy-done | bytes 524312
  9.1 2.9 %shard_map.101 = (bf16[80,1024]{1,0:T(8,128)(2,1)S(1)}, s32[4,12]{1,0:T(4,128)S(1)}) custom-call(bf16[4,64,256]{2,1,0:T(8,128)(2,1)S(1)} %copy-done.7, bf16[4,64,64]{2,1,0:T(8,128)(2,1)S(1)} %copy-done.5, bf16[2,64,64]{2,1,0:T(8,128)(2,1)S(1)} %copy-done.6, s32[4,13]{1,0:T(4,128)S(1)} %pad_add_fusion.lists_ref, ...), custom_call_target="tpu_custom_call" | custom-call | flops 1024 | bytes 536870912 | tf_op jit(solution)/shard_map/pallas_call | solution.py:141
  12.0 1.6 %collective-permute-start.3 = (bf16[80,1024]{1,0:T(8,128)(2,1)S(1)}, bf16[80,1024]{1,0:T(8,128)(2,1)S(1)}, u32[]{:S(2)}, u32[]{:S(2)}) collective-permute-start(bf16[80,1024]{1,0:T(8,128)(2,1)S(1)} %get-tuple-element.66.rest_0_), channel_id=1, source_target_pairs={{0,4},{1,5},{2,6},{3,7},{4,8},{5,9},{6,10},{7,11},{8,12},{9,13},{1... | collective-permute-start | bytes 491528 | tf_op jit(solution)/shard_map/ppermute | solution.py:390
  13.7 0.5 collective-permute-start.6
  14.2 2.1 %collective-permute-start.4 = (bf16[80,1024]{1,0:T(8,128)(2,1)S(1)}, bf16[80,1024]{1,0:T(8,128)(2,1)S(1)}, u32[]{:S(2)}, u32[]{:S(2)}) collective-permute-start(bf16[80,1024]{1,0:T(8,128)(2,1)S(1)} %get-tuple-element.66.rest_0_), channel_id=1, source_target_pairs={{0,12},{1,13},{2,14},{3,15},{4,0},{5,1},{6,2},{7,3},{8,4},{9,5},{1... | collective-permute-start | bytes 491528 | tf_op jit(solution)/shard_map/ppermute | solution.py:390
  16.3 4.6 %collective-permute-done.3.behind_ref.rest_3_ = bf16[80,1024]{1,0:T(8,128)(2,1)S(1)} collective-permute-done((bf16[80,1024]{1,0:T(8,128)(2,1)S(1)}, bf16[80,1024]{1,0:T(8,128)(2,1)S(1)}, u32[]{:S(2)}, u32[]{:S(2)}) %collective-permute-start.3) | collective-permute-done | bytes 163872 | tf_op jit(solution)/shard_map/ppermute | solution.py:390
  21.0 5.3 %collective-permute-start.8 = (bf16[80,1024]{1,0:T(8,128)(2,1)S(1)}, bf16[80,1024]{1,0:T(8,128)(2,1)S(1)}, u32[]{:S(2)}, u32[]{:S(2)}) collective-permute-start(bf16[80,1024]{1,0:T(8,128)(2,1)S(1)} %get-tuple-element.66.rest_0_), channel_id=1, source_target_pairs={{0,8},{1,9},{2,10},{3,11},{4,12},{5,13},{6,14},{7,15},{8,0},{9,1},... | collective-permute-start | bytes 491528 | tf_op jit(solution)/shard_map/ppermute | solution.py:390
  26.3 0.9 %copy-done.8 = bf16[4,64,256]{2,1,0:T(8,128)(2,1)S(1)} copy-done((bf16[4,64,256]{2,1,0:T(8,128)(2,1)S(1)}, bf16[4,64,256]{2,1,0:T(8,128)(2,1)}, u32[]{:S(2)}) %copy-start.8) | copy-done | bytes 131096
  27.2 1.5 %shard_map.102 = (bf16[1152,256]{1,0:T(8,128)(2,1)S(1)}, bf16[4,256,192]{2,1,0:T(8,128)(2,1)S(1)}, bf16[64,512]{1,0:T(8,128)(2,1)S(1)}) custom-call(s32[1,6]{1,0:T(1,128)S(1)} %copy-done.10, bf16[4,64,256]{2,1,0:T(8,128)(2,1)S(1)} %copy-done.8, bf16[4,64,64]{2,1,0:T(8,128)(2,1)S(1)} %copy-done.5, ...), custom_call_target="tpu_custom_call", output_to_operand_aliasing={{0}: (5, {})} | custom-call | flops 1024 | bytes 1048576 | tf_op jit(solution)/shard_map/pallas_call | solution.py:183
  28.7 0.0 collective-permute-done.4.ahead_ref.rest_1_
  28.7 0.6 collective-permute-start.1
  29.3 0.7 shard_map.103.wish_ref
  30.0 0.6 shard_map.104
  30.6 0.1 collective-permute-start.7
  30.7 3.0 %collective-permute-done.8.rest_2_ = bf16[80,1024]{1,0:T(8,128)(2,1)S(1)} collective-permute-done((bf16[80,1024]{1,0:T(8,128)(2,1)S(1)}, bf16[80,1024]{1,0:T(8,128)(2,1)S(1)}, u32[]{:S(2)}, u32[]{:S(2)}) %collective-permute-start.8) | collective-permute-done | bytes 163872 | tf_op jit(solution)/shard_map/ppermute | solution.py:390
  33.6 0.0 collective-permute-start.5
  33.6 0.0 collective-permute-done.6.arrived_ref.rest_2_
  33.6 1.3 %collective-permute-start.9 = (bf16[512,256]{1,0:T(8,128)(2,1)S(1)}, bf16[512,256]{1,0:T(8,128)(2,1)S(1)}, u32[]{:S(2)}, u32[]{:S(2)}) collective-permute-start(bf16[512,256]{1,0:T(8,128)(2,1)S(1)} %get-tuple-element.62), channel_id=1, source_target_pairs={{1,4},{2,15},{5,8},{6,3},{9,12},{10,7},{13,0},{14,11},{17,20},{18,... | collective-permute-start | bytes 786440 | tf_op jit(solution)/shard_map/ppermute | solution.py:390
  34.9 3.9 %collective-permute-done.7.rest_4_ = bf16[512,256]{1,0:T(8,128)(2,1)S(1)} collective-permute-done((bf16[512,256]{1,0:T(8,128)(2,1)S(1)}, bf16[512,256]{1,0:T(8,128)(2,1)S(1)}, u32[]{:S(2)}, u32[]{:S(2)}) %collective-permute-start.7) | collective-permute-done | bytes 262176 | tf_op jit(solution)/shard_map/ppermute | solution.py:390
  38.8 0.6 shard_map.105
  39.4 0.1 collective-permute-start.10
  39.5 3.9 %collective-permute-done.1.carrier_ref.arrived_ref.rest_2_ = bf16[1152,256]{1,0:T(8,128)(2,1)S(1)} collective-permute-done((bf16[1152,256]{1,0:T(8,128)(2,1)S(1)}, bf16[1152,256]{1,0:T(8,128)(2,1)S(1)}, u32[]{:S(2)}, u32[]{:S(2)}) %collective-permute-start.1) | collective-permute-done | bytes 589856 | tf_op jit(solution)/shard_map/ppermute | solution.py:390
  43.4 0.5 collective-permute-start.13
  43.9 1.7 %collective-permute-start.15 = (bf16[1024,256]{1,0:T(8,128)(2,1)}, bf16[1024,256]{1,0:T(8,128)(2,1)S(1)}, u32[]{:S(2)}, u32[]{:S(2)}) collective-permute-start(bf16[1024,256]{1,0:T(8,128)(2,1)} %copy-done.2), channel_id=1, source_target_pairs={{0,2},{1,3},{2,0},{3,1},{4,6},{5,7},{6,4},{7,5},{8,10},{9,11},{10,... | collective-permute-start | bytes 1572872 | tf_op jit(solution)/shard_map/ppermute | solution.py:390
  45.7 3.1 %collective-permute-done.10.rest_4_ = bf16[512,256]{1,0:T(8,128)(2,1)S(1)} collective-permute-done((bf16[512,256]{1,0:T(8,128)(2,1)S(1)}, bf16[512,256]{1,0:T(8,128)(2,1)S(1)}, u32[]{:S(2)}, u32[]{:S(2)}) %collective-permute-start.10) | collective-permute-done | bytes 262176 | tf_op jit(solution)/shard_map/ppermute | solution.py:390
  48.7 0.0 collective-permute-start.16
  48.7 0.0 collective-permute-done.12.rest_5_
  48.7 0.5 collective-permute-start.14
  49.2 0.0 collective-permute-done.13.rest_6_
  49.2 0.1 collective-permute-start.11
  49.3 0.6 shard_map.108
  49.9 1.0 %collective-permute-done.14.rest_7_ = bf16[80,1024]{1,0:T(8,128)(2,1)S(1)} collective-permute-done((bf16[80,1024]{1,0:T(8,128)(2,1)S(1)}, bf16[80,1024]{1,0:T(8,128)(2,1)S(1)}, u32[]{:S(2)}, u32[]{:S(2)}) %collective-permute-start.14) | collective-permute-done | bytes 163872 | tf_op jit(solution)/shard_map/ppermute | solution.py:390
  50.9 1.3 %collective-permute-start.18 = (bf16[512,256]{1,0:T(8,128)(2,1)S(1)}, bf16[512,256]{1,0:T(8,128)(2,1)S(1)}, u32[]{:S(2)}, u32[]{:S(2)}) collective-permute-start(bf16[512,256]{1,0:T(8,128)(2,1)S(1)} %get-tuple-element.75), channel_id=1, source_target_pairs={{1,4},{2,15},{5,8},{6,3},{9,12},{10,7},{13,0},{14,11},{17,20},{18,... | collective-permute-start | bytes 786440 | tf_op jit(solution)/shard_map/ppermute | solution.py:390
  52.2 0.1 collective-permute-start.19
  52.3 0.5 collective-permute-start.22
  52.8 0.5 shard_map.106
  53.3 3.1 %shard_map.107.rest_0_ = f32[1024,256]{1,0:T(8,128)S(1)} custom-call(s32[4,12]{1,0:T(4,128)S(1)} %get-tuple-element.52.entry_ref, bf16[4,12,256,256]{3,2,1,0:T(8,128)(2,1)S(1)} %copy-done, bf16[1024,256]{1,0:T(8,128)(2,1)} %get-tuple-element.48.rest_0_, bf16[1024,1024]{1,0:T(8,128)(2,1)S(1)} %collective-permute-done.17.rest_1_, ...), custom_call_target="tpu_custom_call" | custom-call | flops 1024 | bytes 8388608 | tf_op jit(solution)/shard_map/pallas_call | solution.py:286
  56.3 1.7 %collective-permute-done.15.arrived_ref.rest_2_ = bf16[1024,256]{1,0:T(8,128)(2,1)S(1)} collective-permute-done((bf16[1024,256]{1,0:T(8,128)(2,1)}, bf16[1024,256]{1,0:T(8,128)(2,1)S(1)}, u32[]{:S(2)}, u32[]{:S(2)}) %collective-permute-start.15) | collective-permute-done | bytes 524320 | tf_op jit(solution)/shard_map/ppermute | solution.py:390
  58.0 1.3 %collective-permute-start.23 = (bf16[512,256]{1,0:T(8,128)(2,1)S(1)}, bf16[512,256]{1,0:T(8,128)(2,1)S(1)}, u32[]{:S(2)}, u32[]{:S(2)}) collective-permute-start(bf16[512,256]{1,0:T(8,128)(2,1)S(1)} %get-tuple-element.85), channel_id=1, source_target_pairs={{1,4},{2,15},{5,8},{6,3},{9,12},{10,7},{13,0},{14,11},{17,20},{18,... | collective-permute-start | bytes 786440 | tf_op jit(solution)/shard_map/ppermute | solution.py:390
  59.3 3.8 %collective-permute-done.18.rest_5_ = bf16[512,256]{1,0:T(8,128)(2,1)S(1)} collective-permute-done((bf16[512,256]{1,0:T(8,128)(2,1)S(1)}, bf16[512,256]{1,0:T(8,128)(2,1)S(1)}, u32[]{:S(2)}, u32[]{:S(2)}) %collective-permute-start.18) | collective-permute-done | bytes 262176 | tf_op jit(solution)/shard_map/ppermute | solution.py:390
  63.1 0.0 collective-permute-done.16.rest_3_
  63.1 0.1 collective-permute-done.19.rest_4_
  63.2 2.6 %collective-permute-start.21 = (bf16[1024,256]{1,0:T(8,128)(2,1)S(1)}, bf16[1024,256]{1,0:T(8,128)(2,1)S(1)}, u32[]{:S(2)}, u32[]{:S(2)}) collective-permute-start(bf16[1024,256]{1,0:T(8,128)(2,1)S(1)} %collective-permute-done.15.arrived_ref.rest_2_), channel_id=1, source_target_pairs={{0,1},{1,0},{2,3},{3,2},{4,5},{5,4},{6,7},{7,6},{8,9},{9,8},{10,11... | collective-permute-start | bytes 1572872 | tf_op jit(solution)/shard_map/ppermute | solution.py:390
  65.8 0.6 shard_map.112
  66.4 0.1 collective-permute-start.24
  66.4 2.3 %collective-permute-done.23.rest_5_ = bf16[512,256]{1,0:T(8,128)(2,1)S(1)} collective-permute-done((bf16[512,256]{1,0:T(8,128)(2,1)S(1)}, bf16[512,256]{1,0:T(8,128)(2,1)S(1)}, u32[]{:S(2)}, u32[]{:S(2)}) %collective-permute-start.23) | collective-permute-done | bytes 262176 | tf_op jit(solution)/shard_map/ppermute | solution.py:390
  68.8 1.3 %collective-permute-start.25 = (bf16[512,256]{1,0:T(8,128)(2,1)S(1)}, bf16[512,256]{1,0:T(8,128)(2,1)S(1)}, u32[]{:S(2)}, u32[]{:S(2)}) collective-permute-start(bf16[512,256]{1,0:T(8,128)(2,1)S(1)} %get-tuple-element.87), channel_id=1, source_target_pairs={{1,4},{2,15},{5,8},{6,3},{9,12},{10,7},{13,0},{14,11},{17,20},{18,... | collective-permute-start | bytes 786440 | tf_op jit(solution)/shard_map/ppermute | solution.py:390
  70.1 3.1 %shard_map.109.rest_1_ = f32[1024,256]{1,0:T(8,128)S(1)} custom-call(s32[4,12]{1,0:T(4,128)S(1)} %get-tuple-element.52.entry_ref, bf16[4,12,256,256]{3,2,1,0:T(8,128)(2,1)S(1)} %copy-done, bf16[1024,256]{1,0:T(8,128)(2,1)} %get-tuple-element.49.rest_1_.rest_0_, bf16[1024,1024]{1,0:T(8,128)(2,1)S(1)} %collective-permute-done.17.rest_1_, ...), custom_call_target="tpu_custom_call" | custom-call | flops 1024 | bytes 8388608 | tf_op jit(solution)/shard_map/pallas_call | solution.py:286
  73.1 0.0 collective-permute-done.22.rest_3_
  73.2 2.6 %shard_map.110.rest_2_ = f32[1024,256]{1,0:T(8,128)S(1)} custom-call(s32[4,12]{1,0:T(4,128)S(1)} %get-tuple-element.52.entry_ref, bf16[4,12,256,256]{3,2,1,0:T(8,128)(2,1)S(1)} %copy-done, bf16[1152,256]{1,0:T(8,128)(2,1)S(1)} %get-tuple-element.54.rest_0_, bf16[1024,1024]{1,0:T(8,128)(2,1)S(1)} %collective-permute-done.17.rest_1_, ...), custom_call_target="tpu_custom_call" | custom-call | flops 1024 | bytes 8388608 | tf_op jit(solution)/shard_map/pallas_call | solution.py:286
  75.7 0.0 collective-permute-done.20.partner_sum_ref
  75.8 1.5 %shard_map.111.rest_6_ = bf16[1024,1024]{1,0:T(8,128)(2,1)} custom-call(f32[64,1024]{1,0:T(8,128)S(1)} %get-tuple-element.70.own_sum_ref, f32[64,1024]{1,0:T(8,128)S(1)} %collective-permute-done.20.partner_sum_ref, bf16[4,256,192]{2,1,0:T(8,128)(2,1)S(1)} %get-tuple-element.78.down_ref, f32[1024,256]{1,0:T(8,128)S(1)} %shard_map.107.rest_0_, ...), custom_call_target="tpu_custom_call" | custom-call | flops 1024 | bytes 4194304 | tf_op jit(solution)/shard_map/pallas_call | solution.py:358
  77.2 0.2 collective-permute-done.24.rest_4_
  77.4 1.8 %collective-permute-done.25.rest_5_ = bf16[512,256]{1,0:T(8,128)(2,1)S(1)} collective-permute-done((bf16[512,256]{1,0:T(8,128)(2,1)S(1)}, bf16[512,256]{1,0:T(8,128)(2,1)S(1)}, u32[]{:S(2)}, u32[]{:S(2)}) %collective-permute-start.25) | collective-permute-done | bytes 262176 | tf_op jit(solution)/shard_map/ppermute | solution.py:390
  79.3 3.4 %shard_map.113 = bf16[1024,1024]{1,0:T(8,128)(2,1)} custom-call(s32[4,12]{1,0:T(4,128)S(1)} %get-tuple-element.52.entry_ref, bf16[4,12,256,256]{3,2,1,0:T(8,128)(2,1)S(1)} %copy-done, f32[64,1024]{1,0:T(8,128)S(1)} %get-tuple-element.70.own_sum_ref, f32[64,1024]{1,0:T(8,128)S(1)} %collective-permute-done.20.partner_sum_ref, ...), custom_call_target="tpu_custom_call", output_to_operand_aliasing={{}: (11, {})} | custom-call | flops 1024 | bytes 8388608 | tf_op jit(solution)/shard_map/pallas_call | solution.py:318
  (30 shorter events, 0.1 us)
Async XLA Ops:
  0.0 52.2 %collective-permute-start.17 = (bf16[1024,1024]{1,0:T(8,128)(2,1)}, bf16[1024,1024]{1,0:T(8,128)(2,1)S(1)}, u32[]{:S(2)}, u32[]{:S(2)}) collective-permute-start(bf16[1024,1024]{1,0:T(8,128)(2,1)} %rhs_any.1), channel_id=1, source_target_pairs={{0,1},{1,0},{2,3},{3,2},{4,5},{5,4},{6,7},{7,6},{8,9},{9,8},{10,11... | collective-permute-start | bytes 6291464 | tf_op jit(solution)/shard_map/ppermute | solution.py:390
  0.5 1.6 %copy-start.1 = (bf16[1024,1024]{1,0:T(8,128)(2,1)S(1)}, bf16[1024,1024]{1,0:T(8,128)(2,1)}, u32[]{:S(2)}) copy-start(bf16[1024,1024]{1,0:T(8,128)(2,1)} %rhs_any.1) | copy-start | bytes 6291460
  2.0 4.7 %copy-start.12 = (s32[4]{0:T(128)S(1)}, s32[4]{0:T(128)}, u32[]{:S(2)}) copy-start(s32[4]{0:T(128)} %param.13) | copy-start | bytes 52
  2.0 4.8 %copy-start.11 = (s32[4,12]{1,0:T(4,128)S(1)}, s32[4,12]{1,0:T(4,128)}, u32[]{:S(2)}) copy-start(s32[4,12]{1,0:T(4,128)} %param.12) | copy-start | bytes 580
  2.0 6.0 %copy-start.5 = (bf16[4,64,64]{2,1,0:T(8,128)(2,1)S(1)}, bf16[4,64,64]{2,1,0:T(8,128)(2,1)}, u32[]{:S(2)}) copy-start(bf16[4,64,64]{2,1,0:T(8,128)(2,1)} %leaf_ref.1) | copy-start | bytes 98308
  2.1 6.0 %copy-start.6 = (bf16[2,64,64]{2,1,0:T(8,128)(2,1)S(1)}, bf16[2,64,64]{2,1,0:T(8,128)(2,1)}, u32[]{:S(2)}) copy-start(bf16[2,64,64]{2,1,0:T(8,128)(2,1)} %mid_ref.1) | copy-start | bytes 49156
  2.1 6.0 %copy-start.7 = (bf16[4,64,256]{2,1,0:T(8,128)(2,1)S(1)}, bf16[4,64,256]{2,1,0:T(8,128)(2,1)}, u32[]{:S(2)}) copy-start(bf16[4,64,256]{2,1,0:T(8,128)(2,1)} %source_any.1) | copy-start | bytes 393220
  2.1 24.2 %copy-start.9 = (bf16[1,6,64,64]{3,2,1,0:T(8,128)(2,1)S(1)}, bf16[1,6,64,64]{3,2,1,0:T(8,128)(2,1)}, u32[]{:S(2)}) copy-start(bf16[1,6,64,64]{3,2,1,0:T(8,128)(2,1)} %param.18) | copy-start | bytes 147460
  2.1 24.2 %copy-start.10 = (s32[1,6]{1,0:T(1,128)S(1)}, s32[1,6]{1,0:T(1,128)}, u32[]{:S(2)}) copy-start(s32[1,6]{1,0:T(1,128)} %far_ref.1) | copy-start | bytes 76
  3.4 0.8 %copy-start.2 = (bf16[1024,256]{1,0:T(8,128)(2,1)}, bf16[1024,256]{1,0:T(8,128)(2,1)S(1)}, u32[]{:S(2)}) copy-start(bf16[1024,256]{1,0:T(8,128)(2,1)S(1)} %get-tuple-element.51.rest_3_.rest_0_) | copy-start | bytes 1572868
  4.2 25.1 %collective-permute-start.2 = (bf16[1024,256]{1,0:T(8,128)(2,1)}, bf16[1024,256]{1,0:T(8,128)(2,1)S(1)}, u32[]{:S(2)}, u32[]{:S(2)}) collective-permute-start(bf16[1024,256]{1,0:T(8,128)(2,1)} %get-tuple-element.48.rest_0_), channel_id=1, source_target_pairs={{0,2},{1,3},{2,0},{3,1},{4,6},{5,7},{6,4},{7,5},{8,10},{9,11},{10,... | collective-permute-start | bytes 1572872 | tf_op jit(solution)/shard_map/ppermute | solution.py:390
  6.9 1.2 %collective-permute-start = (s32[4,13]{1,0:T(4,128)S(1)}, s32[4,13]{1,0:T(4,128)S(1)}, u32[]{:S(2)}, u32[]{:S(2)}) collective-permute-start(s32[4,13]{1,0:T(4,128)S(1)} %pad_add_fusion.lists_ref), channel_id=1, source_target_pairs={{0,1},{1,0},{2,3},{3,2},{4,5},{5,4},{6,7},{7,6},{8,9},{9,8},{10,11... | collective-permute-start | bytes 632 | tf_op jit(solution)/shard_map/ppermute | solution.py:390
  8.1 1.0 %copy-start.3 = (bf16[1024,256]{1,0:T(8,128)(2,1)S(1)}, bf16[1024,256]{1,0:T(8,128)(2,1)}, u32[]{:S(2)}) copy-start(bf16[1024,256]{1,0:T(8,128)(2,1)} %copy-done.2) | copy-start | bytes 1572868
  9.1 44.2 %copy-start = (bf16[4,12,256,256]{3,2,1,0:T(8,128)(2,1)S(1)}, bf16[4,12,256,256]{3,2,1,0:T(8,128)(2,1)}, u32[]{:S(2)}) copy-start(bf16[4,12,256,256]{3,2,1,0:T(8,128)(2,1)} %near_ref.7) | copy-start | bytes 18874372
  12.0 8.9 %collective-permute-start.3 = (bf16[80,1024]{1,0:T(8,128)(2,1)S(1)}, bf16[80,1024]{1,0:T(8,128)(2,1)S(1)}, u32[]{:S(2)}, u32[]{:S(2)}) collective-permute-start(bf16[80,1024]{1,0:T(8,128)(2,1)S(1)} %get-tuple-element.66.rest_0_), channel_id=1, source_target_pairs={{0,4},{1,5},{2,6},{3,7},{4,8},{5,9},{6,10},{7,11},{8,12},{9,13},{1... | collective-permute-start | bytes 491528 | tf_op jit(solution)/shard_map/ppermute | solution.py:390
  13.7 20.0 %collective-permute-start.6 = (bf16[1024,256]{1,0:T(8,128)(2,1)}, bf16[1024,256]{1,0:T(8,128)(2,1)S(1)}, u32[]{:S(2)}, u32[]{:S(2)}) collective-permute-start(bf16[1024,256]{1,0:T(8,128)(2,1)} %get-tuple-element.49.rest_1_.rest_0_), channel_id=1, source_target_pairs={{0,2},{1,3},{2,0},{3,1},{4,6},{5,7},{6,4},{7,5},{8,10},{9,11},{10,... | collective-permute-start | bytes 1572872 | tf_op jit(solution)/shard_map/ppermute | solution.py:390
  14.2 14.5 %collective-permute-start.4 = (bf16[80,1024]{1,0:T(8,128)(2,1)S(1)}, bf16[80,1024]{1,0:T(8,128)(2,1)S(1)}, u32[]{:S(2)}, u32[]{:S(2)}) collective-permute-start(bf16[80,1024]{1,0:T(8,128)(2,1)S(1)} %get-tuple-element.66.rest_0_), channel_id=1, source_target_pairs={{0,12},{1,13},{2,14},{3,15},{4,0},{5,1},{6,2},{7,3},{8,4},{9,5},{1... | collective-permute-start | bytes 491528 | tf_op jit(solution)/shard_map/ppermute | solution.py:390
  21.0 12.7 %collective-permute-start.8 = (bf16[80,1024]{1,0:T(8,128)(2,1)S(1)}, bf16[80,1024]{1,0:T(8,128)(2,1)S(1)}, u32[]{:S(2)}, u32[]{:S(2)}) collective-permute-start(bf16[80,1024]{1,0:T(8,128)(2,1)S(1)} %get-tuple-element.66.rest_0_), channel_id=1, source_target_pairs={{0,8},{1,9},{2,10},{3,11},{4,12},{5,13},{6,14},{7,15},{8,0},{9,1},... | collective-permute-start | bytes 491528 | tf_op jit(solution)/shard_map/ppermute | solution.py:390
  26.3 0.9 %copy-start.8 = (bf16[4,64,256]{2,1,0:T(8,128)(2,1)S(1)}, bf16[4,64,256]{2,1,0:T(8,128)(2,1)}, u32[]{:S(2)}) copy-start(bf16[4,64,256]{2,1,0:T(8,128)(2,1)} %target_ref.1) | copy-start | bytes 393220
  28.7 14.7 %collective-permute-start.1 = (bf16[1152,256]{1,0:T(8,128)(2,1)S(1)}, bf16[1152,256]{1,0:T(8,128)(2,1)S(1)}, u32[]{:S(2)}, u32[]{:S(2)}) collective-permute-start(bf16[1152,256]{1,0:T(8,128)(2,1)S(1)} %get-tuple-element.54.rest_0_), channel_id=1, source_target_pairs={{0,2},{1,3},{2,0},{3,1},{4,6},{5,7},{6,4},{7,5},{8,10},{9,11},{10,... | collective-permute-start | bytes 1769480 | tf_op jit(solution)/shard_map/ppermute | solution.py:390
  30.6 8.2 %collective-permute-start.7 = (bf16[512,256]{1,0:T(8,128)(2,1)S(1)}, bf16[512,256]{1,0:T(8,128)(2,1)S(1)}, u32[]{:S(2)}, u32[]{:S(2)}) collective-permute-start(bf16[512,256]{1,0:T(8,128)(2,1)S(1)} %get-tuple-element.59), channel_id=1, source_target_pairs={{0,4},{1,5},{2,14},{3,15},{4,8},{5,9},{6,2},{7,3},{8,12},{9,13},{1... | collective-permute-start | bytes 786440 | tf_op jit(solution)/shard_map/ppermute | solution.py:390
  33.6 10.3 %collective-permute-start.5 = (bf16[1024,256]{1,0:T(8,128)(2,1)S(1)}, bf16[1024,256]{1,0:T(8,128)(2,1)S(1)}, u32[]{:S(2)}, u32[]{:S(2)}) collective-permute-start(bf16[1024,256]{1,0:T(8,128)(2,1)S(1)} %collective-permute-done.2.arrived_ref.rest_2_), channel_id=1, source_target_pairs={{0,1},{1,0},{2,3},{3,2},{4,5},{5,4},{6,7},{7,6},{8,9},{9,8},{10,11... | collective-permute-start | bytes 1572872 | tf_op jit(solution)/shard_map/ppermute | solution.py:390
  33.6 9.8 %collective-permute-start.9 = (bf16[512,256]{1,0:T(8,128)(2,1)S(1)}, bf16[512,256]{1,0:T(8,128)(2,1)S(1)}, u32[]{:S(2)}, u32[]{:S(2)}) collective-permute-start(bf16[512,256]{1,0:T(8,128)(2,1)S(1)} %get-tuple-element.62), channel_id=1, source_target_pairs={{1,4},{2,15},{5,8},{6,3},{9,12},{10,7},{13,0},{14,11},{17,20},{18,... | collective-permute-start | bytes 786440 | tf_op jit(solution)/shard_map/ppermute | solution.py:390
  39.4 9.3 %collective-permute-start.10 = (bf16[512,256]{1,0:T(8,128)(2,1)S(1)}, bf16[512,256]{1,0:T(8,128)(2,1)S(1)}, u32[]{:S(2)}, u32[]{:S(2)}) collective-permute-start(bf16[512,256]{1,0:T(8,128)(2,1)S(1)} %get-tuple-element.64), channel_id=1, source_target_pairs={{0,4},{1,5},{2,14},{3,15},{4,8},{5,9},{6,2},{7,3},{8,12},{9,13},{1... | collective-permute-start | bytes 786440 | tf_op jit(solution)/shard_map/ppermute | solution.py:390
  43.4 5.3 %collective-permute-start.12 = (bf16[80,1024]{1,0:T(8,128)(2,1)S(1)}, bf16[80,1024]{1,0:T(8,128)(2,1)S(1)}, u32[]{:S(2)}, u32[]{:S(2)}) collective-permute-start(bf16[80,1024]{1,0:T(8,128)(2,1)S(1)} %collective-permute-done.4.ahead_ref.rest_1_), channel_id=1, source_target_pairs={{0,1},{1,0},{2,3},{3,2},{4,5},{5,4},{6,7},{7,6},{8,9},{9,8},{10,11... | collective-permute-start | bytes 491528 | tf_op jit(solution)/shard_map/ppermute | solution.py:390
  43.4 5.9 %collective-permute-start.13 = (bf16[80,1024]{1,0:T(8,128)(2,1)S(1)}, bf16[80,1024]{1,0:T(8,128)(2,1)S(1)}, u32[]{:S(2)}, u32[]{:S(2)}) collective-permute-start(bf16[80,1024]{1,0:T(8,128)(2,1)S(1)} %collective-permute-done.8.rest_2_), channel_id=1, source_target_pairs={{0,1},{1,0},{2,3},{3,2},{4,5},{5,4},{6,7},{7,6},{8,9},{9,8},{10,11... | collective-permute-start | bytes 491528 | tf_op jit(solution)/shard_map/ppermute | solution.py:390
  43.9 14.1 %collective-permute-start.15 = (bf16[1024,256]{1,0:T(8,128)(2,1)}, bf16[1024,256]{1,0:T(8,128)(2,1)S(1)}, u32[]{:S(2)}, u32[]{:S(2)}) collective-permute-start(bf16[1024,256]{1,0:T(8,128)(2,1)} %copy-done.2), channel_id=1, source_target_pairs={{0,2},{1,3},{2,0},{3,1},{4,6},{5,7},{6,4},{7,5},{8,10},{9,11},{10,... | collective-permute-start | bytes 1572872 | tf_op jit(solution)/shard_map/ppermute | solution.py:390
  48.7 14.4 %collective-permute-start.16 = (bf16[1024,256]{1,0:T(8,128)(2,1)S(1)}, bf16[1024,256]{1,0:T(8,128)(2,1)S(1)}, u32[]{:S(2)}, u32[]{:S(2)}) collective-permute-start(bf16[1024,256]{1,0:T(8,128)(2,1)S(1)} %collective-permute-done.6.arrived_ref.rest_2_), channel_id=1, source_target_pairs={{0,1},{1,0},{2,3},{3,2},{4,5},{5,4},{6,7},{7,6},{8,9},{9,8},{10,11... | collective-permute-start | bytes 1572872 | tf_op jit(solution)/shard_map/ppermute | solution.py:390
  48.7 2.1 %collective-permute-start.14 = (bf16[80,1024]{1,0:T(8,128)(2,1)S(1)}, bf16[80,1024]{1,0:T(8,128)(2,1)S(1)}, u32[]{:S(2)}, u32[]{:S(2)}) collective-permute-start(bf16[80,1024]{1,0:T(8,128)(2,1)S(1)} %collective-permute-done.3.behind_ref.rest_3_), channel_id=1, source_target_pairs={{0,1},{1,0},{2,3},{3,2},{4,5},{5,4},{6,7},{7,6},{8,9},{9,8},{10,11... | collective-permute-start | bytes 491528 | tf_op jit(solution)/shard_map/ppermute | solution.py:390
  49.2 2.9 %collective-permute-start.11 = (bf16[80,1024]{1,0:T(8,128)(2,1)S(1)}, bf16[80,1024]{1,0:T(8,128)(2,1)S(1)}, u32[]{:S(2)}, u32[]{:S(2)}) collective-permute-start(bf16[80,1024]{1,0:T(8,128)(2,1)S(1)} %get-tuple-element.66.rest_0_), channel_id=1, source_target_pairs={{0,1},{1,0},{2,3},{3,2},{4,5},{5,4},{6,7},{7,6},{8,9},{9,8},{10,11... | collective-permute-start | bytes 491528 | tf_op jit(solution)/shard_map/ppermute | solution.py:390
  50.9 12.2 %collective-permute-start.18 = (bf16[512,256]{1,0:T(8,128)(2,1)S(1)}, bf16[512,256]{1,0:T(8,128)(2,1)S(1)}, u32[]{:S(2)}, u32[]{:S(2)}) collective-permute-start(bf16[512,256]{1,0:T(8,128)(2,1)S(1)} %get-tuple-element.75), channel_id=1, source_target_pairs={{1,4},{2,15},{5,8},{6,3},{9,12},{10,7},{13,0},{14,11},{17,20},{18,... | collective-permute-start | bytes 786440 | tf_op jit(solution)/shard_map/ppermute | solution.py:390
  52.2 11.0 %collective-permute-start.19 = (bf16[512,256]{1,0:T(8,128)(2,1)S(1)}, bf16[512,256]{1,0:T(8,128)(2,1)S(1)}, u32[]{:S(2)}, u32[]{:S(2)}) collective-permute-start(bf16[512,256]{1,0:T(8,128)(2,1)S(1)} %get-tuple-element.76), channel_id=1, source_target_pairs={{0,4},{1,5},{2,14},{3,15},{4,8},{5,9},{6,2},{7,3},{8,12},{9,13},{1... | collective-permute-start | bytes 786440 | tf_op jit(solution)/shard_map/ppermute | solution.py:390
  52.3 20.9 %collective-permute-start.22 = (bf16[1152,256]{1,0:T(8,128)(2,1)S(1)}, bf16[1152,256]{1,0:T(8,128)(2,1)S(1)}, u32[]{:S(2)}, u32[]{:S(2)}) collective-permute-start(bf16[1152,256]{1,0:T(8,128)(2,1)S(1)} %collective-permute-done.1.carrier_ref.arrived_ref.rest_2_), channel_id=1, source_target_pairs={{0,1},{1,0},{2,3},{3,2},{4,5},{5,4},{6,7},{7,6},{8,9},{9,8},{10,11... | collective-permute-start | bytes 1769480 | tf_op jit(solution)/shard_map/ppermute | solution.py:390
  58.0 10.8 %collective-permute-start.23 = (bf16[512,256]{1,0:T(8,128)(2,1)S(1)}, bf16[512,256]{1,0:T(8,128)(2,1)S(1)}, u32[]{:S(2)}, u32[]{:S(2)}) collective-permute-start(bf16[512,256]{1,0:T(8,128)(2,1)S(1)} %get-tuple-element.85), channel_id=1, source_target_pairs={{1,4},{2,15},{5,8},{6,3},{9,12},{10,7},{13,0},{14,11},{17,20},{18,... | collective-permute-start | bytes 786440 | tf_op jit(solution)/shard_map/ppermute | solution.py:390
  63.2 16.1 %collective-permute-start.21 = (bf16[1024,256]{1,0:T(8,128)(2,1)S(1)}, bf16[1024,256]{1,0:T(8,128)(2,1)S(1)}, u32[]{:S(2)}, u32[]{:S(2)}) collective-permute-start(bf16[1024,256]{1,0:T(8,128)(2,1)S(1)} %collective-permute-done.15.arrived_ref.rest_2_), channel_id=1, source_target_pairs={{0,1},{1,0},{2,3},{3,2},{4,5},{5,4},{6,7},{7,6},{8,9},{9,8},{10,11... | collective-permute-start | bytes 1572872 | tf_op jit(solution)/shard_map/ppermute | solution.py:390
  65.8 9.9 %collective-permute-start.20 = (f32[64,1024]{1,0:T(8,128)S(1)}, f32[64,1024]{1,0:T(8,128)S(1)}, u32[]{:S(2)}, u32[]{:S(2)}) collective-permute-start(f32[64,1024]{1,0:T(8,128)S(1)} %get-tuple-element.77), channel_id=1, source_target_pairs={{0,2},{1,3},{2,0},{3,1},{4,6},{5,7},{6,4},{7,5},{8,10},{9,11},{10,... | collective-permute-start | bytes 786440 | tf_op jit(solution)/shard_map/ppermute | solution.py:390
  66.4 11.0 %collective-permute-start.24 = (bf16[512,256]{1,0:T(8,128)(2,1)S(1)}, bf16[512,256]{1,0:T(8,128)(2,1)S(1)}, u32[]{:S(2)}, u32[]{:S(2)}) collective-permute-start(bf16[512,256]{1,0:T(8,128)(2,1)S(1)} %get-tuple-element.86), channel_id=1, source_target_pairs={{0,4},{1,5},{2,14},{3,15},{4,8},{5,9},{6,2},{7,3},{8,12},{9,13},{1... | collective-permute-start | bytes 786440 | tf_op jit(solution)/shard_map/ppermute | solution.py:390
  68.8 10.5 %collective-permute-start.25 = (bf16[512,256]{1,0:T(8,128)(2,1)S(1)}, bf16[512,256]{1,0:T(8,128)(2,1)S(1)}, u32[]{:S(2)}, u32[]{:S(2)}) collective-permute-start(bf16[512,256]{1,0:T(8,128)(2,1)S(1)} %get-tuple-element.87), channel_id=1, source_target_pairs={{1,4},{2,15},{5,8},{6,3},{9,12},{10,7},{13,0},{14,11},{17,20},{18,... | collective-permute-start | bytes 786440 | tf_op jit(solution)/shard_map/ppermute | solution.py:390
  75.7 3.5 %copy-start.4 = (bf16[1024,256]{1,0:T(8,128)(2,1)S(1)}, bf16[1024,256]{1,0:T(8,128)(2,1)}, u32[]{:S(2)}) copy-start(bf16[1024,256]{1,0:T(8,128)(2,1)} %copy-done.2) | copy-start | bytes 1572868

commit v4 on v3

v4 whole, which is shorter than its diff:
```python
import functools

import jax
import jax.numpy as jnp
from jax import lax
from jax.experimental import pallas as pl
from jax.experimental.pallas import tpu as pltpu
from jax.sharding import PartitionSpec as P

LEAF = 256
RANK = 64
B_DEV = 4
NEAR = 12
ROWS = B_DEV * LEAF
SLABS = ((0, 256), (256, 256), (512, 256), (768, 256))
CARRIER = 2
WISH = 16
OWN, CORE, ACROSS, ACROSS_CORE, ALONG, ALONG_CORE, ZERO = 0, 4, 8, 12, 14, 16, 18
HELD = 19
HELD_AT = (
    (ALONG, ALONG_CORE, OWN, CORE, ACROSS),
    (ALONG, CORE, OWN, ACROSS_CORE, ACROSS),
    (ACROSS, ACROSS_CORE, OWN, CORE, ALONG),
    (ACROSS, CORE, OWN, ALONG_CORE, ALONG),
)
MIB = 1024 * 1024
STEP = 0.4
UP_LIMIT = 58
BYTES = 1
ANYWHERE = pl.BlockSpec(memory_space=pl.ANY)
VECTOR = pl.BlockSpec(memory_space=pltpu.VMEM)
SCALAR = pl.BlockSpec(memory_space=pltpu.SMEM)


def cost(microseconds):
    return pl.CostEstimate(flops=int(microseconds * 1.15e9), bytes_accessed=BYTES * MIB, transcendentals=0)


def split(value):
    high = value.astype(jnp.bfloat16)
    low = (value - high.astype(jnp.float32)).astype(jnp.bfloat16)
    return high, low


def dot(a, b):
    return jnp.dot(a, b, preferred_element_type=jnp.float32)


def dot_split(a, b):
    high, low = split(a)
    both = dot(jnp.concatenate([high, low], axis=0), b)
    return both[: a.shape[0]] + both[a.shape[0] :]


def first_two(named):
    first = jnp.where(named[0], 0, jnp.where(named[1], 1, jnp.where(named[2], 2, 3)))
    second = jnp.where(named[1] & (first < 1), 1, jnp.where(named[2] & (first < 2), 2, 3))
    return first, second


def places(members, position, numbers, counts):
    distance = (numbers >> 2) - position + 2
    distance = jnp.where(distance < 0, distance + members, distance)
    distance = jnp.where(distance >= members, distance - members, distance)
    base = jnp.full(numbers.shape, ZERO, jnp.int32)
    for d in range(5):
        at = jnp.int32(HELD_AT[0][d])
        for kind in range(1, 4):
            at = jnp.where(position & 3 == kind, HELD_AT[kind][d], at)
        base = jnp.where(distance == d, at, base)
    row = lax.broadcasted_iota(jnp.int32, (B_DEV, B_DEV), 0)
    column = lax.broadcasted_iota(jnp.int32, (B_DEV, B_DEV), 1)
    counts = jnp.max(jnp.where(row == column, counts, 0), axis=1, keepdims=True)
    live = lax.broadcasted_iota(jnp.int32, numbers.shape, 1) < counts
    base = jnp.where(live, base, ZERO)
    inner = numbers & 3
    picks = []
    for group in (ALONG, ALONG_CORE, ACROSS_CORE):
        named = []
        for box in range(B_DEV):
            here = jnp.where((base == group) & (inner == box), 1, 0)
            named.append(jnp.max(jnp.max(here, axis=1, keepdims=True), axis=0, keepdims=True) > 0)
        picks.append(first_two(named))
    return base, inner, picks


def up_kernel(members, *refs):
    given, rest = refs[:6], refs[6:]
    panel_ref, entry_ref, *parts = rest[: 2 + len(SLABS)]
    *kept, sems = rest[2 + len(SLABS) :]
    pairs = list(zip(given[:5], kept))
    pairs += [(given[5].at[:, pl.ds(start, width)], part.at[pl.ds(0, ROWS)]) for (start, width), part in zip(SLABS, parts)]
    copies = [pltpu.make_async_copy(a, b, sems.at[i]) for i, (a, b) in enumerate(pairs)]
    for copy in copies:
        copy.start()
    source_ref, leaf_ref, mid_ref, ids_ref, count_ref = kept
    for copy in copies[:5]:
        copy.wait()
    base, inner, picks = places(members, lax.axis_index("pts"), ids_ref[...], count_ref[...])
    first = jnp.where(base == ALONG, picks[0][0], jnp.where(base == ALONG_CORE, picks[1][0], picks[2][0]))
    picked = jnp.where(inner == first, 0, 1)
    entry_ref[...] = base + jnp.where(base == ZERO, 0, jnp.where(base >= ACROSS_CORE, picked, inner))
    for k, name in enumerate(pick[n] for pick in picks for n in range(2)):
        panel_ref[pl.ds(RANK, WISH), pl.ds(k * 128, 128)] = jnp.broadcast_to(
            name.astype(jnp.float32), (WISH, 128)
        ).astype(jnp.bfloat16)
    panel_ref[pl.ds(RANK, WISH), pl.ds(6 * 128, 2 * 128)] = jnp.zeros((WISH, 2 * 128), jnp.bfloat16)
    ups = [dot_split(dot(mid_ref[box // 2], leaf_ref[box]), source_ref[box]) for box in range(B_DEV)]
    high, low = split(jnp.concatenate(ups, axis=1))
    both = jnp.concatenate([high, low], axis=0)
    for copy, (start, width), part in zip(copies[5:], SLABS, parts):
        copy.wait()
        sums = dot(both, part[pl.ds(0, ROWS)])
        panel_ref[pl.ds(0, RANK), pl.ds(start, width)] = (sums[:RANK] + sums[RANK:]).astype(jnp.bfloat16)


def up(members, carried, *given):
    columns = given[-1].shape[1]
    shapes = [(ROWS, width) for _, width in SLABS]
    shapes[CARRIER] = (ROWS + RANK * -(-carried // shapes[CARRIER][1]), shapes[CARRIER][1])
    return pl.pallas_call(
        functools.partial(up_kernel, members),
        in_specs=[ANYWHERE] * len(given),
        out_shape=(
            jax.ShapeDtypeStruct((RANK + WISH, columns), jnp.bfloat16),
            jax.ShapeDtypeStruct((B_DEV, NEAR), jnp.int32),
            *[jax.ShapeDtypeStruct(shape, jnp.bfloat16) for shape in shapes],
        ),
        scratch_shapes=[pltpu.VMEM(a.shape, a.dtype) for a in given[:5]]
        + [pltpu.SemaphoreType.DMA((5 + len(SLABS),))],
        compiler_params=pltpu.CompilerParams(vmem_limit_bytes=UP_LIMIT * MIB),
        cost_estimate=cost(2),
        name="up",
    )(*given)


def down_kernel(reach, members, far_ref, target_ref, leaf_ref, mid_ref, coupling_ref, *rest):
    part_ref, down_ref, placed_ref, lines_ref, sem = rest[-5:]
    for box in range(B_DEV):
        chain = dot(mid_ref[box // 2], leaf_ref[box])
        high, low = split(dot_split(chain, target_ref[box]).T)
        down_ref[box] = jnp.concatenate([high, low, high], axis=1)
    position = lax.axis_index("pts")
    quad, side, core = position >> 2, (position >> 1) & 1, position & 1
    for half in range(2):
        blocks = []
        for other in range(2):
            for step in reach:
                held_quad = quad + step
                held_quad = jnp.where(held_quad >= members // 4, held_quad - members // 4, held_quad)
                group = held_quad * 4 + 2 * (side ^ half) + (core ^ other)
                block = jnp.zeros((RANK, RANK), jnp.float32)
                for f in range(coupling_ref.shape[0]):
                    block = jnp.where(far_ref[0, f] == group, coupling_ref[f].astype(jnp.float32), block)
                blocks.append(block)
        placed = jnp.concatenate(blocks, axis=1).astype(jnp.bfloat16)
        if half == 0:
            placed_ref[...] = placed
            continue
        width = part_ref.shape[1]
        for line, at in enumerate(range(0, placed.shape[1], width)):
            taken = placed[:, at : at + width]
            lines_ref[pl.ds(line * RANK, RANK), pl.ds(0, taken.shape[1])] = taken
        copy = pltpu.make_async_copy(lines_ref, part_ref.at[pl.ds(ROWS, lines_ref.shape[0])], sem)
        copy.start()
        copy.wait()


def down(reach, members, far_ids, target_basis, leaf_transfer, mid_transfer, coupling, part, *before):
    return pl.pallas_call(
        functools.partial(down_kernel, reach, members),
        in_specs=[SCALAR] + [VECTOR] * 4 + [ANYWHERE] * (1 + len(before)),
        out_specs=(ANYWHERE, VECTOR, VECTOR),
        out_shape=(
            jax.ShapeDtypeStruct(part.shape, part.dtype),
            jax.ShapeDtypeStruct((B_DEV, LEAF, 3 * RANK), jnp.bfloat16),
            jax.ShapeDtypeStruct((RANK, 2 * len(reach) * RANK), jnp.bfloat16),
        ),
        scratch_shapes=[
            pltpu.VMEM((part.shape[0] - ROWS, part.shape[1]), part.dtype),
            pltpu.SemaphoreType.DMA,
        ],
        input_output_aliases={5: 0},
        compiler_params=pltpu.CompilerParams(vmem_limit_bytes=16 * MIB),
        cost_estimate=cost(1),
        name="down",
    )(far_ids, target_basis, leaf_transfer, mid_transfer, coupling, part, *before)


def ask_kernel(panel_ref, ahead_ref, behind_ref, *rest):
    asked_ref = rest[-1]
    forth = (lax.axis_index("pts") & 2) == 0
    wishes = (pl.ds(RANK, WISH), pl.ds(0, 6 * 128))
    ahead, behind = ahead_ref[wishes].astype(jnp.float32), behind_ref[wishes].astype(jnp.float32)
    asked_ref[pl.ds(0, WISH)] = jnp.where(forth, ahead, behind).astype(jnp.bfloat16)
    asked_ref[pl.ds(WISH, WISH)] = panel_ref[wishes]


def ask(panel, ahead, behind, *before):
    return pl.pallas_call(
        ask_kernel,
        in_specs=[VECTOR] * 3 + [ANYWHERE] * len(before),
        out_shape=jax.ShapeDtypeStruct((2 * WISH, 6 * 128), jnp.bfloat16),
        compiler_params=pltpu.CompilerParams(vmem_limit_bytes=8 * MIB),
        cost_estimate=cost(0.1),
        name="ask",
    )(panel, ahead, behind, *before)


def wishes_kernel(asked_ref, core_asked_ref, wish_ref):
    for name in range(6):
        ref = asked_ref if name < 2 else core_asked_ref
        value = ref[pl.ds(0 if name < 4 else WISH, WISH), pl.ds(name * 128, 128)]
        wish_ref[0, name] = jnp.max(value.astype(jnp.float32)).astype(jnp.int32)


def wishes(asked, core_asked):
    return pl.pallas_call(
        wishes_kernel,
        in_specs=[VECTOR] * 2,
        out_specs=SCALAR,
        out_shape=jax.ShapeDtypeStruct((1, 6), jnp.int32),
        compiler_params=pltpu.CompilerParams(vmem_limit_bytes=8 * MIB),
        cost_estimate=cost(0.1),
        name="wishes",
    )(asked, core_asked)


def couple_kernel(own_ref, carrier_ref, *rest):
    tables, (own_sum_ref, partner_sum_ref) = rest[:-2], rest[-2:]
    depth = own_ref.shape[1]
    table = jnp.concatenate([ref[...] for ref in tables], axis=0)
    lines = [carrier_ref[pl.ds(row, RANK)] for row in range(ROWS, carrier_ref.shape[0], RANK)]
    partner_sum_ref[...] = dot(jnp.concatenate(lines, axis=1)[:, :depth], table)
    own_sum_ref[...] = dot(own_ref[...], table)


def couple(own, carrier, *tables):
    shape = jax.ShapeDtypeStruct((RANK, tables[0].shape[1]), jnp.float32)
    return pl.pallas_call(
        couple_kernel,
        out_shape=(shape, shape),
        compiler_params=pltpu.CompilerParams(vmem_limit_bytes=16 * MIB),
        cost_estimate=cost(0.1),
        name="couple",
    )(own, carrier, *tables)


def pick(wish_ref, at, arrived_ref, picked_ref):
    for k in range(2):
        rows = pl.ds(pl.multiple_of(wish_ref[0, at + k] * LEAF, LEAF), LEAF)
        picked_ref[pl.ds(k * LEAF, LEAF)] = arrived_ref[rows]


def pack_kernel(wish_ref, arrived_ref, *rest):
    for at, picked_ref in enumerate(rest[-3:]):
        pick(wish_ref, 2 * at, arrived_ref, picked_ref)


def pack(wish, arrived, before):
    shape = jax.ShapeDtypeStruct((2 * LEAF, arrived.shape[1]), arrived.dtype)
    return pl.pallas_call(
        pack_kernel,
        in_specs=[SCALAR, VECTOR] + [ANYWHERE] * len(before),
        out_shape=(shape,) * 3,
        compiler_params=pltpu.CompilerParams(vmem_limit_bytes=8 * MIB),
        cost_estimate=cost(0.02),
        name="pack",
    )(wish, arrived, *before)


def gather(start, width, held, pieces):
    own_ref, core_ref, across_ref, across_core_ref, along_ref, along_core_ref = pieces
    for at, boxes, taken in (
        (OWN, B_DEV, own_ref[pl.ds(0, ROWS)]),
        (CORE, B_DEV, core_ref[:, pl.ds(start, width)]),
        (ACROSS, B_DEV, across_ref[pl.ds(0, ROWS)]),
        (ACROSS_CORE, 2, across_core_ref[...]),
        (ALONG, 2, along_ref[...]),
        (ALONG_CORE, 2, along_core_ref[...]),
    ):
        held[pl.ds(at * LEAF, boxes * LEAF)] = taken
    held[pl.ds(ZERO * LEAF, LEAF)] = jnp.zeros((LEAF, width), jnp.bfloat16)


def operands(box, entry_ref, near_ref, held):
    left = [near_ref[box, n] for n in range(NEAR)]
    right = [held[pl.ds(pl.multiple_of(entry_ref[box, n] * LEAF, LEAF), LEAF)] for n in range(NEAR)]
    return left, right


def near_kernel(start, entry_ref, near_ref, *rest):
    pieces, (sum_ref, held) = rest[:6], rest[-2:]
    gather(start, sum_ref.shape[1], held, pieces)
    for box in range(B_DEV):
        left, right = operands(box, entry_ref, near_ref, held)
        sum_ref[pl.ds(box * LEAF, LEAF)] = dot(
            jnp.concatenate(left, axis=1), jnp.concatenate(right, axis=0)
        )


def near(start, width, entry, near_blocks, pieces, before):
    return pl.pallas_call(
        functools.partial(near_kernel, start),
        in_specs=[SCALAR] + [VECTOR] * (1 + len(pieces)) + [ANYWHERE] * len(before),
        out_specs=VECTOR,
        scratch_shapes=[pltpu.VMEM((HELD * LEAF, width), jnp.bfloat16)],
        out_shape=jax.ShapeDtypeStruct((ROWS, width), jnp.float32),
        compiler_params=pltpu.CompilerParams(vmem_limit_bytes=16 * MIB),
        cost_estimate=cost(STEP),
        name="near",
    )(entry, near_blocks, *pieces, *before)


def last_kernel(start, width, entry_ref, near_ref, own_sum_ref, partner_sum_ref, down_ref, *rest):
    pieces, (_, out_ref, held, made, sems) = rest[:-5], rest[-5:]
    gather(start, width, held, pieces)
    taken = pl.ds(start, width)
    high, low = split(own_sum_ref[:, taken] + partner_sum_ref[:, taken])
    coupled = jnp.concatenate([high, high, low], axis=0)
    copies = []
    for box in range(B_DEV):
        left, right = operands(box, entry_ref, near_ref, held)
        rows = pl.ds(box * LEAF, LEAF)
        near_sum = dot(jnp.concatenate(left, axis=1), jnp.concatenate(right, axis=0))
        made[rows] = (near_sum + dot(down_ref[box], coupled)).astype(jnp.bfloat16)
        copy = pltpu.make_async_copy(made.at[rows], out_ref.at[rows, taken], sems.at[box])
        copy.start()
        copies.append(copy)
    for copy in copies:
        copy.wait()


def last(start, width, entry, near_blocks, sums, down_basis, pieces, product):
    given = [entry, near_blocks, *sums, down_basis, *pieces, product]
    return pl.pallas_call(
        functools.partial(last_kernel, start, width),
        in_specs=[SCALAR] + [VECTOR] * (len(given) - 2) + [ANYWHERE],
        out_specs=ANYWHERE,
        scratch_shapes=[
            pltpu.VMEM((HELD * LEAF, width), jnp.bfloat16),
            pltpu.VMEM((ROWS, width), jnp.bfloat16),
            pltpu.SemaphoreType.DMA((B_DEV,)),
        ],
        out_shape=jax.ShapeDtypeStruct(product.shape, product.dtype),
        input_output_aliases={len(given) - 1: 0},
        compiler_params=pltpu.CompilerParams(vmem_limit_bytes=16 * MIB),
        cost_estimate=cost(1),
        name="last",
    )(*given)


def finish_kernel(slabs, own_sum_ref, partner_sum_ref, down_ref, *rest):
    sum_refs = rest[: len(slabs)]
    out_ref, made, sems = rest[-3:]
    start, stop = slabs[0][0], slabs[-1][0] + slabs[-1][1]
    taken = pl.ds(start, stop - start)
    high, low = split(own_sum_ref[:, taken] + partner_sum_ref[:, taken])
    coupled = jnp.concatenate([high, high, low], axis=0)
    copies = []
    for box in range(B_DEV):
        rows = pl.ds(box * LEAF, LEAF)
        far = dot(down_ref[box], coupled)
        for (at, width), sum_ref in zip(slabs, sum_refs):
            columns = slice(at - start, at - start + width)
            made[rows, columns] = (far[:, columns] + sum_ref[rows]).astype(jnp.bfloat16)
        copy = pltpu.make_async_copy(made.at[rows], out_ref.at[rows, taken], sems.at[box])
        copy.start()
        copies.append(copy)
    for copy in copies:
        copy.wait()


def finish(slabs, sums, down_basis, nears):
    columns = sums[0].shape[1]
    given = [*sums, down_basis, *nears]
    return pl.pallas_call(
        functools.partial(finish_kernel, slabs),
        in_specs=[VECTOR] * len(given),
        out_specs=ANYWHERE,
        scratch_shapes=[
            pltpu.VMEM((ROWS, sum(width for _, width in slabs)), jnp.bfloat16),
            pltpu.SemaphoreType.DMA((B_DEV,)),
        ],
        out_shape=jax.ShapeDtypeStruct((ROWS, columns), jnp.bfloat16),
        compiler_params=pltpu.CompilerParams(vmem_limit_bytes=16 * MIB),
        cost_estimate=cost(STEP),
        name="finish",
    )(*given)


def on_device(
    rhs,
    near_blocks,
    near_ids,
    near_count,
    source_basis,
    target_basis,
    leaf_transfer,
    mid_transfer,
    far_coupling,
    far_ids,
):
    members = lax.axis_size("pts")
    every = range(members)
    across_pairs = [(i, i ^ 2) for i in every]
    core_pairs = [(i, i ^ 1) for i in every]
    along_pairs = [(i, (i + (-4 if i & 2 else 4)) % members) for i in every]
    along_core_pairs = [(i, (i + (-3 if i & 2 else 3)) % members) for i in every if i % 4 in (1, 2)]
    permute = lambda value, pairs: lax.ppermute(value, "pts", pairs)
    meet = lambda *values: lax.optimization_barrier(values)
    quads = members // 4
    reach = list(dict.fromkeys(step % quads for step in (0, 1, -1, 2, -2)))

    rhs_core = permute(rhs, core_pairs)
    panel, entry, *parts = up(
        members,
        2 * len(reach) * RANK,
        source_basis,
        leaf_transfer,
        mid_transfer,
        near_ids,
        near_count.reshape(1, B_DEV),
        rhs,
    )
    parts[CARRIER], down_basis, placed = down(
        reach, members, far_ids, target_basis, leaf_transfer, mid_transfer, far_coupling[0], parts[CARRIER]
    )
    across = [permute(part, across_pairs) for part in parts[:3]]
    others = [permute(panel, [(i, (i - 4 * step) % members) for i in every]) for step in reach[1:]]
    across[0], panel, others[0], others[1] = meet(across[0], panel, others[0], others[1])
    asked = ask(panel, others[0], others[1], rhs_core, down_basis)
    wish = wishes(asked, permute(asked, core_pairs))

    nears, along, across_core = [], [], []

    def pieces(k):
        return (parts[k], rhs_core, across[k], across_core[k], *along[k])

    for k in range(len(SLABS)):
        if k >= 2:
            nears.append(near(*SLABS[k - 2], entry, near_blocks, pieces(k - 2), nears[-1:]))
        picks = list(pack(wish, across[k], across_core[-1:] + nears[-1:] if k else others[2:]))
        along.append([permute(picks[0], along_pairs), permute(picks[1], along_core_pairs)])
        if k == 1:
            nearby = jnp.concatenate([each[:RANK] for each in (panel, *others)], axis=0)
            nearby, along[0][1] = meet(nearby, along[0][1])
            core_nearby = permute(nearby, core_pairs)
        if k >= 1:
            picks[2], along[k - 1][0] = meet(picks[2], along[k - 1][0])
        across_core.append(permute(picks[2], core_pairs))
        if k == 1:
            parts[3], along[0][1] = meet(parts[3], along[0][1])
            across.append(permute(parts[3], across_pairs))
        if k == 2:
            own_sum, partner_sum = couple(placed, across[CARRIER], nearby, core_nearby)
            partner_sum, along[1][1] = meet(partner_sum, along[1][1])
            sums = (own_sum, permute(partner_sum, across_pairs))
    nears.append(near(*SLABS[2], entry, near_blocks, pieces(2), nears[-1:]))
    product = finish(SLABS[:-1], sums, down_basis, nears)
    return last(*SLABS[-1], entry, near_blocks, sums, down_basis, pieces(3), product)


def solution(mesh):
    return jax.shard_map(
        on_device,
        mesh=mesh,
        in_specs=(
            P(("parts", "pts"), None),
            P(("parts", "pts"), None, None, None),
            P(("parts", "pts"), None),
            P(("parts", "pts")),
            P(("parts", "pts"), None, None),
            P(("parts", "pts"), None, None),
            P(("parts", "pts"), None, None),
            P(("parts", "pts"), None, None),
            P(("parts", "pts"), None, None, None),
            P(("parts", "pts"), None),
        ),
        out_specs=P(("parts", "pts"), None),
        check_vma=False,
    )
```

time: 83 us -> 79.5 us (0.958)
  local copies, waits for them, and re-layouts: 4.48 us -> 1.01 us
  starting transfers between devices: 24.7 us -> 26.2 us
  waiting for transfers between devices: 30.4 us -> 29.5 us
    unnamed x26, local copies, waits for them, and re-layouts: 4.39 us -> 0.97 us
    ppermute x26 -> x23, starting transfers between devices: 24.7 us -> 26.2 us  [on_device(): permute = lambda value, pairs: lax.ppermute(value, 'pts', pairs)]
    pallas_call x6, Pallas kernels: 4.33 us -> 3.12 us  [the longest x4 2.39 us: pack(): pl.pallas_call(pack_kernel, in_specs=[SCALAR, VECTOR] + [ANYWHERE] * len(...]
    pallas_call x1, Pallas kernels: 2.93 us -> 3.84 us  [up(): pl.pallas_call(functools.partial(up_kernel, members), in_specs=[ANYWHERE]...]
    ppermute x26 -> x23, waiting for transfers between devices: 30.4 us -> 29.5 us  [on_device(): permute = lambda value, pairs: lax.ppermute(value, 'pts', pairs)]
  transfers between devices with their start and end apart: 26 -> 23, of which waited for: 13 -> 11; matrix products, arithmetic and copies ran while one was open for 0% -> 0% of each run, Pallas kernels for 23% -> 24%
where the time goes in v4:
time: 79.5 us; the launch traced here: 79.3 us
  waiting for transfers between devices  29.5 us (37%)
  starting transfers between devices  26.2 us (33%)
  Pallas kernels  22.2 us (28%)
  local copies, waits for them, and re-layouts  1.01 us (1%)
    ppermute x23, waiting for transfers between devices, on_device(): permute = lambda value, pairs: lax.ppermute(value, 'pts', pairs)  29.5 us
    ppermute x23, starting transfers between devices, on_device(): permute = lambda value, pairs: lax.ppermute(value, 'pts', pairs)  26.2 us
    pallas_call x3, Pallas kernels, near(): pl.pallas_call(functools.partial(near_kernel, start), in_specs=[SCALAR] +...  8.08 us
    pallas_call x1, Pallas kernels, up(): pl.pallas_call(functools.partial(up_kernel, members), in_specs=[ANYWHERE]...  3.84 us
    pallas_call x1, Pallas kernels, last(): pl.pallas_call(functools.partial(last_kernel, start, width), in_specs=[SC...  3.36 us
    pallas_call x4, Pallas kernels, pack(): pl.pallas_call(pack_kernel, in_specs=[SCALAR, VECTOR] + [ANYWHERE] * len(...  2.39 us
    pallas_call x1, Pallas kernels, down(): pl.pallas_call(functools.partial(down_kernel, reach, members), in_specs=[...  1.85 us
  transfers between devices with their start and end apart: 23, of which 11 were waited for; matrix products, arithmetic and copies ran while one was open for 0% of the time, Pallas kernels for 24%

profile of v4, /device:TPU:0, one launch (start us, length us, event | category | flops | bytes accessed | tf_op | source)
XLA Modules:
  0.0 79.3 jit_solution(13606418693702956246)
XLA Ops:
  0.0 0.5 collective-permute-start.5
  0.5 0.0 slice-start
  0.5 3.8 %up.1 = (bf16[80,1024]{1,0:T(8,128)(2,1)}, s32[4,12]{1,0:T(4,128)}, bf16[1024,256]{1,0:T(8,128)(2,1)}, bf16[1024,256]{1,0:T(8,128)(2,1)}, bf16[1152,256]{1,0:T(8,128)(2,1)}, /*index=5*/bf16[1024,256]{1,0:T(8,128)(2,1)}) custom-call(bf16[4,64,256]{2,1,0:T(8,128)(2,1)} %refs_0_.1, bf16[4,64,64]{2,1,0:T(8,128)(2,1)} %leaf_ref.1, bf16[2,64,64]{2,1,0:T(8,128)(2,1)} %mid_ref.1, ...), custom_call_target="tpu_custom_call" | custom-call | flops 2300000000 | bytes 1048576 | tf_op jit(solution)/shard_map/up/pallas_call | solution.py:121
  4.3 2.6 %collective-permute-start.1 = (bf16[1024,256]{1,0:T(8,128)(2,1)}, bf16[1024,256]{1,0:T(8,128)(2,1)S(1)}, u32[]{:S(2)}, u32[]{:S(2)}) collective-permute-start(bf16[1024,256]{1,0:T(8,128)(2,1)} %get-tuple-element.48.rest_0_), channel_id=1, source_target_pairs={{0,2},{1,3},{2,0},{3,1},{4,6},{5,7},{6,4},{7,5},{8,10},{9,11},{10,... | collective-permute-start | bytes 1572872 | tf_op jit(solution)/shard_map/ppermute | solution.py:410
  6.9 3.6 %collective-permute-start.2 = (bf16[80,1024]{1,0:T(8,128)(2,1)}, bf16[80,1024]{1,0:T(8,128)(2,1)S(1)}, u32[]{:S(2)}, u32[]{:S(2)}) collective-permute-start(bf16[80,1024]{1,0:T(8,128)(2,1)} %get-tuple-element.50.panel_ref), channel_id=1, source_target_pairs={{0,12},{1,13},{2,14},{3,15},{4,0},{5,1},{6,2},{7,3},{8,4},{9,5},{1... | collective-permute-start | bytes 491528 | tf_op jit(solution)/shard_map/ppermute | solution.py:410
  10.5 0.0 collective-permute-start.3
  10.5 0.5 collective-permute-start.9
  11.0 4.4 %collective-permute-done.2.ahead_ref = bf16[80,1024]{1,0:T(8,128)(2,1)S(1)} collective-permute-done((bf16[80,1024]{1,0:T(8,128)(2,1)}, bf16[80,1024]{1,0:T(8,128)(2,1)S(1)}, u32[]{:S(2)}, u32[]{:S(2)}) %collective-permute-start.2) | collective-permute-done | bytes 163872 | tf_op jit(solution)/shard_map/ppermute | solution.py:410
  15.4 0.9 %collective-permute-start.4 = (bf16[80,1024]{1,0:T(8,128)(2,1)}, bf16[80,1024]{1,0:T(8,128)(2,1)S(1)}, u32[]{:S(2)}, u32[]{:S(2)}) collective-permute-start(bf16[80,1024]{1,0:T(8,128)(2,1)} %get-tuple-element.50.panel_ref), channel_id=1, source_target_pairs={{0,8},{1,9},{2,10},{3,11},{4,12},{5,13},{6,14},{7,15},{8,0},{9,1},... | collective-permute-start | bytes 491528 | tf_op jit(solution)/shard_map/ppermute | solution.py:410
  16.4 0.0 copy-done.6
  16.4 0.0 copy-done.8
  16.4 0.0 slice-start.1
  16.4 1.9 %down.1 = (bf16[1152,256]{1,0:T(8,128)(2,1)}, bf16[4,256,192]{2,1,0:T(8,128)(2,1)S(1)}, bf16[64,512]{1,0:T(8,128)(2,1)S(1)}) custom-call(s32[1,6]{1,0:T(1,128)S(1)} %copy-done.10, bf16[4,64,256]{2,1,0:T(8,128)(2,1)S(1)} %copy-done.6, bf16[4,64,64]{2,1,0:T(8,128)(2,1)S(1)} %copy-done.8, ...), custom_call_target="tpu_custom_call", output_to_operand_aliasing={{0}: (5, {})} | custom-call | flops 1150000000 | bytes 1048576 | tf_op jit(solution)/shard_map/down/pallas_call | solution.py:170
  18.3 0.8 %collective-permute-done.3.behind_ref = bf16[80,1024]{1,0:T(8,128)(2,1)S(1)} collective-permute-done((bf16[80,1024]{1,0:T(8,128)(2,1)}, bf16[80,1024]{1,0:T(8,128)(2,1)S(1)}, u32[]{:S(2)}, u32[]{:S(2)}) %collective-permute-start.3) | collective-permute-done | bytes 163872 | tf_op jit(solution)/shard_map/ppermute | solution.py:410
  19.1 0.8 %collective-permute-done.1.arrived_ref.rest_2_ = bf16[1024,256]{1,0:T(8,128)(2,1)S(1)} collective-permute-done((bf16[1024,256]{1,0:T(8,128)(2,1)}, bf16[1024,256]{1,0:T(8,128)(2,1)S(1)}, u32[]{:S(2)}, u32[]{:S(2)}) %collective-permute-start.1) | collective-permute-done | bytes 524320 | tf_op jit(solution)/shard_map/ppermute | solution.py:410
  19.9 0.0 collective-permute-done.5.rest_0_.rest_1_
  19.9 0.9 %copy-done = bf16[80,1024]{1,0:T(8,128)(2,1)S(1)} copy-done((bf16[80,1024]{1,0:T(8,128)(2,1)S(1)}, bf16[80,1024]{1,0:T(8,128)(2,1)}, u32[]{:S(2)}) %copy-start) | copy-done | bytes 163864
  20.9 0.1 collective-permute-start.6
  20.9 2.0 %collective-permute-start = (bf16[1152,256]{1,0:T(8,128)(2,1)}, bf16[1152,256]{1,0:T(8,128)(2,1)S(1)}, u32[]{:S(2)}, u32[]{:S(2)}) collective-permute-start(bf16[1152,256]{1,0:T(8,128)(2,1)} %get-tuple-element.47.rest_0_), channel_id=1, source_target_pairs={{0,2},{1,3},{2,0},{3,1},{4,6},{5,7},{6,4},{7,5},{8,10},{9,11},{10,... | collective-permute-start | bytes 1769480 | tf_op jit(solution)/shard_map/ppermute | solution.py:410
  22.9 0.0 collective-permute-done.6.core_asked_ref
  22.9 0.7 wishes.1.wish_ref
  23.7 2.3 %collective-permute-done.4.rest_0_ = bf16[80,1024]{1,0:T(8,128)(2,1)S(1)} collective-permute-done((bf16[80,1024]{1,0:T(8,128)(2,1)}, bf16[80,1024]{1,0:T(8,128)(2,1)S(1)}, u32[]{:S(2)}, u32[]{:S(2)}) %collective-permute-start.4) | collective-permute-done | bytes 163872 | tf_op jit(solution)/shard_map/ppermute | solution.py:410
  26.0 0.6 pack.4
  26.6 1.3 %collective-permute-start.7 = (bf16[512,256]{1,0:T(8,128)(2,1)S(1)}, bf16[512,256]{1,0:T(8,128)(2,1)S(1)}, u32[]{:S(2)}, u32[]{:S(2)}) collective-permute-start(bf16[512,256]{1,0:T(8,128)(2,1)S(1)} %get-tuple-element.55), channel_id=1, source_target_pairs={{1,4},{2,15},{5,8},{6,3},{9,12},{10,7},{13,0},{14,11},{17,20},{18,... | collective-permute-start | bytes 786440 | tf_op jit(solution)/shard_map/ppermute | solution.py:410
  27.9 0.9 %collective-permute-start.10 = (bf16[512,256]{1,0:T(8,128)(2,1)S(1)}, bf16[512,256]{1,0:T(8,128)(2,1)S(1)}, u32[]{:S(2)}, u32[]{:S(2)}) collective-permute-start(bf16[512,256]{1,0:T(8,128)(2,1)S(1)} %get-tuple-element.60), channel_id=1, source_target_pairs={{0,1},{1,0},{2,3},{3,2},{4,5},{5,4},{6,7},{7,6},{8,9},{9,8},{10,11... | collective-permute-start | bytes 786440 | tf_op jit(solution)/shard_map/ppermute | solution.py:410
  28.8 0.7 collective-permute-start.14
  29.7 8.3 %collective-permute-done.7.rest_5_ = bf16[512,256]{1,0:T(8,128)(2,1)S(1)} collective-permute-done((bf16[512,256]{1,0:T(8,128)(2,1)S(1)}, bf16[512,256]{1,0:T(8,128)(2,1)S(1)}, u32[]{:S(2)}, u32[]{:S(2)}) %collective-permute-start.7) | collective-permute-done | bytes 262176 | tf_op jit(solution)/shard_map/ppermute | solution.py:410
  38.0 0.0 collective-permute-start.8
  38.0 0.0 collective-permute-done.9.arrived_ref.rest_2_
  38.0 0.0 collective-permute-done.10.rest_0_.rest_3_
  38.0 0.6 pack.5
  38.6 1.2 %collective-permute-done.14.rest_4_ = bf16[512,256]{1,0:T(8,128)(2,1)S(1)} collective-permute-done((bf16[512,256]{1,0:T(8,128)(2,1)S(1)}, bf16[512,256]{1,0:T(8,128)(2,1)S(1)}, u32[]{:S(2)}, u32[]{:S(2)}) %collective-permute-start.14) | collective-permute-done | bytes 262176 | tf_op jit(solution)/shard_map/ppermute | solution.py:410
  39.8 1.7 %collective-permute-start.15 = (bf16[512,256]{1,0:T(8,128)(2,1)S(1)}, bf16[512,256]{1,0:T(8,128)(2,1)S(1)}, u32[]{:S(2)}, u32[]{:S(2)}) collective-permute-start(bf16[512,256]{1,0:T(8,128)(2,1)S(1)} %get-tuple-element.68), channel_id=1, source_target_pairs={{0,1},{1,0},{2,3},{3,2},{4,5},{5,4},{6,7},{7,6},{8,9},{9,8},{10,11... | collective-permute-start | bytes 786440 | tf_op jit(solution)/shard_map/ppermute | solution.py:410
  41.5 0.0 collective-permute-start.16
  41.5 3.1 %collective-permute-start.13 = (bf16[1024,256]{1,0:T(8,128)(2,1)S(1)}, bf16[1024,256]{1,0:T(8,128)(2,1)S(1)}, u32[]{:S(2)}, u32[]{:S(2)}) collective-permute-start(bf16[1024,256]{1,0:T(8,128)(2,1)S(1)} %copy-done.2), channel_id=1, source_target_pairs={{0,2},{1,3},{2,0},{3,1},{4,6},{5,7},{6,4},{7,5},{8,10},{9,11},{10,... | collective-permute-start | bytes 1572872 | tf_op jit(solution)/shard_map/ppermute | solution.py:410
  44.6 0.0 collective-permute-done.carrier_ref.arrived_ref.rest_2_
  44.6 1.3 %collective-permute-start.11 = (bf16[512,256]{1,0:T(8,128)(2,1)S(1)}, bf16[512,256]{1,0:T(8,128)(2,1)S(1)}, u32[]{:S(2)}, u32[]{:S(2)}) collective-permute-start(bf16[512,256]{1,0:T(8,128)(2,1)S(1)} %get-tuple-element.61), channel_id=1, source_target_pairs={{1,4},{2,15},{5,8},{6,3},{9,12},{10,7},{13,0},{14,11},{17,20},{18,... | collective-permute-start | bytes 786440 | tf_op jit(solution)/shard_map/ppermute | solution.py:410
  46.0 2.5 %near.3.rest_1_.rest_6_.rest_0_ = f32[1024,256]{1,0:T(8,128)S(1)} custom-call(s32[4,12]{1,0:T(4,128)S(1)} %copy-done.5, bf16[4,12,256,256]{3,2,1,0:T(8,128)(2,1)S(1)} %bitcast.3, bf16[1024,256]{1,0:T(8,128)(2,1)S(1)} %copy-done.4, bf16[1024,1024]{1,0:T(8,128)(2,1)S(1)} %collective-permute-done.5.rest_0_.rest_1_, ...), custom_call_target="tpu_custom_call" | custom-call | flops 460000000 | bytes 1048576 | tf_op jit(solution)/shard_map/near/pallas_call | solution.py:303
  48.5 0.0 collective-permute-done.15.rest_0_.rest_3_
  48.5 0.6 pack.6
  49.1 2.6 %collective-permute-done.16.rest_4_ = bf16[512,256]{1,0:T(8,128)(2,1)S(1)} collective-permute-done((bf16[512,256]{1,0:T(8,128)(2,1)S(1)}, bf16[512,256]{1,0:T(8,128)(2,1)S(1)}, u32[]{:S(2)}, u32[]{:S(2)}) %collective-permute-start.16) | collective-permute-done | bytes 262176 | tf_op jit(solution)/shard_map/ppermute | solution.py:410
  51.7 0.0 collective-permute-start.17
  51.7 1.0 %collective-permute-start.18 = (bf16[512,256]{1,0:T(8,128)(2,1)S(1)}, bf16[512,256]{1,0:T(8,128)(2,1)S(1)}, u32[]{:S(2)}, u32[]{:S(2)}) collective-permute-start(bf16[512,256]{1,0:T(8,128)(2,1)S(1)} %get-tuple-element.77), channel_id=1, source_target_pairs={{0,4},{1,5},{2,14},{3,15},{4,8},{5,9},{6,2},{7,3},{8,12},{9,13},{1... | collective-permute-start | bytes 786440 | tf_op jit(solution)/shard_map/ppermute | solution.py:410
  52.7 0.0 collective-permute-done.8.rest_1_
  52.7 1.3 %collective-permute-start.22 = (bf16[512,256]{1,0:T(8,128)(2,1)S(1)}, bf16[512,256]{1,0:T(8,128)(2,1)S(1)}, u32[]{:S(2)}, u32[]{:S(2)}) collective-permute-start(bf16[512,256]{1,0:T(8,128)(2,1)S(1)} %get-tuple-element.82), channel_id=1, source_target_pairs={{1,4},{2,15},{5,8},{6,3},{9,12},{10,7},{13,0},{14,11},{17,20},{18,... | collective-permute-start | bytes 786440 | tf_op jit(solution)/shard_map/ppermute | solution.py:410
  54.0 0.5 couple.1
  54.5 0.0 collective-permute-done.11.rest_5_
  54.5 3.3 %collective-permute-start.12 = (f32[64,1024]{1,0:T(8,128)S(1)}, f32[64,1024]{1,0:T(8,128)S(1)}, u32[]{:S(2)}, u32[]{:S(2)}) collective-permute-start(f32[64,1024]{1,0:T(8,128)S(1)} %get-tuple-element.62), channel_id=1, source_target_pairs={{0,2},{1,3},{2,0},{3,1},{4,6},{5,7},{6,4},{7,5},{8,10},{9,11},{10,... | collective-permute-start | bytes 786440 | tf_op jit(solution)/shard_map/ppermute | solution.py:410
  57.7 2.5 %near.4.rest_1_.rest_6_ = f32[1024,256]{1,0:T(8,128)S(1)} custom-call(s32[4,12]{1,0:T(4,128)S(1)} %copy-done.5, bf16[4,12,256,256]{3,2,1,0:T(8,128)(2,1)S(1)} %bitcast.3, bf16[1024,256]{1,0:T(8,128)(2,1)S(1)} %copy-done.3, bf16[1024,1024]{1,0:T(8,128)(2,1)S(1)} %collective-permute-done.5.rest_0_.rest_1_, ...), custom_call_target="tpu_custom_call" | custom-call | flops 460000000 | bytes 1048576 | tf_op jit(solution)/shard_map/near/pallas_call | solution.py:303
  60.3 0.0 collective-permute-done.17.rest_0_.rest_3_
  60.3 0.0 collective-permute-done.13.arrived_ref.rest_2_
  60.3 0.6 pack.7
  60.9 1.7 %collective-permute-done.18.rest_4_ = bf16[512,256]{1,0:T(8,128)(2,1)S(1)} collective-permute-done((bf16[512,256]{1,0:T(8,128)(2,1)S(1)}, bf16[512,256]{1,0:T(8,128)(2,1)S(1)}, u32[]{:S(2)}, u32[]{:S(2)}) %collective-permute-start.18) | collective-permute-done | bytes 262176 | tf_op jit(solution)/shard_map/ppermute | solution.py:410
  62.6 0.0 collective-permute-start.19
  62.6 0.2 collective-permute-start.20
  62.8 1.3 %collective-permute-start.21 = (bf16[512,256]{1,0:T(8,128)(2,1)S(1)}, bf16[512,256]{1,0:T(8,128)(2,1)S(1)}, u32[]{:S(2)}, u32[]{:S(2)}) collective-permute-start(bf16[512,256]{1,0:T(8,128)(2,1)S(1)} %get-tuple-element.80), channel_id=1, source_target_pairs={{1,4},{2,15},{5,8},{6,3},{9,12},{10,7},{13,0},{14,11},{17,20},{18,... | collective-permute-start | bytes 786440 | tf_op jit(solution)/shard_map/ppermute | solution.py:410
  64.1 1.0 %collective-permute-done.22.rest_5_ = bf16[512,256]{1,0:T(8,128)(2,1)S(1)} collective-permute-done((bf16[512,256]{1,0:T(8,128)(2,1)S(1)}, bf16[512,256]{1,0:T(8,128)(2,1)S(1)}, u32[]{:S(2)}, u32[]{:S(2)}) %collective-permute-start.22) | collective-permute-done | bytes 262176 | tf_op jit(solution)/shard_map/ppermute | solution.py:410
  65.0 3.0 %near.5.rest_2_ = f32[1024,256]{1,0:T(8,128)S(1)} custom-call(s32[4,12]{1,0:T(4,128)S(1)} %copy-done.5, bf16[4,12,256,256]{3,2,1,0:T(8,128)(2,1)S(1)} %bitcast.3, bf16[1152,256]{1,0:T(8,128)(2,1)} %get-tuple-element.47.rest_0_, bf16[1024,1024]{1,0:T(8,128)(2,1)S(1)} %collective-permute-done.5.rest_0_.rest_1_, ...), custom_call_target="tpu_custom_call" | custom-call | flops 460000000 | bytes 1048576 | tf_op jit(solution)/shard_map/near/pallas_call | solution.py:303
  68.1 0.0 collective-permute-done.12.partner_sum_ref
  68.1 1.5 %finish.1.rest_6_ = bf16[1024,1024]{1,0:T(8,128)(2,1)} custom-call(f32[64,1024]{1,0:T(8,128)S(1)} %get-tuple-element.57.own_sum_ref, f32[64,1024]{1,0:T(8,128)S(1)} %collective-permute-done.12.partner_sum_ref, bf16[4,256,192]{2,1,0:T(8,128)(2,1)S(1)} %get-tuple-element.53.rest_1_.down_ref, f32[1024,256]{1,0:T(8,128)S(1)} %near.3.rest_1_.rest_6_.rest_0_, ...), custom_call_target="tpu_custom_call" | custom-call | flops 460000000 | bytes 1048576 | tf_op jit(solution)/shard_map/finish/pallas_call | solution.py:377
  69.6 0.0 collective-permute-done.19.rest_3_
  69.6 3.9 %collective-permute-done.20.rest_4_ = bf16[512,256]{1,0:T(8,128)(2,1)S(1)} collective-permute-done((bf16[512,256]{1,0:T(8,128)(2,1)S(1)}, bf16[512,256]{1,0:T(8,128)(2,1)S(1)}, u32[]{:S(2)}, u32[]{:S(2)}) %collective-permute-start.20) | collective-permute-done | bytes 262176 | tf_op jit(solution)/shard_map/ppermute | solution.py:410
  73.5 2.4 %collective-permute-done.21.rest_5_ = bf16[512,256]{1,0:T(8,128)(2,1)S(1)} collective-permute-done((bf16[512,256]{1,0:T(8,128)(2,1)S(1)}, bf16[512,256]{1,0:T(8,128)(2,1)S(1)}, u32[]{:S(2)}, u32[]{:S(2)}) %collective-permute-start.21) | collective-permute-done | bytes 262176 | tf_op jit(solution)/shard_map/ppermute | solution.py:410
  75.9 3.4 %last.1 = bf16[1024,1024]{1,0:T(8,128)(2,1)} custom-call(s32[4,12]{1,0:T(4,128)S(1)} %copy-done.5, bf16[4,12,256,256]{3,2,1,0:T(8,128)(2,1)S(1)} %bitcast.3, f32[64,1024]{1,0:T(8,128)S(1)} %get-tuple-element.57.own_sum_ref, f32[64,1024]{1,0:T(8,128)S(1)} %collective-permute-done.12.partner_sum_ref, ...), custom_call_target="tpu_custom_call", output_to_operand_aliasing={{}: (11, {})} | custom-call | flops 1150000000 | bytes 1048576 | tf_op jit(solution)/shard_map/last/pallas_call | solution.py:336
  (28 shorter events, 0.1 us)
Async XLA Ops:
  0.0 19.9 %collective-permute-start.5 = (bf16[1024,1024]{1,0:T(8,128)(2,1)}, bf16[1024,1024]{1,0:T(8,128)(2,1)S(1)}, u32[]{:S(2)}, u32[]{:S(2)}) collective-permute-start(bf16[1024,1024]{1,0:T(8,128)(2,1)} %refs_5_.1), channel_id=1, source_target_pairs={{0,1},{1,0},{2,3},{3,2},{4,5},{5,4},{6,7},{7,6},{8,9},{9,8},{10,11... | collective-permute-start | bytes 6291464 | tf_op jit(solution)/shard_map/ppermute | solution.py:410
  0.5 15.9 %copy-start.6 = (bf16[4,64,256]{2,1,0:T(8,128)(2,1)S(1)}, bf16[4,64,256]{2,1,0:T(8,128)(2,1)}, u32[]{:S(2)}) copy-start(bf16[4,64,256]{2,1,0:T(8,128)(2,1)} %target_ref.1) | copy-start | bytes 393220
  0.5 15.9 %copy-start.7 = (bf16[1,6,64,64]{3,2,1,0:T(8,128)(2,1)S(1)}, bf16[1,6,64,64]{3,2,1,0:T(8,128)(2,1)}, u32[]{:S(2)}) copy-start(bf16[1,6,64,64]{3,2,1,0:T(8,128)(2,1)} %param.18) | copy-start | bytes 147460
  0.5 15.9 %copy-start.8 = (bf16[4,64,64]{2,1,0:T(8,128)(2,1)S(1)}, bf16[4,64,64]{2,1,0:T(8,128)(2,1)}, u32[]{:S(2)}) copy-start(bf16[4,64,64]{2,1,0:T(8,128)(2,1)} %leaf_ref.1) | copy-start | bytes 98308
  0.5 15.9 %copy-start.9 = (bf16[2,64,64]{2,1,0:T(8,128)(2,1)S(1)}, bf16[2,64,64]{2,1,0:T(8,128)(2,1)}, u32[]{:S(2)}) copy-start(bf16[2,64,64]{2,1,0:T(8,128)(2,1)} %mid_ref.1) | copy-start | bytes 49156
  0.5 15.9 %copy-start.10 = (s32[1,6]{1,0:T(1,128)S(1)}, s32[1,6]{1,0:T(1,128)}, u32[]{:S(2)}) copy-start(s32[1,6]{1,0:T(1,128)} %far_ref.1) | copy-start | bytes 76
  0.5 45.4 %slice-start = ((s8[6291456]{0:T(1024)(128)(4,1)}), s8[2097152]{0:T(1024)(128)(4,1)S(1)}, s32[]{:S(2)}) async-start(s8[6291456]{0:T(1024)(128)(4,1)} %bitcast.2), calls=%async_computation | async-start | bytes 4194304
  4.3 15.6 %collective-permute-start.1 = (bf16[1024,256]{1,0:T(8,128)(2,1)}, bf16[1024,256]{1,0:T(8,128)(2,1)S(1)}, u32[]{:S(2)}, u32[]{:S(2)}) collective-permute-start(bf16[1024,256]{1,0:T(8,128)(2,1)} %get-tuple-element.48.rest_0_), channel_id=1, source_target_pairs={{0,2},{1,3},{2,0},{3,1},{4,6},{5,7},{6,4},{7,5},{8,10},{9,11},{10,... | collective-permute-start | bytes 1572872 | tf_op jit(solution)/shard_map/ppermute | solution.py:410
  6.9 8.5 %collective-permute-start.2 = (bf16[80,1024]{1,0:T(8,128)(2,1)}, bf16[80,1024]{1,0:T(8,128)(2,1)S(1)}, u32[]{:S(2)}, u32[]{:S(2)}) collective-permute-start(bf16[80,1024]{1,0:T(8,128)(2,1)} %get-tuple-element.50.panel_ref), channel_id=1, source_target_pairs={{0,12},{1,13},{2,14},{3,15},{4,0},{5,1},{6,2},{7,3},{8,4},{9,5},{1... | collective-permute-start | bytes 491528 | tf_op jit(solution)/shard_map/ppermute | solution.py:410
  10.5 8.6 %collective-permute-start.3 = (bf16[80,1024]{1,0:T(8,128)(2,1)}, bf16[80,1024]{1,0:T(8,128)(2,1)S(1)}, u32[]{:S(2)}, u32[]{:S(2)}) collective-permute-start(bf16[80,1024]{1,0:T(8,128)(2,1)} %get-tuple-element.50.panel_ref), channel_id=1, source_target_pairs={{0,4},{1,5},{2,6},{3,7},{4,8},{5,9},{6,10},{7,11},{8,12},{9,13},{1... | collective-permute-start | bytes 491528 | tf_op jit(solution)/shard_map/ppermute | solution.py:410
  10.5 27.5 %collective-permute-start.9 = (bf16[1024,256]{1,0:T(8,128)(2,1)}, bf16[1024,256]{1,0:T(8,128)(2,1)S(1)}, u32[]{:S(2)}, u32[]{:S(2)}) collective-permute-start(bf16[1024,256]{1,0:T(8,128)(2,1)} %get-tuple-element.59.rest_0_), channel_id=1, source_target_pairs={{0,2},{1,3},{2,0},{3,1},{4,6},{5,7},{6,4},{7,5},{8,10},{9,11},{10,... | collective-permute-start | bytes 1572872 | tf_op jit(solution)/shard_map/ppermute | solution.py:410
  15.4 10.6 %collective-permute-start.4 = (bf16[80,1024]{1,0:T(8,128)(2,1)}, bf16[80,1024]{1,0:T(8,128)(2,1)S(1)}, u32[]{:S(2)}, u32[]{:S(2)}) collective-permute-start(bf16[80,1024]{1,0:T(8,128)(2,1)} %get-tuple-element.50.panel_ref), channel_id=1, source_target_pairs={{0,8},{1,9},{2,10},{3,11},{4,12},{5,13},{6,14},{7,15},{8,0},{9,1},... | collective-permute-start | bytes 491528 | tf_op jit(solution)/shard_map/ppermute | solution.py:410
  16.4 29.5 %slice-start.1 = ((s8[6291456]{0:T(1024)(128)(4,1)}), s8[4194304]{0:T(1024)(128)(4,1)S(1)}, s32[]{:S(2)}) async-start(s8[6291456]{0:T(1024)(128)(4,1)} %bitcast.2), calls=%async_computation.1 | async-start | bytes 8388608
  19.9 0.9 %copy-start = (bf16[80,1024]{1,0:T(8,128)(2,1)S(1)}, bf16[80,1024]{1,0:T(8,128)(2,1)}, u32[]{:S(2)}) copy-start(bf16[80,1024]{1,0:T(8,128)(2,1)} %get-tuple-element.50.panel_ref) | copy-start | bytes 491524
  20.8 8.8 %copy-start.1 = (bf16[80,1024]{1,0:T(8,128)(2,1)S(1)}, bf16[80,1024]{1,0:T(8,128)(2,1)}, u32[]{:S(2)}) copy-start(bf16[80,1024]{1,0:T(8,128)(2,1)} %get-tuple-element.50.panel_ref) | copy-start | bytes 491524
  20.8 20.7 %copy-start.2 = (bf16[1024,256]{1,0:T(8,128)(2,1)S(1)}, bf16[1024,256]{1,0:T(8,128)(2,1)}, u32[]{:S(2)}) copy-start(bf16[1024,256]{1,0:T(8,128)(2,1)} %get-tuple-element.65.rest_0_) | copy-start | bytes 1572868
  20.8 25.1 %copy-start.4 = (bf16[1024,256]{1,0:T(8,128)(2,1)S(1)}, bf16[1024,256]{1,0:T(8,128)(2,1)}, u32[]{:S(2)}) copy-start(bf16[1024,256]{1,0:T(8,128)(2,1)} %get-tuple-element.48.rest_0_) | copy-start | bytes 1572868
  20.8 25.1 %copy-start.5 = (s32[4,12]{1,0:T(4,128)S(1)}, s32[4,12]{1,0:T(4,128)}, u32[]{:S(2)}) copy-start(s32[4,12]{1,0:T(4,128)} %get-tuple-element.44.entry_ref) | copy-start | bytes 580
  20.9 2.1 %collective-permute-start.6 = (bf16[32,768]{1,0:T(8,128)(2,1)S(1)}, bf16[32,768]{1,0:T(8,128)(2,1)S(1)}, u32[]{:S(2)}, u32[]{:S(2)}) collective-permute-start(bf16[32,768]{1,0:T(8,128)(2,1)S(1)} %ask.1.asked_ref), channel_id=1, source_target_pairs={{0,1},{1,0},{2,3},{3,2},{4,5},{5,4},{6,7},{7,6},{8,9},{9,8},{10,11... | collective-permute-start | bytes 147464 | tf_op jit(solution)/shard_map/ppermute | solution.py:410
  20.9 23.7 %collective-permute-start = (bf16[1152,256]{1,0:T(8,128)(2,1)}, bf16[1152,256]{1,0:T(8,128)(2,1)S(1)}, u32[]{:S(2)}, u32[]{:S(2)}) collective-permute-start(bf16[1152,256]{1,0:T(8,128)(2,1)} %get-tuple-element.47.rest_0_), channel_id=1, source_target_pairs={{0,2},{1,3},{2,0},{3,1},{4,6},{5,7},{6,4},{7,5},{8,10},{9,11},{10,... | collective-permute-start | bytes 1769480 | tf_op jit(solution)/shard_map/ppermute | solution.py:410
  26.6 11.4 %collective-permute-start.7 = (bf16[512,256]{1,0:T(8,128)(2,1)S(1)}, bf16[512,256]{1,0:T(8,128)(2,1)S(1)}, u32[]{:S(2)}, u32[]{:S(2)}) collective-permute-start(bf16[512,256]{1,0:T(8,128)(2,1)S(1)} %get-tuple-element.55), channel_id=1, source_target_pairs={{1,4},{2,15},{5,8},{6,3},{9,12},{10,7},{13,0},{14,11},{17,20},{18,... | collective-permute-start | bytes 786440 | tf_op jit(solution)/shard_map/ppermute | solution.py:410
  27.9 10.1 %collective-permute-start.10 = (bf16[512,256]{1,0:T(8,128)(2,1)S(1)}, bf16[512,256]{1,0:T(8,128)(2,1)S(1)}, u32[]{:S(2)}, u32[]{:S(2)}) collective-permute-start(bf16[512,256]{1,0:T(8,128)(2,1)S(1)} %get-tuple-element.60), channel_id=1, source_target_pairs={{0,1},{1,0},{2,3},{3,2},{4,5},{5,4},{6,7},{7,6},{8,9},{9,8},{10,11... | collective-permute-start | bytes 786440 | tf_op jit(solution)/shard_map/ppermute | solution.py:410
  28.8 11.0 %collective-permute-start.14 = (bf16[512,256]{1,0:T(8,128)(2,1)S(1)}, bf16[512,256]{1,0:T(8,128)(2,1)S(1)}, u32[]{:S(2)}, u32[]{:S(2)}) collective-permute-start(bf16[512,256]{1,0:T(8,128)(2,1)S(1)} %get-tuple-element.67), channel_id=1, source_target_pairs={{0,4},{1,5},{2,14},{3,15},{4,8},{5,9},{6,2},{7,3},{8,12},{9,13},{1... | collective-permute-start | bytes 786440 | tf_op jit(solution)/shard_map/ppermute | solution.py:410
  38.0 14.7 %collective-permute-start.8 = (bf16[256,1024]{1,0:T(8,128)(2,1)S(1)}, bf16[256,1024]{1,0:T(8,128)(2,1)S(1)}, u32[]{:S(2)}, u32[]{:S(2)}) collective-permute-start(bf16[256,1024]{1,0:T(8,128)(2,1)S(1)} %pad_maximum_fusion.rest_0_), channel_id=1, source_target_pairs={{0,1},{1,0},{2,3},{3,2},{4,5},{5,4},{6,7},{7,6},{8,9},{9,8},{10,11... | collective-permute-start | bytes 1572872 | tf_op jit(solution)/shard_map/ppermute | solution.py:410
  39.8 8.7 %collective-permute-start.15 = (bf16[512,256]{1,0:T(8,128)(2,1)S(1)}, bf16[512,256]{1,0:T(8,128)(2,1)S(1)}, u32[]{:S(2)}, u32[]{:S(2)}) collective-permute-start(bf16[512,256]{1,0:T(8,128)(2,1)S(1)} %get-tuple-element.68), channel_id=1, source_target_pairs={{0,1},{1,0},{2,3},{3,2},{4,5},{5,4},{6,7},{7,6},{8,9},{9,8},{10,11... | collective-permute-start | bytes 786440 | tf_op jit(solution)/shard_map/ppermute | solution.py:410
  41.5 10.2 %collective-permute-start.16 = (bf16[512,256]{1,0:T(8,128)(2,1)S(1)}, bf16[512,256]{1,0:T(8,128)(2,1)S(1)}, u32[]{:S(2)}, u32[]{:S(2)}) collective-permute-start(bf16[512,256]{1,0:T(8,128)(2,1)S(1)} %get-tuple-element.72), channel_id=1, source_target_pairs={{0,4},{1,5},{2,14},{3,15},{4,8},{5,9},{6,2},{7,3},{8,12},{9,13},{1... | collective-permute-start | bytes 786440 | tf_op jit(solution)/shard_map/ppermute | solution.py:410
  41.5 18.7 %collective-permute-start.13 = (bf16[1024,256]{1,0:T(8,128)(2,1)S(1)}, bf16[1024,256]{1,0:T(8,128)(2,1)S(1)}, u32[]{:S(2)}, u32[]{:S(2)}) collective-permute-start(bf16[1024,256]{1,0:T(8,128)(2,1)S(1)} %copy-done.2), channel_id=1, source_target_pairs={{0,2},{1,3},{2,0},{3,1},{4,6},{5,7},{6,4},{7,5},{8,10},{9,11},{10,... | collective-permute-start | bytes 1572872 | tf_op jit(solution)/shard_map/ppermute | solution.py:410
  44.6 9.8 %collective-permute-start.11 = (bf16[512,256]{1,0:T(8,128)(2,1)S(1)}, bf16[512,256]{1,0:T(8,128)(2,1)S(1)}, u32[]{:S(2)}, u32[]{:S(2)}) collective-permute-start(bf16[512,256]{1,0:T(8,128)(2,1)S(1)} %get-tuple-element.61), channel_id=1, source_target_pairs={{1,4},{2,15},{5,8},{6,3},{9,12},{10,7},{13,0},{14,11},{17,20},{18,... | collective-permute-start | bytes 786440 | tf_op jit(solution)/shard_map/ppermute | solution.py:410
  48.5 9.2 %copy-start.3 = (bf16[1024,256]{1,0:T(8,128)(2,1)S(1)}, bf16[1024,256]{1,0:T(8,128)(2,1)}, u32[]{:S(2)}) copy-start(bf16[1024,256]{1,0:T(8,128)(2,1)} %get-tuple-element.59.rest_0_) | copy-start | bytes 1572868
  51.7 8.6 %collective-permute-start.17 = (bf16[512,256]{1,0:T(8,128)(2,1)S(1)}, bf16[512,256]{1,0:T(8,128)(2,1)S(1)}, u32[]{:S(2)}, u32[]{:S(2)}) collective-permute-start(bf16[512,256]{1,0:T(8,128)(2,1)S(1)} %get-tuple-element.73), channel_id=1, source_target_pairs={{0,1},{1,0},{2,3},{3,2},{4,5},{5,4},{6,7},{7,6},{8,9},{9,8},{10,11... | collective-permute-start | bytes 786440 | tf_op jit(solution)/shard_map/ppermute | solution.py:410
  51.7 10.9 %collective-permute-start.18 = (bf16[512,256]{1,0:T(8,128)(2,1)S(1)}, bf16[512,256]{1,0:T(8,128)(2,1)S(1)}, u32[]{:S(2)}, u32[]{:S(2)}) collective-permute-start(bf16[512,256]{1,0:T(8,128)(2,1)S(1)} %get-tuple-element.77), channel_id=1, source_target_pairs={{0,4},{1,5},{2,14},{3,15},{4,8},{5,9},{6,2},{7,3},{8,12},{9,13},{1... | collective-permute-start | bytes 786440 | tf_op jit(solution)/shard_map/ppermute | solution.py:410
  52.7 12.3 %collective-permute-start.22 = (bf16[512,256]{1,0:T(8,128)(2,1)S(1)}, bf16[512,256]{1,0:T(8,128)(2,1)S(1)}, u32[]{:S(2)}, u32[]{:S(2)}) collective-permute-start(bf16[512,256]{1,0:T(8,128)(2,1)S(1)} %get-tuple-element.82), channel_id=1, source_target_pairs={{1,4},{2,15},{5,8},{6,3},{9,12},{10,7},{13,0},{14,11},{17,20},{18,... | collective-permute-start | bytes 786440 | tf_op jit(solution)/shard_map/ppermute | solution.py:410
  54.5 13.6 %collective-permute-start.12 = (f32[64,1024]{1,0:T(8,128)S(1)}, f32[64,1024]{1,0:T(8,128)S(1)}, u32[]{:S(2)}, u32[]{:S(2)}) collective-permute-start(f32[64,1024]{1,0:T(8,128)S(1)} %get-tuple-element.62), channel_id=1, source_target_pairs={{0,2},{1,3},{2,0},{3,1},{4,6},{5,7},{6,4},{7,5},{8,10},{9,11},{10,... | collective-permute-start | bytes 786440 | tf_op jit(solution)/shard_map/ppermute | solution.py:410
  62.6 7.0 %collective-permute-start.19 = (bf16[512,256]{1,0:T(8,128)(2,1)S(1)}, bf16[512,256]{1,0:T(8,128)(2,1)S(1)}, u32[]{:S(2)}, u32[]{:S(2)}) collective-permute-start(bf16[512,256]{1,0:T(8,128)(2,1)S(1)} %get-tuple-element.78), channel_id=1, source_target_pairs={{0,1},{1,0},{2,3},{3,2},{4,5},{5,4},{6,7},{7,6},{8,9},{9,8},{10,11... | collective-permute-start | bytes 786440 | tf_op jit(solution)/shard_map/ppermute | solution.py:410
  62.6 10.9 %collective-permute-start.20 = (bf16[512,256]{1,0:T(8,128)(2,1)S(1)}, bf16[512,256]{1,0:T(8,128)(2,1)S(1)}, u32[]{:S(2)}, u32[]{:S(2)}) collective-permute-start(bf16[512,256]{1,0:T(8,128)(2,1)S(1)} %get-tuple-element.79), channel_id=1, source_target_pairs={{0,4},{1,5},{2,14},{3,15},{4,8},{5,9},{6,2},{7,3},{8,12},{9,13},{1... | collective-permute-start | bytes 786440 | tf_op jit(solution)/shard_map/ppermute | solution.py:410
  62.8 13.2 %collective-permute-start.21 = (bf16[512,256]{1,0:T(8,128)(2,1)S(1)}, bf16[512,256]{1,0:T(8,128)(2,1)S(1)}, u32[]{:S(2)}, u32[]{:S(2)}) collective-permute-start(bf16[512,256]{1,0:T(8,128)(2,1)S(1)} %get-tuple-element.80), channel_id=1, source_target_pairs={{1,4},{2,15},{5,8},{6,3},{9,12},{10,7},{13,0},{14,11},{17,20},{18,... | collective-permute-start | bytes 786440 | tf_op jit(solution)/shard_map/ppermute | solution.py:410

commit v5 on v4

--- a/solution.py
+++ b/solution.py
@@ -27,6 +27,9 @@
 STEP = 0.4
 UP_LIMIT = 58
 BYTES = 1
+XJOIN = 3
+ZJ = 1.5
+XC0 = 0
 ANYWHERE = pl.BlockSpec(memory_space=pl.ANY)
 VECTOR = pl.BlockSpec(memory_space=pltpu.VMEM)
 SCALAR = pl.BlockSpec(memory_space=pltpu.SMEM)
@@ -85,11 +88,15 @@
 
 
 def up_kernel(members, *refs):
-    given, rest = refs[:6], refs[6:]
-    panel_ref, entry_ref, *parts = rest[: 2 + len(SLABS)]
-    *kept, sems = rest[2 + len(SLABS) :]
+    given, rest = refs[:7], refs[7:]
+    panel_ref, entry_ref, *parts = rest[: 1 + len(SLABS)]
+    *kept, first_ref, sems = rest[1 + len(SLABS) :]
     pairs = list(zip(given[:5], kept))
-    pairs += [(given[5].at[:, pl.ds(start, width)], part.at[pl.ds(0, ROWS)]) for (start, width), part in zip(SLABS, parts)]
+    pairs += [
+        (given[5].at[:, pl.ds(start, width)], part.at[pl.ds(0, ROWS)])
+        for (start, width), part in zip(SLABS[1:], parts)
+    ]
+    pairs.append((given[6], first_ref))
     copies = [pltpu.make_async_copy(a, b, sems.at[i]) for i, (a, b) in enumerate(pairs)]
     for copy in copies:
         copy.start()
@@ -108,14 +115,14 @@
     ups = [dot_split(dot(mid_ref[box // 2], leaf_ref[box]), source_ref[box]) for box in range(B_DEV)]
     high, low = split(jnp.concatenate(ups, axis=1))
     both = jnp.concatenate([high, low], axis=0)
-    for copy, (start, width), part in zip(copies[5:], SLABS, parts):
+    for copy, (start, width), part in zip(copies[5:], SLABS[1:] + SLABS[:1], [*parts, first_ref]):
         copy.wait()
         sums = dot(both, part[pl.ds(0, ROWS)])
         panel_ref[pl.ds(0, RANK), pl.ds(start, width)] = (sums[:RANK] + sums[RANK:]).astype(jnp.bfloat16)
 
 
 def up(members, carried, *given):
-    columns = given[-1].shape[1]
+    columns = given[5].shape[1]
     shapes = [(ROWS, width) for _, width in SLABS]
     shapes[CARRIER] = (ROWS + RANK * -(-carried // shapes[CARRIER][1]), shapes[CARRIER][1])
     return pl.pallas_call(
@@ -124,9 +131,9 @@
         out_shape=(
             jax.ShapeDtypeStruct((RANK + WISH, columns), jnp.bfloat16),
             jax.ShapeDtypeStruct((B_DEV, NEAR), jnp.int32),
-            *[jax.ShapeDtypeStruct(shape, jnp.bfloat16) for shape in shapes],
+            *[jax.ShapeDtypeStruct(shape, jnp.bfloat16) for shape in shapes[1:]],
         ),
-        scratch_shapes=[pltpu.VMEM(a.shape, a.dtype) for a in given[:5]]
+        scratch_shapes=[pltpu.VMEM(a.shape, a.dtype) for a in (*given[:5], given[6])]
         + [pltpu.SemaphoreType.DMA((5 + len(SLABS),))],
         compiler_params=pltpu.CompilerParams(vmem_limit_bytes=UP_LIMIT * MIB),
         cost_estimate=cost(2),
@@ -169,7 +176,7 @@
 def down(reach, members, far_ids, target_basis, leaf_transfer, mid_transfer, coupling, part, *before):
     return pl.pallas_call(
         functools.partial(down_kernel, reach, members),
-        in_specs=[SCALAR] + [VECTOR] * 4 + [ANYWHERE] * (1 + len(before)),
+        in_specs=[SCALAR] + [VECTOR] * 4 + [ANYWHERE] + [VECTOR] * len(before),
         out_specs=(ANYWHERE, VECTOR, VECTOR),
         out_shape=(
             jax.ShapeDtypeStruct(part.shape, part.dtype),
@@ -226,24 +233,42 @@
     )(asked, core_asked)
 
 
-def couple_kernel(own_ref, carrier_ref, *rest):
-    tables, (own_sum_ref, partner_sum_ref) = rest[:-2], rest[-2:]
+def join_kernel(*refs):
+    refs[-1][...] = jnp.zeros_like(refs[-1])
+
+
+def join(microseconds, *values):
+    return pl.pallas_call(
+        join_kernel,
+        in_specs=[ANYWHERE] * len(values),
+        out_shape=jax.ShapeDtypeStruct((8, 128), jnp.float32),
+        compiler_params=pltpu.CompilerParams(vmem_limit_bytes=MIB),
+        cost_estimate=cost(microseconds),
+        name="join",
+    )(*values)
+
+
+def couple_kernel(own_ref, carrier_ref, core_ref, *rest):
+    panels, (own_sum_ref, partner_sum_ref) = rest[:-2], rest[-2:]
     depth = own_ref.shape[1]
-    table = jnp.concatenate([ref[...] for ref in tables], axis=0)
+    lines = [core_ref[pl.ds(row, depth // 2)] for row in range(2 * LEAF, core_ref.shape[0], depth // 2)]
+    table = [ref[pl.ds(0, RANK)] for ref in panels] + [jnp.concatenate(lines, axis=1)]
+    table = jnp.concatenate(table, axis=0)
     lines = [carrier_ref[pl.ds(row, RANK)] for row in range(ROWS, carrier_ref.shape[0], RANK)]
-    partner_sum_ref[...] = dot(jnp.concatenate(lines, axis=1)[:, :depth], table)
+    partner_sum = dot(jnp.concatenate(lines, axis=1)[:, :depth], table)
+    partner_sum_ref[...] = partner_sum.astype(jnp.bfloat16)
     own_sum_ref[...] = dot(own_ref[...], table)
 
 
-def couple(own, carrier, *tables):
-    shape = jax.ShapeDtypeStruct((RANK, tables[0].shape[1]), jnp.float32)
+def couple(own, carrier, core, *panels):
+    shape = (RANK, panels[0].shape[1])
     return pl.pallas_call(
         couple_kernel,
-        out_shape=(shape, shape),
+        out_shape=(jax.ShapeDtypeStruct(shape, jnp.float32), jax.ShapeDtypeStruct(shape, jnp.bfloat16)),
         compiler_params=pltpu.CompilerParams(vmem_limit_bytes=16 * MIB),
         cost_estimate=cost(0.1),
         name="couple",
-    )(own, carrier, *tables)
+    )(own, carrier, core, *panels)
 
 
 def pick(wish_ref, at, arrived_ref, picked_ref):
@@ -252,21 +277,28 @@
         picked_ref[pl.ds(k * LEAF, LEAF)] = arrived_ref[rows]
 
 
-def pack_kernel(wish_ref, arrived_ref, *rest):
+def pack_kernel(panels, wish_ref, arrived_ref, *rest):
     for at, picked_ref in enumerate(rest[-3:]):
         pick(wish_ref, 2 * at, arrived_ref, picked_ref)
-
-
-def pack(wish, arrived, before):
-    shape = jax.ShapeDtypeStruct((2 * LEAF, arrived.shape[1]), arrived.dtype)
-    return pl.pallas_call(
-        pack_kernel,
-        in_specs=[SCALAR, VECTOR] + [ANYWHERE] * len(before),
-        out_shape=(shape,) * 3,
+    to = 2 * LEAF
+    for at in range(0, rest[0].shape[1] if panels else 0, arrived_ref.shape[1]):
+        for ref in rest[:panels]:
+            rest[-1][pl.ds(to, RANK)] = ref[pl.ds(0, RANK), pl.ds(at, arrived_ref.shape[1])]
+            to += RANK
+
+
+def pack(wish, arrived, panels, before):
+    width = arrived.shape[1]
+    shape = jax.ShapeDtypeStruct((2 * LEAF, width), arrived.dtype)
+    further = sum(RANK * panel.shape[1] // width for panel in panels)
+    return pl.pallas_call(
+        functools.partial(pack_kernel, len(panels)),
+        in_specs=[SCALAR] + [VECTOR] * (1 + len(panels)) + [ANYWHERE] * len(before),
+        out_shape=(shape, shape, jax.ShapeDtypeStruct((2 * LEAF + further, width), arrived.dtype)),
         compiler_params=pltpu.CompilerParams(vmem_limit_bytes=8 * MIB),
         cost_estimate=cost(0.02),
         name="pack",
-    )(wish, arrived, *before)
+    )(wish, arrived, *panels, *before)
 
 
 def gather(start, width, held, pieces):
@@ -275,7 +307,7 @@
         (OWN, B_DEV, own_ref[pl.ds(0, ROWS)]),
         (CORE, B_DEV, core_ref[:, pl.ds(start, width)]),
         (ACROSS, B_DEV, across_ref[pl.ds(0, ROWS)]),
-        (ACROSS_CORE, 2, across_core_ref[...]),
+        (ACROSS_CORE, 2, across_core_ref[pl.ds(0, 2 * LEAF)]),
         (ALONG, 2, along_ref[...]),
         (ALONG_CORE, 2, along_core_ref[...]),
     ):
@@ -313,10 +345,10 @@
 
 
 def last_kernel(start, width, entry_ref, near_ref, own_sum_ref, partner_sum_ref, down_ref, *rest):
-    pieces, (_, out_ref, held, made, sems) = rest[:-5], rest[-5:]
+    pieces, (out_ref, held, made, sems) = rest[:6], rest[-4:]
     gather(start, width, held, pieces)
     taken = pl.ds(start, width)
-    high, low = split(own_sum_ref[:, taken] + partner_sum_ref[:, taken])
+    high, low = split(own_sum_ref[:, taken] + partner_sum_ref[:, taken].astype(jnp.float32))
     coupled = jnp.concatenate([high, high, low], axis=0)
     copies = []
     for box in range(B_DEV):
@@ -331,11 +363,11 @@
         copy.wait()
 
 
-def last(start, width, entry, near_blocks, sums, down_basis, pieces, product):
-    given = [entry, near_blocks, *sums, down_basis, *pieces, product]
+def last(start, width, entry, near_blocks, sums, down_basis, pieces, mark, product):
+    given = [entry, near_blocks, *sums, down_basis, *pieces, mark, product]
     return pl.pallas_call(
         functools.partial(last_kernel, start, width),
-        in_specs=[SCALAR] + [VECTOR] * (len(given) - 2) + [ANYWHERE],
+        in_specs=[SCALAR] + [VECTOR] * (len(given) - 3) + [ANYWHERE] * 2,
         out_specs=ANYWHERE,
         scratch_shapes=[
             pltpu.VMEM((HELD * LEAF, width), jnp.bfloat16),
@@ -355,7 +387,7 @@
     out_ref, made, sems = rest[-3:]
     start, stop = slabs[0][0], slabs[-1][0] + slabs[-1][1]
     taken = pl.ds(start, stop - start)
-    high, low = split(own_sum_ref[:, taken] + partner_sum_ref[:, taken])
+    high, low = split(own_sum_ref[:, taken] + partner_sum_ref[:, taken].astype(jnp.float32))
     coupled = jnp.concatenate([high, high, low], axis=0)
     copies = []
     for box in range(B_DEV):
@@ -413,6 +445,7 @@
     reach = list(dict.fromkeys(step % quads for step in (0, 1, -1, 2, -2)))
 
     rhs_core = permute(rhs, core_pairs)
+    first = rhs[:, : SLABS[0][1]]
     panel, entry, *parts = up(
         members,
         2 * len(reach) * RANK,
@@ -422,9 +455,11 @@
         near_ids,
         near_count.reshape(1, B_DEV),
         rhs,
+        first,
     )
+    parts = [first, *parts]
     parts[CARRIER], down_basis, placed = down(
-        reach, members, far_ids, target_basis, leaf_transfer, mid_transfer, far_coupling[0], parts[CARRIER]
+        reach, members, far_ids, target_basis, leaf_transfer, mid_transfer, far_coupling[0], parts[CARRIER], panel
     )
     across = [permute(part, across_pairs) for part in parts[:3]]
     others = [permute(panel, [(i, (i - 4 * step) % members) for i in every]) for step in reach[1:]]
@@ -439,26 +474,24 @@
 
     for k in range(len(SLABS)):
         if k >= 2:
-            nears.append(near(*SLABS[k - 2], entry, near_blocks, pieces(k - 2), nears[-1:]))
-        picks = list(pack(wish, across[k], across_core[-1:] + nears[-1:] if k else others[2:]))
+            nears.append(near(*SLABS[k - 2], entry, near_blocks, pieces(k - 2), nears[-1:] + [join(ZJ, *along[k - 2])]))
+        panels = [panel, *others] if k == 0 else []
+        before = nears[-1:] + (across_core[:1] if k == 1 and XC0 else [])
+        if k == 1 and XJOIN:
+            before.append(join(XJOIN, across[1]))
+        picks = list(pack(wish, across[k], panels, before))
         along.append([permute(picks[0], along_pairs), permute(picks[1], along_core_pairs)])
-        if k == 1:
-            nearby = jnp.concatenate([each[:RANK] for each in (panel, *others)], axis=0)
-            nearby, along[0][1] = meet(nearby, along[0][1])
-            core_nearby = permute(nearby, core_pairs)
         if k >= 1:
             picks[2], along[k - 1][0] = meet(picks[2], along[k - 1][0])
         across_core.append(permute(picks[2], core_pairs))
         if k == 1:
             parts[3], along[0][1] = meet(parts[3], along[0][1])
             across.append(permute(parts[3], across_pairs))
-        if k == 2:
-            own_sum, partner_sum = couple(placed, across[CARRIER], nearby, core_nearby)
-            partner_sum, along[1][1] = meet(partner_sum, along[1][1])
-            sums = (own_sum, permute(partner_sum, across_pairs))
-    nears.append(near(*SLABS[2], entry, near_blocks, pieces(2), nears[-1:]))
+    own_sum, partner_sum = couple(placed, across[CARRIER], across_core[0], panel, *others)
+    sums = (own_sum, permute(partner_sum, across_pairs))
+    nears.append(near(*SLABS[2], entry, near_blocks, pieces(2), nears[-1:] + [join(ZJ, *along[2])]))
     product = finish(SLABS[:-1], sums, down_basis, nears)
-    return last(*SLABS[-1], entry, near_blocks, sums, down_basis, pieces(3), product)
+    return last(*SLABS[-1], entry, near_blocks, sums, down_basis, pieces(3), join(ZJ, *along[3]), product)
 
 
 def solution(mesh):

time: 79.5 us -> 73.3 us (0.922)
  waiting for transfers between devices: 29.5 us -> 22.7 us
  local copies, waits for them, and re-layouts: 1.01 us -> 2.94 us
  starting transfers between devices: 26.2 us -> 24.9 us
    ppermute x23 -> x22, waiting for transfers between devices: 29.5 us -> 22.7 us  [on_device(): permute = lambda value, pairs: lax.ppermute(value, 'pts', pairs)]
    ppermute x23 -> x22, starting transfers between devices: 26.2 us -> 24.9 us  [on_device(): permute = lambda value, pairs: lax.ppermute(value, 'pts', pairs)]
    slice x4 -> x1, local copies, waits for them, and re-layouts: 0.04 us -> 1.08 us  [on_device(): first = rhs[:, :SLABS[0][1]]]
    unnamed x26 -> x28, local copies, waits for them, and re-layouts: 0.97 us -> 1.86 us
    pallas_call x5 -> x10, Pallas kernels: 2.87 us -> 2.92 us  [the longest x4 2.43 us: pack(): pl.pallas_call(functools.partial(pack_kernel, len(panels)), in_specs=[SCA...]
  transfers between devices with their start and end apart: 23 -> 22, of which waited for: 11 -> 11; matrix products, arithmetic and copies ran while one was open for 0% -> 1% of each run, Pallas kernels for 24% -> 26%
where the time goes in v5:
time: 73.3 us; the launch traced here: 73 us
  starting transfers between devices  24.9 us (34%)
  waiting for transfers between devices  22.7 us (31%)
  Pallas kernels  22.1 us (30%)
  local copies, waits for them, and re-layouts  2.94 us (4%)
    ppermute x22, starting transfers between devices, on_device(): permute = lambda value, pairs: lax.ppermute(value, 'pts', pairs)  24.9 us
    ppermute x22, waiting for transfers between devices, on_device(): permute = lambda value, pairs: lax.ppermute(value, 'pts', pairs)  22.7 us
    pallas_call x3, Pallas kernels, near(): pl.pallas_call(functools.partial(near_kernel, start), in_specs=[SCALAR] +...  8.17 us
    pallas_call x1, Pallas kernels, up(): pl.pallas_call(functools.partial(up_kernel, members), in_specs=[ANYWHERE]...  3.56 us
    pallas_call x1, Pallas kernels, last(): pl.pallas_call(functools.partial(last_kernel, start, width), in_specs=[SC...  3.41 us
    pallas_call x4, Pallas kernels, pack(): pl.pallas_call(functools.partial(pack_kernel, len(panels)), in_specs=[SCA...  2.43 us
    unnamed x28, local copies, waits for them, and re-layouts  1.86 us
    pallas_call x1, Pallas kernels, down(): pl.pallas_call(functools.partial(down_kernel, reach, members), in_specs=[...  1.84 us
  transfers between devices with their start and end apart: 22, of which 11 were waited for; matrix products, arithmetic and copies ran while one was open for 1% of the time, Pallas kernels for 26%

profile of v5, /device:TPU:0, one launch (start us, length us, event | category | flops | bytes accessed | tf_op | source)
XLA Modules:
  0.0 73.0 jit_solution(10571250852692588015)
XLA Ops:
  0.0 0.5 collective-permute-start.4
  0.5 1.1 %slice.3.refs_6_.rest_0_ = bf16[1024,256]{1,0:T(8,128)(2,1)S(1)} slice(bf16[1024,1024]{1,0:T(8,128)(2,1)} %refs_5_.1), slice={[0:1024], [0:256]} | slice | bytes 1048576 | tf_op jit(solution)/shard_map/slice | solution.py:448
  1.5 0.0 copy-start
  1.5 2.6 %collective-permute-start.1 = (bf16[1024,256]{1,0:T(8,128)(2,1)S(1)}, bf16[1024,256]{1,0:T(8,128)(2,1)S(1)}, u32[]{:S(2)}, u32[]{:S(2)}) collective-permute-start(bf16[1024,256]{1,0:T(8,128)(2,1)S(1)} %slice.3.refs_6_.rest_0_), channel_id=1, source_target_pairs={{0,2},{1,3},{2,0},{3,1},{4,6},{5,7},{6,4},{7,5},{8,10},{9,11},{10,... | collective-permute-start | bytes 1572872 | tf_op jit(solution)/shard_map/ppermute | solution.py:442
  4.1 0.0 copy-done
  4.1 0.0 copy-start.10
  4.1 0.0 copy-start.11
  4.1 3.6 %up.1 = (bf16[80,1024]{1,0:T(8,128)(2,1)}, s32[4,12]{1,0:T(4,128)}, bf16[1024,256]{1,0:T(8,128)(2,1)}, bf16[1152,256]{1,0:T(8,128)(2,1)}, bf16[1024,256]{1,0:T(8,128)(2,1)}) custom-call(bf16[4,64,256]{2,1,0:T(8,128)(2,1)} %refs_0_.1, bf16[4,64,64]{2,1,0:T(8,128)(2,1)} %leaf_ref.1, bf16[2,64,64]{2,1,0:T(8,128)(2,1)} %mid_ref.1, s32[4,12]{1,0:T(4,128)} %refs_3_.1, ...), custom_call_target="tpu_custom_call" | custom-call | flops 2300000000 | bytes 1048576 | tf_op jit(solution)/shard_map/up/pallas_call | solution.py:128
  7.7 3.7 %collective-permute-start.2 = (bf16[80,1024]{1,0:T(8,128)(2,1)}, bf16[80,1024]{1,0:T(8,128)(2,1)S(1)}, u32[]{:S(2)}, u32[]{:S(2)}) collective-permute-start(bf16[80,1024]{1,0:T(8,128)(2,1)} %get-tuple-element.44.rest_1_.panel_ref.rest_0_), channel_id=1, source_target_pairs={{0,12},{1,13},{2,14},{3,15},{4,0},{5,1},{6,2},{7,3},{8,4},{9,5},{1... | collective-permute-start | bytes 491528 | tf_op jit(solution)/shard_map/ppermute | solution.py:442
  11.4 0.0 collective-permute-start.3
  11.4 1.0 %collective-permute-start.6 = (bf16[80,1024]{1,0:T(8,128)(2,1)}, bf16[80,1024]{1,0:T(8,128)(2,1)S(1)}, u32[]{:S(2)}, u32[]{:S(2)}) collective-permute-start(bf16[80,1024]{1,0:T(8,128)(2,1)} %get-tuple-element.44.rest_1_.panel_ref.rest_0_), channel_id=1, source_target_pairs={{0,8},{1,9},{2,10},{3,11},{4,12},{5,13},{6,14},{7,15},{8,0},{9,1},... | collective-permute-start | bytes 491528 | tf_op jit(solution)/shard_map/ppermute | solution.py:442
  12.4 3.9 %collective-permute-done.2.ahead_ref.rest_1_ = bf16[80,1024]{1,0:T(8,128)(2,1)S(1)} collective-permute-done((bf16[80,1024]{1,0:T(8,128)(2,1)}, bf16[80,1024]{1,0:T(8,128)(2,1)S(1)}, u32[]{:S(2)}, u32[]{:S(2)}) %collective-permute-start.2) | collective-permute-done | bytes 163872 | tf_op jit(solution)/shard_map/ppermute | solution.py:442
  16.3 0.7 collective-permute-start.11
  17.0 0.9 %copy-done.2 = bf16[80,1024]{1,0:T(8,128)(2,1)S(1)} copy-done((bf16[80,1024]{1,0:T(8,128)(2,1)S(1)}, bf16[80,1024]{1,0:T(8,128)(2,1)}, u32[]{:S(2)}) %copy-start.2) | copy-done | bytes 163864
  17.9 1.8 %down.1 = (bf16[1152,256]{1,0:T(8,128)(2,1)}, bf16[4,256,192]{2,1,0:T(8,128)(2,1)S(1)}, bf16[64,512]{1,0:T(8,128)(2,1)S(1)}) custom-call(s32[1,6]{1,0:T(1,128)S(1)} %copy-done.11, bf16[4,64,256]{2,1,0:T(8,128)(2,1)S(1)} %copy-done.7, bf16[4,64,64]{2,1,0:T(8,128)(2,1)S(1)} %copy-done.9, ...), custom_call_target="tpu_custom_call", output_to_operand_aliasing={{0}: (5, {})} | custom-call | flops 1150000000 | bytes 1048576 | tf_op jit(solution)/shard_map/down/pallas_call | solution.py:177
  19.7 0.8 %collective-permute-done.3.behind_ref.rest_2_ = bf16[80,1024]{1,0:T(8,128)(2,1)S(1)} collective-permute-done((bf16[80,1024]{1,0:T(8,128)(2,1)}, bf16[80,1024]{1,0:T(8,128)(2,1)S(1)}, u32[]{:S(2)}, u32[]{:S(2)}) %collective-permute-start.3) | collective-permute-done | bytes 163872 | tf_op jit(solution)/shard_map/ppermute | solution.py:442
  20.5 0.0 collective-permute-done.1.arrived_ref.rest_2_
  20.5 0.0 collective-permute-done.4.rest_0_.rest_1_
  20.6 0.1 collective-permute-start.5
  20.7 1.2 %collective-permute-done.5.core_asked_ref = bf16[32,768]{1,0:T(8,128)(2,1)S(1)} collective-permute-done((bf16[32,768]{1,0:T(8,128)(2,1)S(1)}, bf16[32,768]{1,0:T(8,128)(2,1)S(1)}, u32[]{:S(2)}, u32[]{:S(2)}) %collective-permute-start.5) | collective-permute-done | bytes 49184 | tf_op jit(solution)/shard_map/ppermute | solution.py:442
  21.9 0.7 wishes.1.wish_ref
  22.6 3.2 %collective-permute-done.6.rest_3_ = bf16[80,1024]{1,0:T(8,128)(2,1)S(1)} collective-permute-done((bf16[80,1024]{1,0:T(8,128)(2,1)}, bf16[80,1024]{1,0:T(8,128)(2,1)S(1)}, u32[]{:S(2)}, u32[]{:S(2)}) %collective-permute-start.6) | collective-permute-done | bytes 163872 | tf_op jit(solution)/shard_map/ppermute | solution.py:442
  25.8 0.6 pack.4
  26.5 0.1 collective-permute-start.7
  26.6 1.4 %collective-permute-start.9 = (bf16[512,256]{1,0:T(8,128)(2,1)S(1)}, bf16[512,256]{1,0:T(8,128)(2,1)S(1)}, u32[]{:S(2)}, u32[]{:S(2)}) collective-permute-start(bf16[512,256]{1,0:T(8,128)(2,1)S(1)} %get-tuple-element.53), channel_id=1, source_target_pairs={{1,4},{2,15},{5,8},{6,3},{9,12},{10,7},{13,0},{14,11},{17,20},{18,... | collective-permute-start | bytes 786440 | tf_op jit(solution)/shard_map/ppermute | solution.py:442
  28.0 4.3 %collective-permute-start = (bf16[1152,256]{1,0:T(8,128)(2,1)}, bf16[1152,256]{1,0:T(8,128)(2,1)S(1)}, u32[]{:S(2)}, u32[]{:S(2)}) collective-permute-start(bf16[1152,256]{1,0:T(8,128)(2,1)} %get-tuple-element.43.rest_0_), channel_id=1, source_target_pairs={{0,2},{1,3},{2,0},{3,1},{4,6},{5,7},{6,4},{7,5},{8,10},{9,11},{10,... | collective-permute-start | bytes 1769480 | tf_op jit(solution)/shard_map/ppermute | solution.py:442
  32.3 0.0 collective-permute-start.12
  32.3 3.9 %collective-permute-done.9.refs_1_.rest_5_ = bf16[512,256]{1,0:T(8,128)(2,1)S(1)} collective-permute-done((bf16[512,256]{1,0:T(8,128)(2,1)S(1)}, bf16[512,256]{1,0:T(8,128)(2,1)S(1)}, u32[]{:S(2)}, u32[]{:S(2)}) %collective-permute-start.9) | collective-permute-done | bytes 262176 | tf_op jit(solution)/shard_map/ppermute | solution.py:442
  36.2 1.4 %collective-permute-start.10 = (bf16[1024,256]{1,0:T(8,128)(2,1)S(1)}, bf16[1024,256]{1,0:T(8,128)(2,1)S(1)}, u32[]{:S(2)}, u32[]{:S(2)}) collective-permute-start(bf16[1024,256]{1,0:T(8,128)(2,1)S(1)} %copy-done.4), channel_id=1, source_target_pairs={{0,2},{1,3},{2,0},{3,1},{4,6},{5,7},{6,4},{7,5},{8,10},{9,11},{10,... | collective-permute-start | bytes 1572872 | tf_op jit(solution)/shard_map/ppermute | solution.py:442
  37.6 0.0 collective-permute-done.11.refs_0_.arrived_ref.rest_2_
  37.6 0.6 pack.5
  38.2 0.7 collective-permute-start.14
  38.9 2.9 %collective-permute-done.12.refs_0_.rest_4_ = bf16[512,256]{1,0:T(8,128)(2,1)S(1)} collective-permute-done((bf16[512,256]{1,0:T(8,128)(2,1)S(1)}, bf16[512,256]{1,0:T(8,128)(2,1)S(1)}, u32[]{:S(2)}, u32[]{:S(2)}) %collective-permute-start.12) | collective-permute-done | bytes 262176 | tf_op jit(solution)/shard_map/ppermute | solution.py:442
  41.8 1.3 %collective-permute-start.15 = (bf16[512,256]{1,0:T(8,128)(2,1)S(1)}, bf16[512,256]{1,0:T(8,128)(2,1)S(1)}, u32[]{:S(2)}, u32[]{:S(2)}) collective-permute-start(bf16[512,256]{1,0:T(8,128)(2,1)S(1)} %get-tuple-element.64), channel_id=1, source_target_pairs={{1,4},{2,15},{5,8},{6,3},{9,12},{10,7},{13,0},{14,11},{17,20},{18,... | collective-permute-start | bytes 786440 | tf_op jit(solution)/shard_map/ppermute | solution.py:442
  43.1 0.0 collective-permute-done.7.core_ref.rest_3_
  43.1 0.1 collective-permute-start.13
  43.2 0.9 %copy-done.1 = bf16[1024,256]{1,0:T(8,128)(2,1)S(1)} copy-done((bf16[1024,256]{1,0:T(8,128)(2,1)S(1)}, bf16[1024,256]{1,0:T(8,128)(2,1)}, u32[]{:S(2)}) %copy-start.1) | copy-done | bytes 524312
  44.1 2.5 %near.3.rest_0_.rest_6_ = f32[1024,256]{1,0:T(8,128)S(1)} custom-call(s32[4,12]{1,0:T(4,128)S(1)} %copy-done.6, bf16[4,12,256,256]{3,2,1,0:T(8,128)(2,1)S(1)} %bitcast.3, bf16[1024,256]{1,0:T(8,128)(2,1)S(1)} %copy-done.1, bf16[1024,1024]{1,0:T(8,128)(2,1)S(1)} %collective-permute-done.4.rest_0_.rest_1_, ...), custom_call_target="tpu_custom_call" | custom-call | flops 460000000 | bytes 1048576 | tf_op jit(solution)/shard_map/near/pallas_call | solution.py:335
  46.7 0.0 collective-permute-done.carrier_ref.arrived_ref.rest_2_
  46.7 0.6 pack.6
  47.3 0.1 collective-permute-start.16
  47.4 1.9 %collective-permute-done.14.refs_0_.rest_4_ = bf16[512,256]{1,0:T(8,128)(2,1)S(1)} collective-permute-done((bf16[512,256]{1,0:T(8,128)(2,1)S(1)}, bf16[512,256]{1,0:T(8,128)(2,1)S(1)}, u32[]{:S(2)}, u32[]{:S(2)}) %collective-permute-start.14) | collective-permute-done | bytes 262176 | tf_op jit(solution)/shard_map/ppermute | solution.py:442
  49.3 1.3 %collective-permute-start.21 = (bf16[512,256]{1,0:T(8,128)(2,1)S(1)}, bf16[512,256]{1,0:T(8,128)(2,1)S(1)}, u32[]{:S(2)}, u32[]{:S(2)}) collective-permute-start(bf16[512,256]{1,0:T(8,128)(2,1)S(1)} %get-tuple-element.72), channel_id=1, source_target_pairs={{1,4},{2,15},{5,8},{6,3},{9,12},{10,7},{13,0},{14,11},{17,20},{18,... | collective-permute-start | bytes 786440 | tf_op jit(solution)/shard_map/ppermute | solution.py:442
  50.6 1.5 %collective-permute-done.15.refs_1_.rest_5_ = bf16[512,256]{1,0:T(8,128)(2,1)S(1)} collective-permute-done((bf16[512,256]{1,0:T(8,128)(2,1)S(1)}, bf16[512,256]{1,0:T(8,128)(2,1)S(1)}, u32[]{:S(2)}, u32[]{:S(2)}) %collective-permute-start.15) | collective-permute-done | bytes 262176 | tf_op jit(solution)/shard_map/ppermute | solution.py:442
  52.0 0.0 collective-permute-start.20
  52.0 0.0 collective-permute-done.13.rest_3_
  52.0 2.6 %near.4.rest_0_.rest_6_.rest_1_ = f32[1024,256]{1,0:T(8,128)S(1)} custom-call(s32[4,12]{1,0:T(4,128)S(1)} %copy-done.6, bf16[4,12,256,256]{3,2,1,0:T(8,128)(2,1)S(1)} %bitcast.3, bf16[1024,256]{1,0:T(8,128)(2,1)S(1)} %copy-done.5, bf16[1024,1024]{1,0:T(8,128)(2,1)S(1)} %collective-permute-done.4.rest_0_.rest_1_, ...), custom_call_target="tpu_custom_call" | custom-call | flops 460000000 | bytes 1048576 | tf_op jit(solution)/shard_map/near/pallas_call | solution.py:335
  54.6 0.8 %collective-permute-done.10.arrived_ref.rest_2_ = bf16[1024,256]{1,0:T(8,128)(2,1)S(1)} collective-permute-done((bf16[1024,256]{1,0:T(8,128)(2,1)S(1)}, bf16[1024,256]{1,0:T(8,128)(2,1)S(1)}, u32[]{:S(2)}, u32[]{:S(2)}) %collective-permute-start.10) | collective-permute-done | bytes 524320 | tf_op jit(solution)/shard_map/ppermute | solution.py:442
  55.4 0.6 pack.7
  56.0 1.5 %collective-permute-start.18 = (bf16[512,256]{1,0:T(8,128)(2,1)S(1)}, bf16[512,256]{1,0:T(8,128)(2,1)S(1)}, u32[]{:S(2)}, u32[]{:S(2)}) collective-permute-start(bf16[512,256]{1,0:T(8,128)(2,1)S(1)} %get-tuple-element.68), channel_id=1, source_target_pairs={{0,4},{1,5},{2,14},{3,15},{4,8},{5,9},{6,2},{7,3},{8,12},{9,13},{1... | collective-permute-start | bytes 786440 | tf_op jit(solution)/shard_map/ppermute | solution.py:442
  57.5 1.3 %collective-permute-start.19 = (bf16[512,256]{1,0:T(8,128)(2,1)S(1)}, bf16[512,256]{1,0:T(8,128)(2,1)S(1)}, u32[]{:S(2)}, u32[]{:S(2)}) collective-permute-start(bf16[512,256]{1,0:T(8,128)(2,1)S(1)} %get-tuple-element.69), channel_id=1, source_target_pairs={{1,4},{2,15},{5,8},{6,3},{9,12},{10,7},{13,0},{14,11},{17,20},{18,... | collective-permute-start | bytes 786440 | tf_op jit(solution)/shard_map/ppermute | solution.py:442
  58.8 0.5 couple.1
  59.3 0.0 collective-permute-done.16.refs_0_.rest_4_
  59.3 3.1 %collective-permute-start.8 = (bf16[64,1024]{1,0:T(8,128)(2,1)S(1)}, bf16[64,1024]{1,0:T(8,128)(2,1)S(1)}, u32[]{:S(2)}, u32[]{:S(2)}) collective-permute-start(bf16[64,1024]{1,0:T(8,128)(2,1)S(1)} %get-tuple-element.51), channel_id=1, source_target_pairs={{0,2},{1,3},{2,0},{3,1},{4,6},{5,7},{6,4},{7,5},{8,10},{9,11},{10,... | collective-permute-start | bytes 393224 | tf_op jit(solution)/shard_map/ppermute | solution.py:442
  62.4 0.0 collective-permute-done.21.refs_1_.rest_5_
  62.4 0.0 collective-permute-start.17
  62.4 0.0 collective-permute-done.20.rest_3_
  62.4 3.1 %near.5.rest_2_ = f32[1024,256]{1,0:T(8,128)S(1)} custom-call(s32[4,12]{1,0:T(4,128)S(1)} %copy-done.6, bf16[4,12,256,256]{3,2,1,0:T(8,128)(2,1)S(1)} %bitcast.3, bf16[1152,256]{1,0:T(8,128)(2,1)} %get-tuple-element.43.rest_0_, bf16[1024,1024]{1,0:T(8,128)(2,1)S(1)} %collective-permute-done.4.rest_0_.rest_1_, ...), custom_call_target="tpu_custom_call" | custom-call | flops 460000000 | bytes 1048576 | tf_op jit(solution)/shard_map/near/pallas_call | solution.py:335
  65.5 0.2 collective-permute-done.8.partner_sum_ref
  65.7 1.5 %finish.1.rest_7_ = bf16[1024,1024]{1,0:T(8,128)(2,1)} custom-call(f32[64,1024]{1,0:T(8,128)S(1)} %get-tuple-element.50.own_sum_ref, bf16[64,1024]{1,0:T(8,128)(2,1)S(1)} %collective-permute-done.8.partner_sum_ref, bf16[4,256,192]{2,1,0:T(8,128)(2,1)S(1)} %get-tuple-element.47.rest_1_.down_ref, f32[1024,256]{1,0:T(8,128)S(1)} %near.3.rest_0_.rest_6_, ...), custom_call_target="tpu_custom_call" | custom-call | flops 460000000 | bytes 1048576 | tf_op jit(solution)/shard_map/finish/pallas_call | solution.py:409
  67.2 0.0 collective-permute-done.18.refs_0_.rest_4_
  67.2 2.4 %collective-permute-done.19.refs_1_.rest_5_ = bf16[512,256]{1,0:T(8,128)(2,1)S(1)} collective-permute-done((bf16[512,256]{1,0:T(8,128)(2,1)S(1)}, bf16[512,256]{1,0:T(8,128)(2,1)S(1)}, u32[]{:S(2)}, u32[]{:S(2)}) %collective-permute-start.19) | collective-permute-done | bytes 262176 | tf_op jit(solution)/shard_map/ppermute | solution.py:442
  69.6 0.0 collective-permute-done.17.rest_3_
  69.6 3.4 %last.1 = bf16[1024,1024]{1,0:T(8,128)(2,1)} custom-call(s32[4,12]{1,0:T(4,128)S(1)} %copy-done.6, bf16[4,12,256,256]{3,2,1,0:T(8,128)(2,1)S(1)} %bitcast.3, f32[64,1024]{1,0:T(8,128)S(1)} %get-tuple-element.50.own_sum_ref, bf16[64,1024]{1,0:T(8,128)(2,1)S(1)} %collective-permute-done.8.partner_sum_ref, ...), custom_call_target="tpu_custom_call", output_to_operand_aliasing={{}: (12, {})} | custom-call | flops 1150000000 | bytes 1048576 | tf_op jit(solution)/shard_map/last/pallas_call | solution.py:368
  (29 shorter events, 0.1 us)
Async XLA Ops:
  0.0 20.5 %collective-permute-start.4 = (bf16[1024,1024]{1,0:T(8,128)(2,1)}, bf16[1024,1024]{1,0:T(8,128)(2,1)S(1)}, u32[]{:S(2)}, u32[]{:S(2)}) collective-permute-start(bf16[1024,1024]{1,0:T(8,128)(2,1)} %refs_5_.1), channel_id=1, source_target_pairs={{0,1},{1,0},{2,3},{3,2},{4,5},{5,4},{6,7},{7,6},{8,9},{9,8},{10,11... | collective-permute-start | bytes 6291464 | tf_op jit(solution)/shard_map/ppermute | solution.py:442
  1.5 2.6 %copy-start = (bf16[1024,256]{1,0:T(8,128)(2,1)}, bf16[1024,256]{1,0:T(8,128)(2,1)S(1)}, u32[]{:S(2)}) copy-start(bf16[1024,256]{1,0:T(8,128)(2,1)S(1)} %slice.3.refs_6_.rest_0_) | copy-start | bytes 1572868
  1.5 19.0 %collective-permute-start.1 = (bf16[1024,256]{1,0:T(8,128)(2,1)S(1)}, bf16[1024,256]{1,0:T(8,128)(2,1)S(1)}, u32[]{:S(2)}, u32[]{:S(2)}) collective-permute-start(bf16[1024,256]{1,0:T(8,128)(2,1)S(1)} %slice.3.refs_6_.rest_0_), channel_id=1, source_target_pairs={{0,2},{1,3},{2,0},{3,1},{4,6},{5,7},{6,4},{7,5},{8,10},{9,11},{10,... | collective-permute-start | bytes 1572872 | tf_op jit(solution)/shard_map/ppermute | solution.py:442
  4.1 12.8 %copy-start.7 = (bf16[4,64,256]{2,1,0:T(8,128)(2,1)S(1)}, bf16[4,64,256]{2,1,0:T(8,128)(2,1)}, u32[]{:S(2)}) copy-start(bf16[4,64,256]{2,1,0:T(8,128)(2,1)} %target_ref.1) | copy-start | bytes 393220
  4.1 12.8 %copy-start.8 = (bf16[1,6,64,64]{3,2,1,0:T(8,128)(2,1)S(1)}, bf16[1,6,64,64]{3,2,1,0:T(8,128)(2,1)}, u32[]{:S(2)}) copy-start(bf16[1,6,64,64]{3,2,1,0:T(8,128)(2,1)} %param.18) | copy-start | bytes 147460
  4.1 12.8 %copy-start.9 = (bf16[4,64,64]{2,1,0:T(8,128)(2,1)S(1)}, bf16[4,64,64]{2,1,0:T(8,128)(2,1)}, u32[]{:S(2)}) copy-start(bf16[4,64,64]{2,1,0:T(8,128)(2,1)} %leaf_ref.1) | copy-start | bytes 98308
  4.1 12.8 %copy-start.10 = (bf16[2,64,64]{2,1,0:T(8,128)(2,1)S(1)}, bf16[2,64,64]{2,1,0:T(8,128)(2,1)}, u32[]{:S(2)}) copy-start(bf16[2,64,64]{2,1,0:T(8,128)(2,1)} %mid_ref.1) | copy-start | bytes 49156
  4.1 12.8 %copy-start.11 = (s32[1,6]{1,0:T(1,128)S(1)}, s32[1,6]{1,0:T(1,128)}, u32[]{:S(2)}) copy-start(s32[1,6]{1,0:T(1,128)} %far_ref.1) | copy-start | bytes 76
  7.7 8.6 %collective-permute-start.2 = (bf16[80,1024]{1,0:T(8,128)(2,1)}, bf16[80,1024]{1,0:T(8,128)(2,1)S(1)}, u32[]{:S(2)}, u32[]{:S(2)}) collective-permute-start(bf16[80,1024]{1,0:T(8,128)(2,1)} %get-tuple-element.44.rest_1_.panel_ref.rest_0_), channel_id=1, source_target_pairs={{0,12},{1,13},{2,14},{3,15},{4,0},{5,1},{6,2},{7,3},{8,4},{9,5},{1... | collective-permute-start | bytes 491528 | tf_op jit(solution)/shard_map/ppermute | solution.py:442
  11.4 9.2 %collective-permute-start.3 = (bf16[80,1024]{1,0:T(8,128)(2,1)}, bf16[80,1024]{1,0:T(8,128)(2,1)S(1)}, u32[]{:S(2)}, u32[]{:S(2)}) collective-permute-start(bf16[80,1024]{1,0:T(8,128)(2,1)} %get-tuple-element.44.rest_1_.panel_ref.rest_0_), channel_id=1, source_target_pairs={{0,4},{1,5},{2,6},{3,7},{4,8},{5,9},{6,10},{7,11},{8,12},{9,13},{1... | collective-permute-start | bytes 491528 | tf_op jit(solution)/shard_map/ppermute | solution.py:442
  11.4 14.5 %collective-permute-start.6 = (bf16[80,1024]{1,0:T(8,128)(2,1)}, bf16[80,1024]{1,0:T(8,128)(2,1)S(1)}, u32[]{:S(2)}, u32[]{:S(2)}) collective-permute-start(bf16[80,1024]{1,0:T(8,128)(2,1)} %get-tuple-element.44.rest_1_.panel_ref.rest_0_), channel_id=1, source_target_pairs={{0,8},{1,9},{2,10},{3,11},{4,12},{5,13},{6,14},{7,15},{8,0},{9,1},... | collective-permute-start | bytes 491528 | tf_op jit(solution)/shard_map/ppermute | solution.py:442
  16.3 21.4 %collective-permute-start.11 = (bf16[1024,256]{1,0:T(8,128)(2,1)}, bf16[1024,256]{1,0:T(8,128)(2,1)S(1)}, u32[]{:S(2)}, u32[]{:S(2)}) collective-permute-start(bf16[1024,256]{1,0:T(8,128)(2,1)} %get-tuple-element.55.rest_0_), channel_id=1, source_target_pairs={{0,2},{1,3},{2,0},{3,1},{4,6},{5,7},{6,4},{7,5},{8,10},{9,11},{10,... | collective-permute-start | bytes 1572872 | tf_op jit(solution)/shard_map/ppermute | solution.py:442
  17.0 0.9 %copy-start.2 = (bf16[80,1024]{1,0:T(8,128)(2,1)S(1)}, bf16[80,1024]{1,0:T(8,128)(2,1)}, u32[]{:S(2)}) copy-start(bf16[80,1024]{1,0:T(8,128)(2,1)} %get-tuple-element.44.rest_1_.panel_ref.rest_0_) | copy-start | bytes 491524
  20.5 15.6 %copy-start.4 = (bf16[1024,256]{1,0:T(8,128)(2,1)S(1)}, bf16[1024,256]{1,0:T(8,128)(2,1)}, u32[]{:S(2)}) copy-start(bf16[1024,256]{1,0:T(8,128)(2,1)} %get-tuple-element.54.rest_0_) | copy-start | bytes 1572868
  20.6 1.3 %collective-permute-start.5 = (bf16[32,768]{1,0:T(8,128)(2,1)S(1)}, bf16[32,768]{1,0:T(8,128)(2,1)S(1)}, u32[]{:S(2)}, u32[]{:S(2)}) collective-permute-start(bf16[32,768]{1,0:T(8,128)(2,1)S(1)} %ask.1.asked_ref), channel_id=1, source_target_pairs={{0,1},{1,0},{2,3},{3,2},{4,5},{5,4},{6,7},{7,6},{8,9},{9,8},{10,11... | collective-permute-start | bytes 147464 | tf_op jit(solution)/shard_map/ppermute | solution.py:442
  25.8 17.4 %slice-start = ((s8[6291456]{0:T(1024)(128)(4,1)}), s8[4194304]{0:T(1024)(128)(4,1)S(1)}, s32[]{:S(2)}) async-start(s8[6291456]{0:T(1024)(128)(4,1)} %bitcast.2), calls=%async_computation | async-start | bytes 8388608
  26.5 16.6 %collective-permute-start.7 = (bf16[1536,256]{1,0:T(8,128)(2,1)S(1)}, bf16[1536,256]{1,0:T(8,128)(2,1)S(1)}, u32[]{:S(2)}, u32[]{:S(2)}) collective-permute-start(bf16[1536,256]{1,0:T(8,128)(2,1)S(1)} %get-tuple-element.49), channel_id=1, source_target_pairs={{0,1},{1,0},{2,3},{3,2},{4,5},{5,4},{6,7},{7,6},{8,9},{9,8},{10,11... | collective-permute-start | bytes 2359304 | tf_op jit(solution)/shard_map/ppermute | solution.py:442
  26.6 9.6 %collective-permute-start.9 = (bf16[512,256]{1,0:T(8,128)(2,1)S(1)}, bf16[512,256]{1,0:T(8,128)(2,1)S(1)}, u32[]{:S(2)}, u32[]{:S(2)}) collective-permute-start(bf16[512,256]{1,0:T(8,128)(2,1)S(1)} %get-tuple-element.53), channel_id=1, source_target_pairs={{1,4},{2,15},{5,8},{6,3},{9,12},{10,7},{13,0},{14,11},{17,20},{18,... | collective-permute-start | bytes 786440 | tf_op jit(solution)/shard_map/ppermute | solution.py:442
  28.0 18.7 %collective-permute-start = (bf16[1152,256]{1,0:T(8,128)(2,1)}, bf16[1152,256]{1,0:T(8,128)(2,1)S(1)}, u32[]{:S(2)}, u32[]{:S(2)}) collective-permute-start(bf16[1152,256]{1,0:T(8,128)(2,1)} %get-tuple-element.43.rest_0_), channel_id=1, source_target_pairs={{0,2},{1,3},{2,0},{3,1},{4,6},{5,7},{6,4},{7,5},{8,10},{9,11},{10,... | collective-permute-start | bytes 1769480 | tf_op jit(solution)/shard_map/ppermute | solution.py:442
  32.3 9.5 %collective-permute-start.12 = (bf16[512,256]{1,0:T(8,128)(2,1)S(1)}, bf16[512,256]{1,0:T(8,128)(2,1)S(1)}, u32[]{:S(2)}, u32[]{:S(2)}) collective-permute-start(bf16[512,256]{1,0:T(8,128)(2,1)S(1)} %get-tuple-element.57), channel_id=1, source_target_pairs={{0,4},{1,5},{2,14},{3,15},{4,8},{5,9},{6,2},{7,3},{8,12},{9,13},{1... | collective-permute-start | bytes 786440 | tf_op jit(solution)/shard_map/ppermute | solution.py:442
  36.2 7.0 %slice-start.1 = ((s8[6291456]{0:T(1024)(128)(4,1)}), s8[2097152]{0:T(1024)(128)(4,1)S(1)}, s32[]{:S(2)}) async-start(s8[6291456]{0:T(1024)(128)(4,1)} %bitcast.2), calls=%async_computation.1 | async-start | bytes 4194304
  36.2 19.2 %collective-permute-start.10 = (bf16[1024,256]{1,0:T(8,128)(2,1)S(1)}, bf16[1024,256]{1,0:T(8,128)(2,1)S(1)}, u32[]{:S(2)}, u32[]{:S(2)}) collective-permute-start(bf16[1024,256]{1,0:T(8,128)(2,1)S(1)} %copy-done.4), channel_id=1, source_target_pairs={{0,2},{1,3},{2,0},{3,1},{4,6},{5,7},{6,4},{7,5},{8,10},{9,11},{10,... | collective-permute-start | bytes 1572872 | tf_op jit(solution)/shard_map/ppermute | solution.py:442
  38.2 11.0 %collective-permute-start.14 = (bf16[512,256]{1,0:T(8,128)(2,1)S(1)}, bf16[512,256]{1,0:T(8,128)(2,1)S(1)}, u32[]{:S(2)}, u32[]{:S(2)}) collective-permute-start(bf16[512,256]{1,0:T(8,128)(2,1)S(1)} %get-tuple-element.62), channel_id=1, source_target_pairs={{0,4},{1,5},{2,14},{3,15},{4,8},{5,9},{6,2},{7,3},{8,12},{9,13},{1... | collective-permute-start | bytes 786440 | tf_op jit(solution)/shard_map/ppermute | solution.py:442
  41.8 10.2 %collective-permute-start.15 = (bf16[512,256]{1,0:T(8,128)(2,1)S(1)}, bf16[512,256]{1,0:T(8,128)(2,1)S(1)}, u32[]{:S(2)}, u32[]{:S(2)}) collective-permute-start(bf16[512,256]{1,0:T(8,128)(2,1)S(1)} %get-tuple-element.64), channel_id=1, source_target_pairs={{1,4},{2,15},{5,8},{6,3},{9,12},{10,7},{13,0},{14,11},{17,20},{18,... | collective-permute-start | bytes 786440 | tf_op jit(solution)/shard_map/ppermute | solution.py:442
  43.1 1.0 %copy-start.1 = (bf16[1024,256]{1,0:T(8,128)(2,1)S(1)}, bf16[1024,256]{1,0:T(8,128)(2,1)}, u32[]{:S(2)}) copy-start(bf16[1024,256]{1,0:T(8,128)(2,1)} %copy-done) | copy-start | bytes 1572868
  43.1 1.0 %copy-start.6 = (s32[4,12]{1,0:T(4,128)S(1)}, s32[4,12]{1,0:T(4,128)}, u32[]{:S(2)}) copy-start(s32[4,12]{1,0:T(4,128)} %get-tuple-element.39.entry_ref) | copy-start | bytes 580
  43.1 8.9 %collective-permute-start.13 = (bf16[512,256]{1,0:T(8,128)(2,1)S(1)}, bf16[512,256]{1,0:T(8,128)(2,1)S(1)}, u32[]{:S(2)}, u32[]{:S(2)}) collective-permute-start(bf16[512,256]{1,0:T(8,128)(2,1)S(1)} %get-tuple-element.58), channel_id=1, source_target_pairs={{0,1},{1,0},{2,3},{3,2},{4,5},{5,4},{6,7},{7,6},{8,9},{9,8},{10,11... | collective-permute-start | bytes 786440 | tf_op jit(solution)/shard_map/ppermute | solution.py:442
  47.3 12.0 %collective-permute-start.16 = (bf16[512,256]{1,0:T(8,128)(2,1)S(1)}, bf16[512,256]{1,0:T(8,128)(2,1)S(1)}, u32[]{:S(2)}, u32[]{:S(2)}) collective-permute-start(bf16[512,256]{1,0:T(8,128)(2,1)S(1)} %get-tuple-element.66), channel_id=1, source_target_pairs={{0,4},{1,5},{2,14},{3,15},{4,8},{5,9},{6,2},{7,3},{8,12},{9,13},{1... | collective-permute-start | bytes 786440 | tf_op jit(solution)/shard_map/ppermute | solution.py:442
  49.3 13.2 %collective-permute-start.21 = (bf16[512,256]{1,0:T(8,128)(2,1)S(1)}, bf16[512,256]{1,0:T(8,128)(2,1)S(1)}, u32[]{:S(2)}, u32[]{:S(2)}) collective-permute-start(bf16[512,256]{1,0:T(8,128)(2,1)S(1)} %get-tuple-element.72), channel_id=1, source_target_pairs={{1,4},{2,15},{5,8},{6,3},{9,12},{10,7},{13,0},{14,11},{17,20},{18,... | collective-permute-start | bytes 786440 | tf_op jit(solution)/shard_map/ppermute | solution.py:442
  50.6 1.5 %copy-start.5 = (bf16[1024,256]{1,0:T(8,128)(2,1)S(1)}, bf16[1024,256]{1,0:T(8,128)(2,1)}, u32[]{:S(2)}) copy-start(bf16[1024,256]{1,0:T(8,128)(2,1)} %get-tuple-element.55.rest_0_) | copy-start | bytes 1572868
  52.0 10.4 %collective-permute-start.20 = (bf16[512,256]{1,0:T(8,128)(2,1)S(1)}, bf16[512,256]{1,0:T(8,128)(2,1)S(1)}, u32[]{:S(2)}, u32[]{:S(2)}) collective-permute-start(bf16[512,256]{1,0:T(8,128)(2,1)S(1)} %get-tuple-element.70), channel_id=1, source_target_pairs={{0,1},{1,0},{2,3},{3,2},{4,5},{5,4},{6,7},{7,6},{8,9},{9,8},{10,11... | collective-permute-start | bytes 786440 | tf_op jit(solution)/shard_map/ppermute | solution.py:442
  52.0 6.8 %copy-start.3 = (bf16[80,1024]{1,0:T(8,128)(2,1)S(1)}, bf16[80,1024]{1,0:T(8,128)(2,1)}, u32[]{:S(2)}) copy-start(bf16[80,1024]{1,0:T(8,128)(2,1)} %get-tuple-element.44.rest_1_.panel_ref.rest_0_) | copy-start | bytes 491524
  56.0 11.2 %collective-permute-start.18 = (bf16[512,256]{1,0:T(8,128)(2,1)S(1)}, bf16[512,256]{1,0:T(8,128)(2,1)S(1)}, u32[]{:S(2)}, u32[]{:S(2)}) collective-permute-start(bf16[512,256]{1,0:T(8,128)(2,1)S(1)} %get-tuple-element.68), channel_id=1, source_target_pairs={{0,4},{1,5},{2,14},{3,15},{4,8},{5,9},{6,2},{7,3},{8,12},{9,13},{1... | collective-permute-start | bytes 786440 | tf_op jit(solution)/shard_map/ppermute | solution.py:442
  57.5 12.1 %collective-permute-start.19 = (bf16[512,256]{1,0:T(8,128)(2,1)S(1)}, bf16[512,256]{1,0:T(8,128)(2,1)S(1)}, u32[]{:S(2)}, u32[]{:S(2)}) collective-permute-start(bf16[512,256]{1,0:T(8,128)(2,1)S(1)} %get-tuple-element.69), channel_id=1, source_target_pairs={{1,4},{2,15},{5,8},{6,3},{9,12},{10,7},{13,0},{14,11},{17,20},{18,... | collective-permute-start | bytes 786440 | tf_op jit(solution)/shard_map/ppermute | solution.py:442
  59.3 6.4 %collective-permute-start.8 = (bf16[64,1024]{1,0:T(8,128)(2,1)S(1)}, bf16[64,1024]{1,0:T(8,128)(2,1)S(1)}, u32[]{:S(2)}, u32[]{:S(2)}) collective-permute-start(bf16[64,1024]{1,0:T(8,128)(2,1)S(1)} %get-tuple-element.51), channel_id=1, source_target_pairs={{0,2},{1,3},{2,0},{3,1},{4,6},{5,7},{6,4},{7,5},{8,10},{9,11},{10,... | collective-permute-start | bytes 393224 | tf_op jit(solution)/shard_map/ppermute | solution.py:442
  62.4 7.2 %collective-permute-start.17 = (bf16[512,256]{1,0:T(8,128)(2,1)S(1)}, bf16[512,256]{1,0:T(8,128)(2,1)S(1)}, u32[]{:S(2)}, u32[]{:S(2)}) collective-permute-start(bf16[512,256]{1,0:T(8,128)(2,1)S(1)} %get-tuple-element.67), channel_id=1, source_target_pairs={{0,1},{1,0},{2,3},{3,2},{4,5},{5,4},{6,7},{7,6},{8,9},{9,8},{10,11... | collective-permute-start | bytes 786440 | tf_op jit(solution)/shard_map/ppermute | solution.py:442

commit v6 on v5

--- a/solution.py
+++ b/solution.py
@@ -24,12 +24,15 @@
     (ACROSS, CORE, OWN, ALONG_CORE, ALONG),
 )
 MIB = 1024 * 1024
-STEP = 0.4
 UP_LIMIT = 58
 BYTES = 1
-XJOIN = 3
-ZJ = 1.5
-XC0 = 0
+XJ = (0, 3, 0, 0)
+ZJ = (1.5, 1.5, 1.5, 1.5)
+XC = (0, 0, 0)
+MC = (1, 1, 1)
+M3 = 1
+PK = 0
+COSTS = (2, 1, 0.4, 0.4, 1, 0.02, 0.1)
 ANYWHERE = pl.BlockSpec(memory_space=pl.ANY)
 VECTOR = pl.BlockSpec(memory_space=pltpu.VMEM)
 SCALAR = pl.BlockSpec(memory_space=pltpu.SMEM)
@@ -136,7 +139,7 @@
         scratch_shapes=[pltpu.VMEM(a.shape, a.dtype) for a in (*given[:5], given[6])]
         + [pltpu.SemaphoreType.DMA((5 + len(SLABS),))],
         compiler_params=pltpu.CompilerParams(vmem_limit_bytes=UP_LIMIT * MIB),
-        cost_estimate=cost(2),
+        cost_estimate=cost(COSTS[0]),
         name="up",
     )(*given)
 
@@ -189,7 +192,7 @@
         ],
         input_output_aliases={5: 0},
         compiler_params=pltpu.CompilerParams(vmem_limit_bytes=16 * MIB),
-        cost_estimate=cost(1),
+        cost_estimate=cost(COSTS[1]),
         name="down",
     )(far_ids, target_basis, leaf_transfer, mid_transfer, coupling, part, *before)
 
@@ -266,7 +269,7 @@
         couple_kernel,
         out_shape=(jax.ShapeDtypeStruct(shape, jnp.float32), jax.ShapeDtypeStruct(shape, jnp.bfloat16)),
         compiler_params=pltpu.CompilerParams(vmem_limit_bytes=16 * MIB),
-        cost_estimate=cost(0.1),
+        cost_estimate=cost(COSTS[6]),
         name="couple",
     )(own, carrier, core, *panels)
 
@@ -296,7 +299,7 @@
         in_specs=[SCALAR] + [VECTOR] * (1 + len(panels)) + [ANYWHERE] * len(before),
         out_shape=(shape, shape, jax.ShapeDtypeStruct((2 * LEAF + further, width), arrived.dtype)),
         compiler_params=pltpu.CompilerParams(vmem_limit_bytes=8 * MIB),
-        cost_estimate=cost(0.02),
+        cost_estimate=cost(COSTS[5]),
         name="pack",
     )(wish, arrived, *panels, *before)
 
@@ -339,7 +342,7 @@
         scratch_shapes=[pltpu.VMEM((HELD * LEAF, width), jnp.bfloat16)],
         out_shape=jax.ShapeDtypeStruct((ROWS, width), jnp.float32),
         compiler_params=pltpu.CompilerParams(vmem_limit_bytes=16 * MIB),
-        cost_estimate=cost(STEP),
+        cost_estimate=cost(COSTS[2]),
         name="near",
     )(entry, near_blocks, *pieces, *before)
 
@@ -377,7 +380,7 @@
         out_shape=jax.ShapeDtypeStruct(product.shape, product.dtype),
         input_output_aliases={len(given) - 1: 0},
         compiler_params=pltpu.CompilerParams(vmem_limit_bytes=16 * MIB),
-        cost_estimate=cost(1),
+        cost_estimate=cost(COSTS[4]),
         name="last",
     )(*given)
 
@@ -416,7 +419,7 @@
         ],
         out_shape=jax.ShapeDtypeStruct((ROWS, columns), jnp.bfloat16),
         compiler_params=pltpu.CompilerParams(vmem_limit_bytes=16 * MIB),
-        cost_estimate=cost(STEP),
+        cost_estimate=cost(COSTS[3]),
         name="finish",
     )(*given)
 
@@ -469,29 +472,33 @@
 
     nears, along, across_core = [], [], []
 
+    def marked(microseconds, *values):
+        return [join(microseconds, *values)] if microseconds else []
+
     def pieces(k):
         return (parts[k], rhs_core, across[k], across_core[k], *along[k])
 
     for k in range(len(SLABS)):
         if k >= 2:
-            nears.append(near(*SLABS[k - 2], entry, near_blocks, pieces(k - 2), nears[-1:] + [join(ZJ, *along[k - 2])]))
-        panels = [panel, *others] if k == 0 else []
-        before = nears[-1:] + (across_core[:1] if k == 1 and XC0 else [])
-        if k == 1 and XJOIN:
-            before.append(join(XJOIN, across[1]))
+            nears.append(near(*SLABS[k - 2], entry, near_blocks, pieces(k - 2), nears[-1:] + marked(ZJ[k - 2], *along[k - 2])))
+        panels = [panel, *others] if k == PK else []
+        before = nears[-1:] + marked(XJ[k], across[k])
+        if k and XC[k - 1]:
+            before.append(across_core[k - 1])
         picks = list(pack(wish, across[k], panels, before))
         along.append([permute(picks[0], along_pairs), permute(picks[1], along_core_pairs)])
-        if k >= 1:
+        if k and MC[k - 1]:
             picks[2], along[k - 1][0] = meet(picks[2], along[k - 1][0])
         across_core.append(permute(picks[2], core_pairs))
         if k == 1:
-            parts[3], along[0][1] = meet(parts[3], along[0][1])
+            if M3:
+                parts[3], along[0][M3 - 1] = meet(parts[3], along[0][M3 - 1])
             across.append(permute(parts[3], across_pairs))
-    own_sum, partner_sum = couple(placed, across[CARRIER], across_core[0], panel, *others)
+    own_sum, partner_sum = couple(placed, across[CARRIER], across_core[PK], panel, *others)
     sums = (own_sum, permute(partner_sum, across_pairs))
-    nears.append(near(*SLABS[2], entry, near_blocks, pieces(2), nears[-1:] + [join(ZJ, *along[2])]))
+    nears.append(near(*SLABS[2], entry, near_blocks, pieces(2), nears[-1:] + marked(ZJ[2], *along[2])))
     product = finish(SLABS[:-1], sums, down_basis, nears)
-    return last(*SLABS[-1], entry, near_blocks, sums, down_basis, pieces(3), join(ZJ, *along[3]), product)
+    return last(*SLABS[-1], entry, near_blocks, sums, down_basis, pieces(3), join(ZJ[3], *along[3]), product)
 
 
 def solution(mesh):

time: 73.3 us -> 71.9 us (0.981)
  local copies, waits for them, and re-layouts: 2.94 us -> 2.04 us
  starting transfers between devices: 24.9 us -> 24 us
    ppermute x22, starting transfers between devices: 24.9 us -> 24 us  [on_device(): permute = lambda value, pairs: lax.ppermute(value, 'pts', pairs)]
    unnamed x28, local copies, waits for them, and re-layouts: 1.86 us -> 0.96 us
  transfers between devices with their start and end apart: 22 -> 22, of which waited for: 11 -> 9; matrix products, arithmetic and copies ran while one was open for 1% -> 2% of each run, Pallas kernels for 26% -> 26%
where the time goes in v6:
time: 71.9 us; the launch traced here: 71.6 us
  starting transfers between devices  24 us (33%)
  waiting for transfers between devices  23.1 us (32%)
  Pallas kernels  22.1 us (31%)
  local copies, waits for them, and re-layouts  2.04 us (3%)
    ppermute x22, starting transfers between devices, on_device(): permute = lambda value, pairs: lax.ppermute(value, 'pts', pairs)  24 us
    ppermute x22, waiting for transfers between devices, on_device(): permute = lambda value, pairs: lax.ppermute(value, 'pts', pairs)  23.1 us
    pallas_call x3, Pallas kernels, near(): pl.pallas_call(functools.partial(near_kernel, start), in_specs=[SCALAR] +...  8.17 us
    pallas_call x1, Pallas kernels, up(): pl.pallas_call(functools.partial(up_kernel, members), in_specs=[ANYWHERE]...  3.56 us
    pallas_call x1, Pallas kernels, last(): pl.pallas_call(functools.partial(last_kernel, start, width), in_specs=[SC...  3.41 us
    pallas_call x4, Pallas kernels, pack(): pl.pallas_call(functools.partial(pack_kernel, len(panels)), in_specs=[SCA...  2.43 us
    pallas_call x1, Pallas kernels, down(): pl.pallas_call(functools.partial(down_kernel, reach, members), in_specs=[...  1.84 us
    pallas_call x1, Pallas kernels, finish(): pl.pallas_call(functools.partial(finish_kernel, slabs), in_specs=[VECTOR]...  1.47 us
  transfers between devices with their start and end apart: 22, of which 9 were waited for; matrix products, arithmetic and copies ran while one was open for 2% of the time, Pallas kernels for 26%

profile of v6, /device:TPU:0, one launch (start us, length us, event | category | flops | bytes accessed | tf_op | source)
XLA Modules:
  0.0 71.6 jit_solution(14410359078412539448)
XLA Ops:
  0.0 0.5 collective-permute-start.4
  0.5 1.1 %slice.3.refs_6_.rest_0_ = bf16[1024,256]{1,0:T(8,128)(2,1)S(1)} slice(bf16[1024,1024]{1,0:T(8,128)(2,1)} %refs_5_.1), slice={[0:1024], [0:256]} | slice | bytes 1048576 | tf_op jit(solution)/shard_map/slice | solution.py:451
  1.5 0.0 copy-start
  1.5 2.6 %collective-permute-start.1 = (bf16[1024,256]{1,0:T(8,128)(2,1)S(1)}, bf16[1024,256]{1,0:T(8,128)(2,1)S(1)}, u32[]{:S(2)}, u32[]{:S(2)}) collective-permute-start(bf16[1024,256]{1,0:T(8,128)(2,1)S(1)} %slice.3.refs_6_.rest_0_), channel_id=1, source_target_pairs={{0,2},{1,3},{2,0},{3,1},{4,6},{5,7},{6,4},{7,5},{8,10},{9,11},{10,... | collective-permute-start | bytes 1572872 | tf_op jit(solution)/shard_map/ppermute | solution.py:445
  4.1 0.0 copy-start.10
  4.1 0.0 copy-start.11
  4.1 3.6 %up.1 = (bf16[80,1024]{1,0:T(8,128)(2,1)}, s32[4,12]{1,0:T(4,128)}, bf16[1024,256]{1,0:T(8,128)(2,1)}, bf16[1152,256]{1,0:T(8,128)(2,1)}, bf16[1024,256]{1,0:T(8,128)(2,1)}) custom-call(bf16[4,64,256]{2,1,0:T(8,128)(2,1)} %refs_0_.1, bf16[4,64,64]{2,1,0:T(8,128)(2,1)} %leaf_ref.1, bf16[2,64,64]{2,1,0:T(8,128)(2,1)} %mid_ref.1, s32[4,12]{1,0:T(4,128)} %refs_3_.1, ...), custom_call_target="tpu_custom_call" | custom-call | flops 2300000000 | bytes 1048576 | tf_op jit(solution)/shard_map/up/pallas_call | solution.py:131
  7.7 3.7 %collective-permute-start.2 = (bf16[80,1024]{1,0:T(8,128)(2,1)}, bf16[80,1024]{1,0:T(8,128)(2,1)S(1)}, u32[]{:S(2)}, u32[]{:S(2)}) collective-permute-start(bf16[80,1024]{1,0:T(8,128)(2,1)} %get-tuple-element.44.rest_1_.panel_ref.rest_0_), channel_id=1, source_target_pairs={{0,12},{1,13},{2,14},{3,15},{4,0},{5,1},{6,2},{7,3},{8,4},{9,5},{1... | collective-permute-start | bytes 491528 | tf_op jit(solution)/shard_map/ppermute | solution.py:445
  11.4 0.0 collective-permute-start.3
  11.4 1.0 %collective-permute-start.6 = (bf16[80,1024]{1,0:T(8,128)(2,1)}, bf16[80,1024]{1,0:T(8,128)(2,1)S(1)}, u32[]{:S(2)}, u32[]{:S(2)}) collective-permute-start(bf16[80,1024]{1,0:T(8,128)(2,1)} %get-tuple-element.44.rest_1_.panel_ref.rest_0_), channel_id=1, source_target_pairs={{0,8},{1,9},{2,10},{3,11},{4,12},{5,13},{6,14},{7,15},{8,0},{9,1},... | collective-permute-start | bytes 491528 | tf_op jit(solution)/shard_map/ppermute | solution.py:445
  12.4 3.9 %collective-permute-done.2.ahead_ref.rest_1_ = bf16[80,1024]{1,0:T(8,128)(2,1)S(1)} collective-permute-done((bf16[80,1024]{1,0:T(8,128)(2,1)}, bf16[80,1024]{1,0:T(8,128)(2,1)S(1)}, u32[]{:S(2)}, u32[]{:S(2)}) %collective-permute-start.2) | collective-permute-done | bytes 163872 | tf_op jit(solution)/shard_map/ppermute | solution.py:445
  16.3 0.7 collective-permute-start.9
  16.9 0.0 copy-done.8
  16.9 0.0 copy-done.10
  17.0 0.9 %copy-done.2 = bf16[80,1024]{1,0:T(8,128)(2,1)S(1)} copy-done((bf16[80,1024]{1,0:T(8,128)(2,1)S(1)}, bf16[80,1024]{1,0:T(8,128)(2,1)}, u32[]{:S(2)}) %copy-start.2) | copy-done | bytes 163864
  17.9 1.8 %down.1 = (bf16[1152,256]{1,0:T(8,128)(2,1)}, bf16[4,256,192]{2,1,0:T(8,128)(2,1)S(1)}, bf16[64,512]{1,0:T(8,128)(2,1)S(1)}) custom-call(s32[1,6]{1,0:T(1,128)S(1)} %copy-done.11, bf16[4,64,256]{2,1,0:T(8,128)(2,1)S(1)} %copy-done.7, bf16[4,64,64]{2,1,0:T(8,128)(2,1)S(1)} %copy-done.9, ...), custom_call_target="tpu_custom_call", output_to_operand_aliasing={{0}: (5, {})} | custom-call | flops 1150000000 | bytes 1048576 | tf_op jit(solution)/shard_map/down/pallas_call | solution.py:180
  19.7 0.8 %collective-permute-done.3.behind_ref.rest_2_ = bf16[80,1024]{1,0:T(8,128)(2,1)S(1)} collective-permute-done((bf16[80,1024]{1,0:T(8,128)(2,1)}, bf16[80,1024]{1,0:T(8,128)(2,1)S(1)}, u32[]{:S(2)}, u32[]{:S(2)}) %collective-permute-start.3) | collective-permute-done | bytes 163872 | tf_op jit(solution)/shard_map/ppermute | solution.py:445
  20.5 0.0 collective-permute-done.1.arrived_ref.rest_2_
  20.5 0.0 collective-permute-done.4.rest_0_.rest_1_
  20.6 0.1 collective-permute-start.5
  20.6 1.2 %collective-permute-done.5.core_asked_ref = bf16[32,768]{1,0:T(8,128)(2,1)S(1)} collective-permute-done((bf16[32,768]{1,0:T(8,128)(2,1)S(1)}, bf16[32,768]{1,0:T(8,128)(2,1)S(1)}, u32[]{:S(2)}, u32[]{:S(2)}) %collective-permute-start.5) | collective-permute-done | bytes 49184 | tf_op jit(solution)/shard_map/ppermute | solution.py:445
  21.9 0.7 %wishes.1.wish_ref = s32[1,6]{1,0:T(1,128)S(1)} custom-call(bf16[32,768]{1,0:T(8,128)(2,1)S(1)} %ask.1.asked_ref, bf16[32,768]{1,0:T(8,128)(2,1)S(1)} %collective-permute-done.5.core_asked_ref), custom_call_target="tpu_custom_call" | custom-call | flops 115000000 | bytes 1048576 | tf_op jit(solution)/shard_map/wishes/pallas_call | solution.py:228
  22.6 3.2 %collective-permute-done.6.rest_3_ = bf16[80,1024]{1,0:T(8,128)(2,1)S(1)} collective-permute-done((bf16[80,1024]{1,0:T(8,128)(2,1)}, bf16[80,1024]{1,0:T(8,128)(2,1)S(1)}, u32[]{:S(2)}, u32[]{:S(2)}) %collective-permute-start.6) | collective-permute-done | bytes 163872 | tf_op jit(solution)/shard_map/ppermute | solution.py:445
  25.8 0.6 pack.4
  26.5 0.1 collective-permute-start.7
  26.6 1.1 %collective-permute-start = (bf16[1152,256]{1,0:T(8,128)(2,1)}, bf16[1152,256]{1,0:T(8,128)(2,1)S(1)}, u32[]{:S(2)}, u32[]{:S(2)}) collective-permute-start(bf16[1152,256]{1,0:T(8,128)(2,1)} %get-tuple-element.43.rest_0_), channel_id=1, source_target_pairs={{0,2},{1,3},{2,0},{3,1},{4,6},{5,7},{6,4},{7,5},{8,10},{9,11},{10,... | collective-permute-start | bytes 1769480 | tf_op jit(solution)/shard_map/ppermute | solution.py:445
  27.6 0.0 collective-permute-start.10
  27.6 1.4 %collective-permute-start.13 = (bf16[512,256]{1,0:T(8,128)(2,1)S(1)}, bf16[512,256]{1,0:T(8,128)(2,1)S(1)}, u32[]{:S(2)}, u32[]{:S(2)}) collective-permute-start(bf16[512,256]{1,0:T(8,128)(2,1)S(1)} %get-tuple-element.60), channel_id=1, source_target_pairs={{1,4},{2,15},{5,8},{6,3},{9,12},{10,7},{13,0},{14,11},{17,20},{18,... | collective-permute-start | bytes 786440 | tf_op jit(solution)/shard_map/ppermute | solution.py:445
  29.0 0.0 collective-permute-done.9.refs_0_.arrived_ref.rest_2_
  29.1 0.6 pack.5
  29.7 8.9 %collective-permute-done.10.refs_0_.rest_4_ = bf16[512,256]{1,0:T(8,128)(2,1)S(1)} collective-permute-done((bf16[512,256]{1,0:T(8,128)(2,1)S(1)}, bf16[512,256]{1,0:T(8,128)(2,1)S(1)}, u32[]{:S(2)}, u32[]{:S(2)}) %collective-permute-start.10) | collective-permute-done | bytes 262176 | tf_op jit(solution)/shard_map/ppermute | solution.py:445
  38.6 0.0 collective-permute-start.11
  38.6 0.0 collective-permute-start.14
  38.6 2.0 %collective-permute-done.13.refs_1_.rest_5_ = bf16[512,256]{1,0:T(8,128)(2,1)S(1)} collective-permute-done((bf16[512,256]{1,0:T(8,128)(2,1)S(1)}, bf16[512,256]{1,0:T(8,128)(2,1)S(1)}, u32[]{:S(2)}, u32[]{:S(2)}) %collective-permute-start.13) | collective-permute-done | bytes 262176 | tf_op jit(solution)/shard_map/ppermute | solution.py:445
  40.6 1.4 %collective-permute-start.15 = (bf16[512,256]{1,0:T(8,128)(2,1)S(1)}, bf16[512,256]{1,0:T(8,128)(2,1)S(1)}, u32[]{:S(2)}, u32[]{:S(2)}) collective-permute-start(bf16[512,256]{1,0:T(8,128)(2,1)S(1)} %get-tuple-element.64), channel_id=1, source_target_pairs={{1,4},{2,15},{5,8},{6,3},{9,12},{10,7},{13,0},{14,11},{17,20},{18,... | collective-permute-start | bytes 786440 | tf_op jit(solution)/shard_map/ppermute | solution.py:445
  42.0 0.0 collective-permute-done.7.core_ref.rest_3_
  42.0 0.1 collective-permute-start.12
  42.2 2.5 %near.3.rest_0_.rest_6_ = f32[1024,256]{1,0:T(8,128)S(1)} custom-call(s32[4,12]{1,0:T(4,128)S(1)} %copy-done.6, bf16[4,12,256,256]{3,2,1,0:T(8,128)(2,1)S(1)} %bitcast.3, bf16[1024,256]{1,0:T(8,128)(2,1)S(1)} %copy-done.1, bf16[1024,1024]{1,0:T(8,128)(2,1)S(1)} %collective-permute-done.4.rest_0_.rest_1_, ...), custom_call_target="tpu_custom_call" | custom-call | flops 460000000 | bytes 1048576 | tf_op jit(solution)/shard_map/near/pallas_call | solution.py:338
  44.7 0.0 collective-permute-done.carrier_ref.arrived_ref.rest_2_
  44.7 0.6 pack.6
  45.3 2.8 %collective-permute-start.16 = (bf16[512,256]{1,0:T(8,128)(2,1)S(1)}, bf16[512,256]{1,0:T(8,128)(2,1)S(1)}, u32[]{:S(2)}, u32[]{:S(2)}) collective-permute-start(bf16[512,256]{1,0:T(8,128)(2,1)S(1)} %get-tuple-element.66), channel_id=1, source_target_pairs={{0,4},{1,5},{2,14},{3,15},{4,8},{5,9},{6,2},{7,3},{8,12},{9,13},{1... | collective-permute-start | bytes 786440 | tf_op jit(solution)/shard_map/ppermute | solution.py:445
  48.1 0.0 collective-permute-done.14.refs_0_.rest_4_
  48.1 1.3 %collective-permute-start.21 = (bf16[512,256]{1,0:T(8,128)(2,1)S(1)}, bf16[512,256]{1,0:T(8,128)(2,1)S(1)}, u32[]{:S(2)}, u32[]{:S(2)}) collective-permute-start(bf16[512,256]{1,0:T(8,128)(2,1)S(1)} %get-tuple-element.72), channel_id=1, source_target_pairs={{1,4},{2,15},{5,8},{6,3},{9,12},{10,7},{13,0},{14,11},{17,20},{18,... | collective-permute-start | bytes 786440 | tf_op jit(solution)/shard_map/ppermute | solution.py:445
  49.4 0.8 %collective-permute-done.15.refs_1_.rest_5_ = bf16[512,256]{1,0:T(8,128)(2,1)S(1)} collective-permute-done((bf16[512,256]{1,0:T(8,128)(2,1)S(1)}, bf16[512,256]{1,0:T(8,128)(2,1)S(1)}, u32[]{:S(2)}, u32[]{:S(2)}) %collective-permute-start.15) | collective-permute-done | bytes 262176 | tf_op jit(solution)/shard_map/ppermute | solution.py:445
  50.2 0.9 %collective-permute-start.20 = (bf16[512,256]{1,0:T(8,128)(2,1)S(1)}, bf16[512,256]{1,0:T(8,128)(2,1)S(1)}, u32[]{:S(2)}, u32[]{:S(2)}) collective-permute-start(bf16[512,256]{1,0:T(8,128)(2,1)S(1)} %get-tuple-element.70), channel_id=1, source_target_pairs={{0,1},{1,0},{2,3},{3,2},{4,5},{5,4},{6,7},{7,6},{8,9},{9,8},{10,11... | collective-permute-start | bytes 786440 | tf_op jit(solution)/shard_map/ppermute | solution.py:445
  51.2 0.0 collective-permute-done.12.rest_3_
  51.2 2.6 %near.4.rest_0_.rest_6_.rest_1_ = f32[1024,256]{1,0:T(8,128)S(1)} custom-call(s32[4,12]{1,0:T(4,128)S(1)} %copy-done.6, bf16[4,12,256,256]{3,2,1,0:T(8,128)(2,1)S(1)} %bitcast.3, bf16[1024,256]{1,0:T(8,128)(2,1)S(1)} %copy-done.5, bf16[1024,1024]{1,0:T(8,128)(2,1)S(1)} %collective-permute-done.4.rest_0_.rest_1_, ...), custom_call_target="tpu_custom_call" | custom-call | flops 460000000 | bytes 1048576 | tf_op jit(solution)/shard_map/near/pallas_call | solution.py:338
  53.7 0.0 collective-permute-done.11.arrived_ref.rest_2_
  53.8 0.6 pack.7
  54.4 2.1 %collective-permute-start.18 = (bf16[512,256]{1,0:T(8,128)(2,1)S(1)}, bf16[512,256]{1,0:T(8,128)(2,1)S(1)}, u32[]{:S(2)}, u32[]{:S(2)}) collective-permute-start(bf16[512,256]{1,0:T(8,128)(2,1)S(1)} %get-tuple-element.68), channel_id=1, source_target_pairs={{0,4},{1,5},{2,14},{3,15},{4,8},{5,9},{6,2},{7,3},{8,12},{9,13},{1... | collective-permute-start | bytes 786440 | tf_op jit(solution)/shard_map/ppermute | solution.py:445
  56.4 1.3 %collective-permute-start.19 = (bf16[512,256]{1,0:T(8,128)(2,1)S(1)}, bf16[512,256]{1,0:T(8,128)(2,1)S(1)}, u32[]{:S(2)}, u32[]{:S(2)}) collective-permute-start(bf16[512,256]{1,0:T(8,128)(2,1)S(1)} %get-tuple-element.69), channel_id=1, source_target_pairs={{1,4},{2,15},{5,8},{6,3},{9,12},{10,7},{13,0},{14,11},{17,20},{18,... | collective-permute-start | bytes 786440 | tf_op jit(solution)/shard_map/ppermute | solution.py:445
  57.7 0.5 couple.1
  58.2 0.0 collective-permute-done.16.refs_0_.rest_4_
  58.2 3.2 %collective-permute-start.8 = (bf16[64,1024]{1,0:T(8,128)(2,1)S(1)}, bf16[64,1024]{1,0:T(8,128)(2,1)S(1)}, u32[]{:S(2)}, u32[]{:S(2)}) collective-permute-start(bf16[64,1024]{1,0:T(8,128)(2,1)S(1)} %get-tuple-element.51), channel_id=1, source_target_pairs={{0,2},{1,3},{2,0},{3,1},{4,6},{5,7},{6,4},{7,5},{8,10},{9,11},{10,... | collective-permute-start | bytes 393224 | tf_op jit(solution)/shard_map/ppermute | solution.py:445
  61.5 0.0 collective-permute-done.21.refs_1_.rest_5_
  61.5 0.0 collective-permute-start.17
  61.5 0.0 collective-permute-done.20.rest_3_
  61.5 3.1 %near.5.rest_2_ = f32[1024,256]{1,0:T(8,128)S(1)} custom-call(s32[4,12]{1,0:T(4,128)S(1)} %copy-done.6, bf16[4,12,256,256]{3,2,1,0:T(8,128)(2,1)S(1)} %bitcast.3, bf16[1152,256]{1,0:T(8,128)(2,1)} %get-tuple-element.43.rest_0_, bf16[1024,1024]{1,0:T(8,128)(2,1)S(1)} %collective-permute-done.4.rest_0_.rest_1_, ...), custom_call_target="tpu_custom_call" | custom-call | flops 460000000 | bytes 1048576 | tf_op jit(solution)/shard_map/near/pallas_call | solution.py:338
  64.6 0.1 collective-permute-done.8.partner_sum_ref
  64.6 1.5 %finish.1.rest_7_ = bf16[1024,1024]{1,0:T(8,128)(2,1)} custom-call(f32[64,1024]{1,0:T(8,128)S(1)} %get-tuple-element.50.own_sum_ref, bf16[64,1024]{1,0:T(8,128)(2,1)S(1)} %collective-permute-done.8.partner_sum_ref, bf16[4,256,192]{2,1,0:T(8,128)(2,1)S(1)} %get-tuple-element.47.rest_1_.down_ref, f32[1024,256]{1,0:T(8,128)S(1)} %near.3.rest_0_.rest_6_, ...), custom_call_target="tpu_custom_call" | custom-call | flops 460000000 | bytes 1048576 | tf_op jit(solution)/shard_map/finish/pallas_call | solution.py:412
  66.1 0.0 collective-permute-done.18.refs_0_.rest_4_
  66.1 2.0 %collective-permute-done.19.refs_1_.rest_5_ = bf16[512,256]{1,0:T(8,128)(2,1)S(1)} collective-permute-done((bf16[512,256]{1,0:T(8,128)(2,1)S(1)}, bf16[512,256]{1,0:T(8,128)(2,1)S(1)}, u32[]{:S(2)}, u32[]{:S(2)}) %collective-permute-start.19) | collective-permute-done | bytes 262176 | tf_op jit(solution)/shard_map/ppermute | solution.py:445
  68.2 0.0 collective-permute-done.17.rest_3_
  68.2 3.4 %last.1 = bf16[1024,1024]{1,0:T(8,128)(2,1)} custom-call(s32[4,12]{1,0:T(4,128)S(1)} %copy-done.6, bf16[4,12,256,256]{3,2,1,0:T(8,128)(2,1)S(1)} %bitcast.3, f32[64,1024]{1,0:T(8,128)S(1)} %get-tuple-element.50.own_sum_ref, bf16[64,1024]{1,0:T(8,128)(2,1)S(1)} %collective-permute-done.8.partner_sum_ref, ...), custom_call_target="tpu_custom_call", output_to_operand_aliasing={{}: (12, {})} | custom-call | flops 1150000000 | bytes 1048576 | tf_op jit(solution)/shard_map/last/pallas_call | solution.py:371
  (29 shorter events, 0.1 us)
Async XLA Ops:
  0.0 20.5 %collective-permute-start.4 = (bf16[1024,1024]{1,0:T(8,128)(2,1)}, bf16[1024,1024]{1,0:T(8,128)(2,1)S(1)}, u32[]{:S(2)}, u32[]{:S(2)}) collective-permute-start(bf16[1024,1024]{1,0:T(8,128)(2,1)} %refs_5_.1), channel_id=1, source_target_pairs={{0,1},{1,0},{2,3},{3,2},{4,5},{5,4},{6,7},{7,6},{8,9},{9,8},{10,11... | collective-permute-start | bytes 6291464 | tf_op jit(solution)/shard_map/ppermute | solution.py:445
  1.5 2.6 %copy-start = (bf16[1024,256]{1,0:T(8,128)(2,1)}, bf16[1024,256]{1,0:T(8,128)(2,1)S(1)}, u32[]{:S(2)}) copy-start(bf16[1024,256]{1,0:T(8,128)(2,1)S(1)} %slice.3.refs_6_.rest_0_) | copy-start | bytes 1572868
  1.5 19.0 %collective-permute-start.1 = (bf16[1024,256]{1,0:T(8,128)(2,1)S(1)}, bf16[1024,256]{1,0:T(8,128)(2,1)S(1)}, u32[]{:S(2)}, u32[]{:S(2)}) collective-permute-start(bf16[1024,256]{1,0:T(8,128)(2,1)S(1)} %slice.3.refs_6_.rest_0_), channel_id=1, source_target_pairs={{0,2},{1,3},{2,0},{3,1},{4,6},{5,7},{6,4},{7,5},{8,10},{9,11},{10,... | collective-permute-start | bytes 1572872 | tf_op jit(solution)/shard_map/ppermute | solution.py:445
  4.1 12.8 %copy-start.7 = (bf16[4,64,256]{2,1,0:T(8,128)(2,1)S(1)}, bf16[4,64,256]{2,1,0:T(8,128)(2,1)}, u32[]{:S(2)}) copy-start(bf16[4,64,256]{2,1,0:T(8,128)(2,1)} %target_ref.1) | copy-start | bytes 393220
  4.1 12.8 %copy-start.8 = (bf16[1,6,64,64]{3,2,1,0:T(8,128)(2,1)S(1)}, bf16[1,6,64,64]{3,2,1,0:T(8,128)(2,1)}, u32[]{:S(2)}) copy-start(bf16[1,6,64,64]{3,2,1,0:T(8,128)(2,1)} %param.18) | copy-start | bytes 147460
  4.1 12.8 %copy-start.9 = (bf16[4,64,64]{2,1,0:T(8,128)(2,1)S(1)}, bf16[4,64,64]{2,1,0:T(8,128)(2,1)}, u32[]{:S(2)}) copy-start(bf16[4,64,64]{2,1,0:T(8,128)(2,1)} %leaf_ref.1) | copy-start | bytes 98308
  4.1 12.8 %copy-start.10 = (bf16[2,64,64]{2,1,0:T(8,128)(2,1)S(1)}, bf16[2,64,64]{2,1,0:T(8,128)(2,1)}, u32[]{:S(2)}) copy-start(bf16[2,64,64]{2,1,0:T(8,128)(2,1)} %mid_ref.1) | copy-start | bytes 49156
  4.1 12.8 %copy-start.11 = (s32[1,6]{1,0:T(1,128)S(1)}, s32[1,6]{1,0:T(1,128)}, u32[]{:S(2)}) copy-start(s32[1,6]{1,0:T(1,128)} %far_ref.1) | copy-start | bytes 76
  7.7 8.6 %collective-permute-start.2 = (bf16[80,1024]{1,0:T(8,128)(2,1)}, bf16[80,1024]{1,0:T(8,128)(2,1)S(1)}, u32[]{:S(2)}, u32[]{:S(2)}) collective-permute-start(bf16[80,1024]{1,0:T(8,128)(2,1)} %get-tuple-element.44.rest_1_.panel_ref.rest_0_), channel_id=1, source_target_pairs={{0,12},{1,13},{2,14},{3,15},{4,0},{5,1},{6,2},{7,3},{8,4},{9,5},{1... | collective-permute-start | bytes 491528 | tf_op jit(solution)/shard_map/ppermute | solution.py:445
  11.4 9.2 %collective-permute-start.3 = (bf16[80,1024]{1,0:T(8,128)(2,1)}, bf16[80,1024]{1,0:T(8,128)(2,1)S(1)}, u32[]{:S(2)}, u32[]{:S(2)}) collective-permute-start(bf16[80,1024]{1,0:T(8,128)(2,1)} %get-tuple-element.44.rest_1_.panel_ref.rest_0_), channel_id=1, source_target_pairs={{0,4},{1,5},{2,6},{3,7},{4,8},{5,9},{6,10},{7,11},{8,12},{9,13},{1... | collective-permute-start | bytes 491528 | tf_op jit(solution)/shard_map/ppermute | solution.py:445
  11.4 14.5 %collective-permute-start.6 = (bf16[80,1024]{1,0:T(8,128)(2,1)}, bf16[80,1024]{1,0:T(8,128)(2,1)S(1)}, u32[]{:S(2)}, u32[]{:S(2)}) collective-permute-start(bf16[80,1024]{1,0:T(8,128)(2,1)} %get-tuple-element.44.rest_1_.panel_ref.rest_0_), channel_id=1, source_target_pairs={{0,8},{1,9},{2,10},{3,11},{4,12},{5,13},{6,14},{7,15},{8,0},{9,1},... | collective-permute-start | bytes 491528 | tf_op jit(solution)/shard_map/ppermute | solution.py:445
  16.3 12.8 %collective-permute-start.9 = (bf16[1024,256]{1,0:T(8,128)(2,1)}, bf16[1024,256]{1,0:T(8,128)(2,1)S(1)}, u32[]{:S(2)}, u32[]{:S(2)}) collective-permute-start(bf16[1024,256]{1,0:T(8,128)(2,1)} %get-tuple-element.53.rest_0_), channel_id=1, source_target_pairs={{0,2},{1,3},{2,0},{3,1},{4,6},{5,7},{6,4},{7,5},{8,10},{9,11},{10,... | collective-permute-start | bytes 1572872 | tf_op jit(solution)/shard_map/ppermute | solution.py:445
  17.0 0.9 %copy-start.2 = (bf16[80,1024]{1,0:T(8,128)(2,1)S(1)}, bf16[80,1024]{1,0:T(8,128)(2,1)}, u32[]{:S(2)}) copy-start(bf16[80,1024]{1,0:T(8,128)(2,1)} %get-tuple-element.44.rest_1_.panel_ref.rest_0_) | copy-start | bytes 491524
  20.6 1.3 %collective-permute-start.5 = (bf16[32,768]{1,0:T(8,128)(2,1)S(1)}, bf16[32,768]{1,0:T(8,128)(2,1)S(1)}, u32[]{:S(2)}, u32[]{:S(2)}) collective-permute-start(bf16[32,768]{1,0:T(8,128)(2,1)S(1)} %ask.1.asked_ref), channel_id=1, source_target_pairs={{0,1},{1,0},{2,3},{3,2},{4,5},{5,4},{6,7},{7,6},{8,9},{9,8},{10,11... | collective-permute-start | bytes 147464 | tf_op jit(solution)/shard_map/ppermute | solution.py:445
  25.8 16.3 %slice-start = ((s8[6291456]{0:T(1024)(128)(4,1)}), s8[4194304]{0:T(1024)(128)(4,1)S(1)}, s32[]{:S(2)}) async-start(s8[6291456]{0:T(1024)(128)(4,1)} %bitcast.2), calls=%async_computation | async-start | bytes 8388608
  26.5 15.5 %collective-permute-start.7 = (bf16[1536,256]{1,0:T(8,128)(2,1)S(1)}, bf16[1536,256]{1,0:T(8,128)(2,1)S(1)}, u32[]{:S(2)}, u32[]{:S(2)}) collective-permute-start(bf16[1536,256]{1,0:T(8,128)(2,1)S(1)} %get-tuple-element.49), channel_id=1, source_target_pairs={{0,1},{1,0},{2,3},{3,2},{4,5},{5,4},{6,7},{7,6},{8,9},{9,8},{10,11... | collective-permute-start | bytes 2359304 | tf_op jit(solution)/shard_map/ppermute | solution.py:445
  26.6 18.2 %collective-permute-start = (bf16[1152,256]{1,0:T(8,128)(2,1)}, bf16[1152,256]{1,0:T(8,128)(2,1)S(1)}, u32[]{:S(2)}, u32[]{:S(2)}) collective-permute-start(bf16[1152,256]{1,0:T(8,128)(2,1)} %get-tuple-element.43.rest_0_), channel_id=1, source_target_pairs={{0,2},{1,3},{2,0},{3,1},{4,6},{5,7},{6,4},{7,5},{8,10},{9,11},{10,... | collective-permute-start | bytes 1769480 | tf_op jit(solution)/shard_map/ppermute | solution.py:445
  27.6 10.9 %collective-permute-start.10 = (bf16[512,256]{1,0:T(8,128)(2,1)S(1)}, bf16[512,256]{1,0:T(8,128)(2,1)S(1)}, u32[]{:S(2)}, u32[]{:S(2)}) collective-permute-start(bf16[512,256]{1,0:T(8,128)(2,1)S(1)} %get-tuple-element.55), channel_id=1, source_target_pairs={{0,4},{1,5},{2,14},{3,15},{4,8},{5,9},{6,2},{7,3},{8,12},{9,13},{1... | collective-permute-start | bytes 786440 | tf_op jit(solution)/shard_map/ppermute | solution.py:445
  27.6 10.9 %copy-start.4 = (bf16[1024,256]{1,0:T(8,128)(2,1)S(1)}, bf16[1024,256]{1,0:T(8,128)(2,1)}, u32[]{:S(2)}) copy-start(bf16[1024,256]{1,0:T(8,128)(2,1)} %get-tuple-element.57.rest_0_) | copy-start | bytes 1572868
  27.6 14.5 %slice-start.1 = ((s8[6291456]{0:T(1024)(128)(4,1)}), s8[2097152]{0:T(1024)(128)(4,1)S(1)}, s32[]{:S(2)}) async-start(s8[6291456]{0:T(1024)(128)(4,1)} %bitcast.2), calls=%async_computation.1 | async-start | bytes 4194304
  27.6 13.0 %collective-permute-start.13 = (bf16[512,256]{1,0:T(8,128)(2,1)S(1)}, bf16[512,256]{1,0:T(8,128)(2,1)S(1)}, u32[]{:S(2)}, u32[]{:S(2)}) collective-permute-start(bf16[512,256]{1,0:T(8,128)(2,1)S(1)} %get-tuple-element.60), channel_id=1, source_target_pairs={{1,4},{2,15},{5,8},{6,3},{9,12},{10,7},{13,0},{14,11},{17,20},{18,... | collective-permute-start | bytes 786440 | tf_op jit(solution)/shard_map/ppermute | solution.py:445
  38.6 15.2 %collective-permute-start.11 = (bf16[1024,256]{1,0:T(8,128)(2,1)S(1)}, bf16[1024,256]{1,0:T(8,128)(2,1)S(1)}, u32[]{:S(2)}, u32[]{:S(2)}) collective-permute-start(bf16[1024,256]{1,0:T(8,128)(2,1)S(1)} %copy-done.4), channel_id=1, source_target_pairs={{0,2},{1,3},{2,0},{3,1},{4,6},{5,7},{6,4},{7,5},{8,10},{9,11},{10,... | collective-permute-start | bytes 1572872 | tf_op jit(solution)/shard_map/ppermute | solution.py:445
  38.6 9.5 %collective-permute-start.14 = (bf16[512,256]{1,0:T(8,128)(2,1)S(1)}, bf16[512,256]{1,0:T(8,128)(2,1)S(1)}, u32[]{:S(2)}, u32[]{:S(2)}) collective-permute-start(bf16[512,256]{1,0:T(8,128)(2,1)S(1)} %get-tuple-element.62), channel_id=1, source_target_pairs={{0,4},{1,5},{2,14},{3,15},{4,8},{5,9},{6,2},{7,3},{8,12},{9,13},{1... | collective-permute-start | bytes 786440 | tf_op jit(solution)/shard_map/ppermute | solution.py:445
  40.6 1.5 %copy-start.1 = (bf16[1024,256]{1,0:T(8,128)(2,1)S(1)}, bf16[1024,256]{1,0:T(8,128)(2,1)}, u32[]{:S(2)}) copy-start(bf16[1024,256]{1,0:T(8,128)(2,1)} %copy-done) | copy-start | bytes 1572868
  40.6 1.6 %copy-start.6 = (s32[4,12]{1,0:T(4,128)S(1)}, s32[4,12]{1,0:T(4,128)}, u32[]{:S(2)}) copy-start(s32[4,12]{1,0:T(4,128)} %get-tuple-element.39.entry_ref) | copy-start | bytes 580
  40.6 9.6 %collective-permute-start.15 = (bf16[512,256]{1,0:T(8,128)(2,1)S(1)}, bf16[512,256]{1,0:T(8,128)(2,1)S(1)}, u32[]{:S(2)}, u32[]{:S(2)}) collective-permute-start(bf16[512,256]{1,0:T(8,128)(2,1)S(1)} %get-tuple-element.64), channel_id=1, source_target_pairs={{1,4},{2,15},{5,8},{6,3},{9,12},{10,7},{13,0},{14,11},{17,20},{18,... | collective-permute-start | bytes 786440 | tf_op jit(solution)/shard_map/ppermute | solution.py:445
  42.0 9.1 %collective-permute-start.12 = (bf16[512,256]{1,0:T(8,128)(2,1)S(1)}, bf16[512,256]{1,0:T(8,128)(2,1)S(1)}, u32[]{:S(2)}, u32[]{:S(2)}) collective-permute-start(bf16[512,256]{1,0:T(8,128)(2,1)S(1)} %get-tuple-element.58), channel_id=1, source_target_pairs={{0,1},{1,0},{2,3},{3,2},{4,5},{5,4},{6,7},{7,6},{8,9},{9,8},{10,11... | collective-permute-start | bytes 786440 | tf_op jit(solution)/shard_map/ppermute | solution.py:445
  45.3 12.9 %collective-permute-start.16 = (bf16[512,256]{1,0:T(8,128)(2,1)S(1)}, bf16[512,256]{1,0:T(8,128)(2,1)S(1)}, u32[]{:S(2)}, u32[]{:S(2)}) collective-permute-start(bf16[512,256]{1,0:T(8,128)(2,1)S(1)} %get-tuple-element.66), channel_id=1, source_target_pairs={{0,4},{1,5},{2,14},{3,15},{4,8},{5,9},{6,2},{7,3},{8,12},{9,13},{1... | collective-permute-start | bytes 786440 | tf_op jit(solution)/shard_map/ppermute | solution.py:445
  48.1 13.3 %collective-permute-start.21 = (bf16[512,256]{1,0:T(8,128)(2,1)S(1)}, bf16[512,256]{1,0:T(8,128)(2,1)S(1)}, u32[]{:S(2)}, u32[]{:S(2)}) collective-permute-start(bf16[512,256]{1,0:T(8,128)(2,1)S(1)} %get-tuple-element.72), channel_id=1, source_target_pairs={{1,4},{2,15},{5,8},{6,3},{9,12},{10,7},{13,0},{14,11},{17,20},{18,... | collective-permute-start | bytes 786440 | tf_op jit(solution)/shard_map/ppermute | solution.py:445
  49.4 1.8 %copy-start.5 = (bf16[1024,256]{1,0:T(8,128)(2,1)S(1)}, bf16[1024,256]{1,0:T(8,128)(2,1)}, u32[]{:S(2)}) copy-start(bf16[1024,256]{1,0:T(8,128)(2,1)} %get-tuple-element.53.rest_0_) | copy-start | bytes 1572868
  50.2 11.3 %collective-permute-start.20 = (bf16[512,256]{1,0:T(8,128)(2,1)S(1)}, bf16[512,256]{1,0:T(8,128)(2,1)S(1)}, u32[]{:S(2)}, u32[]{:S(2)}) collective-permute-start(bf16[512,256]{1,0:T(8,128)(2,1)S(1)} %get-tuple-element.70), channel_id=1, source_target_pairs={{0,1},{1,0},{2,3},{3,2},{4,5},{5,4},{6,7},{7,6},{8,9},{9,8},{10,11... | collective-permute-start | bytes 786440 | tf_op jit(solution)/shard_map/ppermute | solution.py:445
  51.1 6.6 %copy-start.3 = (bf16[80,1024]{1,0:T(8,128)(2,1)S(1)}, bf16[80,1024]{1,0:T(8,128)(2,1)}, u32[]{:S(2)}) copy-start(bf16[80,1024]{1,0:T(8,128)(2,1)} %get-tuple-element.44.rest_1_.panel_ref.rest_0_) | copy-start | bytes 491524
  54.4 11.7 %collective-permute-start.18 = (bf16[512,256]{1,0:T(8,128)(2,1)S(1)}, bf16[512,256]{1,0:T(8,128)(2,1)S(1)}, u32[]{:S(2)}, u32[]{:S(2)}) collective-permute-start(bf16[512,256]{1,0:T(8,128)(2,1)S(1)} %get-tuple-element.68), channel_id=1, source_target_pairs={{0,4},{1,5},{2,14},{3,15},{4,8},{5,9},{6,2},{7,3},{8,12},{9,13},{1... | collective-permute-start | bytes 786440 | tf_op jit(solution)/shard_map/ppermute | solution.py:445
  56.4 11.7 %collective-permute-start.19 = (bf16[512,256]{1,0:T(8,128)(2,1)S(1)}, bf16[512,256]{1,0:T(8,128)(2,1)S(1)}, u32[]{:S(2)}, u32[]{:S(2)}) collective-permute-start(bf16[512,256]{1,0:T(8,128)(2,1)S(1)} %get-tuple-element.69), channel_id=1, source_target_pairs={{1,4},{2,15},{5,8},{6,3},{9,12},{10,7},{13,0},{14,11},{17,20},{18,... | collective-permute-start | bytes 786440 | tf_op jit(solution)/shard_map/ppermute | solution.py:445
  58.2 6.4 %collective-permute-start.8 = (bf16[64,1024]{1,0:T(8,128)(2,1)S(1)}, bf16[64,1024]{1,0:T(8,128)(2,1)S(1)}, u32[]{:S(2)}, u32[]{:S(2)}) collective-permute-start(bf16[64,1024]{1,0:T(8,128)(2,1)S(1)} %get-tuple-element.51), channel_id=1, source_target_pairs={{0,2},{1,3},{2,0},{3,1},{4,6},{5,7},{6,4},{7,5},{8,10},{9,11},{10,... | collective-permute-start | bytes 393224 | tf_op jit(solution)/shard_map/ppermute | solution.py:445
  61.5 6.7 %collective-permute-start.17 = (bf16[512,256]{1,0:T(8,128)(2,1)S(1)}, bf16[512,256]{1,0:T(8,128)(2,1)S(1)}, u32[]{:S(2)}, u32[]{:S(2)}) collective-permute-start(bf16[512,256]{1,0:T(8,128)(2,1)S(1)} %get-tuple-element.67), channel_id=1, source_target_pairs={{0,1},{1,0},{2,3},{3,2},{4,5},{5,4},{6,7},{7,6},{8,9},{9,8},{10,11... | collective-permute-start | bytes 786440 | tf_op jit(solution)/shard_map/ppermute | solution.py:445

commit v7 on v6

--- a/solution.py
+++ b/solution.py
@@ -92,8 +92,8 @@
 
 def up_kernel(members, *refs):
     given, rest = refs[:7], refs[7:]
-    panel_ref, entry_ref, *parts = rest[: 1 + len(SLABS)]
-    *kept, first_ref, sems = rest[1 + len(SLABS) :]
+    panel_ref, plain_ref, entry_ref, *parts = rest[: 2 + len(SLABS)]
+    *kept, first_ref, sems = rest[2 + len(SLABS) :]
     pairs = list(zip(given[:5], kept))
     pairs += [
         (given[5].at[:, pl.ds(start, width)], part.at[pl.ds(0, ROWS)])
@@ -121,7 +121,9 @@
     for copy, (start, width), part in zip(copies[5:], SLABS[1:] + SLABS[:1], [*parts, first_ref]):
         copy.wait()
         sums = dot(both, part[pl.ds(0, ROWS)])
-        panel_ref[pl.ds(0, RANK), pl.ds(start, width)] = (sums[:RANK] + sums[RANK:]).astype(jnp.bfloat16)
+        made = (sums[:RANK] + sums[RANK:]).astype(jnp.bfloat16)
+        panel_ref[pl.ds(0, RANK), pl.ds(start, width)] = made
+        plain_ref[:, pl.ds(start, width)] = made
 
 
 def up(members, carried, *given):
@@ -133,6 +135,7 @@
         in_specs=[ANYWHERE] * len(given),
         out_shape=(
             jax.ShapeDtypeStruct((RANK + WISH, columns), jnp.bfloat16),
+            jax.ShapeDtypeStruct((RANK, columns), jnp.bfloat16),
             jax.ShapeDtypeStruct((B_DEV, NEAR), jnp.int32),
             *[jax.ShapeDtypeStruct(shape, jnp.bfloat16) for shape in shapes[1:]],
         ),
@@ -449,7 +452,7 @@
 
     rhs_core = permute(rhs, core_pairs)
     first = rhs[:, : SLABS[0][1]]
-    panel, entry, *parts = up(
+    panel, plain, entry, *parts = up(
         members,
         2 * len(reach) * RANK,
         source_basis,
@@ -465,7 +468,9 @@
         reach, members, far_ids, target_basis, leaf_transfer, mid_transfer, far_coupling[0], parts[CARRIER], panel
     )
     across = [permute(part, across_pairs) for part in parts[:3]]
-    others = [permute(panel, [(i, (i - 4 * step) % members) for i in every]) for step in reach[1:]]
+    back = lambda step: [(i, (i - 4 * step) % members) for i in every]
+    others = [permute(panel, back(step)) for step in reach[1:3]]
+    others += [permute(plain, back(step)) for step in reach[3:]]
     across[0], panel, others[0], others[1] = meet(across[0], panel, others[0], others[1])
     asked = ask(panel, others[0], others[1], rhs_core, down_basis)
     wish = wishes(asked, permute(asked, core_pairs))

time: 71.9 us -> 70.5 us (0.981)
  waiting for transfers between devices: 23.1 us -> 21.4 us
    ppermute x22, waiting for transfers between devices: 23.1 us -> 21.4 us  [on_device(): permute = lambda value, pairs: lax.ppermute(value, 'pts', pairs)]
  transfers between devices with their start and end apart: 22 -> 22, of which waited for: 9 -> 10; matrix products, arithmetic and copies ran while one was open for 2% -> 2% of each run, Pallas kernels for 26% -> 27%
where the time goes in v7:
time: 70.5 us; the launch traced here: 70.2 us
  starting transfers between devices  24.3 us (34%)
  Pallas kernels  22.2 us (31%)
  waiting for transfers between devices  21.4 us (30%)
  local copies, waits for them, and re-layouts  2.04 us (3%)
    ppermute x22, starting transfers between devices, on_device(): permute = lambda value, pairs: lax.ppermute(value, 'pts', pairs)  24.3 us
    ppermute x22, waiting for transfers between devices, on_device(): permute = lambda value, pairs: lax.ppermute(value, 'pts', pairs)  21.4 us
    pallas_call x3, Pallas kernels, near(): pl.pallas_call(functools.partial(near_kernel, start), in_specs=[SCALAR] +...  8.18 us
    pallas_call x1, Pallas kernels, up(): pl.pallas_call(functools.partial(up_kernel, members), in_specs=[ANYWHERE]...  3.6 us
    pallas_call x1, Pallas kernels, last(): pl.pallas_call(functools.partial(last_kernel, start, width), in_specs=[SC...  3.41 us
    pallas_call x4, Pallas kernels, pack(): pl.pallas_call(functools.partial(pack_kernel, len(panels)), in_specs=[SCA...  2.43 us
    pallas_call x1, Pallas kernels, down(): pl.pallas_call(functools.partial(down_kernel, reach, members), in_specs=[...  1.84 us
    pallas_call x1, Pallas kernels, finish(): pl.pallas_call(functools.partial(finish_kernel, slabs), in_specs=[VECTOR]...  1.48 us
  transfers between devices with their start and end apart: 22, of which 10 were waited for; matrix products, arithmetic and copies ran while one was open for 2% of the time, Pallas kernels for 27%

profile of v7, /device:TPU:0, one launch (start us, length us, event | category | flops | bytes accessed | tf_op | source)
XLA Modules:
  0.0 70.2 jit_solution(11755675415444168904)
XLA Ops:
  0.0 0.5 collective-permute-start.4
  0.5 1.1 %slice.3.refs_6_.rest_0_ = bf16[1024,256]{1,0:T(8,128)(2,1)S(1)} slice(bf16[1024,1024]{1,0:T(8,128)(2,1)} %refs_5_.1), slice={[0:1024], [0:256]} | slice | bytes 1048576 | tf_op jit(solution)/shard_map/slice | solution.py:454
  1.5 0.0 copy-start
  1.5 2.6 %collective-permute-start.1 = (bf16[1024,256]{1,0:T(8,128)(2,1)S(1)}, bf16[1024,256]{1,0:T(8,128)(2,1)S(1)}, u32[]{:S(2)}, u32[]{:S(2)}) collective-permute-start(bf16[1024,256]{1,0:T(8,128)(2,1)S(1)} %slice.3.refs_6_.rest_0_), channel_id=1, source_target_pairs={{0,2},{1,3},{2,0},{3,1},{4,6},{5,7},{6,4},{7,5},{8,10},{9,11},{10,... | collective-permute-start | bytes 1572872 | tf_op jit(solution)/shard_map/ppermute | solution.py:448
  4.1 0.0 copy-start.10
  4.1 0.0 copy-start.11
  4.1 3.6 %up.1 = (bf16[80,1024]{1,0:T(8,128)(2,1)}, bf16[64,1024]{1,0:T(8,128)(2,1)}, s32[4,12]{1,0:T(4,128)}, bf16[1024,256]{1,0:T(8,128)(2,1)}, bf16[1152,256]{1,0:T(8,128)(2,1)}, /*index=5*/bf16[1024,256]{1,0:T(8,128)(2,1)}) custom-call(bf16[4,64,256]{2,1,0:T(8,128)(2,1)} %refs_0_.1, bf16[4,64,64]{2,1,0:T(8,128)(2,1)} %leaf_ref.1, bf16[2,64,64]{2,1,0:T(8,128)(2,1)} %mid_ref.1, ...), custom_call_target="tpu_custom_call" | custom-call | flops 2300000000 | bytes 1048576 | tf_op jit(solution)/shard_map/up/pallas_call | solution.py:133
  7.7 3.7 %collective-permute-start.2 = (bf16[80,1024]{1,0:T(8,128)(2,1)}, bf16[80,1024]{1,0:T(8,128)(2,1)S(1)}, u32[]{:S(2)}, u32[]{:S(2)}) collective-permute-start(bf16[80,1024]{1,0:T(8,128)(2,1)} %get-tuple-element.45.rest_1_.panel_ref.rest_0_), channel_id=1, source_target_pairs={{0,12},{1,13},{2,14},{3,15},{4,0},{5,1},{6,2},{7,3},{8,4},{9,5},{1... | collective-permute-start | bytes 491528 | tf_op jit(solution)/shard_map/ppermute | solution.py:448
  11.4 0.0 collective-permute-start.3
  11.4 1.0 %collective-permute-start.6 = (bf16[64,1024]{1,0:T(8,128)(2,1)}, bf16[64,1024]{1,0:T(8,128)(2,1)S(1)}, u32[]{:S(2)}, u32[]{:S(2)}) collective-permute-start(bf16[64,1024]{1,0:T(8,128)(2,1)} %get-tuple-element.50), channel_id=1, source_target_pairs={{0,8},{1,9},{2,10},{3,11},{4,12},{5,13},{6,14},{7,15},{8,0},{9,1},... | collective-permute-start | bytes 393224 | tf_op jit(solution)/shard_map/ppermute | solution.py:448
  12.4 3.9 %collective-permute-done.2.ahead_ref.rest_1_ = bf16[80,1024]{1,0:T(8,128)(2,1)S(1)} collective-permute-done((bf16[80,1024]{1,0:T(8,128)(2,1)}, bf16[80,1024]{1,0:T(8,128)(2,1)S(1)}, u32[]{:S(2)}, u32[]{:S(2)}) %collective-permute-start.2) | collective-permute-done | bytes 163872 | tf_op jit(solution)/shard_map/ppermute | solution.py:448
  16.3 0.7 collective-permute-start.9
  17.0 0.0 copy-done.7
  17.0 0.0 copy-done.11
  17.0 0.9 %copy-done.2 = bf16[80,1024]{1,0:T(8,128)(2,1)S(1)} copy-done((bf16[80,1024]{1,0:T(8,128)(2,1)S(1)}, bf16[80,1024]{1,0:T(8,128)(2,1)}, u32[]{:S(2)}) %copy-start.2) | copy-done | bytes 163864
  17.9 1.8 %down.1 = (bf16[1152,256]{1,0:T(8,128)(2,1)}, bf16[4,256,192]{2,1,0:T(8,128)(2,1)S(1)}, bf16[64,512]{1,0:T(8,128)(2,1)S(1)}) custom-call(s32[1,6]{1,0:T(1,128)S(1)} %copy-done.11, bf16[4,64,256]{2,1,0:T(8,128)(2,1)S(1)} %copy-done.7, bf16[4,64,64]{2,1,0:T(8,128)(2,1)S(1)} %copy-done.9, ...), custom_call_target="tpu_custom_call", output_to_operand_aliasing={{0}: (5, {})} | custom-call | flops 1150000000 | bytes 1048576 | tf_op jit(solution)/shard_map/down/pallas_call | solution.py:183
  19.8 0.8 %collective-permute-done.3.behind_ref.rest_2_ = bf16[80,1024]{1,0:T(8,128)(2,1)S(1)} collective-permute-done((bf16[80,1024]{1,0:T(8,128)(2,1)}, bf16[80,1024]{1,0:T(8,128)(2,1)S(1)}, u32[]{:S(2)}, u32[]{:S(2)}) %collective-permute-start.3) | collective-permute-done | bytes 163872 | tf_op jit(solution)/shard_map/ppermute | solution.py:448
  20.6 0.0 collective-permute-done.1.arrived_ref.rest_2_
  20.6 0.0 collective-permute-done.4.rest_0_.rest_1_
  20.6 0.1 collective-permute-start.5
  20.7 1.2 %collective-permute-done.5.core_asked_ref = bf16[32,768]{1,0:T(8,128)(2,1)S(1)} collective-permute-done((bf16[32,768]{1,0:T(8,128)(2,1)S(1)}, bf16[32,768]{1,0:T(8,128)(2,1)S(1)}, u32[]{:S(2)}, u32[]{:S(2)}) %collective-permute-start.5) | collective-permute-done | bytes 49184 | tf_op jit(solution)/shard_map/ppermute | solution.py:448
  21.9 0.7 %wishes.1.wish_ref = s32[1,6]{1,0:T(1,128)S(1)} custom-call(bf16[32,768]{1,0:T(8,128)(2,1)S(1)} %ask.1.asked_ref, bf16[32,768]{1,0:T(8,128)(2,1)S(1)} %collective-permute-done.5.core_asked_ref), custom_call_target="tpu_custom_call" | custom-call | flops 115000000 | bytes 1048576 | tf_op jit(solution)/shard_map/wishes/pallas_call | solution.py:231
  22.6 1.8 %collective-permute-done.6.rest_3_ = bf16[64,1024]{1,0:T(8,128)(2,1)S(1)} collective-permute-done((bf16[64,1024]{1,0:T(8,128)(2,1)}, bf16[64,1024]{1,0:T(8,128)(2,1)S(1)}, u32[]{:S(2)}, u32[]{:S(2)}) %collective-permute-start.6) | collective-permute-done | bytes 131104 | tf_op jit(solution)/shard_map/ppermute | solution.py:448
  24.5 0.6 pack.4
  25.1 0.1 collective-permute-start.7
  25.2 1.0 %collective-permute-start = (bf16[1152,256]{1,0:T(8,128)(2,1)}, bf16[1152,256]{1,0:T(8,128)(2,1)S(1)}, u32[]{:S(2)}, u32[]{:S(2)}) collective-permute-start(bf16[1152,256]{1,0:T(8,128)(2,1)} %get-tuple-element.44.rest_0_), channel_id=1, source_target_pairs={{0,2},{1,3},{2,0},{3,1},{4,6},{5,7},{6,4},{7,5},{8,10},{9,11},{10,... | collective-permute-start | bytes 1769480 | tf_op jit(solution)/shard_map/ppermute | solution.py:448
  26.3 0.0 collective-permute-start.10
  26.3 1.4 %collective-permute-start.13 = (bf16[512,256]{1,0:T(8,128)(2,1)S(1)}, bf16[512,256]{1,0:T(8,128)(2,1)S(1)}, u32[]{:S(2)}, u32[]{:S(2)}) collective-permute-start(bf16[512,256]{1,0:T(8,128)(2,1)S(1)} %get-tuple-element.62), channel_id=1, source_target_pairs={{1,4},{2,15},{5,8},{6,3},{9,12},{10,7},{13,0},{14,11},{17,20},{18,... | collective-permute-start | bytes 786440 | tf_op jit(solution)/shard_map/ppermute | solution.py:448
  27.7 1.8 %collective-permute-done.9.refs_0_.arrived_ref.rest_2_ = bf16[1024,256]{1,0:T(8,128)(2,1)S(1)} collective-permute-done((bf16[1024,256]{1,0:T(8,128)(2,1)}, bf16[1024,256]{1,0:T(8,128)(2,1)S(1)}, u32[]{:S(2)}, u32[]{:S(2)}) %collective-permute-start.9) | collective-permute-done | bytes 524320 | tf_op jit(solution)/shard_map/ppermute | solution.py:448
  29.5 0.6 pack.5
  30.1 7.1 %collective-permute-done.10.refs_0_.rest_4_ = bf16[512,256]{1,0:T(8,128)(2,1)S(1)} collective-permute-done((bf16[512,256]{1,0:T(8,128)(2,1)S(1)}, bf16[512,256]{1,0:T(8,128)(2,1)S(1)}, u32[]{:S(2)}, u32[]{:S(2)}) %collective-permute-start.10) | collective-permute-done | bytes 262176 | tf_op jit(solution)/shard_map/ppermute | solution.py:448
  37.2 0.0 collective-permute-start.11
  37.2 0.0 collective-permute-start.14
  37.2 2.0 %collective-permute-done.13.refs_1_.rest_5_ = bf16[512,256]{1,0:T(8,128)(2,1)S(1)} collective-permute-done((bf16[512,256]{1,0:T(8,128)(2,1)S(1)}, bf16[512,256]{1,0:T(8,128)(2,1)S(1)}, u32[]{:S(2)}, u32[]{:S(2)}) %collective-permute-start.13) | collective-permute-done | bytes 262176 | tf_op jit(solution)/shard_map/ppermute | solution.py:448
  39.2 1.4 %collective-permute-start.15 = (bf16[512,256]{1,0:T(8,128)(2,1)S(1)}, bf16[512,256]{1,0:T(8,128)(2,1)S(1)}, u32[]{:S(2)}, u32[]{:S(2)}) collective-permute-start(bf16[512,256]{1,0:T(8,128)(2,1)S(1)} %get-tuple-element.66), channel_id=1, source_target_pairs={{1,4},{2,15},{5,8},{6,3},{9,12},{10,7},{13,0},{14,11},{17,20},{18,... | collective-permute-start | bytes 786440 | tf_op jit(solution)/shard_map/ppermute | solution.py:448
  40.7 0.0 collective-permute-done.7.core_ref.rest_3_
  40.7 0.1 collective-permute-start.12
  40.8 2.5 %near.3.rest_0_.rest_6_ = f32[1024,256]{1,0:T(8,128)S(1)} custom-call(s32[4,12]{1,0:T(4,128)S(1)} %copy-done.6, bf16[4,12,256,256]{3,2,1,0:T(8,128)(2,1)S(1)} %bitcast.3, bf16[1024,256]{1,0:T(8,128)(2,1)S(1)} %copy-done.1, bf16[1024,1024]{1,0:T(8,128)(2,1)S(1)} %collective-permute-done.4.rest_0_.rest_1_, ...), custom_call_target="tpu_custom_call" | custom-call | flops 460000000 | bytes 1048576 | tf_op jit(solution)/shard_map/near/pallas_call | solution.py:341
  43.4 0.0 collective-permute-done.carrier_ref.arrived_ref.rest_2_
  43.4 0.6 pack.6
  44.0 2.8 %collective-permute-start.16 = (bf16[512,256]{1,0:T(8,128)(2,1)S(1)}, bf16[512,256]{1,0:T(8,128)(2,1)S(1)}, u32[]{:S(2)}, u32[]{:S(2)}) collective-permute-start(bf16[512,256]{1,0:T(8,128)(2,1)S(1)} %get-tuple-element.68), channel_id=1, source_target_pairs={{0,4},{1,5},{2,14},{3,15},{4,8},{5,9},{6,2},{7,3},{8,12},{9,13},{1... | collective-permute-start | bytes 786440 | tf_op jit(solution)/shard_map/ppermute | solution.py:448
  46.8 0.0 collective-permute-done.14.refs_0_.rest_4_
  46.8 1.3 %collective-permute-start.21 = (bf16[512,256]{1,0:T(8,128)(2,1)S(1)}, bf16[512,256]{1,0:T(8,128)(2,1)S(1)}, u32[]{:S(2)}, u32[]{:S(2)}) collective-permute-start(bf16[512,256]{1,0:T(8,128)(2,1)S(1)} %get-tuple-element.74), channel_id=1, source_target_pairs={{1,4},{2,15},{5,8},{6,3},{9,12},{10,7},{13,0},{14,11},{17,20},{18,... | collective-permute-start | bytes 786440 | tf_op jit(solution)/shard_map/ppermute | solution.py:448
  48.1 0.8 %collective-permute-done.15.refs_1_.rest_5_ = bf16[512,256]{1,0:T(8,128)(2,1)S(1)} collective-permute-done((bf16[512,256]{1,0:T(8,128)(2,1)S(1)}, bf16[512,256]{1,0:T(8,128)(2,1)S(1)}, u32[]{:S(2)}, u32[]{:S(2)}) %collective-permute-start.15) | collective-permute-done | bytes 262176 | tf_op jit(solution)/shard_map/ppermute | solution.py:448
  48.9 0.9 %collective-permute-start.20 = (bf16[512,256]{1,0:T(8,128)(2,1)S(1)}, bf16[512,256]{1,0:T(8,128)(2,1)S(1)}, u32[]{:S(2)}, u32[]{:S(2)}) collective-permute-start(bf16[512,256]{1,0:T(8,128)(2,1)S(1)} %get-tuple-element.72), channel_id=1, source_target_pairs={{0,1},{1,0},{2,3},{3,2},{4,5},{5,4},{6,7},{7,6},{8,9},{9,8},{10,11... | collective-permute-start | bytes 786440 | tf_op jit(solution)/shard_map/ppermute | solution.py:448
  49.8 0.0 collective-permute-done.12.rest_3_
  49.8 2.6 %near.4.rest_0_.rest_6_.rest_1_ = f32[1024,256]{1,0:T(8,128)S(1)} custom-call(s32[4,12]{1,0:T(4,128)S(1)} %copy-done.6, bf16[4,12,256,256]{3,2,1,0:T(8,128)(2,1)S(1)} %bitcast.3, bf16[1024,256]{1,0:T(8,128)(2,1)S(1)} %copy-done.5, bf16[1024,1024]{1,0:T(8,128)(2,1)S(1)} %collective-permute-done.4.rest_0_.rest_1_, ...), custom_call_target="tpu_custom_call" | custom-call | flops 460000000 | bytes 1048576 | tf_op jit(solution)/shard_map/near/pallas_call | solution.py:341
  52.4 0.6 collective-permute-done.11.arrived_ref.rest_2_
  52.9 0.6 pack.7
  53.5 1.5 %collective-permute-start.18 = (bf16[512,256]{1,0:T(8,128)(2,1)S(1)}, bf16[512,256]{1,0:T(8,128)(2,1)S(1)}, u32[]{:S(2)}, u32[]{:S(2)}) collective-permute-start(bf16[512,256]{1,0:T(8,128)(2,1)S(1)} %get-tuple-element.70), channel_id=1, source_target_pairs={{0,4},{1,5},{2,14},{3,15},{4,8},{5,9},{6,2},{7,3},{8,12},{9,13},{1... | collective-permute-start | bytes 786440 | tf_op jit(solution)/shard_map/ppermute | solution.py:448
  55.1 1.3 %collective-permute-start.19 = (bf16[512,256]{1,0:T(8,128)(2,1)S(1)}, bf16[512,256]{1,0:T(8,128)(2,1)S(1)}, u32[]{:S(2)}, u32[]{:S(2)}) collective-permute-start(bf16[512,256]{1,0:T(8,128)(2,1)S(1)} %get-tuple-element.71), channel_id=1, source_target_pairs={{1,4},{2,15},{5,8},{6,3},{9,12},{10,7},{13,0},{14,11},{17,20},{18,... | collective-permute-start | bytes 786440 | tf_op jit(solution)/shard_map/ppermute | solution.py:448
  56.4 0.5 couple.1
  56.8 0.0 collective-permute-done.16.refs_0_.rest_4_
  56.8 4.1 %collective-permute-start.8 = (bf16[64,1024]{1,0:T(8,128)(2,1)S(1)}, bf16[64,1024]{1,0:T(8,128)(2,1)S(1)}, u32[]{:S(2)}, u32[]{:S(2)}) collective-permute-start(bf16[64,1024]{1,0:T(8,128)(2,1)S(1)} %get-tuple-element.53), channel_id=1, source_target_pairs={{0,2},{1,3},{2,0},{3,1},{4,6},{5,7},{6,4},{7,5},{8,10},{9,11},{10,... | collective-permute-start | bytes 393224 | tf_op jit(solution)/shard_map/ppermute | solution.py:448
  60.9 0.0 collective-permute-done.21.refs_1_.rest_5_
  60.9 0.0 collective-permute-start.17
  60.9 0.0 collective-permute-done.20.rest_3_
  61.0 3.1 %near.5.rest_2_ = f32[1024,256]{1,0:T(8,128)S(1)} custom-call(s32[4,12]{1,0:T(4,128)S(1)} %copy-done.6, bf16[4,12,256,256]{3,2,1,0:T(8,128)(2,1)S(1)} %bitcast.3, bf16[1152,256]{1,0:T(8,128)(2,1)} %get-tuple-element.44.rest_0_, bf16[1024,1024]{1,0:T(8,128)(2,1)S(1)} %collective-permute-done.4.rest_0_.rest_1_, ...), custom_call_target="tpu_custom_call" | custom-call | flops 460000000 | bytes 1048576 | tf_op jit(solution)/shard_map/near/pallas_call | solution.py:341
  64.0 0.0 collective-permute-done.8.partner_sum_ref
  64.0 1.5 %finish.1.rest_7_ = bf16[1024,1024]{1,0:T(8,128)(2,1)} custom-call(f32[64,1024]{1,0:T(8,128)S(1)} %get-tuple-element.52.own_sum_ref, bf16[64,1024]{1,0:T(8,128)(2,1)S(1)} %collective-permute-done.8.partner_sum_ref, bf16[4,256,192]{2,1,0:T(8,128)(2,1)S(1)} %get-tuple-element.48.rest_1_.down_ref, f32[1024,256]{1,0:T(8,128)S(1)} %near.3.rest_0_.rest_6_, ...), custom_call_target="tpu_custom_call" | custom-call | flops 460000000 | bytes 1048576 | tf_op jit(solution)/shard_map/finish/pallas_call | solution.py:415
  65.5 0.0 collective-permute-done.18.refs_0_.rest_4_
  65.5 1.2 %collective-permute-done.19.refs_1_.rest_5_ = bf16[512,256]{1,0:T(8,128)(2,1)S(1)} collective-permute-done((bf16[512,256]{1,0:T(8,128)(2,1)S(1)}, bf16[512,256]{1,0:T(8,128)(2,1)S(1)}, u32[]{:S(2)}, u32[]{:S(2)}) %collective-permute-start.19) | collective-permute-done | bytes 262176 | tf_op jit(solution)/shard_map/ppermute | solution.py:448
  66.8 0.0 collective-permute-done.17.rest_3_
  66.8 3.4 %last.1 = bf16[1024,1024]{1,0:T(8,128)(2,1)} custom-call(s32[4,12]{1,0:T(4,128)S(1)} %copy-done.6, bf16[4,12,256,256]{3,2,1,0:T(8,128)(2,1)S(1)} %bitcast.3, f32[64,1024]{1,0:T(8,128)S(1)} %get-tuple-element.52.own_sum_ref, bf16[64,1024]{1,0:T(8,128)(2,1)S(1)} %collective-permute-done.8.partner_sum_ref, ...), custom_call_target="tpu_custom_call", output_to_operand_aliasing={{}: (12, {})} | custom-call | flops 1150000000 | bytes 1048576 | tf_op jit(solution)/shard_map/last/pallas_call | solution.py:374
  (29 shorter events, 0.1 us)
Async XLA Ops:
  0.0 20.6 %collective-permute-start.4 = (bf16[1024,1024]{1,0:T(8,128)(2,1)}, bf16[1024,1024]{1,0:T(8,128)(2,1)S(1)}, u32[]{:S(2)}, u32[]{:S(2)}) collective-permute-start(bf16[1024,1024]{1,0:T(8,128)(2,1)} %refs_5_.1), channel_id=1, source_target_pairs={{0,1},{1,0},{2,3},{3,2},{4,5},{5,4},{6,7},{7,6},{8,9},{9,8},{10,11... | collective-permute-start | bytes 6291464 | tf_op jit(solution)/shard_map/ppermute | solution.py:448
  1.5 2.6 %copy-start = (bf16[1024,256]{1,0:T(8,128)(2,1)}, bf16[1024,256]{1,0:T(8,128)(2,1)S(1)}, u32[]{:S(2)}) copy-start(bf16[1024,256]{1,0:T(8,128)(2,1)S(1)} %slice.3.refs_6_.rest_0_) | copy-start | bytes 1572868
  1.5 19.0 %collective-permute-start.1 = (bf16[1024,256]{1,0:T(8,128)(2,1)S(1)}, bf16[1024,256]{1,0:T(8,128)(2,1)S(1)}, u32[]{:S(2)}, u32[]{:S(2)}) collective-permute-start(bf16[1024,256]{1,0:T(8,128)(2,1)S(1)} %slice.3.refs_6_.rest_0_), channel_id=1, source_target_pairs={{0,2},{1,3},{2,0},{3,1},{4,6},{5,7},{6,4},{7,5},{8,10},{9,11},{10,... | collective-permute-start | bytes 1572872 | tf_op jit(solution)/shard_map/ppermute | solution.py:448
  4.1 12.9 %copy-start.7 = (bf16[4,64,256]{2,1,0:T(8,128)(2,1)S(1)}, bf16[4,64,256]{2,1,0:T(8,128)(2,1)}, u32[]{:S(2)}) copy-start(bf16[4,64,256]{2,1,0:T(8,128)(2,1)} %target_ref.1) | copy-start | bytes 393220
  4.1 12.9 %copy-start.8 = (bf16[1,6,64,64]{3,2,1,0:T(8,128)(2,1)S(1)}, bf16[1,6,64,64]{3,2,1,0:T(8,128)(2,1)}, u32[]{:S(2)}) copy-start(bf16[1,6,64,64]{3,2,1,0:T(8,128)(2,1)} %param.18) | copy-start | bytes 147460
  4.1 12.9 %copy-start.9 = (bf16[4,64,64]{2,1,0:T(8,128)(2,1)S(1)}, bf16[4,64,64]{2,1,0:T(8,128)(2,1)}, u32[]{:S(2)}) copy-start(bf16[4,64,64]{2,1,0:T(8,128)(2,1)} %leaf_ref.1) | copy-start | bytes 98308
  4.1 12.9 %copy-start.10 = (bf16[2,64,64]{2,1,0:T(8,128)(2,1)S(1)}, bf16[2,64,64]{2,1,0:T(8,128)(2,1)}, u32[]{:S(2)}) copy-start(bf16[2,64,64]{2,1,0:T(8,128)(2,1)} %mid_ref.1) | copy-start | bytes 49156
  4.1 12.9 %copy-start.11 = (s32[1,6]{1,0:T(1,128)S(1)}, s32[1,6]{1,0:T(1,128)}, u32[]{:S(2)}) copy-start(s32[1,6]{1,0:T(1,128)} %far_ref.1) | copy-start | bytes 76
  7.7 8.6 %collective-permute-start.2 = (bf16[80,1024]{1,0:T(8,128)(2,1)}, bf16[80,1024]{1,0:T(8,128)(2,1)S(1)}, u32[]{:S(2)}, u32[]{:S(2)}) collective-permute-start(bf16[80,1024]{1,0:T(8,128)(2,1)} %get-tuple-element.45.rest_1_.panel_ref.rest_0_), channel_id=1, source_target_pairs={{0,12},{1,13},{2,14},{3,15},{4,0},{5,1},{6,2},{7,3},{8,4},{9,5},{1... | collective-permute-start | bytes 491528 | tf_op jit(solution)/shard_map/ppermute | solution.py:448
  11.4 9.2 %collective-permute-start.3 = (bf16[80,1024]{1,0:T(8,128)(2,1)}, bf16[80,1024]{1,0:T(8,128)(2,1)S(1)}, u32[]{:S(2)}, u32[]{:S(2)}) collective-permute-start(bf16[80,1024]{1,0:T(8,128)(2,1)} %get-tuple-element.45.rest_1_.panel_ref.rest_0_), channel_id=1, source_target_pairs={{0,4},{1,5},{2,6},{3,7},{4,8},{5,9},{6,10},{7,11},{8,12},{9,13},{1... | collective-permute-start | bytes 491528 | tf_op jit(solution)/shard_map/ppermute | solution.py:448
  11.4 13.1 %collective-permute-start.6 = (bf16[64,1024]{1,0:T(8,128)(2,1)}, bf16[64,1024]{1,0:T(8,128)(2,1)S(1)}, u32[]{:S(2)}, u32[]{:S(2)}) collective-permute-start(bf16[64,1024]{1,0:T(8,128)(2,1)} %get-tuple-element.50), channel_id=1, source_target_pairs={{0,8},{1,9},{2,10},{3,11},{4,12},{5,13},{6,14},{7,15},{8,0},{9,1},... | collective-permute-start | bytes 393224 | tf_op jit(solution)/shard_map/ppermute | solution.py:448
  16.3 13.2 %collective-permute-start.9 = (bf16[1024,256]{1,0:T(8,128)(2,1)}, bf16[1024,256]{1,0:T(8,128)(2,1)S(1)}, u32[]{:S(2)}, u32[]{:S(2)}) collective-permute-start(bf16[1024,256]{1,0:T(8,128)(2,1)} %get-tuple-element.55.rest_0_), channel_id=1, source_target_pairs={{0,2},{1,3},{2,0},{3,1},{4,6},{5,7},{6,4},{7,5},{8,10},{9,11},{10,... | collective-permute-start | bytes 1572872 | tf_op jit(solution)/shard_map/ppermute | solution.py:448
  17.0 0.9 %copy-start.2 = (bf16[80,1024]{1,0:T(8,128)(2,1)S(1)}, bf16[80,1024]{1,0:T(8,128)(2,1)}, u32[]{:S(2)}) copy-start(bf16[80,1024]{1,0:T(8,128)(2,1)} %get-tuple-element.45.rest_1_.panel_ref.rest_0_) | copy-start | bytes 491524
  20.6 1.3 %collective-permute-start.5 = (bf16[32,768]{1,0:T(8,128)(2,1)S(1)}, bf16[32,768]{1,0:T(8,128)(2,1)S(1)}, u32[]{:S(2)}, u32[]{:S(2)}) collective-permute-start(bf16[32,768]{1,0:T(8,128)(2,1)S(1)} %ask.1.asked_ref), channel_id=1, source_target_pairs={{0,1},{1,0},{2,3},{3,2},{4,5},{5,4},{6,7},{7,6},{8,9},{9,8},{10,11... | collective-permute-start | bytes 147464 | tf_op jit(solution)/shard_map/ppermute | solution.py:448
  24.5 16.3 %slice-start = ((s8[6291456]{0:T(1024)(128)(4,1)}), s8[4194304]{0:T(1024)(128)(4,1)S(1)}, s32[]{:S(2)}) async-start(s8[6291456]{0:T(1024)(128)(4,1)} %bitcast.2), calls=%async_computation | async-start | bytes 8388608
  25.1 15.5 %collective-permute-start.7 = (bf16[1536,256]{1,0:T(8,128)(2,1)S(1)}, bf16[1536,256]{1,0:T(8,128)(2,1)S(1)}, u32[]{:S(2)}, u32[]{:S(2)}) collective-permute-start(bf16[1536,256]{1,0:T(8,128)(2,1)S(1)} %get-tuple-element.51), channel_id=1, source_target_pairs={{0,1},{1,0},{2,3},{3,2},{4,5},{5,4},{6,7},{7,6},{8,9},{9,8},{10,11... | collective-permute-start | bytes 2359304 | tf_op jit(solution)/shard_map/ppermute | solution.py:448
  25.2 18.2 %collective-permute-start = (bf16[1152,256]{1,0:T(8,128)(2,1)}, bf16[1152,256]{1,0:T(8,128)(2,1)S(1)}, u32[]{:S(2)}, u32[]{:S(2)}) collective-permute-start(bf16[1152,256]{1,0:T(8,128)(2,1)} %get-tuple-element.44.rest_0_), channel_id=1, source_target_pairs={{0,2},{1,3},{2,0},{3,1},{4,6},{5,7},{6,4},{7,5},{8,10},{9,11},{10,... | collective-permute-start | bytes 1769480 | tf_op jit(solution)/shard_map/ppermute | solution.py:448
  26.3 10.9 %collective-permute-start.10 = (bf16[512,256]{1,0:T(8,128)(2,1)S(1)}, bf16[512,256]{1,0:T(8,128)(2,1)S(1)}, u32[]{:S(2)}, u32[]{:S(2)}) collective-permute-start(bf16[512,256]{1,0:T(8,128)(2,1)S(1)} %get-tuple-element.57), channel_id=1, source_target_pairs={{0,4},{1,5},{2,14},{3,15},{4,8},{5,9},{6,2},{7,3},{8,12},{9,13},{1... | collective-permute-start | bytes 786440 | tf_op jit(solution)/shard_map/ppermute | solution.py:448
  26.3 10.9 %copy-start.4 = (bf16[1024,256]{1,0:T(8,128)(2,1)S(1)}, bf16[1024,256]{1,0:T(8,128)(2,1)}, u32[]{:S(2)}) copy-start(bf16[1024,256]{1,0:T(8,128)(2,1)} %get-tuple-element.59.rest_0_) | copy-start | bytes 1572868
  26.3 14.5 %slice-start.1 = ((s8[6291456]{0:T(1024)(128)(4,1)}), s8[2097152]{0:T(1024)(128)(4,1)S(1)}, s32[]{:S(2)}) async-start(s8[6291456]{0:T(1024)(128)(4,1)} %bitcast.2), calls=%async_computation.1 | async-start | bytes 4194304
  26.3 13.0 %collective-permute-start.13 = (bf16[512,256]{1,0:T(8,128)(2,1)S(1)}, bf16[512,256]{1,0:T(8,128)(2,1)S(1)}, u32[]{:S(2)}, u32[]{:S(2)}) collective-permute-start(bf16[512,256]{1,0:T(8,128)(2,1)S(1)} %get-tuple-element.62), channel_id=1, source_target_pairs={{1,4},{2,15},{5,8},{6,3},{9,12},{10,7},{13,0},{14,11},{17,20},{18,... | collective-permute-start | bytes 786440 | tf_op jit(solution)/shard_map/ppermute | solution.py:448
  37.2 15.7 %collective-permute-start.11 = (bf16[1024,256]{1,0:T(8,128)(2,1)S(1)}, bf16[1024,256]{1,0:T(8,128)(2,1)S(1)}, u32[]{:S(2)}, u32[]{:S(2)}) collective-permute-start(bf16[1024,256]{1,0:T(8,128)(2,1)S(1)} %copy-done.4), channel_id=1, source_target_pairs={{0,2},{1,3},{2,0},{3,1},{4,6},{5,7},{6,4},{7,5},{8,10},{9,11},{10,... | collective-permute-start | bytes 1572872 | tf_op jit(solution)/shard_map/ppermute | solution.py:448
  37.2 9.6 %collective-permute-start.14 = (bf16[512,256]{1,0:T(8,128)(2,1)S(1)}, bf16[512,256]{1,0:T(8,128)(2,1)S(1)}, u32[]{:S(2)}, u32[]{:S(2)}) collective-permute-start(bf16[512,256]{1,0:T(8,128)(2,1)S(1)} %get-tuple-element.64), channel_id=1, source_target_pairs={{0,4},{1,5},{2,14},{3,15},{4,8},{5,9},{6,2},{7,3},{8,12},{9,13},{1... | collective-permute-start | bytes 786440 | tf_op jit(solution)/shard_map/ppermute | solution.py:448
  39.2 1.5 %copy-start.1 = (bf16[1024,256]{1,0:T(8,128)(2,1)S(1)}, bf16[1024,256]{1,0:T(8,128)(2,1)}, u32[]{:S(2)}) copy-start(bf16[1024,256]{1,0:T(8,128)(2,1)} %copy-done) | copy-start | bytes 1572868
  39.2 1.6 %copy-start.6 = (s32[4,12]{1,0:T(4,128)S(1)}, s32[4,12]{1,0:T(4,128)}, u32[]{:S(2)}) copy-start(s32[4,12]{1,0:T(4,128)} %get-tuple-element.40.entry_ref) | copy-start | bytes 580
  39.2 9.6 %collective-permute-start.15 = (bf16[512,256]{1,0:T(8,128)(2,1)S(1)}, bf16[512,256]{1,0:T(8,128)(2,1)S(1)}, u32[]{:S(2)}, u32[]{:S(2)}) collective-permute-start(bf16[512,256]{1,0:T(8,128)(2,1)S(1)} %get-tuple-element.66), channel_id=1, source_target_pairs={{1,4},{2,15},{5,8},{6,3},{9,12},{10,7},{13,0},{14,11},{17,20},{18,... | collective-permute-start | bytes 786440 | tf_op jit(solution)/shard_map/ppermute | solution.py:448
  40.7 9.1 %collective-permute-start.12 = (bf16[512,256]{1,0:T(8,128)(2,1)S(1)}, bf16[512,256]{1,0:T(8,128)(2,1)S(1)}, u32[]{:S(2)}, u32[]{:S(2)}) collective-permute-start(bf16[512,256]{1,0:T(8,128)(2,1)S(1)} %get-tuple-element.60), channel_id=1, source_target_pairs={{0,1},{1,0},{2,3},{3,2},{4,5},{5,4},{6,7},{7,6},{8,9},{9,8},{10,11... | collective-permute-start | bytes 786440 | tf_op jit(solution)/shard_map/ppermute | solution.py:448
  44.0 12.9 %collective-permute-start.16 = (bf16[512,256]{1,0:T(8,128)(2,1)S(1)}, bf16[512,256]{1,0:T(8,128)(2,1)S(1)}, u32[]{:S(2)}, u32[]{:S(2)}) collective-permute-start(bf16[512,256]{1,0:T(8,128)(2,1)S(1)} %get-tuple-element.68), channel_id=1, source_target_pairs={{0,4},{1,5},{2,14},{3,15},{4,8},{5,9},{6,2},{7,3},{8,12},{9,13},{1... | collective-permute-start | bytes 786440 | tf_op jit(solution)/shard_map/ppermute | solution.py:448
  46.8 14.2 %collective-permute-start.21 = (bf16[512,256]{1,0:T(8,128)(2,1)S(1)}, bf16[512,256]{1,0:T(8,128)(2,1)S(1)}, u32[]{:S(2)}, u32[]{:S(2)}) collective-permute-start(bf16[512,256]{1,0:T(8,128)(2,1)S(1)} %get-tuple-element.74), channel_id=1, source_target_pairs={{1,4},{2,15},{5,8},{6,3},{9,12},{10,7},{13,0},{14,11},{17,20},{18,... | collective-permute-start | bytes 786440 | tf_op jit(solution)/shard_map/ppermute | solution.py:448
  48.0 1.7 %copy-start.5 = (bf16[1024,256]{1,0:T(8,128)(2,1)S(1)}, bf16[1024,256]{1,0:T(8,128)(2,1)}, u32[]{:S(2)}) copy-start(bf16[1024,256]{1,0:T(8,128)(2,1)} %get-tuple-element.55.rest_0_) | copy-start | bytes 1572868
  48.9 12.1 %collective-permute-start.20 = (bf16[512,256]{1,0:T(8,128)(2,1)S(1)}, bf16[512,256]{1,0:T(8,128)(2,1)S(1)}, u32[]{:S(2)}, u32[]{:S(2)}) collective-permute-start(bf16[512,256]{1,0:T(8,128)(2,1)S(1)} %get-tuple-element.72), channel_id=1, source_target_pairs={{0,1},{1,0},{2,3},{3,2},{4,5},{5,4},{6,7},{7,6},{8,9},{9,8},{10,11... | collective-permute-start | bytes 786440 | tf_op jit(solution)/shard_map/ppermute | solution.py:448
  49.8 6.6 %copy-start.3 = (bf16[80,1024]{1,0:T(8,128)(2,1)S(1)}, bf16[80,1024]{1,0:T(8,128)(2,1)}, u32[]{:S(2)}) copy-start(bf16[80,1024]{1,0:T(8,128)(2,1)} %get-tuple-element.45.rest_1_.panel_ref.rest_0_) | copy-start | bytes 491524
  53.5 12.0 %collective-permute-start.18 = (bf16[512,256]{1,0:T(8,128)(2,1)S(1)}, bf16[512,256]{1,0:T(8,128)(2,1)S(1)}, u32[]{:S(2)}, u32[]{:S(2)}) collective-permute-start(bf16[512,256]{1,0:T(8,128)(2,1)S(1)} %get-tuple-element.70), channel_id=1, source_target_pairs={{0,4},{1,5},{2,14},{3,15},{4,8},{5,9},{6,2},{7,3},{8,12},{9,13},{1... | collective-permute-start | bytes 786440 | tf_op jit(solution)/shard_map/ppermute | solution.py:448
  55.1 11.7 %collective-permute-start.19 = (bf16[512,256]{1,0:T(8,128)(2,1)S(1)}, bf16[512,256]{1,0:T(8,128)(2,1)S(1)}, u32[]{:S(2)}, u32[]{:S(2)}) collective-permute-start(bf16[512,256]{1,0:T(8,128)(2,1)S(1)} %get-tuple-element.71), channel_id=1, source_target_pairs={{1,4},{2,15},{5,8},{6,3},{9,12},{10,7},{13,0},{14,11},{17,20},{18,... | collective-permute-start | bytes 786440 | tf_op jit(solution)/shard_map/ppermute | solution.py:448
  56.8 7.2 %collective-permute-start.8 = (bf16[64,1024]{1,0:T(8,128)(2,1)S(1)}, bf16[64,1024]{1,0:T(8,128)(2,1)S(1)}, u32[]{:S(2)}, u32[]{:S(2)}) collective-permute-start(bf16[64,1024]{1,0:T(8,128)(2,1)S(1)} %get-tuple-element.53), channel_id=1, source_target_pairs={{0,2},{1,3},{2,0},{3,1},{4,6},{5,7},{6,4},{7,5},{8,10},{9,11},{10,... | collective-permute-start | bytes 393224 | tf_op jit(solution)/shard_map/ppermute | solution.py:448
  60.9 5.9 %collective-permute-start.17 = (bf16[512,256]{1,0:T(8,128)(2,1)S(1)}, bf16[512,256]{1,0:T(8,128)(2,1)S(1)}, u32[]{:S(2)}, u32[]{:S(2)}) collective-permute-start(bf16[512,256]{1,0:T(8,128)(2,1)S(1)} %get-tuple-element.69), channel_id=1, source_target_pairs={{0,1},{1,0},{2,3},{3,2},{4,5},{5,4},{6,7},{7,6},{8,9},{9,8},{10,11... | collective-permute-start | bytes 786440 | tf_op jit(solution)/shard_map/ppermute | solution.py:448
